TPU v7x, 128 devices: a whole 4x4x4 slice. The times are simulated.
128 devices in a mesh: ctx: 16 (over z, y), pool: 2 (over x_hi), tp: 4 (over x_lo, core).
Axes of the slice: x: 4 (x_hi: 2, x_lo: 2; x = x_hi * 2 + x_lo), y: 4, z: 4, core: 2. Of those that a mesh axis runs over, the one named last changes fastest.
Arguments:
- span_hidden_states: bfloat16 [4096, 8192], P(('ctx', 'pool'), 'tp'), may hold values from -6 to 6
- span_token_queries: bfloat16 [4096, 8192], P(('ctx', 'pool'), 'tp'), as said below
- earlier_key_values: bfloat16 [8, 4096, 256], P('tp', ('ctx', 'pool')), as said below
- decode_hidden_states: bfloat16 [512, 4, 8192], P(('ctx', 'pool'), None, 'tp'), may hold values from -6 to 6
- decode_token_queries: bfloat16 [512, 4, 8192], P(('ctx', 'pool'), None, 'tp'), as said below
- decode_row_cache: bfloat16 [512, 8, 256, 256], P(('ctx', 'pool'), 'tp'), as said below
- key_value_weight: bfloat16 [8192, 2048], P('tp'), may hold values from -0.0625 to 0.0625
- adapter_down_weight: bfloat16 [8192, 128], P('tp'), may hold values from -0.0625 to 0.0625
- adapter_up_weight: bfloat16 [128, 2048], replicated, may hold values from -1.5 to 1.5
- prompt_adapter: int32 [4096], P(('ctx', 'pool')), may hold values from 0 to 7
- row_adapter_index: int32 [512], P(('ctx', 'pool')), may hold values from 0 to 7
- group_live_rows: int32 [32], P(('ctx', 'pool')), may hold values from 1 to 16, as said below
- cached_row_lengths: int32 [512], P(('ctx', 'pool')), may hold values from 2 to 256, as said below
- block_target_page: int32 [256], replicated, may hold values from 0 to 255, each once
Outputs:
- span_attention: bfloat16 [4096, 8192], P(('ctx', 'pool'), 'tp')
- handoff_pages: bfloat16 [256, 8, 16, 256], P(('ctx', 'pool'), 'tp')
- decode_attention: bfloat16 [512, 4, 8192], P(('ctx', 'pool'), None, 'tp')
Inputs may be any that keep to these rules, and one draw needn't show every extreme that they name: `span_token_queries`: queries of the span. `earlier_key_values`: keys and values of the earlier tokens. `decode_token_queries`: queries of the decode tokens. `decode_row_cache`: cached keys and values; slots at or past a row's length are never read. `group_live_rows`: live rows of each group of 16 slots are its first ones; some group is full. `cached_row_lengths`: some row uses all 256 slots.
All inputs are finite; a program needn't handle non-finite values.
Results may differ from a plain program's by a relative error of at most 0.0081.
Values may be sent and summed in bfloat16 or wider, within the bound.
No kernel may reach another device: no remote copies, remote signals or barrier semaphores. Data moves between devices by JAX's collectives and lax.ppermute only.
A program may use at most 192 MiB of HBM per device.

v0:
```python
import math

import jax
import jax.numpy as jnp
from jax import lax
from jax.sharding import PartitionSpec as P

HQ = 64
KEY_VALUE_HEADS = 8
HEAD_SIZE = 128
ADAPTER_RANK = 16
BLK = 16


neg_large = -1e30


def absorb(softmax_state, scores, visible, values, einsum_form):
    running_max, running_sum, numerator = softmax_state
    masked_scores = jnp.where(visible, scores, neg_large)
    new_max = jnp.maximum(running_max, jnp.max(masked_scores, axis=-1))
    weights = jnp.where(visible, jnp.exp(masked_scores - new_max[..., None]), 0.0)
    rescale = jnp.exp(running_max - new_max)
    running_sum = running_sum * rescale + jnp.sum(weights, axis=-1)
    numerator = numerator * rescale[..., None] + jnp.einsum(
        einsum_form, weights.astype(jnp.bfloat16), values, preferred_element_type=jnp.float32
    )
    return (new_max, running_sum, numerator)


def fresh_state(lead_shape, head_dim):
    return (
        jnp.full(lead_shape, neg_large, jnp.float32),
        jnp.zeros(lead_shape, jnp.float32),
        jnp.zeros(lead_shape + (head_dim,), jnp.float32),
    )


def finish(softmax_state):
    return softmax_state[2] / softmax_state[1][..., None]


def pick_pages(page_rows, piece_kv, wanted):
    length = piece_kv.shape[1]
    inside = (wanted >= 0) & (wanted < length)
    taken_rows = jnp.take(piece_kv, jnp.clip(wanted, 0, length - 1), axis=1)
    return jnp.where(inside[None, :, None], taken_rows, page_rows)


def per_device(
    span_hidden_states,
    span_token_queries,
    earlier_key_values,
    decode_hidden_states,
    decode_token_queries,
    decode_row_cache,
    key_value_weight,
    adapter_down_weight,
    adapter_up_weight,
    prompt_adapter,
    row_adapter_index,
    group_live_rows,
    cached_row_lengths,
    block_target_page,
):
    token_count = span_hidden_states.shape[0]
    row_count = decode_hidden_states.shape[0]
    step_count = decode_hidden_states.shape[1]
    feature_local = span_hidden_states.shape[1]
    head_local = earlier_key_values.shape[0]
    prior_local = earlier_key_values.shape[1]
    cache_size = decode_row_cache.shape[2]
    group_size = HQ // KEY_VALUE_HEADS
    scale_factor = 1.0 / math.sqrt(HEAD_SIZE)
    tp_index = lax.axis_index("tp")
    shard_index = lax.axis_index(("ctx", "pool"))
    stacked_values = jnp.concatenate(
        [span_hidden_states, decode_hidden_states.reshape(row_count * step_count, feature_local)],
        axis=0,
    )
    adapter_indices = jnp.concatenate([prompt_adapter, jnp.repeat(row_adapter_index, step_count)])
    column_holder = jnp.arange(adapter_down_weight.shape[1], dtype=jnp.int32) // ADAPTER_RANK
    selected = column_holder[None, :] == adapter_indices[:, None]
    partial_rank_sums = jnp.dot(
        stacked_values, adapter_down_weight, preferred_element_type=jnp.float32
    )
    weight_heads = key_value_weight.reshape(feature_local, KEY_VALUE_HEADS, 2 * HEAD_SIZE)
    up_weight_heads = adapter_up_weight.reshape(
        adapter_up_weight.shape[0], KEY_VALUE_HEADS, 2 * HEAD_SIZE
    ).astype(jnp.float32)
    narrow_rank = lax.psum(partial_rank_sums, "tp")
    masked_scores = jnp.where(selected, narrow_rank, 0.0)
    base_sum = lax.psum_scatter(
        jnp.einsum("nd,dhc->hnc", stacked_values, weight_heads, preferred_element_type=jnp.float32),
        "tp",
        scatter_dimension=0,
        tiled=True,
    )
    own_up = lax.dynamic_slice_in_dim(up_weight_heads, tp_index * head_local, head_local, 1)
    own_kv = base_sum + jnp.einsum(
        "nr,rhc->hnc", masked_scores, own_up, precision=lax.Precision.HIGHEST
    )
    own_kv = own_kv.astype(jnp.bfloat16)
    span_key_values = own_kv[:, :token_count]
    newest_key_values = own_kv[:, token_count:].reshape(
        head_local, row_count, step_count, 2 * HEAD_SIZE
    )
    queries = span_token_queries.reshape(token_count, head_local, group_size, HEAD_SIZE)
    local_keys = jnp.concatenate([earlier_key_values, span_key_values], axis=1)
    stride = prior_local + token_count
    query_pos = shard_index * token_count + jnp.arange(token_count, dtype=jnp.int32)
    initial = fresh_state((token_count, head_local, group_size), HEAD_SIZE)
    pages_local = token_count // BLK
    page_ids = shard_index * pages_local + jnp.arange(pages_local, dtype=jnp.int32)
    block_ids = jnp.arange(block_target_page.shape[0], dtype=jnp.int32)
    source_block = jnp.sum(
        jnp.where(block_target_page[None, :] == page_ids[:, None], block_ids[None, :], 0), axis=1
    )
    wanted_tokens = (
        source_block[:, None] * BLK + jnp.arange(BLK, dtype=jnp.int32)[None, :]
    ).reshape(pages_local * BLK)
    empty_pages = jnp.zeros((head_local, pages_local * BLK, 2 * HEAD_SIZE), jnp.bfloat16)
    piece_kv = lax.all_gather(local_keys, ("ctx", "pool"), axis=1, tiled=True)
    key_row = jnp.arange(piece_kv.shape[1], dtype=jnp.int32)
    within = key_row % stride
    key_pos = key_row // stride * token_count + within - prior_local
    visible = (within < prior_local)[None, :] | (key_pos[None, :] <= query_pos[:, None])
    scores = (
        jnp.einsum(
            "thgc,hnc->thgn",
            queries,
            piece_kv[:, :, :HEAD_SIZE],
            preferred_element_type=jnp.float32,
        )
        * scale_factor
    )
    softmax_state = absorb(
        initial, scores, visible[:, None, None, :], piece_kv[:, :, HEAD_SIZE:], "thgn,hnc->thgc"
    )
    page_rows = pick_pages(
        empty_pages,
        lax.all_gather(span_key_values, ("ctx", "pool"), axis=1, tiled=True),
        wanted_tokens,
    )
    span_attention = (
        finish(softmax_state)
        .reshape(token_count, head_local * group_size * HEAD_SIZE)
        .astype(jnp.bfloat16)
    )
    handoff_pages = jnp.transpose(
        page_rows.reshape(head_local, pages_local, BLK, 2 * HEAD_SIZE), (1, 0, 2, 3)
    )
    dec_queries = decode_token_queries.reshape(
        row_count, step_count, head_local, group_size, HEAD_SIZE
    )
    sweep = cache_size // 4
    decode_state = fresh_state((row_count, step_count, head_local, group_size), HEAD_SIZE)
    for block_index in range(4):
        first_slot = block_index * sweep
        block_kv = lax.dynamic_slice_in_dim(decode_row_cache, first_slot, sweep, 2)
        absorb_scores = (
            jnp.einsum(
                "rshgc,rhnc->rshgn",
                dec_queries,
                block_kv[..., :HEAD_SIZE],
                preferred_element_type=jnp.float32,
            )
            * scale_factor
        )
        slot_pos = first_slot + jnp.arange(sweep, dtype=jnp.int32)
        absorb_visible = slot_pos[None, :] < cached_row_lengths[:, None]
        decode_state = absorb(
            decode_state,
            absorb_scores,
            absorb_visible[:, None, None, None, :],
            block_kv[..., HEAD_SIZE:],
            "rshgn,rhnc->rshgc",
        )
    fresh_scores = (
        jnp.einsum(
            "rshgc,hrtc->rshgt",
            dec_queries,
            newest_key_values[..., :HEAD_SIZE],
            preferred_element_type=jnp.float32,
        )
        * scale_factor
    )
    step_index = jnp.arange(step_count, dtype=jnp.int32)
    fresh_visible = step_index[None, :] <= step_index[:, None]
    decode_state = absorb(
        decode_state,
        fresh_scores,
        fresh_visible[None, :, None, None, :],
        newest_key_values[..., HEAD_SIZE:],
        "rshgt,hrtc->rshgc",
    )
    live_rows = jnp.arange(row_count, dtype=jnp.int32) < group_live_rows[0]
    decoded = jnp.where(live_rows[:, None, None, None, None], finish(decode_state), 0.0)
    decode_attention = decoded.reshape(
        row_count, step_count, head_local * group_size * HEAD_SIZE
    ).astype(jnp.bfloat16)
    return (span_attention, handoff_pages, decode_attention)


def solution(mesh):
    in_specs = (
        P(("ctx", "pool"), "tp"),
        P(("ctx", "pool"), "tp"),
        P("tp", ("ctx", "pool"), None),
        P(("ctx", "pool"), None, "tp"),
        P(("ctx", "pool"), None, "tp"),
        P(("ctx", "pool"), "tp", None, None),
        P("tp", None),
        P("tp", None),
        P(),
        P(("ctx", "pool")),
        P(("ctx", "pool")),
        P(("ctx", "pool")),
        P(("ctx", "pool")),
        P(),
    )
    out_specs = (
        P(("ctx", "pool"), "tp"),
        P(("ctx", "pool"), "tp", None, None),
        P(("ctx", "pool"), None, "tp"),
    )
    return jax.shard_map(
        per_device, mesh=mesh, in_specs=in_specs, out_specs=out_specs, check_vma=False
    )
```

profile of v0, /device:TPU:0, one launch (start us, length us, event | category | flops | bytes accessed | tf_op | source)
XLA Modules:
  0.0 349.6 jit_solution(646034327332463133)
XLA Ops:
  7.2 1.1 constant_dynamic-update-slice_fusion.1
  10.6 6.4 %fusion.10 = f32[8,192,256]{2,1,0:T(8,128)} fusion(bf16[256,8,8,256]{3,2,1,0:T(8,128)(2,1)} %bitcast.190, bf16[192,2048]{1,0:T(8,128)(2,1)S(1)} %constant_dynamic-update-slice_fusion), kind=kOutput, calls=%fused_computation.15 | convolution fusion | flops 1610612736 | bytes 10747904 | tf_op jit(solution)/shard_map/nd,dhc->hnc/dot_general | solution.py:94
  17.6 31.4 %all-reduce.2.cloned.1.call-done = f32[192,128]{1,0:T(8,128)} async-done(((f32[192,128]{1,0:T(8,128)}), f32[192,128]{1,0:T(8,128)}) %all-reduce.2.cloned.1.call-update) | async-done | bytes 98320 | tf_op jit(solution)/shard_map/psum | solution.py:91
  49.0 27.5 %reduce-scatter.2.cloned.1.call-done = f32[2,192,256]{2,1,0:T(8,128)} async-done(((f32[8,192,256]{2,1,0:T(8,128)}), f32[2,192,256]{2,1,0:T(8,128)}) %reduce-scatter.2.cloned.1.call-update) | async-done | bytes 393232 | tf_op jit(solution)/shard_map/reduce_scatter | solution.py:93
  76.5 1.4 fusion.40
  78.8 1.6 pad_maximum_fusion
  84.4 2.2 fusion.137
  86.6 2.9 fusion.138
  89.5 2.2 fusion.139
  91.7 1.5 fusion.140
  93.2 2.8 compare_or_fusion
  96.0 2.2 fusion.136
  100.2 1.9 fusion.67
  103.1 1.5 convolution_bitcast_fusion.1
  104.6 1.5 convolution_bitcast_fusion.2
  106.1 1.4 convolution_bitcast_fusion.3
  107.5 2.0 fusion.27
  110.8 51.0 %all-gather.5.cloned.1.call-done = bf16[2,4096,256]{2,1,0:T(8,128)(2,1)} async-done(((bf16[2,128,256]{2,1,0:T(8,128)(2,1)}), bf16[2,4096,256]{2,1,0:T(8,128)(2,1)}) %all-gather.5.cloned.1.call-update) | async-done | bytes 4194320 | tf_op jit(solution)/shard_map/all_gather | solution.py:142
  161.8 10.1 %copy.54 = bf16[2,4096,256]{2,0,1:T(2,128)(2,1)} copy(bf16[2,4096,256]{2,1,0:T(8,128)(2,1)} %all-gather.5.cloned.1.call-done) | data formatting | bytes 8388608 | tf_op jit(solution)/shard_map/all_gather | solution.py:142
  171.9 3.2 gather_fusion
  175.9 92.2 %all-gather.3.cloned.1.call-done = bf16[2,8192,256]{2,1,0:T(8,128)(2,1)} async-done(((bf16[2,256,256]{2,1,0:T(8,128)(2,1)}), bf16[2,8192,256]{2,1,0:T(8,128)(2,1)}) %all-gather.3.cloned.1.call-update) | async-done | bytes 8388624 | tf_op jit(solution)/shard_map/all_gather | solution.py:123
  268.0 25.3 %fusion = (f32[128,2,8]{0,2,1:T(8,128)S(1)}, f32[2,8192,128,8]{2,1,3,0:T(8,128)}) fusion(pred[128,8192]{0,1:T(8,128)(4,1)S(1)} %compare_or_fusion, bf16[128,2,8,128]{3,2,1,0:T(8,128)(2,1)S(1)} %bitcast.187, bf16[2,8192,256]{2,1,0:T(8,128)(2,1)} %all-gather.3.cloned.1.call-done), kind=kOutput, calls=%fused_computation.3 | convolution fusion | flops 4345296896 | bytes 72884224 | tf_op jit(solution)/shard_map/thgc,hnc->thgn/dot_general | solution.py:129
  293.3 21.4 %fusion.1 = f32[128,2,8]{0,2,1:T(8,128)S(1)} fusion(f32[2,8192,128,8]{2,1,3,0:T(8,128)} %get-tuple-element.34, f32[128,2,8]{0,2,1:T(8,128)S(1)} %broadcast_maximum_fusion.1, pred[128,8192]{0,1:T(8,128)(4,1)S(1)} %compare_or_fusion), kind=kLoop, calls=%fused_computation.4 | loop fusion | flops 83884032 | bytes 68173824 | tf_op jit(solution)/shard_map/reduce_sum | solution.py:24
  314.8 27.2 %divide_convert_fusion = bf16[128,2,8,128]{0,3,2,1:T(8,128)(2,1)S(1)} fusion(f32[2,8192,128,8]{2,1,3,0:T(8,128)} %get-tuple-element.34, f32[128,2,8]{0,2,1:T(8,128)S(1)} %broadcast_maximum_fusion.1, pred[128,8192]{0,1:T(8,128)(4,1)S(1)} %compare_or_fusion, bf16[2,8192,256]{2,1,0:T(8,128)(2,1)} %all-gather.3.cloned.1.call-done, ...), kind=kOutput, calls=%fused_computation.53 | convolution fusion | flops 4379639808 | bytes 72900608 | tf_op jit(solution)/shard_map/thgn,hnc->thgc/dot_general | solution.py:25
  (78 shorter events, 12.7 us)
Async XLA Ops:
  7.2 2.2 copy-start
  7.2 41.8 %all-reduce.2.cloned.1.call-start = ((), (), s32[]{:S(2)}) async-start(), calls=%async_computation.2 | async-start | bytes 196608 | tf_op jit(solution)/shard_map/psum | solution.py:91
  9.4 7.7 %copy-start.1 = (bf16[128,2048]{1,0:T(8,128)(2,1)S(1)}, bf16[128,2048]{1,0:T(8,128)(2,1)}, u32[]{:S(2)}) copy-start(bf16[128,2048]{1,0:T(8,128)(2,1)} %param.22) | copy-start | bytes 1572868
  10.4 6.9 %copy-start.10 = (s32[16]{0:T(128)S(1)}, s32[16]{0:T(128)}, u32[]{:S(2)}) copy-start(s32[16]{0:T(128)} %param.24) | copy-start | bytes 196
  10.5 7.1 %copy-start.12 = (s32[128]{0:T(128)S(1)}, s32[128]{0:T(128)}, u32[]{:S(2)}) copy-start(s32[128]{0:T(128)} %param.23) | copy-start | bytes 1540
  10.5 66.0 %reduce-scatter.2.cloned.1.call-start = ((), (), s32[]{:S(2)}) async-start(), calls=%async_computation.1 | async-start | bytes 1966080 | tf_op jit(solution)/shard_map/reduce_scatter | solution.py:93
  10.5 68.3 %copy-start.5 = (bf16[2,128,256]{2,1,0:T(8,128)(2,1)S(1)}, bf16[2,128,256]{2,1,0:T(8,128)(2,1)}, u32[]{:S(2)}) copy-start(bf16[2,128,256]{2,1,0:T(8,128)(2,1)} %param.16) | copy-start | bytes 393220
  10.5 70.0 %copy-start.2 = (bf16[128,2048]{1,0:T(8,128)(2,1)S(1)}, bf16[128,2048]{1,0:T(8,128)(2,1)}, u32[]{:S(2)}) copy-start(bf16[128,2048]{1,0:T(8,128)(2,1)} %param.15) | copy-start | bytes 1572868
  10.5 70.1 %copy-start.8 = (s32[256]{0:T(256)S(1)}, s32[256]{0:T(256)}, u32[]{:S(2)}) copy-start(s32[256]{0:T(256)} %param.27) | copy-start | bytes 3076
  10.6 70.5 %copy-start.3 = (bf16[16,4,2048]{2,1,0:T(4,128)(2,1)S(1)}, bf16[16,4,2048]{2,1,0:T(4,128)(2,1)}, u32[]{:S(2)}) copy-start(bf16[16,4,2048]{2,1,0:T(4,128)(2,1)} %param.18) | copy-start | bytes 786436
  10.6 73.7 %copy-start.11 = (s32[16]{0:T(128)S(1)}, s32[16]{0:T(128)}, u32[]{:S(2)}) copy-start(s32[16]{0:T(128)} %param.26) | copy-start | bytes 196
  17.0 144.8 %all-gather.5.cloned.1.call-start = ((), (), s32[]{:S(2)}) async-start(), calls=%async_computation.4 | async-start | bytes 4325376 | tf_op jit(solution)/shard_map/all_gather | solution.py:142
  78.6 189.4 %all-gather.3.cloned.1.call-start = ((), (), s32[]{:S(2)}) async-start(), calls=%async_computation.3 | async-start | bytes 8650752 | tf_op jit(solution)/shard_map/all_gather | solution.py:123
  81.2 10.5 %copy-start.4 = (bf16[16,4,2,8,128]{4,3,2,1,0:T(8,128)(2,1)}, bf16[16,4,2,8,128]{4,3,2,1,0:T(8,128)(2,1)S(1)}, u32[]{:S(2)}) copy-start(bf16[16,4,2,8,128]{4,3,2,1,0:T(8,128)(2,1)S(1)} %reshape.410) | copy-start | bytes 786436
  104.6 4.9 %copy-start.9 = (pred[4,4]{1,0:T(4,128)(4,1)S(1)}, pred[4,4]{1,0:T(4,128)(4,1)}, u32[]{:S(2)}) copy-start(pred[4,4]{1,0:T(4,128)(4,1)} %iota_compare_fusion.1) | copy-start | bytes 52
  104.6 4.9 %copy-start.13 = (pred[16]{0:T(512)(128)(4,1)S(1)}, pred[16]{0:T(512)(128)(4,1)}, u32[]{:S(2)}) copy-start(pred[16]{0:T(512)(128)(4,1)} %iota_compare_fusion.2) | copy-start | bytes 52
  109.5 65.6 %copy-start.6 = (pred[8,16]{1,0:T(8,128)(4,1)S(1)}, pred[8,16]{1,0:T(8,128)(4,1)}, u32[]{:S(2)}) copy-start(pred[8,16]{1,0:T(8,128)(4,1)} %get-tuple-element.31) | copy-start | bytes 388
  109.5 65.6 %copy-start.7 = (pred[8,16]{1,0:T(8,128)(4,1)S(1)}, pred[8,16]{1,0:T(8,128)(4,1)}, u32[]{:S(2)}) copy-start(pred[8,16]{1,0:T(8,128)(4,1)} %get-tuple-element.32) | copy-start | bytes 388
Sparse Core Ops, SparseCore 0:
  11.1 37.9 all-reduce.1
  51.6 24.8 reduce-scatter.1
  80.6 81.0 all-gather.4
  165.2 102.7 all-gather.2
where the time goes:
time: 351 us; the launch traced here: 350 us
  waiting for transfers between devices  202 us (58%)
  matrix products  79.3 us (23%)
  other arithmetic  34.1 us (10%)
  local copies, waits for them, and re-layouts  18.9 us (5%)
  between operations  14.8 us (4%)
    all_gather x1, waiting for transfers between devices, per_device(): piece_kv = lax.all_gather(local_keys, ('ctx', 'pool'), axis=1, tiled=True)  92.2 us
    all_gather x1, waiting for transfers between devices, per_device(): lax.all_gather(span_key_values, ('ctx', 'pool'), axis=1, tiled=True)  51 us
    dot_general x6, matrix products, absorb(): jnp.einsum(einsum_form, weights.astype(jnp.bfloat16), values, preferred_e...  34.1 us
    psum x1, waiting for transfers between devices, per_device(): narrow_rank = lax.psum(partial_rank_sums, 'tp')  31.4 us
    reduce_scatter x1, waiting for transfers between devices, per_device(): lax.psum_scatter(jnp.einsum('nd,dhc->hnc', stacked_values, weight_heads,...  27.5 us
    dot_general x1, matrix products, per_device(): jnp.einsum('thgc,hnc->thgn', queries, piece_kv[:, :, :HEAD_SIZE], preferr...  25.3 us
    reduce_sum x4, other arithmetic, absorb(): running_sum = running_sum * rescale + jnp.sum(weights, axis=-1)  25 us
    all_gather x1, local copies, waits for them, and re-layouts, per_device(): lax.all_gather(span_key_values, ('ctx', 'pool'), axis=1, tiled=True)  10.1 us
  transfers between devices with their start and end apart: 4, of which 4 were waited for; matrix products, arithmetic and copies ran while one was open for 15% of the time, Pallas kernels for 0%

commit v1 on v0

v1 whole, which is shorter than its diff:
```python
import functools
import math

import jax
import jax.numpy as jnp
from jax import lax
from jax.experimental import pallas as pl
from jax.experimental.pallas import tpu as pltpu
from jax.sharding import PartitionSpec as P

HQ = 64
KEY_VALUE_HEADS = 8
HEAD_SIZE = 128
ADAPTER_RANK = 16
BLK = 16
STEPS = 4
GROUP = HQ // KEY_VALUE_HEADS
SHARDS = 16
SIDE = 4
TOKENS = 128
ROWS = 16
DECODE = ROWS * STEPS
ALL_ROWS = TOKENS + DECODE
LOG2_SCALE = math.log2(math.e) / math.sqrt(HEAD_SIZE)
neg_large = -1e30
MIB = 2**20


def split3(x):
    hi = x.astype(jnp.bfloat16)
    rest = x - hi.astype(jnp.float32)
    mid = rest.astype(jnp.bfloat16)
    low = (rest - mid.astype(jnp.float32)).astype(jnp.bfloat16)
    return hi, mid, low


def project_kernel(
    block_ref, row_adapter_ref, span_ref, decode_ref, weight_ref, down_ref, up_ref, adapter_ref, out_ref, rank_ref
):
    hidden = jnp.concatenate([span_ref[...], decode_ref[...]], axis=0)

    @pl.when(pl.program_id(0) == 0)
    def _():
        narrow = jnp.dot(hidden, down_ref[...], preferred_element_type=jnp.float32)
        span_owner = jnp.transpose(jnp.broadcast_to(adapter_ref[...], (TOKENS, TOKENS)))
        row = lax.broadcasted_iota(jnp.int32, (DECODE, TOKENS), 0) // STEPS
        decode_owner = jnp.zeros((DECODE, TOKENS), jnp.int32)
        for r in range(ROWS):
            decode_owner = jnp.where(row == r, row_adapter_ref[r], decode_owner)
        owner = jnp.concatenate([span_owner, decode_owner], axis=0)
        column = lax.broadcasted_iota(jnp.int32, (ALL_ROWS, TOKENS), 1) // ADAPTER_RANK
        hi, mid, low = split3(jnp.where(column == owner, narrow, 0.0))
        rank_ref[:, :TOKENS] = hi
        rank_ref[:, TOKENS : 2 * TOKENS] = mid
        rank_ref[:, 2 * TOKENS :] = low

    up = up_ref[...]
    out_ref[0] = jnp.dot(hidden, weight_ref[...], preferred_element_type=jnp.float32) + jnp.dot(
        rank_ref[...], jnp.concatenate([up, up, up], axis=0), preferred_element_type=jnp.float32
    )


def project(blocks, row_adapter, span, decode, weight, down, up, adapter):
    count = blocks.shape[0]
    depth = span.shape[1]
    width = 2 * HEAD_SIZE
    whole = lambda i, *_: (0, 0)
    return pl.pallas_call(
        project_kernel,
        grid_spec=pltpu.PrefetchScalarGridSpec(
            num_scalar_prefetch=2,
            grid=(count,),
            in_specs=[
                pl.BlockSpec((TOKENS, depth), whole),
                pl.BlockSpec((DECODE, depth), whole),
                pl.BlockSpec((depth, width), lambda i, blocks, rows: (0, blocks[i])),
                pl.BlockSpec((depth, TOKENS), whole),
                pl.BlockSpec((TOKENS, width), lambda i, blocks, rows: (0, blocks[i])),
                pl.BlockSpec((1, TOKENS), whole),
            ],
            out_specs=pl.BlockSpec((1, ALL_ROWS, width), lambda i, *_: (i, 0, 0)),
            scratch_shapes=[pltpu.VMEM((ALL_ROWS, 3 * TOKENS), jnp.bfloat16)],
        ),
        out_shape=jax.ShapeDtypeStruct((count, ALL_ROWS, width), jnp.float32),
        compiler_params=pltpu.CompilerParams(vmem_limit_bytes=16 * MIB),
        cost_estimate=pl.CostEstimate(
            flops=2 * ALL_ROWS * depth * width * count,
            bytes_accessed=depth * width * count * 2 + 2 * MIB,
            transcendentals=0,
        ),
        name="project",
    )(blocks, row_adapter, span, decode, weight, down, up, adapter)


TILE = 2
KEYS = 1024
PER = KEYS // TOKENS


def attend_kernel(partner, visible_ref, q_ref, prior_ref, *refs):
    pieces = refs[:SIDE]
    refs = refs[SIDE:]
    if partner:
        out_ref, top_ref, acc_ref, ext_ref, key_ref = refs
    else:
        other_ref, out_ref, top_ref, acc_ref, ext_ref, key_ref = refs
    rows = TILE * TOKENS
    tiles = GROUP // TILE
    queries = [
        jnp.concatenate(
            [q_ref[:, (i * TILE + j) * HEAD_SIZE : (i * TILE + j + 1) * HEAD_SIZE] for j in range(TILE)], axis=0
        )
        for i in range(tiles)
    ]
    ext_ref[:, HEAD_SIZE:] = jnp.ones((2 * KEYS, HEAD_SIZE), jnp.bfloat16)
    lane = lax.broadcasted_iota(jnp.int32, (TOKENS, HEAD_SIZE), 1)
    if partner:
        stats = jnp.zeros((TOKENS, HEAD_SIZE), jnp.bfloat16)
    else:
        other_stats = other_ref[:, GROUP * HEAD_SIZE :].astype(jnp.float32)
    blocks = 2 * SHARDS // PER
    for b in range(blocks):
        slot = (b % 2) * KEYS
        if b < blocks // 2:
            kv = prior_ref[b * PER : (b + 1) * PER, 0].reshape(KEYS, 2 * HEAD_SIZE)
            keys = kv[:, :HEAD_SIZE]
            ext_ref[slot : slot + KEYS, :HEAD_SIZE] = kv[:, HEAD_SIZE:]
        else:
            first = (b - blocks // 2) * PER
            for n in range(PER):
                kv = pieces[(first + n) // SIDE][(first + n) % SIDE]
                seen = visible_ref[first + n] != 0
                here = slice(slot + n * TOKENS, slot + (n + 1) * TOKENS)
                key_ref[here, :] = jnp.where(seen, kv[:, :HEAD_SIZE], prior_ref[0, 0, :, :HEAD_SIZE])
                ext_ref[here, :HEAD_SIZE] = jnp.where(seen, kv[:, HEAD_SIZE:], jnp.zeros_like(kv[:, HEAD_SIZE:]))
                ext_ref[here, HEAD_SIZE:] = jnp.where(seen, 1.0, 0.0).astype(jnp.bfloat16) * jnp.ones(
                    (TOKENS, HEAD_SIZE), jnp.bfloat16
                )
            keys = key_ref[slot : slot + KEYS, :]
        for i in range(tiles):
            here = slice(i * rows, (i + 1) * rows)
            scores = lax.dot_general(
                queries[i], keys, (((1,), (1,)), ((), ())), preferred_element_type=jnp.float32
            )
            if b == blocks // 2 and not partner:
                token = lax.broadcasted_iota(jnp.int32, (rows, TOKENS), 0) % TOKENS
                key = lax.broadcasted_iota(jnp.int32, (rows, TOKENS), 1)
                scores = jnp.concatenate(
                    [jnp.where(key <= token, scores[:, :TOKENS], neg_large), scores[:, TOKENS:]], axis=1
                )
            top = jnp.max(scores, axis=1, keepdims=True) * LOG2_SCALE
            if b > 0:
                before = top_ref[here, :1]
                top = jnp.maximum(before, top)
                rescale = jnp.exp2(before - top)
            weights = jnp.exp2(scores * LOG2_SCALE - top)
            total = jnp.dot(
                weights.astype(jnp.bfloat16), ext_ref[slot : slot + KEYS, :], preferred_element_type=jnp.float32
            )
            if b > 0:
                total = acc_ref[here] * rescale + total
            if b < blocks - 1:
                acc_ref[here] = total
                top_ref[here] = jnp.broadcast_to(top, (rows, HEAD_SIZE))
                continue
            out = total[:, :HEAD_SIZE] / total[:, HEAD_SIZE:]
            level = top + jnp.log2(total[:, HEAD_SIZE:])
            for j in range(TILE):
                g = i * TILE + j
                columns = slice(g * HEAD_SIZE, (g + 1) * HEAD_SIZE)
                own = slice(j * TOKENS, (j + 1) * TOKENS)
                if partner:
                    out_ref[:, columns] = out[own].astype(jnp.bfloat16)
                    for part, piece in enumerate(split3(level[own])):
                        stats = jnp.where(lane == part * GROUP + g, piece, stats)
                else:
                    other_level = (
                        other_stats[:, g : g + 1]
                        + other_stats[:, GROUP + g : GROUP + g + 1]
                        + other_stats[:, 2 * GROUP + g : 2 * GROUP + g + 1]
                    )
                    peak = jnp.maximum(level[own], other_level)
                    mine = jnp.exp2(level[own] - peak)
                    theirs = jnp.exp2(other_level - peak)
                    mixed = mine * out[own] + theirs * other_ref[:, columns].astype(jnp.float32)
                    out_ref[:, columns] = (mixed / (mine + theirs)).astype(jnp.bfloat16)
    if partner:
        out_ref[:, GROUP * HEAD_SIZE :] = stats


def attend(visible, queries, head, prior, pieces, other=None):
    partner = other is None
    width = GROUP * HEAD_SIZE
    out_width = width + HEAD_SIZE if partner else width
    whole3 = lambda i, *_: (0, 0, 0)
    in_specs = [
        pl.BlockSpec((TOKENS, width), lambda i, *_: (0, head)),
        pl.BlockSpec((SHARDS, 1, TOKENS, 2 * HEAD_SIZE), lambda i, *_: (0, head, 0, 0)),
    ] + [pl.BlockSpec((SIDE, TOKENS, 2 * HEAD_SIZE), whole3)] * SIDE
    operands = [queries, prior] + list(pieces)
    if not partner:
        in_specs.append(pl.BlockSpec((TOKENS, width + HEAD_SIZE), lambda i, *_: (0, 0)))
        operands.append(other)
    rows = GROUP * TOKENS
    total_keys = 2 * SHARDS * TOKENS
    return pl.pallas_call(
        functools.partial(attend_kernel, partner),
        grid_spec=pltpu.PrefetchScalarGridSpec(
            num_scalar_prefetch=1,
            grid=(1,),
            in_specs=in_specs,
            out_specs=pl.BlockSpec((TOKENS, out_width), lambda i, *_: (0, 0)),
            scratch_shapes=[
                pltpu.VMEM((rows, HEAD_SIZE), jnp.float32),
                pltpu.VMEM((rows, 2 * HEAD_SIZE), jnp.float32),
                pltpu.VMEM((2 * KEYS, 2 * HEAD_SIZE), jnp.bfloat16),
                pltpu.VMEM((2 * KEYS, HEAD_SIZE), jnp.bfloat16),
            ],
        ),
        out_shape=jax.ShapeDtypeStruct((TOKENS, out_width), jnp.bfloat16),
        compiler_params=pltpu.CompilerParams(vmem_limit_bytes=32 * MIB),
        cost_estimate=pl.CostEstimate(
            flops=8 * rows * total_keys * HEAD_SIZE, bytes_accessed=3 * MIB, transcendentals=rows * total_keys
        ),
        name="attend_partner" if partner else "attend_own",
    )(visible, *operands)


ROW_BLOCK = 4


def decode_kernel(length_ref, live_ref, q_ref, cache_ref, fresh_ref, out_ref):
    first = pl.program_id(0) * ROW_BLOCK
    query_rows = STEPS * GROUP
    cache_size = cache_ref.shape[2]
    fresh_row = lax.broadcasted_iota(jnp.int32, (query_rows, DECODE), 1) // STEPS
    fresh_step = lax.broadcasted_iota(jnp.int32, (query_rows, DECODE), 1) % STEPS
    step = lax.broadcasted_iota(jnp.int32, (query_rows, DECODE), 0) // GROUP
    slot = lax.broadcasted_iota(jnp.int32, (query_rows, cache_size), 1)
    contract = (((1,), (1,)), ((), ()))
    for n in range(ROW_BLOCK):
        row = first + n
        length = length_ref[row]
        live = row < live_ref[0]
        for h in range(2):
            queries = q_ref[n, h]
            cached = lax.dot_general(
                queries, cache_ref[n, h, :, :HEAD_SIZE], contract, preferred_element_type=jnp.float32
            )
            fresh = lax.dot_general(
                queries, fresh_ref[h, :, :HEAD_SIZE], contract, preferred_element_type=jnp.float32
            )
            cached = jnp.where(slot < length, cached, neg_large)
            fresh = jnp.where((fresh_row == row) & (fresh_step <= step), fresh, neg_large)
            top = jnp.maximum(jnp.max(cached, axis=1, keepdims=True), jnp.max(fresh, axis=1, keepdims=True))
            cached = jnp.exp2((cached - top) * LOG2_SCALE)
            fresh = jnp.exp2((fresh - top) * LOG2_SCALE)
            total = jnp.sum(cached, axis=1, keepdims=True) + jnp.sum(fresh, axis=1, keepdims=True)
            out = jnp.dot(
                cached.astype(jnp.bfloat16), cache_ref[n, h, :, HEAD_SIZE:], preferred_element_type=jnp.float32
            ) + jnp.dot(
                fresh.astype(jnp.bfloat16), fresh_ref[h, :, HEAD_SIZE:], preferred_element_type=jnp.float32
            )
            out_ref[n, h] = jnp.where(live, out / total, 0.0).astype(jnp.bfloat16)


def decode_attend(lengths, live, queries, cache, fresh):
    rows, heads, query_rows, _ = queries.shape
    cache_size = cache.shape[2]
    return pl.pallas_call(
        decode_kernel,
        grid_spec=pltpu.PrefetchScalarGridSpec(
            num_scalar_prefetch=2,
            grid=(rows // ROW_BLOCK,),
            in_specs=[
                pl.BlockSpec((ROW_BLOCK, heads, query_rows, HEAD_SIZE), lambda i, *_: (i, 0, 0, 0)),
                pl.BlockSpec((ROW_BLOCK, heads, cache_size, 2 * HEAD_SIZE), lambda i, *_: (i, 0, 0, 0)),
                pl.BlockSpec((heads, DECODE, 2 * HEAD_SIZE), lambda i, *_: (0, 0, 0)),
            ],
            out_specs=pl.BlockSpec((ROW_BLOCK, heads, query_rows, HEAD_SIZE), lambda i, *_: (i, 0, 0, 0)),
        ),
        out_shape=jax.ShapeDtypeStruct(queries.shape, jnp.bfloat16),
        compiler_params=pltpu.CompilerParams(vmem_limit_bytes=16 * MIB),
        cost_estimate=pl.CostEstimate(
            flops=8 * rows * heads * query_rows * cache_size * HEAD_SIZE,
            bytes_accessed=5 * MIB,
            transcendentals=rows * heads * query_rows * cache_size,
        ),
        name="decode",
    )(lengths, live, queries, cache, fresh)


def pages_kernel(count, where_ref, *refs):
    first_head, second_head = refs[:SIDE], refs[SIDE : 2 * SIDE]
    out_ref, sems = refs[2 * SIDE :]

    def copies(n, k):
        dz, dy, block = where_ref[0, n], where_ref[1, n], where_ref[2, n]
        rows = pl.ds(pl.multiple_of(block * BLK, BLK), BLK)
        return (
            (dz, pltpu.make_async_copy(first_head[k].at[dy, rows], out_ref.at[n, 0], sems.at[n, 0])),
            (dy, pltpu.make_async_copy(second_head[k].at[dz, rows], out_ref.at[n, 1], sems.at[n, 1])),
        )

    for n in range(count):
        for k in range(SIDE):
            for piece, copy in copies(n, k):

                @pl.when(piece == k)
                def _():
                    copy.start()

    for n in range(count):
        for _, copy in copies(n, 0):
            copy.wait()


def pick_pages(where, first_head, second_head):
    count = where.shape[1]
    return pl.pallas_call(
        functools.partial(pages_kernel, count),
        grid_spec=pltpu.PrefetchScalarGridSpec(
            num_scalar_prefetch=1,
            grid=(1,),
            in_specs=[pl.BlockSpec(memory_space=pl.ANY)] * (2 * SIDE),
            out_specs=pl.BlockSpec(memory_space=pl.ANY),
            scratch_shapes=[pltpu.SemaphoreType.DMA((count, 2))],
        ),
        out_shape=jax.ShapeDtypeStruct((count, 2, BLK, 2 * HEAD_SIZE), jnp.bfloat16),
        cost_estimate=pl.CostEstimate(flops=0, bytes_accessed=MIB, transcendentals=0),
        name="pages",
    )(where, *first_head, *second_head)


def shift(x, dz, dy):
    perm = [
        (z * SIDE + y, ((z + dz) % SIDE) * SIDE + (y + dy) % SIDE) for z in range(SIDE) for y in range(SIDE)
    ]
    return lax.ppermute(x, "ctx", perm)


def swap_pool(x):
    return lax.ppermute(x, "pool", [(0, 1), (1, 0)])


def swap_tp(x, bit):
    return lax.ppermute(x, "tp", [(i, i ^ bit) for i in range(4)])


def ring(x, along_z):
    move = (lambda d: shift(x, d, 0)) if along_z else (lambda d: shift(x, 0, d))
    far = {1: move(1), 3: move(3), 2: move(2)}
    return [x, far[1], far[2], far[3]]


def per_device(
    span_hidden_states,
    span_token_queries,
    earlier_key_values,
    decode_hidden_states,
    decode_token_queries,
    decode_row_cache,
    key_value_weight,
    adapter_down_weight,
    adapter_up_weight,
    prompt_adapter,
    row_adapter_index,
    group_live_rows,
    cached_row_lengths,
    block_target_page,
):
    tp = lax.axis_index("tp")
    ctx = lax.axis_index("ctx")
    pool = lax.axis_index("pool")
    my_z, my_y = ctx // SIDE, ctx % SIDE
    depth = span_hidden_states.shape[1]

    prior = lax.all_gather(earlier_key_values, "ctx", axis=0)

    decode_hidden = decode_hidden_states.reshape(DECODE, depth)

    def heads_of(bits):
        return jnp.stack([2 * jnp.bitwise_xor(tp, bit) + j for bit in bits for j in range(2)]).astype(jnp.int32)

    def partial_kv(bits):
        return project(
            heads_of(bits),
            row_adapter_index,
            span_hidden_states,
            decode_hidden,
            key_value_weight,
            adapter_down_weight,
            adapter_up_weight,
            prompt_adapter.reshape(1, TOKENS),
        )

    from_core = swap_tp(partial_kv((1, 3)), 1)
    summed = partial_kv((0, 2)) + from_core
    from_chip = swap_tp(summed[2:].astype(jnp.bfloat16), 2)
    own_kv = (summed[:2] + from_chip.astype(jnp.float32)).astype(jnp.bfloat16)

    planes0 = ring(jnp.concatenate([p[None] for p in ring(own_kv[0, :TOKENS], False)]), True)
    planes1 = ring(jnp.concatenate([p[None] for p in ring(own_kv[1, :TOKENS], True)]), False)

    queries = decode_token_queries.reshape(ROWS, STEPS, 2, GROUP, HEAD_SIZE)
    queries = jnp.transpose(queries, (0, 2, 1, 3, 4)).reshape(ROWS, 2, STEPS * GROUP, HEAD_SIZE)
    decoded = decode_attend(
        cached_row_lengths, group_live_rows, queries, decode_row_cache, own_kv[:, TOKENS:]
    )
    decoded = jnp.transpose(decoded.reshape(ROWS, 2, STEPS, GROUP, HEAD_SIZE), (0, 2, 1, 3, 4))
    decode_attention = decoded.reshape(ROWS, STEPS, 2 * GROUP * HEAD_SIZE)

    far = jnp.arange(SIDE, dtype=jnp.int32)
    shard_z, shard_y = jnp.mod(my_z - far, SIDE), jnp.mod(my_y - far, SIDE)
    place = shard_z[:, None] * SIDE + shard_y[None, :]
    partner_sees = (place < ctx) | ((place == ctx) & (pool == 0))
    own_sees = place <= ctx
    visible = [[m.reshape(-1), m.T.reshape(-1)] for m in (partner_sees.astype(jnp.int32), own_sees.astype(jnp.int32))]
    partner_queries = swap_pool(span_token_queries)
    planes = [planes0, planes1]
    sent = [swap_pool(attend(visible[0][h], partner_queries, h, prior, planes[h])) for h in range(2)]
    span_attention = jnp.concatenate(
        [attend(visible[1][h], span_token_queries, h, prior, planes[h], sent[h]) for h in range(2)], axis=1
    )

    pages = TOKENS // BLK
    shard = ctx * 2 + pool
    partner_shard = ctx * 2 + 1 - pool
    page_ids = jnp.concatenate([shard * pages + jnp.arange(pages), partner_shard * pages + jnp.arange(pages)])
    block_ids = jnp.arange(block_target_page.shape[0], dtype=jnp.int32)
    source = jnp.sum(
        jnp.where(block_target_page[None, :] == page_ids[:, None], block_ids[None, :], 0), axis=1
    )
    source_shard = source // pages
    source_ctx = source_shard // 2
    where = jnp.stack(
        [
            jnp.mod(my_z - source_ctx // SIDE, SIDE),
            jnp.mod(my_y - source_ctx % SIDE, SIDE),
            source % pages,
        ]
    ).astype(jnp.int32)
    found = pick_pages(where, planes0, planes1)
    from_partner = swap_pool(found[pages:])
    mine = (source_shard % 2 == pool)[:pages]
    handoff_pages = jnp.where(mine[:, None, None, None], found[:pages], from_partner)
    return (span_attention, handoff_pages, decode_attention)


def solution(mesh):
    in_specs = (
        P(("ctx", "pool"), "tp"),
        P(("ctx", "pool"), "tp"),
        P("tp", ("ctx", "pool"), None),
        P(("ctx", "pool"), None, "tp"),
        P(("ctx", "pool"), None, "tp"),
        P(("ctx", "pool"), "tp", None, None),
        P("tp", None),
        P("tp", None),
        P(),
        P(("ctx", "pool")),
        P(("ctx", "pool")),
        P(("ctx", "pool")),
        P(("ctx", "pool")),
        P(),
    )
    out_specs = (
        P(("ctx", "pool"), "tp"),
        P(("ctx", "pool"), "tp", None, None),
        P(("ctx", "pool"), None, "tp"),
    )
    return jax.shard_map(
        per_device, mesh=mesh, in_specs=in_specs, out_specs=out_specs, check_vma=False
    )
```

time: 351 us -> 150 us (0.43)
  waiting for transfers between devices: 202 us -> 24.1 us
  matrix products: 79.3 us -> 0 us
  Pallas kernels: 0 us -> 53.2 us
  starting transfers between devices: 0.34 us -> 31.3 us
  other arithmetic: 34.1 us -> 4.14 us
    all_gather x2 -> x1, waiting for transfers between devices: 143 us -> 0.01 us  [per_device(): prior = lax.all_gather(earlier_key_values, 'ctx', axis=0)]
    dot_general x15 -> x0, matrix products: 79.3 us -> none  [the longest x6 34.1 us: absorb(): jnp.einsum(einsum_form, weights.astype(jnp.bfloat16), values, preferred_e...]
    pallas_call x0 -> x8, Pallas kernels: none -> 53.2 us  [the longest x4 27.3 us: attend(): pl.pallas_call(functools.partial(attend_kernel, partner), grid_spec=pltpu...]
    psum x1 -> x0, waiting for transfers between devices: 31.4 us -> none  [per_device(): narrow_rank = lax.psum(partial_rank_sums, 'tp')]
    ppermute x0 -> x18, starting transfers between devices: none -> 31.2 us  [the longest x12 19 us: shift(): return lax.ppermute(x, 'ctx', perm)]
    reduce_scatter x1 -> x0, waiting for transfers between devices: 27.5 us -> none  [per_device(): lax.psum_scatter(jnp.einsum('nd,dhc->hnc', stacked_values, weight_heads,...]
    reduce_sum x4 -> x0, other arithmetic: 25 us -> none  [absorb(): running_sum = running_sum * rescale + jnp.sum(weights, axis=-1)]
    ppermute x0 -> x18, waiting for transfers between devices: none -> 23.4 us  [the longest x12 17.8 us: shift(): return lax.ppermute(x, 'ctx', perm)]
  transfers between devices with their start and end apart: 4 -> 19, of which waited for: 4 -> 8; matrix products, arithmetic and copies ran while one was open for 15% -> 5% of each run, Pallas kernels for 0% -> 27%
where the time goes in v1:
time: 150 us; the launch traced here: 149 us
  Pallas kernels  53.2 us (35%)
  starting transfers between devices  31.3 us (21%)
  waiting for transfers between devices  24.1 us (16%)
  local copies, waits for them, and re-layouts  20.9 us (14%)
  between operations  15.2 us (10%)
  other arithmetic  4.14 us (3%)
    pallas_call x4, Pallas kernels, attend(): pl.pallas_call(functools.partial(attend_kernel, partner), grid_spec=pltpu...  27.3 us
    ppermute x12, starting transfers between devices, shift(): return lax.ppermute(x, 'ctx', perm)  19 us
    ppermute x12, waiting for transfers between devices, shift(): return lax.ppermute(x, 'ctx', perm)  17.8 us
    unnamed x70, local copies, waits for them, and re-layouts  16.6 us
    ppermute x4, starting transfers between devices, swap_pool(): return lax.ppermute(x, 'pool', [(0, 1), (1, 0)])  10.5 us
    pallas_call x1, Pallas kernels, pick_pages(): pl.pallas_call(functools.partial(pages_kernel, count), grid_spec=pltpu.Pr...  10 us
    pallas_call x1, Pallas kernels, decode_attend(): pl.pallas_call(decode_kernel, grid_spec=pltpu.PrefetchScalarGridSpec(num_...  8.79 us
    pallas_call x2, Pallas kernels, project(): pl.pallas_call(project_kernel, grid_spec=pltpu.PrefetchScalarGridSpec(num...  7.02 us
  transfers between devices with their start and end apart: 19, of which 8 were waited for; matrix products, arithmetic and copies ran while one was open for 5% of the time, Pallas kernels for 27%

profile of v1, /device:TPU:0, one launch (start us, length us, event | category | flops | bytes accessed | tf_op | source)
XLA Modules:
  0.0 148.8 jit_solution(7224962222808899243)
XLA Ops:
  9.0 3.4 %copy-done = bf16[2048,2048]{1,0:T(8,128)(2,1)S(1)} copy-done((bf16[2048,2048]{1,0:T(8,128)(2,1)S(1)}, bf16[2048,2048]{1,0:T(8,128)(2,1)}, u32[]{:S(2)}) %copy-start) | copy-done | bytes 8388632
  16.8 3.5 %project.3 = f32[4,192,256]{2,1,0:T(8,128)S(1)} custom-call(s32[4]{0:T(128)S(1)} %pad_add_fusion.2.block_ref, s32[16]{0:T(128)S(1)} %copy-done.25, bf16[128,2048]{1,0:T(8,128)(2,1)S(1)} %copy-done.3, bf16[64,2048]{1,0:T(8,128)(2,1)S(1)} %reshape.353.decode_ref, bf16[2048,2048]{1,0:T(8,128)(2,1)S(1)} %copy-done, bf16[2048,128]{1,0:T(8,128)(2,1)S(1)} %copy-done.5, ...), custom_call_target="tpu_custom_call" | custom-call | flops 805306368 | bytes 6291456 | tf_op jit(solution)/shard_map/project/pallas_call | solution.py:68
  20.6 3.5 %copy-done.1 = bf16[2048,2048]{1,0:T(8,128)(2,1)S(1)} copy-done((bf16[2048,2048]{1,0:T(8,128)(2,1)S(1)}, bf16[2048,2048]{1,0:T(8,128)(2,1)}, u32[]{:S(2)}) %copy-start.1) | copy-done | bytes 8388632
  24.2 3.5 %project.2 = f32[4,192,256]{2,1,0:T(8,128)S(1)} custom-call(s32[4]{0:T(128)S(1)} %pad_add_fusion.1.block_ref, s32[16]{0:T(128)S(1)} %copy-done.26, bf16[128,2048]{1,0:T(8,128)(2,1)S(1)} %copy-done.4, bf16[64,2048]{1,0:T(8,128)(2,1)S(1)} %reshape.353.decode_ref, bf16[2048,2048]{1,0:T(8,128)(2,1)S(1)} %copy-done.1, bf16[2048,128]{1,0:T(8,128)(2,1)S(1)} %copy-done.6, ...), custom_call_target="tpu_custom_call" | custom-call | flops 805306368 | bytes 6291456 | tf_op jit(solution)/shard_map/project/pallas_call | solution.py:68
  29.1 1.6 %collective-permute-start.1 = (bf16[2,192,256]{2,1,0:T(8,128)(2,1)S(1)}, bf16[2,192,256]{2,1,0:T(8,128)(2,1)S(1)}, u32[]{:S(2)}, u32[]{:S(2)}) collective-permute-start(bf16[2,192,256]{2,1,0:T(8,128)(2,1)S(1)} %slice.47), channel_id=1, source_target_pairs={{0,2},{1,3},{2,0},{3,1},{4,6},{5,7},{6,4},{7,5},{8,10},{9,11},{10,... | collective-permute-start | bytes 589832 | tf_op jit(solution)/shard_map/ppermute | solution.py:347
  30.8 5.6 %collective-permute-done.1 = bf16[2,192,256]{2,1,0:T(8,128)(2,1)S(1)} collective-permute-done((bf16[2,192,256]{2,1,0:T(8,128)(2,1)S(1)}, bf16[2,192,256]{2,1,0:T(8,128)(2,1)S(1)}, u32[]{:S(2)}, u32[]{:S(2)}) %collective-permute-start.1) | collective-permute-done | bytes 196640 | tf_op jit(solution)/shard_map/ppermute | solution.py:347
  36.5 4.1 %collective-permute-start.12 = (bf16[128,256]{1,0:T(8,128)(2,1)S(1)}, bf16[128,256]{1,0:T(8,128)(2,1)S(1)}, u32[]{:S(2)}, u32[]{:S(2)}) collective-permute-start(bf16[128,256]{1,0:T(8,128)(2,1)S(1)} %get-tuple-element.5), channel_id=1, source_target_pairs={{0,96},{8,104},{16,112},{24,120},{32,0},{40,8},{48,16},{56,24},{64... | collective-permute-start | bytes 196616 | tf_op jit(solution)/shard_map/ppermute | solution.py:339
  42.5 4.0 %collective-permute-done.11 = bf16[128,256]{1,0:T(8,128)(2,1)S(1)} collective-permute-done((bf16[128,256]{1,0:T(8,128)(2,1)S(1)}, bf16[128,256]{1,0:T(8,128)(2,1)S(1)}, u32[]{:S(2)}, u32[]{:S(2)}) %collective-permute-start.11) | collective-permute-done | bytes 65568 | tf_op jit(solution)/shard_map/ppermute | solution.py:339
  47.6 1.7 %collective-permute-start.13 = (bf16[4,128,256]{2,1,0:T(8,128)(2,1)S(1)}, bf16[4,128,256]{2,1,0:T(8,128)(2,1)S(1)}, u32[]{:S(2)}, u32[]{:S(2)}) collective-permute-start(bf16[4,128,256]{2,1,0:T(8,128)(2,1)S(1)} %pad_maximum_fusion.2.refs_0_.refs_4_), channel_id=1, source_target_pairs={{0,8},{8,16},{16,24},{24,0},{32,40},{40,48},{48,56},{56,32},{64,72... | collective-permute-start | bytes 786440 | tf_op jit(solution)/shard_map/ppermute | solution.py:339
  50.9 2.1 %collective-permute-start.3 = (bf16[128,256]{1,0:T(8,128)(2,1)S(1)}, bf16[128,256]{1,0:T(8,128)(2,1)S(1)}, u32[]{:S(2)}, u32[]{:S(2)}) collective-permute-start(bf16[128,256]{1,0:T(8,128)(2,1)S(1)} %get-tuple-element.4), channel_id=1, source_target_pairs={{0,16},{8,24},{16,0},{24,8},{32,48},{40,56},{48,32},{56,40},{64,80... | collective-permute-start | bytes 196616 | tf_op jit(solution)/shard_map/ppermute | solution.py:339
  53.8 1.9 %collective-permute-start.14 = (bf16[4,128,256]{2,1,0:T(8,128)(2,1)S(1)}, bf16[4,128,256]{2,1,0:T(8,128)(2,1)S(1)}, u32[]{:S(2)}, u32[]{:S(2)}) collective-permute-start(bf16[4,128,256]{2,1,0:T(8,128)(2,1)S(1)} %pad_maximum_fusion.2.refs_0_.refs_4_), channel_id=1, source_target_pairs={{0,16},{8,24},{16,0},{24,8},{32,48},{40,56},{48,32},{56,40},{64,80... | collective-permute-start | bytes 786440 | tf_op jit(solution)/shard_map/ppermute | solution.py:339
  57.4 7.7 %collective-permute-done.3 = bf16[128,256]{1,0:T(8,128)(2,1)S(1)} collective-permute-done((bf16[128,256]{1,0:T(8,128)(2,1)S(1)}, bf16[128,256]{1,0:T(8,128)(2,1)S(1)}, u32[]{:S(2)}, u32[]{:S(2)}) %collective-permute-start.3) | collective-permute-done | bytes 65568 | tf_op jit(solution)/shard_map/ppermute | solution.py:339
  65.2 3.4 %collective-permute-start.6 = (bf16[4,128,256]{2,1,0:T(8,128)(2,1)S(1)}, bf16[4,128,256]{2,1,0:T(8,128)(2,1)S(1)}, u32[]{:S(2)}, u32[]{:S(2)}) collective-permute-start(bf16[4,128,256]{2,1,0:T(8,128)(2,1)S(1)} %pad_maximum_fusion.1.refs_0_), channel_id=1, source_target_pairs={{0,64},{8,72},{16,80},{24,88},{32,96},{40,104},{48,112},{56,120},{... | collective-permute-start | bytes 786440 | tf_op jit(solution)/shard_map/ppermute | solution.py:339
  70.2 3.0 %collective-permute-start.8 = (bf16[128,2048]{1,0:T(8,128)(2,1)S(1)}, bf16[128,2048]{1,0:T(8,128)(2,1)S(1)}, u32[]{:S(2)}, u32[]{:S(2)}) collective-permute-start(bf16[128,2048]{1,0:T(8,128)(2,1)S(1)} %copy-done.32), channel_id=1, source_target_pairs={{0,4},{4,0},{1,5},{5,1},{2,6},{6,2},{3,7},{7,3},{8,12},{12,8},{9,1... | collective-permute-start | bytes 1572872 | tf_op jit(solution)/shard_map/ppermute | solution.py:343
  74.5 2.8 %collective-permute-done.6.refs_2_ = bf16[4,128,256]{2,1,0:T(8,128)(2,1)S(1)} collective-permute-done((bf16[4,128,256]{2,1,0:T(8,128)(2,1)S(1)}, bf16[4,128,256]{2,1,0:T(8,128)(2,1)S(1)}, u32[]{:S(2)}, u32[]{:S(2)}) %collective-permute-start.6) | collective-permute-done | bytes 262176 | tf_op jit(solution)/shard_map/ppermute | solution.py:339
  78.7 10.0 %pages.1 = bf16[16,2,16,256]{3,2,1,0:T(8,128)(2,1)} custom-call(s32[3,16]{1,0:T(4,128)} %pad_add_fusion.where_ref, bf16[4,128,256]{2,1,0:T(8,128)(2,1)} %copy-done.11, bf16[4,128,256]{2,1,0:T(8,128)(2,1)} %copy-done.19, bf16[4,128,256]{2,1,0:T(8,128)(2,1)} %copy-done.21, bf16[4,128,256]{2,1,0:T(8,128)(2,1)} %copy-done.23, bf16[4,128,256]{2,1,0:T(8,128)(2,1)} %copy-done.9, ...), custom_call_target="tpu_custom_call" | custom-call | bytes 1048576 | tf_op jit(solution)/shard_map/pages/pallas_call | solution.py:320
  89.8 3.3 %collective-permute-start.17 = (bf16[8,2,16,256]{3,2,1,0:T(8,128)(2,1)S(1)}, bf16[8,2,16,256]{3,2,1,0:T(8,128)(2,1)S(1)}, u32[]{:S(2)}, u32[]{:S(2)}) collective-permute-start(bf16[8,2,16,256]{3,2,1,0:T(8,128)(2,1)S(1)} %slice.38), channel_id=1, source_target_pairs={{0,4},{4,0},{1,5},{5,1},{2,6},{6,2},{3,7},{7,3},{8,12},{12,8},{9,1... | collective-permute-start | bytes 393224 | tf_op jit(solution)/shard_map/ppermute | solution.py:343
  95.4 2.2 %copy-done.2 = bf16[16,2,256,256]{3,2,1,0:T(8,128)(2,1)S(1)} copy-done((bf16[16,2,256,256]{3,2,1,0:T(8,128)(2,1)S(1)}, bf16[16,2,256,256]{3,2,1,0:T(8,128)(2,1)}, u32[]{:S(2)}) %copy-start.2) | copy-done | bytes 4194328
  97.6 8.8 %decode.1 = bf16[16,2,32,128]{3,2,1,0:T(8,128)(2,1)S(1)} custom-call(s32[16]{0:T(128)S(1)} %copy-done.29, s32[1]{0:T(128)S(6)} %copy.25.live_ref, bf16[16,2,32,128]{3,2,1,0:T(8,128)(2,1)S(1)} %bitcast.56, bf16[16,2,256,256]{3,2,1,0:T(8,128)(2,1)S(1)} %copy-done.2, bf16[2,64,256]{2,1,0:T(8,128)(2,1)S(1)} %slice.39.fresh_ref), custom_call_target="tpu_custom_call" | custom-call | flops 268435456 | bytes 5242880 | tf_op jit(solution)/shard_map/decode/pallas_call | solution.py:270
  109.6 6.7 %attend_partner.3 = bf16[128,1152]{1,0:T(8,128)(2,1)S(1)} custom-call(s32[16]{0:T(128)S(1)} %reshape.362.visible_ref, bf16[128,2048]{1,0:T(8,128)(2,1)S(1)} %collective-permute-done.8.q_ref, bf16[16,2,128,256]{3,2,1,0:T(8,128)(2,1)S(1)} %bitcast.60, bf16[4,128,256]{2,1,0:T(8,128)(2,1)S(1)} %copy-done.10, bf16[4,128,256]{2,1,0:T(8,128)(2,1)S(1)} %copy-done.14, ...), custom_call_target="tpu_custom_call" | custom-call | flops 4294967296 | bytes 3145728 | tf_op jit(solution)/shard_map/attend_partner/pallas_call | solution.py:206
  117.1 6.7 %attend_partner.2 = bf16[128,1152]{1,0:T(8,128)(2,1)S(1)} custom-call(s32[16]{0:T(128)S(1)} %reshape.360.visible_ref, bf16[128,2048]{1,0:T(8,128)(2,1)S(1)} %collective-permute-done.8.q_ref, bf16[16,2,128,256]{3,2,1,0:T(8,128)(2,1)S(1)} %bitcast.61, bf16[4,128,256]{2,1,0:T(8,128)(2,1)S(1)} %copy-done.12, bf16[4,128,256]{2,1,0:T(8,128)(2,1)S(1)} %copy-done.20, ...), custom_call_target="tpu_custom_call" | custom-call | flops 4294967296 | bytes 3145728 | tf_op jit(solution)/shard_map/attend_partner/pallas_call | solution.py:206
  123.8 3.4 %collective-permute-start.9 = (bf16[128,1152]{1,0:T(8,128)(2,1)S(1)}, bf16[128,1152]{1,0:T(8,128)(2,1)S(1)}, u32[]{:S(2)}, u32[]{:S(2)}) collective-permute-start(bf16[128,1152]{1,0:T(8,128)(2,1)S(1)} %attend_partner.2), channel_id=1, source_target_pairs={{0,4},{4,0},{1,5},{5,1},{2,6},{6,2},{3,7},{7,3},{8,12},{12,8},{9,1... | collective-permute-start | bytes 884744 | tf_op jit(solution)/shard_map/ppermute | solution.py:343
  127.2 7.0 %attend_own.3 = bf16[128,1024]{1,0:T(8,128)(2,1)S(1)} custom-call(s32[16]{0:T(128)S(1)} %reshape.361.visible_ref, bf16[128,2048]{1,0:T(8,128)(2,1)S(1)} %copy-done.32, bf16[16,2,128,256]{3,2,1,0:T(8,128)(2,1)S(1)} %bitcast.62, bf16[4,128,256]{2,1,0:T(8,128)(2,1)S(1)} %copy-done.10, bf16[4,128,256]{2,1,0:T(8,128)(2,1)S(1)} %copy-done.14, ...), custom_call_target="tpu_custom_call" | custom-call | flops 4294967296 | bytes 3145728 | tf_op jit(solution)/shard_map/attend_own/pallas_call | solution.py:206
  134.2 6.9 %attend_own.2 = bf16[128,1024]{1,0:T(8,128)(2,1)S(1)} custom-call(s32[16]{0:T(128)S(1)} %reshape.359.visible_ref, bf16[128,2048]{1,0:T(8,128)(2,1)S(1)} %copy-done.32, bf16[16,2,128,256]{3,2,1,0:T(8,128)(2,1)S(1)} %bitcast.63, bf16[4,128,256]{2,1,0:T(8,128)(2,1)S(1)} %copy-done.12, bf16[4,128,256]{2,1,0:T(8,128)(2,1)S(1)} %copy-done.20, ...), custom_call_target="tpu_custom_call" | custom-call | flops 4294967296 | bytes 3145728 | tf_op jit(solution)/shard_map/attend_own/pallas_call | solution.py:206
  (122 shorter events, 26.8 us)
Async XLA Ops:
  7.2 100.8 %all-gather.3.cloned.1.call-start = ((), (), s32[]{:S(2)}) async-start(), calls=%async_computation | async-start | bytes 2228224 | tf_op jit(solution)/shard_map/all_gather | solution.py:378
  20.4 7.3 %collective-permute-start = (f32[4,192,256]{2,1,0:T(8,128)S(1)}, f32[4,192,256]{2,1,0:T(8,128)}, u32[]{:S(2)}, u32[]{:S(2)}) collective-permute-start(f32[4,192,256]{2,1,0:T(8,128)S(1)} %project.3), channel_id=1, source_target_pairs={{0,1},{1,0},{2,3},{3,2},{4,5},{5,4},{6,7},{7,6},{8,9},{9,8},{10,11... | collective-permute-start | bytes 2359304 | tf_op jit(solution)/shard_map/ppermute | solution.py:347
  27.7 26.0 %copy-start.34 = (s32[256]{0:T(256)S(1)}, s32[256]{0:T(256)}, u32[]{:S(2)}) copy-start(s32[256]{0:T(256)} %param.27) | copy-start | bytes 3076
  27.7 42.5 %copy-start.32 = (bf16[128,2048]{1,0:T(8,128)(2,1)S(1)}, bf16[128,2048]{1,0:T(8,128)(2,1)}, u32[]{:S(2)}) copy-start(bf16[128,2048]{1,0:T(8,128)(2,1)} %q_ref.3) | copy-start | bytes 1572868
  27.7 67.6 %copy-start.29 = (s32[16]{0:T(128)S(1)}, s32[16]{0:T(128)}, u32[]{:S(2)}) copy-start(s32[16]{0:T(128)} %length_ref.1) | copy-start | bytes 196
  29.1 7.3 %collective-permute-start.1 = (bf16[2,192,256]{2,1,0:T(8,128)(2,1)S(1)}, bf16[2,192,256]{2,1,0:T(8,128)(2,1)S(1)}, u32[]{:S(2)}, u32[]{:S(2)}) collective-permute-start(bf16[2,192,256]{2,1,0:T(8,128)(2,1)S(1)} %slice.47), channel_id=1, source_target_pairs={{0,2},{1,3},{2,0},{3,1},{4,6},{5,7},{6,4},{7,5},{8,10},{9,11},{10,... | collective-permute-start | bytes 589832 | tf_op jit(solution)/shard_map/ppermute | solution.py:347
  36.5 6.0 %collective-permute-start.12 = (bf16[128,256]{1,0:T(8,128)(2,1)S(1)}, bf16[128,256]{1,0:T(8,128)(2,1)S(1)}, u32[]{:S(2)}, u32[]{:S(2)}) collective-permute-start(bf16[128,256]{1,0:T(8,128)(2,1)S(1)} %get-tuple-element.5), channel_id=1, source_target_pairs={{0,96},{8,104},{16,112},{24,120},{32,0},{40,8},{48,16},{56,24},{64... | collective-permute-start | bytes 196616 | tf_op jit(solution)/shard_map/ppermute | solution.py:339
  40.6 5.9 %collective-permute-start.11 = (bf16[128,256]{1,0:T(8,128)(2,1)S(1)}, bf16[128,256]{1,0:T(8,128)(2,1)S(1)}, u32[]{:S(2)}, u32[]{:S(2)}) collective-permute-start(bf16[128,256]{1,0:T(8,128)(2,1)S(1)} %get-tuple-element.5), channel_id=1, source_target_pairs={{0,64},{8,72},{16,80},{24,88},{32,96},{40,104},{48,112},{56,120},{... | collective-permute-start | bytes 196616 | tf_op jit(solution)/shard_map/ppermute | solution.py:339
  40.6 6.9 %collective-permute-start.10 = (bf16[128,256]{1,0:T(8,128)(2,1)S(1)}, bf16[128,256]{1,0:T(8,128)(2,1)S(1)}, u32[]{:S(2)}, u32[]{:S(2)}) collective-permute-start(bf16[128,256]{1,0:T(8,128)(2,1)S(1)} %get-tuple-element.5), channel_id=1, source_target_pairs={{0,32},{8,40},{16,48},{24,56},{32,64},{40,72},{48,80},{56,88},{64,... | collective-permute-start | bytes 196616 | tf_op jit(solution)/shard_map/ppermute | solution.py:339
  47.5 29.8 %copy-start.9 = (bf16[4,128,256]{2,1,0:T(8,128)(2,1)}, bf16[4,128,256]{2,1,0:T(8,128)(2,1)S(1)}, u32[]{:S(2)}) copy-start(bf16[4,128,256]{2,1,0:T(8,128)(2,1)S(1)} %pad_maximum_fusion.2.refs_0_.refs_4_) | copy-start | bytes 786436
  47.6 21.0 %collective-permute-start.13 = (bf16[4,128,256]{2,1,0:T(8,128)(2,1)S(1)}, bf16[4,128,256]{2,1,0:T(8,128)(2,1)S(1)}, u32[]{:S(2)}, u32[]{:S(2)}) collective-permute-start(bf16[4,128,256]{2,1,0:T(8,128)(2,1)S(1)} %pad_maximum_fusion.2.refs_0_.refs_4_), channel_id=1, source_target_pairs={{0,8},{8,16},{16,24},{24,0},{32,40},{40,48},{48,56},{56,32},{64,72... | collective-permute-start | bytes 786440 | tf_op jit(solution)/shard_map/ppermute | solution.py:339
  49.3 6.4 %collective-permute-start.4 = (bf16[128,256]{1,0:T(8,128)(2,1)S(1)}, bf16[128,256]{1,0:T(8,128)(2,1)S(1)}, u32[]{:S(2)}, u32[]{:S(2)}) collective-permute-start(bf16[128,256]{1,0:T(8,128)(2,1)S(1)} %get-tuple-element.4), channel_id=1, source_target_pairs={{0,24},{8,0},{16,8},{24,16},{32,56},{40,32},{48,40},{56,48},{64,88... | collective-permute-start | bytes 196616 | tf_op jit(solution)/shard_map/ppermute | solution.py:339
  50.9 14.1 %collective-permute-start.3 = (bf16[128,256]{1,0:T(8,128)(2,1)S(1)}, bf16[128,256]{1,0:T(8,128)(2,1)S(1)}, u32[]{:S(2)}, u32[]{:S(2)}) collective-permute-start(bf16[128,256]{1,0:T(8,128)(2,1)S(1)} %get-tuple-element.4), channel_id=1, source_target_pairs={{0,16},{8,24},{16,0},{24,8},{32,48},{40,56},{48,32},{56,40},{64,80... | collective-permute-start | bytes 196616 | tf_op jit(solution)/shard_map/ppermute | solution.py:339
  53.0 12.0 %collective-permute-start.2 = (bf16[128,256]{1,0:T(8,128)(2,1)S(1)}, bf16[128,256]{1,0:T(8,128)(2,1)S(1)}, u32[]{:S(2)}, u32[]{:S(2)}) collective-permute-start(bf16[128,256]{1,0:T(8,128)(2,1)S(1)} %get-tuple-element.4), channel_id=1, source_target_pairs={{0,8},{8,16},{16,24},{24,0},{32,40},{40,48},{48,56},{56,32},{64,72... | collective-permute-start | bytes 196616 | tf_op jit(solution)/shard_map/ppermute | solution.py:339
  53.8 16.4 %collective-permute-start.14 = (bf16[4,128,256]{2,1,0:T(8,128)(2,1)S(1)}, bf16[4,128,256]{2,1,0:T(8,128)(2,1)S(1)}, u32[]{:S(2)}, u32[]{:S(2)}) collective-permute-start(bf16[4,128,256]{2,1,0:T(8,128)(2,1)S(1)} %pad_maximum_fusion.2.refs_0_.refs_4_), channel_id=1, source_target_pairs={{0,16},{8,24},{16,0},{24,8},{32,48},{40,56},{48,32},{56,40},{64,80... | collective-permute-start | bytes 786440 | tf_op jit(solution)/shard_map/ppermute | solution.py:339
  55.7 18.1 %collective-permute-start.15 = (bf16[4,128,256]{2,1,0:T(8,128)(2,1)S(1)}, bf16[4,128,256]{2,1,0:T(8,128)(2,1)S(1)}, u32[]{:S(2)}, u32[]{:S(2)}) collective-permute-start(bf16[4,128,256]{2,1,0:T(8,128)(2,1)S(1)} %pad_maximum_fusion.2.refs_0_.refs_4_), channel_id=1, source_target_pairs={{0,24},{8,0},{16,8},{24,16},{32,56},{40,32},{48,40},{56,48},{64,88... | collective-permute-start | bytes 786440 | tf_op jit(solution)/shard_map/ppermute | solution.py:339
  65.1 9.4 %collective-permute-start.5 = (bf16[4,128,256]{2,1,0:T(8,128)(2,1)S(1)}, bf16[4,128,256]{2,1,0:T(8,128)(2,1)S(1)}, u32[]{:S(2)}, u32[]{:S(2)}) collective-permute-start(bf16[4,128,256]{2,1,0:T(8,128)(2,1)S(1)} %pad_maximum_fusion.1.refs_0_), channel_id=1, source_target_pairs={{0,32},{8,40},{16,48},{24,56},{32,64},{40,72},{48,80},{56,88},{64,... | collective-permute-start | bytes 786440 | tf_op jit(solution)/shard_map/ppermute | solution.py:339
  65.2 12.1 %collective-permute-start.6 = (bf16[4,128,256]{2,1,0:T(8,128)(2,1)S(1)}, bf16[4,128,256]{2,1,0:T(8,128)(2,1)S(1)}, u32[]{:S(2)}, u32[]{:S(2)}) collective-permute-start(bf16[4,128,256]{2,1,0:T(8,128)(2,1)S(1)} %pad_maximum_fusion.1.refs_0_), channel_id=1, source_target_pairs={{0,64},{8,72},{16,80},{24,88},{32,96},{40,104},{48,112},{56,120},{... | collective-permute-start | bytes 786440 | tf_op jit(solution)/shard_map/ppermute | solution.py:339
  68.6 8.7 %collective-permute-start.7 = (bf16[4,128,256]{2,1,0:T(8,128)(2,1)S(1)}, bf16[4,128,256]{2,1,0:T(8,128)(2,1)S(1)}, u32[]{:S(2)}, u32[]{:S(2)}) collective-permute-start(bf16[4,128,256]{2,1,0:T(8,128)(2,1)S(1)} %pad_maximum_fusion.1.refs_0_), channel_id=1, source_target_pairs={{0,96},{8,104},{16,112},{24,120},{32,0},{40,8},{48,16},{56,24},{64... | collective-permute-start | bytes 786440 | tf_op jit(solution)/shard_map/ppermute | solution.py:339
  70.2 37.7 %collective-permute-start.8 = (bf16[128,2048]{1,0:T(8,128)(2,1)S(1)}, bf16[128,2048]{1,0:T(8,128)(2,1)S(1)}, u32[]{:S(2)}, u32[]{:S(2)}) collective-permute-start(bf16[128,2048]{1,0:T(8,128)(2,1)S(1)} %copy-done.32), channel_id=1, source_target_pairs={{0,4},{4,0},{1,5},{5,1},{2,6},{6,2},{3,7},{7,3},{8,12},{12,8},{9,1... | collective-permute-start | bytes 1572872 | tf_op jit(solution)/shard_map/ppermute | solution.py:343
  88.8 19.1 %copy-start.10 = (bf16[4,128,256]{2,1,0:T(8,128)(2,1)S(1)}, bf16[4,128,256]{2,1,0:T(8,128)(2,1)}, u32[]{:S(2)}) copy-start(bf16[4,128,256]{2,1,0:T(8,128)(2,1)} %copy-done.9) | copy-start | bytes 786436
  89.8 17.3 %collective-permute-start.17 = (bf16[8,2,16,256]{3,2,1,0:T(8,128)(2,1)S(1)}, bf16[8,2,16,256]{3,2,1,0:T(8,128)(2,1)S(1)}, u32[]{:S(2)}, u32[]{:S(2)}) collective-permute-start(bf16[8,2,16,256]{3,2,1,0:T(8,128)(2,1)S(1)} %slice.38), channel_id=1, source_target_pairs={{0,4},{4,0},{1,5},{5,1},{2,6},{6,2},{3,7},{7,3},{8,12},{12,8},{9,1... | collective-permute-start | bytes 393224 | tf_op jit(solution)/shard_map/ppermute | solution.py:343
  116.3 10.9 %collective-permute-start.16 = (bf16[128,1152]{1,0:T(8,128)(2,1)S(1)}, bf16[128,1152]{1,0:T(8,128)(2,1)S(1)}, u32[]{:S(2)}, u32[]{:S(2)}) collective-permute-start(bf16[128,1152]{1,0:T(8,128)(2,1)S(1)} %attend_partner.3), channel_id=1, source_target_pairs={{0,4},{4,0},{1,5},{5,1},{2,6},{6,2},{3,7},{7,3},{8,12},{12,8},{9,1... | collective-permute-start | bytes 884744 | tf_op jit(solution)/shard_map/ppermute | solution.py:343
  123.8 10.4 %collective-permute-start.9 = (bf16[128,1152]{1,0:T(8,128)(2,1)S(1)}, bf16[128,1152]{1,0:T(8,128)(2,1)S(1)}, u32[]{:S(2)}, u32[]{:S(2)}) collective-permute-start(bf16[128,1152]{1,0:T(8,128)(2,1)S(1)} %attend_partner.2), channel_id=1, source_target_pairs={{0,4},{4,0},{1,5},{5,1},{2,6},{6,2},{3,7},{7,3},{8,12},{12,8},{9,1... | collective-permute-start | bytes 884744 | tf_op jit(solution)/shard_map/ppermute | solution.py:343
  (30 other events, 186.2 us)
Sparse Core Ops, SparseCore 0:
  10.1 54.7 all-gather.2

commit v2 on v1

v2 whole, which is shorter than its diff:
```python
import functools
import math

import jax
import jax.numpy as jnp
from jax import lax
from jax.experimental import pallas as pl
from jax.experimental.pallas import tpu as pltpu
from jax.sharding import PartitionSpec as P

HQ = 64
KEY_VALUE_HEADS = 8
HEAD_SIZE = 128
ADAPTER_RANK = 16
BLK = 16
STEPS = 4
GROUP = HQ // KEY_VALUE_HEADS
SHARDS = 16
SIDE = 4
TOKENS = 128
ROWS = 16
DECODE = ROWS * STEPS
ALL_ROWS = TOKENS + DECODE
LOG2_SCALE = math.log2(math.e) / math.sqrt(HEAD_SIZE)
neg_large = -1e30
MIB = 2**20
WIDTH = 2 * HEAD_SIZE


def estimate(us):
    return pl.CostEstimate(flops=int(us * 1.1e9), bytes_accessed=MIB, transcendentals=0)


def split3(x):
    hi = x.astype(jnp.bfloat16)
    rest = x - hi.astype(jnp.float32)
    mid = rest.astype(jnp.bfloat16)
    low = (rest - mid.astype(jnp.float32)).astype(jnp.bfloat16)
    return hi, mid, low


def project_kernel(
    block_ref, row_adapter_ref, span_ref, decode_ref, weight_ref, down_ref, up_ref, adapter_ref, out_ref, rank_ref
):
    hidden = jnp.concatenate([span_ref[...], decode_ref[...]], axis=0)

    @pl.when(pl.program_id(0) == 0)
    def _():
        narrow = jnp.dot(hidden, down_ref[...], preferred_element_type=jnp.float32)
        span_owner = jnp.transpose(jnp.broadcast_to(adapter_ref[...], (TOKENS, TOKENS)))
        row = lax.broadcasted_iota(jnp.int32, (DECODE, TOKENS), 0) // STEPS
        decode_owner = jnp.zeros((DECODE, TOKENS), jnp.int32)
        for r in range(ROWS):
            decode_owner = jnp.where(row == r, row_adapter_ref[r], decode_owner)
        owner = jnp.concatenate([span_owner, decode_owner], axis=0)
        column = lax.broadcasted_iota(jnp.int32, (ALL_ROWS, TOKENS), 1) // ADAPTER_RANK
        hi, mid, low = split3(jnp.where(column == owner, narrow, 0.0))
        rank_ref[:, :TOKENS] = hi
        rank_ref[:, TOKENS : 2 * TOKENS] = mid
        rank_ref[:, 2 * TOKENS :] = low

    up = up_ref[...]
    out = jnp.dot(hidden, weight_ref[...], preferred_element_type=jnp.float32) + jnp.dot(
        rank_ref[...], jnp.concatenate([up, up, up], axis=0), preferred_element_type=jnp.float32
    )
    out_ref[0] = out[:, :WIDTH]
    out_ref[1] = out[:, WIDTH:]


def project(blocks, row_adapter, span, decode, weight, down, up, adapter):
    count = blocks.shape[0]
    depth = span.shape[1]
    whole = lambda i, *_: (0, 0)
    return pl.pallas_call(
        project_kernel,
        grid_spec=pltpu.PrefetchScalarGridSpec(
            num_scalar_prefetch=2,
            grid=(count,),
            in_specs=[
                pl.BlockSpec((TOKENS, depth), whole),
                pl.BlockSpec((DECODE, depth), whole),
                pl.BlockSpec((depth, 2 * WIDTH), lambda i, blocks, rows: (0, blocks[i])),
                pl.BlockSpec((depth, TOKENS), whole),
                pl.BlockSpec((TOKENS, 2 * WIDTH), lambda i, blocks, rows: (0, blocks[i])),
                pl.BlockSpec((1, TOKENS), whole),
            ],
            out_specs=pl.BlockSpec((2, ALL_ROWS, WIDTH), lambda i, *_: (i, 0, 0)),
            scratch_shapes=[pltpu.VMEM((ALL_ROWS, 3 * TOKENS), jnp.bfloat16)],
        ),
        out_shape=jax.ShapeDtypeStruct((2 * count, ALL_ROWS, WIDTH), jnp.float32),
        compiler_params=pltpu.CompilerParams(vmem_limit_bytes=56 * MIB),
        cost_estimate=estimate(3.5),
        name="project",
    )(blocks, row_adapter, span, decode, weight, down, up, adapter)


TILE = 2
TILE_ROWS = TILE * TOKENS
TILES = GROUP // TILE
KEYS = 1024
PER = KEYS // TOKENS
HEAD_ROWS = GROUP * TOKENS
HEAD_COLUMNS = GROUP * HEAD_SIZE


def query_tiles(q_ref):
    return [
        jnp.concatenate(
            [q_ref[:, (i * TILE + j) * HEAD_SIZE : (i * TILE + j + 1) * HEAD_SIZE] for j in range(TILE)], axis=0
        )
        for i in range(TILES)
    ]


def absorb(scores, values, top_before, total_before):
    top = jnp.max(scores, axis=1, keepdims=True) * LOG2_SCALE
    if top_before is not None:
        top = jnp.maximum(top_before, top)
    weights = jnp.exp2(scores * LOG2_SCALE - top).astype(jnp.bfloat16)
    total = jnp.dot(weights, values, preferred_element_type=jnp.float32)
    if top_before is not None:
        total = total_before * jnp.exp2(top_before - top) + total
    return top, total


def score(queries, keys):
    return lax.dot_general(queries, keys, (((1,), (1,)), ((), ())), preferred_element_type=jnp.float32)


def prior_kernel(q_ref, *refs):
    pieces = refs[:SIDE]
    top_ref, acc_ref, ext_ref = refs[SIDE + 1 :]
    queries = query_tiles(q_ref)
    ext_ref[:, HEAD_SIZE:] = jnp.ones((2 * KEYS, HEAD_SIZE), jnp.bfloat16)
    for b in range(SHARDS // PER):
        slot = (b % 2) * KEYS
        half = slice(slot, slot + KEYS)
        kv = jnp.concatenate(
            [pieces[b * 2 + j][:, 0].reshape(SIDE * TOKENS, WIDTH) for j in range(PER // SIDE)], axis=0
        )
        ext_ref[half, :HEAD_SIZE] = kv[:, HEAD_SIZE:]
        keys = kv[:, :HEAD_SIZE]
        for i in range(TILES):
            here = slice(i * TILE_ROWS, (i + 1) * TILE_ROWS)
            before = (top_ref[0, here, :1], acc_ref[0, here]) if b else (None, None)
            top, total = absorb(score(queries[i], keys), ext_ref[half, :], *before)
            acc_ref[0, here] = total
            top_ref[0, here] = jnp.broadcast_to(top, (TILE_ROWS, HEAD_SIZE))


def attend_prior(queries, pieces, after):
    return pl.pallas_call(
        prior_kernel,
        grid=(2,),
        in_specs=[pl.BlockSpec((TOKENS, HEAD_COLUMNS), lambda h: (0, h))]
        + [pl.BlockSpec((SIDE, 1, TOKENS, WIDTH), lambda h: (0, h, 0, 0))] * SIDE
        + [pl.BlockSpec(memory_space=pl.ANY)],
        out_specs=[
            pl.BlockSpec((1, HEAD_ROWS, HEAD_SIZE), lambda h: (h, 0, 0)),
            pl.BlockSpec((1, HEAD_ROWS, WIDTH), lambda h: (h, 0, 0)),
        ],
        out_shape=[
            jax.ShapeDtypeStruct((2, HEAD_ROWS, HEAD_SIZE), jnp.float32),
            jax.ShapeDtypeStruct((2, HEAD_ROWS, WIDTH), jnp.float32),
        ],
        scratch_shapes=[pltpu.VMEM((2 * KEYS, WIDTH), jnp.bfloat16)],
        compiler_params=pltpu.CompilerParams(vmem_limit_bytes=24 * MIB),
        cost_estimate=estimate(7),
        name="attend_prior",
    )(queries, *pieces, after)


def span_kernel(partner, visible_ref, q_ref, known_ref, top_in_ref, acc_in_ref, *refs):
    pieces = refs[:SIDE]
    out_ref, top_ref, acc_ref, ext_ref, key_ref = refs[SIDE:]
    queries = query_tiles(q_ref)
    lane = lax.broadcasted_iota(jnp.int32, (TOKENS, HEAD_SIZE), 1)
    stats = jnp.zeros((TOKENS, HEAD_SIZE), out_ref.dtype)
    blocks = SHARDS // PER
    for b in range(blocks):
        slot = (b % 2) * KEYS
        half = slice(slot, slot + KEYS)
        for n in range(PER):
            shard = b * PER + n
            kv = pieces[shard // SIDE][shard % SIDE, 0]
            seen = visible_ref[shard] != 0
            here = slice(slot + n * TOKENS, slot + (n + 1) * TOKENS)
            key_ref[here, :] = jnp.where(seen, kv[:, :HEAD_SIZE], known_ref[0, 0, :, :HEAD_SIZE])
            ext_ref[here, :HEAD_SIZE] = jnp.where(seen, kv[:, HEAD_SIZE:], jnp.zeros_like(kv[:, HEAD_SIZE:]))
            ext_ref[here, HEAD_SIZE:] = jnp.where(
                seen, jnp.ones((TOKENS, HEAD_SIZE), jnp.bfloat16), jnp.zeros((TOKENS, HEAD_SIZE), jnp.bfloat16)
            )
        keys = key_ref[half, :]
        for i in range(TILES):
            here = slice(i * TILE_ROWS, (i + 1) * TILE_ROWS)
            scores = score(queries[i], keys)
            if b == 0 and not partner:
                token = lax.broadcasted_iota(jnp.int32, (TILE_ROWS, TOKENS), 0) % TOKENS
                key = lax.broadcasted_iota(jnp.int32, (TILE_ROWS, TOKENS), 1)
                scores = jnp.concatenate(
                    [jnp.where(key <= token, scores[:, :TOKENS], neg_large), scores[:, TOKENS:]], axis=1
                )
            before = (top_ref[here, :1], acc_ref[here]) if b else (top_in_ref[0, here, :1], acc_in_ref[0, here])
            top, total = absorb(scores, ext_ref[half, :], *before)
            if b < blocks - 1:
                acc_ref[here] = total
                top_ref[here] = jnp.broadcast_to(top, (TILE_ROWS, HEAD_SIZE))
                continue
            out = total[:, :HEAD_SIZE] / total[:, HEAD_SIZE:]
            level = top + jnp.log2(total[:, HEAD_SIZE:])
            for j in range(TILE):
                g = i * TILE + j
                own = slice(j * TOKENS, (j + 1) * TOKENS)
                out_ref[:, g * HEAD_SIZE : (g + 1) * HEAD_SIZE] = out[own].astype(out_ref.dtype)
                parts = split3(level[own]) if partner else (level[own],)
                for part, piece in enumerate(parts):
                    stats = jnp.where(lane == part * GROUP + g, piece, stats)
    out_ref[:, HEAD_COLUMNS:] = stats


def attend_span(partner, visible, queries, head, known, state, pieces):
    out_width = HEAD_COLUMNS + HEAD_SIZE
    dtype = jnp.bfloat16 if partner else jnp.float32
    return pl.pallas_call(
        functools.partial(span_kernel, partner),
        grid_spec=pltpu.PrefetchScalarGridSpec(
            num_scalar_prefetch=1,
            grid=(1,),
            in_specs=[
                pl.BlockSpec((TOKENS, HEAD_COLUMNS), lambda i, *_: (0, head)),
                pl.BlockSpec((1, 1, TOKENS, WIDTH), lambda i, *_: (0, head, 0, 0)),
                pl.BlockSpec((1, HEAD_ROWS, HEAD_SIZE), lambda i, *_: (head, 0, 0)),
                pl.BlockSpec((1, HEAD_ROWS, WIDTH), lambda i, *_: (head, 0, 0)),
            ]
            + [pl.BlockSpec((SIDE, 1, TOKENS, WIDTH), lambda i, *_: (0, head, 0, 0))] * SIDE,
            out_specs=pl.BlockSpec((TOKENS, out_width), lambda i, *_: (0, 0)),
            scratch_shapes=[
                pltpu.VMEM((HEAD_ROWS, HEAD_SIZE), jnp.float32),
                pltpu.VMEM((HEAD_ROWS, WIDTH), jnp.float32),
                pltpu.VMEM((2 * KEYS, WIDTH), jnp.bfloat16),
                pltpu.VMEM((2 * KEYS, HEAD_SIZE), jnp.bfloat16),
            ],
        ),
        out_shape=jax.ShapeDtypeStruct((TOKENS, out_width), dtype),
        compiler_params=pltpu.CompilerParams(vmem_limit_bytes=24 * MIB),
        cost_estimate=estimate(4),
        name="attend_partner" if partner else "attend_own",
    )(visible, queries, known, *state, *pieces)


def combine_kernel(*refs):
    out_ref = refs[4]
    for h in range(2):
        own_ref, other_ref = refs[h], refs[2 + h]
        own_level = own_ref[:, HEAD_COLUMNS:]
        other_parts = other_ref[:, HEAD_COLUMNS:].astype(jnp.float32)
        for g in range(GROUP):
            mine = own_level[:, g : g + 1]
            theirs = (
                other_parts[:, g : g + 1]
                + other_parts[:, GROUP + g : GROUP + g + 1]
                + other_parts[:, 2 * GROUP + g : 2 * GROUP + g + 1]
            )
            peak = jnp.maximum(mine, theirs)
            mine = jnp.exp2(mine - peak)
            theirs = jnp.exp2(theirs - peak)
            whole = mine + theirs
            columns = slice(g * HEAD_SIZE, (g + 1) * HEAD_SIZE)
            mixed = (mine / whole) * own_ref[:, columns] + (theirs / whole) * other_ref[:, columns].astype(
                jnp.float32
            )
            out_ref[:, h * HEAD_COLUMNS + g * HEAD_SIZE : h * HEAD_COLUMNS + (g + 1) * HEAD_SIZE] = mixed.astype(
                jnp.bfloat16
            )


def combine(own, other):
    return pl.pallas_call(
        combine_kernel,
        out_shape=jax.ShapeDtypeStruct((TOKENS, 2 * HEAD_COLUMNS), jnp.bfloat16),
        compiler_params=pltpu.CompilerParams(vmem_limit_bytes=16 * MIB),
        cost_estimate=estimate(1.5),
        name="combine",
    )(*own, *other)


ROW_BLOCK = 4


def decode_kernel(length_ref, live_ref, q_ref, cache_ref, fresh_ref, out_ref):
    first = pl.program_id(0) * ROW_BLOCK
    query_rows = STEPS * GROUP
    cache_size = cache_ref.shape[2]
    fresh_row = lax.broadcasted_iota(jnp.int32, (query_rows, DECODE), 1) // STEPS
    fresh_step = lax.broadcasted_iota(jnp.int32, (query_rows, DECODE), 1) % STEPS
    step = lax.broadcasted_iota(jnp.int32, (query_rows, DECODE), 0) // GROUP
    slot = lax.broadcasted_iota(jnp.int32, (query_rows, cache_size), 1)
    contract = (((1,), (1,)), ((), ()))
    for n in range(ROW_BLOCK):
        row = first + n
        length = length_ref[row]
        live = row < live_ref[0]
        for h in range(2):
            queries = q_ref[n, h]
            cached = lax.dot_general(
                queries, cache_ref[n, h, :, :HEAD_SIZE], contract, preferred_element_type=jnp.float32
            )
            fresh = lax.dot_general(
                queries, fresh_ref[h, :, :HEAD_SIZE], contract, preferred_element_type=jnp.float32
            )
            cached = jnp.where(slot < length, cached, neg_large)
            fresh = jnp.where((fresh_row == row) & (fresh_step <= step), fresh, neg_large)
            top = jnp.maximum(jnp.max(cached, axis=1, keepdims=True), jnp.max(fresh, axis=1, keepdims=True))
            cached = jnp.exp2((cached - top) * LOG2_SCALE)
            fresh = jnp.exp2((fresh - top) * LOG2_SCALE)
            total = jnp.sum(cached, axis=1, keepdims=True) + jnp.sum(fresh, axis=1, keepdims=True)
            out = jnp.dot(
                cached.astype(jnp.bfloat16), cache_ref[n, h, :, HEAD_SIZE:], preferred_element_type=jnp.float32
            ) + jnp.dot(
                fresh.astype(jnp.bfloat16), fresh_ref[h, :, HEAD_SIZE:], preferred_element_type=jnp.float32
            )
            out_ref[n, h] = jnp.where(live, out / total, 0.0).astype(jnp.bfloat16)


def decode_attend(lengths, live, queries, cache, fresh):
    rows, heads, query_rows, _ = queries.shape
    cache_size = cache.shape[2]
    return pl.pallas_call(
        decode_kernel,
        grid_spec=pltpu.PrefetchScalarGridSpec(
            num_scalar_prefetch=2,
            grid=(rows // ROW_BLOCK,),
            in_specs=[
                pl.BlockSpec((ROW_BLOCK, heads, query_rows, HEAD_SIZE), lambda i, *_: (i, 0, 0, 0)),
                pl.BlockSpec((ROW_BLOCK, heads, cache_size, 2 * HEAD_SIZE), lambda i, *_: (i, 0, 0, 0)),
                pl.BlockSpec((heads, DECODE, 2 * HEAD_SIZE), lambda i, *_: (0, 0, 0)),
            ],
            out_specs=pl.BlockSpec((ROW_BLOCK, heads, query_rows, HEAD_SIZE), lambda i, *_: (i, 0, 0, 0)),
        ),
        out_shape=jax.ShapeDtypeStruct(queries.shape, jnp.bfloat16),
        compiler_params=pltpu.CompilerParams(vmem_limit_bytes=16 * MIB),
        cost_estimate=estimate(8),
        name="decode",
    )(lengths, live, queries, cache, fresh)


def pages_kernel(where_ref, *refs):
    pieces = refs[:SIDE]
    out_ref = refs[SIDE]
    for n in range(out_ref.shape[0]):
        dy, dz = where_ref[0, n], where_ref[1, n]
        rows = pl.ds(pl.multiple_of(where_ref[2, n] * BLK, BLK), BLK)
        for h in range(2):
            page = pieces[0][dz, h, rows, :]
            for k in range(1, SIDE):
                page = jnp.where(dy == k, pieces[k][dz, h, rows, :], page)
            out_ref[n, h] = page


def pick_pages(where, pieces):
    count = where.shape[1]
    return pl.pallas_call(
        pages_kernel,
        grid_spec=pltpu.PrefetchScalarGridSpec(
            num_scalar_prefetch=1,
            grid=(1,),
            in_specs=[pl.BlockSpec((SIDE, 2, TOKENS, WIDTH), lambda i, *_: (0, 0, 0, 0))] * SIDE,
            out_specs=pl.BlockSpec((count, 2, BLK, WIDTH), lambda i, *_: (0, 0, 0, 0)),
        ),
        out_shape=jax.ShapeDtypeStruct((count, 2, BLK, WIDTH), jnp.bfloat16),
        compiler_params=pltpu.CompilerParams(vmem_limit_bytes=16 * MIB),
        cost_estimate=estimate(1.5),
        name="pages",
    )(where, *pieces)


def shift(x, dz, dy):
    perm = [
        (z * SIDE + y, ((z + dz) % SIDE) * SIDE + (y + dy) % SIDE) for z in range(SIDE) for y in range(SIDE)
    ]
    return lax.ppermute(x, "ctx", perm)


def swap_pool(x):
    return lax.ppermute(x, "pool", [(0, 1), (1, 0)])


def swap_tp(x, bit):
    return lax.ppermute(x, "tp", [(i, i ^ bit) for i in range(4)])


def ring(x, along_z):
    move = (lambda d: shift(x, d, 0)) if along_z else (lambda d: shift(x, 0, d))
    far = {1: move(1), 3: move(3), 2: move(2)}
    return [x, far[1], far[2], far[3]]


def per_device(
    span_hidden_states,
    span_token_queries,
    earlier_key_values,
    decode_hidden_states,
    decode_token_queries,
    decode_row_cache,
    key_value_weight,
    adapter_down_weight,
    adapter_up_weight,
    prompt_adapter,
    row_adapter_index,
    group_live_rows,
    cached_row_lengths,
    block_target_page,
):
    tp = lax.axis_index("tp")
    ctx = lax.axis_index("ctx")
    pool = lax.axis_index("pool")
    my_z, my_y = ctx // SIDE, ctx % SIDE
    depth = span_hidden_states.shape[1]

    prior = ring(jnp.stack(ring(earlier_key_values, False)), True)

    decode_hidden = decode_hidden_states.reshape(DECODE, depth)

    def partial_kv(bits):
        return project(
            jnp.stack([jnp.bitwise_xor(tp, bit) for bit in bits]).astype(jnp.int32),
            row_adapter_index,
            span_hidden_states,
            decode_hidden,
            key_value_weight,
            adapter_down_weight,
            adapter_up_weight,
            prompt_adapter.reshape(1, TOKENS),
        )

    from_core = swap_tp(partial_kv((1, 3)), 1)
    kept = partial_kv((0, 2))

    def owned(rows):
        from_chip = swap_tp(kept[2:, rows] + from_core[2:, rows], 2)
        return (kept[:2, rows] + from_core[:2, rows] + from_chip).astype(jnp.bfloat16)

    span_kv = owned(slice(0, TOKENS))
    decode_kv = owned(slice(TOKENS, ALL_ROWS))

    column = jnp.stack(ring(span_kv, True))
    planes = ring(column, False)

    queries = decode_token_queries.reshape(ROWS, STEPS, 2, GROUP, HEAD_SIZE)
    queries = jnp.transpose(queries, (0, 2, 1, 3, 4)).reshape(ROWS, 2, STEPS * GROUP, HEAD_SIZE)
    decoded = decode_attend(cached_row_lengths, group_live_rows, queries, decode_row_cache, decode_kv)
    decoded = jnp.transpose(decoded.reshape(ROWS, 2, STEPS, GROUP, HEAD_SIZE), (0, 2, 1, 3, 4))
    decode_attention = decoded.reshape(ROWS, STEPS, 2 * GROUP * HEAD_SIZE)

    partner_queries = swap_pool(span_token_queries)
    own_state = attend_prior(span_token_queries, prior, column)
    partner_state = attend_prior(partner_queries, prior, column)

    pages = TOKENS // BLK
    shard = ctx * 2 + pool
    partner_shard = ctx * 2 + 1 - pool
    page_ids = jnp.concatenate([shard * pages + jnp.arange(pages), partner_shard * pages + jnp.arange(pages)])
    block_ids = jnp.arange(block_target_page.shape[0], dtype=jnp.int32)
    source = jnp.sum(
        jnp.where(block_target_page[None, :] == page_ids[:, None], block_ids[None, :], 0), axis=1
    )
    source_shard = source // pages
    source_ctx = source_shard // 2
    where = jnp.stack(
        [
            jnp.mod(my_y - source_ctx % SIDE, SIDE),
            jnp.mod(my_z - source_ctx // SIDE, SIDE),
            source % pages,
        ]
    ).astype(jnp.int32)
    planes, own_state, partner_state, decode_attention = lax.optimization_barrier(
        (planes, own_state, partner_state, decode_attention)
    )
    found = pick_pages(where, planes)
    found, planes = lax.optimization_barrier((found, planes))
    from_partner = swap_pool(found[pages:])
    mine = (source_shard % 2 == pool)[:pages]
    handoff_pages = jnp.where(mine[:, None, None, None], found[:pages], from_partner)

    far = jnp.arange(SIDE, dtype=jnp.int32)
    shard_z, shard_y = jnp.mod(my_z - far, SIDE), jnp.mod(my_y - far, SIDE)
    place = shard_z[None, :] * SIDE + shard_y[:, None]
    partner_sees = ((place < ctx) | ((place == ctx) & (pool == 0))).astype(jnp.int32).reshape(-1)
    own_sees = (place <= ctx).astype(jnp.int32).reshape(-1)
    other = [
        swap_pool(attend_span(True, partner_sees, partner_queries, h, prior[0], partner_state, planes))
        for h in range(2)
    ]
    own = [attend_span(False, own_sees, span_token_queries, h, prior[0], own_state, planes) for h in range(2)]
    span_attention = combine(own, other)
    return (span_attention, handoff_pages, decode_attention)


def solution(mesh):
    in_specs = (
        P(("ctx", "pool"), "tp"),
        P(("ctx", "pool"), "tp"),
        P("tp", ("ctx", "pool"), None),
        P(("ctx", "pool"), None, "tp"),
        P(("ctx", "pool"), None, "tp"),
        P(("ctx", "pool"), "tp", None, None),
        P("tp", None),
        P("tp", None),
        P(),
        P(("ctx", "pool")),
        P(("ctx", "pool")),
        P(("ctx", "pool")),
        P(("ctx", "pool")),
        P(),
    )
    out_specs = (
        P(("ctx", "pool"), "tp"),
        P(("ctx", "pool"), "tp", None, None),
        P(("ctx", "pool"), None, "tp"),
    )
    return jax.shard_map(
        per_device, mesh=mesh, in_specs=in_specs, out_specs=out_specs, check_vma=False
    )
```

time: 150 us -> 122 us (0.81)
  local copies, waits for them, and re-layouts: 20.9 us -> 2.94 us
  between operations: 15.2 us -> 1.5 us
  waiting for transfers between devices: 24.1 us -> 28.3 us
  other arithmetic: 4.14 us -> 7.26 us
  starting transfers between devices: 31.3 us -> 29.2 us
    unnamed x70 -> x12, local copies, waits for them, and re-layouts: 16.6 us -> 0.03 us
    ppermute x12, waiting for transfers between devices: 17.8 us -> 26.5 us  [shift(): return lax.ppermute(x, 'ctx', perm)]
    pallas_call x5 -> x8, Pallas kernels: 37.3 us -> 31.8 us  [the longest x4 15.9 us: attend_span(): pl.pallas_call(functools.partial(span_kernel, partner), grid_spec=pltpu.P...]
    ppermute x2 -> x3, waiting for transfers between devices: 5.61 us -> 0.23 us  [swap_tp(): return lax.ppermute(x, 'tp', [(i, i ^ bit) for i in range(4)])]
    pallas_call x2, Pallas kernels: 7.02 us -> 11.3 us  [project(): pl.pallas_call(project_kernel, grid_spec=pltpu.PrefetchScalarGridSpec(num...]
    ppermute x4, starting transfers between devices: 10.5 us -> 7.52 us  [swap_pool(): return lax.ppermute(x, 'pool', [(0, 1), (1, 0)])]
    convert_element_type x2 -> x3, other arithmetic: 0.13 us -> 2.02 us  [the longest x2 1.94 us: owned(): (kept[:2, rows] + from_core[:2, rows] + from_chip).astype(jnp.bfloat16)]
    ppermute x4, waiting for transfers between devices: 0.01 us -> 1.62 us  [swap_pool(): return lax.ppermute(x, 'pool', [(0, 1), (1, 0)])]
  transfers between devices with their start and end apart: 19 -> 19, of which waited for: 8 -> 5; matrix products, arithmetic and copies ran while one was open for 5% -> 8% of each run, Pallas kernels for 27% -> 41%
where the time goes in v2:
time: 122 us; the launch traced here: 121 us
  Pallas kernels  51.9 us (43%)
  starting transfers between devices  29.2 us (24%)
  waiting for transfers between devices  28.3 us (23%)
  other arithmetic  7.26 us (6%)
  local copies, waits for them, and re-layouts  2.94 us (2%)
  between operations  1.5 us (1%)
    ppermute x12, waiting for transfers between devices, shift(): return lax.ppermute(x, 'ctx', perm)  26.5 us
    ppermute x12, starting transfers between devices, shift(): return lax.ppermute(x, 'ctx', perm)  19.5 us
    pallas_call x4, Pallas kernels, attend_span(): pl.pallas_call(functools.partial(span_kernel, partner), grid_spec=pltpu.P...  15.9 us
    pallas_call x2, Pallas kernels, attend_prior(): pl.pallas_call(prior_kernel, grid=(2,), in_specs=[pl.BlockSpec((TOKENS, H...  13.4 us
    pallas_call x2, Pallas kernels, project(): pl.pallas_call(project_kernel, grid_spec=pltpu.PrefetchScalarGridSpec(num...  11.3 us
    pallas_call x1, Pallas kernels, decode_attend(): pl.pallas_call(decode_kernel, grid_spec=pltpu.PrefetchScalarGridSpec(num_...  8.8 us
    ppermute x4, starting transfers between devices, swap_pool(): return lax.ppermute(x, 'pool', [(0, 1), (1, 0)])  7.52 us
  transfers between devices with their start and end apart: 19, of which 5 were waited for; matrix products, arithmetic and copies ran while one was open for 8% of the time, Pallas kernels for 41%

profile of v2, /device:TPU:0, one launch (start us, length us, event | category | flops | bytes accessed | tf_op | source)
XLA Modules:
  0.0 121.1 jit_solution(6765124833111578157)
XLA Ops:
  0.6 1.7 %collective-permute-start = (bf16[2,128,256]{2,1,0:T(8,128)(2,1)}, bf16[2,128,256]{2,1,0:T(8,128)(2,1)S(1)}, u32[]{:S(2)}, u32[]{:S(2)}) collective-permute-start(bf16[2,128,256]{2,1,0:T(8,128)(2,1)} %param.16), channel_id=1, source_target_pairs={{0,8},{8,16},{16,24},{24,0},{32,40},{40,48},{48,56},{56,32},{64,72... | collective-permute-start | bytes 393224 | tf_op jit(solution)/shard_map/ppermute | solution.py:381
  2.4 1.6 %collective-permute-start.2 = (bf16[2,128,256]{2,1,0:T(8,128)(2,1)}, bf16[2,128,256]{2,1,0:T(8,128)(2,1)S(1)}, u32[]{:S(2)}, u32[]{:S(2)}) collective-permute-start(bf16[2,128,256]{2,1,0:T(8,128)(2,1)} %param.16), channel_id=1, source_target_pairs={{0,24},{8,0},{16,8},{24,16},{32,56},{40,32},{48,40},{56,48},{64,88... | collective-permute-start | bytes 393224 | tf_op jit(solution)/shard_map/ppermute | solution.py:381
  3.9 2.1 %collective-permute-start.1 = (bf16[2,128,256]{2,1,0:T(8,128)(2,1)}, bf16[2,128,256]{2,1,0:T(8,128)(2,1)S(1)}, u32[]{:S(2)}, u32[]{:S(2)}) collective-permute-start(bf16[2,128,256]{2,1,0:T(8,128)(2,1)} %param.16), channel_id=1, source_target_pairs={{0,16},{8,24},{16,0},{24,8},{32,48},{40,56},{48,32},{56,40},{64,80... | collective-permute-start | bytes 393224 | tf_op jit(solution)/shard_map/ppermute | solution.py:381
  6.0 1.7 %reshape.335.decode_ref = bf16[64,2048]{1,0:T(8,128)(2,1)} reshape(bf16[16,4,2048]{2,1,0:T(4,128)(2,1)} %param.17) | data formatting | bytes 524288 | tf_op jit(solution)/shard_map/reshape | solution.py:422
  8.4 5.4 %project.3 = f32[4,192,256]{2,1,0:T(8,128)} custom-call(s32[2]{0:T(128)} %pad_add_fusion.2.block_ref, s32[16]{0:T(128)} %row_adapter_ref.3, bf16[128,2048]{1,0:T(8,128)(2,1)} %span_ref.3, bf16[64,2048]{1,0:T(8,128)(2,1)} %reshape.335.decode_ref, bf16[2048,2048]{1,0:T(8,128)(2,1)} %weight_ref.3, bf16[2048,128]{1,0:T(8,128)(2,1)} %down_ref.3, ...), custom_call_target="tpu_custom_call" | custom-call | flops 3849999872 | bytes 1048576 | tf_op jit(solution)/shard_map/project/pallas_call | solution.py:74
  15.9 5.9 %project.2 = f32[4,192,256]{2,1,0:T(8,128)} custom-call(s32[2]{0:T(128)} %pad_add_fusion.1.block_ref, s32[16]{0:T(128)} %row_adapter_ref.3, bf16[128,2048]{1,0:T(8,128)(2,1)} %span_ref.3, bf16[64,2048]{1,0:T(8,128)(2,1)} %reshape.335.decode_ref, bf16[2048,2048]{1,0:T(8,128)(2,1)} %weight_ref.3, bf16[2048,128]{1,0:T(8,128)(2,1)} %down_ref.3, ...), custom_call_target="tpu_custom_call" | custom-call | flops 3849999872 | bytes 1048576 | tf_op jit(solution)/shard_map/project/pallas_call | solution.py:74
  22.7 1.6 %collective-permute-start.4 = (f32[2,128,256]{2,1,0:T(8,128)S(1)}, f32[2,128,256]{2,1,0:T(8,128)S(1)}, u32[]{:S(2)}, u32[]{:S(2)}) collective-permute-start(f32[2,128,256]{2,1,0:T(8,128)S(1)} %slice_add_fusion), channel_id=1, source_target_pairs={{0,2},{1,3},{2,0},{3,1},{4,6},{5,7},{6,4},{7,5},{8,10},{9,11},{10,... | collective-permute-start | bytes 786440 | tf_op jit(solution)/shard_map/ppermute | solution.py:389
  24.4 4.1 %collective-permute-start.13 = (bf16[4,2,128,256]{3,2,1,0:T(8,128)(2,1)S(1)}, bf16[4,2,128,256]{3,2,1,0:T(8,128)(2,1)S(1)}, u32[]{:S(2)}, u32[]{:S(2)}) collective-permute-start(bf16[4,2,128,256]{3,2,1,0:T(8,128)(2,1)S(1)} %pad_maximum_fusion.refs_0_.known_ref), channel_id=1, source_target_pairs={{0,96},{8,104},{16,112},{24,120},{32,0},{40,8},{48,16},{56,24},{64... | collective-permute-start | bytes 1572872 | tf_op jit(solution)/shard_map/ppermute | solution.py:381
  28.5 1.3 %collective-permute-start.11 = (bf16[4,2,128,256]{3,2,1,0:T(8,128)(2,1)S(1)}, bf16[4,2,128,256]{3,2,1,0:T(8,128)(2,1)S(1)}, u32[]{:S(2)}, u32[]{:S(2)}) collective-permute-start(bf16[4,2,128,256]{3,2,1,0:T(8,128)(2,1)S(1)} %pad_maximum_fusion.refs_0_.known_ref), channel_id=1, source_target_pairs={{0,32},{8,40},{16,48},{24,56},{32,64},{40,72},{48,80},{56,88},{64,... | collective-permute-start | bytes 1572872 | tf_op jit(solution)/shard_map/ppermute | solution.py:381
  32.5 4.5 %collective-permute-start.7 = (bf16[2,128,256]{2,1,0:T(8,128)(2,1)S(1)}, bf16[2,128,256]{2,1,0:T(8,128)(2,1)S(1)}, u32[]{:S(2)}, u32[]{:S(2)}) collective-permute-start(bf16[2,128,256]{2,1,0:T(8,128)(2,1)S(1)} %fusion.1), channel_id=1, source_target_pairs={{0,96},{8,104},{16,112},{24,120},{32,0},{40,8},{48,16},{56,24},{64... | collective-permute-start | bytes 393224 | tf_op jit(solution)/shard_map/ppermute | solution.py:381
  38.0 1.3 %collective-permute-start.6 = (bf16[2,128,256]{2,1,0:T(8,128)(2,1)S(1)}, bf16[2,128,256]{2,1,0:T(8,128)(2,1)S(1)}, u32[]{:S(2)}, u32[]{:S(2)}) collective-permute-start(bf16[2,128,256]{2,1,0:T(8,128)(2,1)S(1)} %fusion.1), channel_id=1, source_target_pairs={{0,64},{8,72},{16,80},{24,88},{32,96},{40,104},{48,112},{56,120},{... | collective-permute-start | bytes 393224 | tf_op jit(solution)/shard_map/ppermute | solution.py:381
  39.2 17.7 %collective-permute-done.7 = bf16[2,128,256]{2,1,0:T(8,128)(2,1)S(1)} collective-permute-done((bf16[2,128,256]{2,1,0:T(8,128)(2,1)S(1)}, bf16[2,128,256]{2,1,0:T(8,128)(2,1)S(1)}, u32[]{:S(2)}, u32[]{:S(2)}) %collective-permute-start.7) | collective-permute-done | bytes 131104 | tf_op jit(solution)/shard_map/ppermute | solution.py:381
  56.9 8.8 %decode.1 = bf16[16,2,32,128]{3,2,1,0:T(8,128)(2,1)S(1)} custom-call(s32[16]{0:T(128)S(1)} %copy-done.2, s32[1]{0:T(128)S(6)} %copy.23.live_ref, bf16[16,2,32,128]{3,2,1,0:T(8,128)(2,1)S(1)} %bitcast.49, bf16[16,2,256,256]{3,2,1,0:T(8,128)(2,1)S(1)} %copy-done, bf16[2,64,256]{2,1,0:T(8,128)(2,1)S(1)} %fusion.3.fresh_ref), custom_call_target="tpu_custom_call" | custom-call | flops 8800000000 | bytes 1048576 | tf_op jit(solution)/shard_map/decode/pallas_call | solution.py:328
  66.6 2.7 %collective-permute-start.14 = (bf16[128,2048]{1,0:T(8,128)(2,1)S(1)}, bf16[128,2048]{1,0:T(8,128)(2,1)S(1)}, u32[]{:S(2)}, u32[]{:S(2)}) collective-permute-start(bf16[128,2048]{1,0:T(8,128)(2,1)S(1)} %copy-done.1), channel_id=1, source_target_pairs={{0,4},{4,0},{1,5},{5,1},{2,6},{6,2},{3,7},{7,3},{8,12},{12,8},{9,1... | collective-permute-start | bytes 1572872 | tf_op jit(solution)/shard_map/ppermute | solution.py:385
  71.4 1.7 %collective-permute-start.9 = (bf16[4,2,128,256]{3,2,1,0:T(8,128)(2,1)S(1)}, bf16[4,2,128,256]{3,2,1,0:T(8,128)(2,1)S(1)}, u32[]{:S(2)}, u32[]{:S(2)}) collective-permute-start(bf16[4,2,128,256]{3,2,1,0:T(8,128)(2,1)S(1)} %pad_maximum_fusion.1.refs_4_.refs_0_), channel_id=1, source_target_pairs={{0,16},{8,24},{16,0},{24,8},{32,48},{40,56},{48,32},{56,40},{64,80... | collective-permute-start | bytes 1572872 | tf_op jit(solution)/shard_map/ppermute | solution.py:381
  73.3 6.7 %attend_prior.2 = (f32[2,1024,128]{2,1,0:T(8,128)S(1)}, f32[2,1024,256]{2,1,0:T(8,128)S(1)}) custom-call(bf16[128,2048]{1,0:T(8,128)(2,1)S(1)} %copy-done.1, bf16[4,2,128,256]{3,2,1,0:T(8,128)(2,1)S(1)} %pad_maximum_fusion.refs_0_.known_ref, bf16[4,2,128,256]{3,2,1,0:T(8,128)(2,1)S(1)} %collective-permute-done.11.refs_1_, ...), custom_call_target="tpu_custom_call" | custom-call | flops 7699999744 | bytes 1048576 | tf_op jit(solution)/shard_map/attend_prior/pallas_call | solution.py:152
  81.3 6.7 %attend_prior.3 = (f32[2,1024,128]{2,1,0:T(8,128)S(1)}, f32[2,1024,256]{2,1,0:T(8,128)S(1)}) custom-call(bf16[128,2048]{1,0:T(8,128)(2,1)S(1)} %collective-permute-done.14.q_ref, bf16[4,2,128,256]{3,2,1,0:T(8,128)(2,1)S(1)} %pad_maximum_fusion.refs_0_.known_ref, bf16[4,2,128,256]{3,2,1,0:T(8,128)(2,1)S(1)} %collective-permute-done.11.refs_1_, ...), custom_call_target="tpu_custom_call" | custom-call | flops 7699999744 | bytes 1048576 | tf_op jit(solution)/shard_map/attend_prior/pallas_call | solution.py:152
  88.1 8.8 %collective-permute-done.8.refs_1_ = bf16[4,2,128,256]{3,2,1,0:T(8,128)(2,1)S(1)} collective-permute-done((bf16[4,2,128,256]{3,2,1,0:T(8,128)(2,1)S(1)}, bf16[4,2,128,256]{3,2,1,0:T(8,128)(2,1)S(1)}, u32[]{:S(2)}, u32[]{:S(2)}) %collective-permute-start.8) | collective-permute-done | bytes 524320 | tf_op jit(solution)/shard_map/ppermute | solution.py:381
  98.4 4.0 %attend_partner.2 = bf16[128,1152]{1,0:T(8,128)(2,1)S(1)} custom-call(s32[16]{0:T(128)S(1)} %reshape.342.visible_ref, bf16[128,2048]{1,0:T(8,128)(2,1)S(1)} %collective-permute-done.14.q_ref, bf16[4,2,128,256]{3,2,1,0:T(8,128)(2,1)S(1)} %pad_maximum_fusion.refs_0_.known_ref, f32[2,1024,128]{2,1,0:T(8,128)S(1)} %get-tuple-element.35.top_in_ref, ...), custom_call_target="tpu_custom_call" | custom-call | flops 4400000000 | bytes 1048576 | tf_op jit(solution)/shard_map/attend_partner/pallas_call | solution.py:224
  102.4 3.0 %collective-permute-start.16 = (bf16[128,1152]{1,0:T(8,128)(2,1)S(1)}, bf16[128,1152]{1,0:T(8,128)(2,1)S(1)}, u32[]{:S(2)}, u32[]{:S(2)}) collective-permute-start(bf16[128,1152]{1,0:T(8,128)(2,1)S(1)} %attend_partner.2), channel_id=1, source_target_pairs={{0,4},{4,0},{1,5},{5,1},{2,6},{6,2},{3,7},{7,3},{8,12},{12,8},{9,1... | collective-permute-start | bytes 884744 | tf_op jit(solution)/shard_map/ppermute | solution.py:385
  105.4 4.0 %attend_partner.3 = bf16[128,1152]{1,0:T(8,128)(2,1)S(1)} custom-call(s32[16]{0:T(128)S(1)} %reshape.342.visible_ref, bf16[128,2048]{1,0:T(8,128)(2,1)S(1)} %collective-permute-done.14.q_ref, bf16[4,2,128,256]{3,2,1,0:T(8,128)(2,1)S(1)} %pad_maximum_fusion.refs_0_.known_ref, f32[2,1024,128]{2,1,0:T(8,128)S(1)} %get-tuple-element.35.top_in_ref, ...), custom_call_target="tpu_custom_call" | custom-call | flops 4400000000 | bytes 1048576 | tf_op jit(solution)/shard_map/attend_partner/pallas_call | solution.py:224
  110.2 4.0 %attend_own.3.refs_1_ = f32[128,1152]{1,0:T(8,128)S(1)} custom-call(s32[16]{0:T(128)S(1)} %reshape.341.visible_ref, bf16[128,2048]{1,0:T(8,128)(2,1)S(1)} %copy-done.1, bf16[4,2,128,256]{3,2,1,0:T(8,128)(2,1)S(1)} %pad_maximum_fusion.refs_0_.known_ref, f32[2,1024,128]{2,1,0:T(8,128)S(1)} %get-tuple-element.25.top_in_ref, ...), custom_call_target="tpu_custom_call" | custom-call | flops 4400000000 | bytes 1048576 | tf_op jit(solution)/shard_map/attend_own/pallas_call | solution.py:224
  114.2 4.0 %attend_own.2.refs_0_ = f32[128,1152]{1,0:T(8,128)S(1)} custom-call(s32[16]{0:T(128)S(1)} %reshape.341.visible_ref, bf16[128,2048]{1,0:T(8,128)(2,1)S(1)} %copy-done.1, bf16[4,2,128,256]{3,2,1,0:T(8,128)(2,1)S(1)} %pad_maximum_fusion.refs_0_.known_ref, f32[2,1024,128]{2,1,0:T(8,128)S(1)} %get-tuple-element.25.top_in_ref, ...), custom_call_target="tpu_custom_call" | custom-call | flops 4400000000 | bytes 1048576 | tf_op jit(solution)/shard_map/attend_own/pallas_call | solution.py:224
  119.3 1.8 %combine.1 = bf16[128,2048]{1,0:T(8,128)(2,1)} custom-call(f32[128,1152]{1,0:T(8,128)S(1)} %attend_own.2.refs_0_, f32[128,1152]{1,0:T(8,128)S(1)} %attend_own.3.refs_1_, bf16[128,1152]{1,0:T(8,128)(2,1)S(1)} %collective-permute-done.16.refs_2_, bf16[128,1152]{1,0:T(8,128)(2,1)S(1)} %collective-permute-done.17.refs_3_), custom_call_target="tpu_custom_call" | custom-call | flops 1650000000 | bytes 1048576 | tf_op jit(solution)/shard_map/combine/pallas_call | solution.py:278
  (62 shorter events, 14.7 us)
Async XLA Ops:
  0.6 23.7 %collective-permute-start = (bf16[2,128,256]{2,1,0:T(8,128)(2,1)}, bf16[2,128,256]{2,1,0:T(8,128)(2,1)S(1)}, u32[]{:S(2)}, u32[]{:S(2)}) collective-permute-start(bf16[2,128,256]{2,1,0:T(8,128)(2,1)} %param.16), channel_id=1, source_target_pairs={{0,8},{8,16},{16,24},{24,0},{32,40},{40,48},{48,56},{56,32},{64,72... | collective-permute-start | bytes 393224 | tf_op jit(solution)/shard_map/ppermute | solution.py:381
  2.4 21.9 %collective-permute-start.2 = (bf16[2,128,256]{2,1,0:T(8,128)(2,1)}, bf16[2,128,256]{2,1,0:T(8,128)(2,1)S(1)}, u32[]{:S(2)}, u32[]{:S(2)}) collective-permute-start(bf16[2,128,256]{2,1,0:T(8,128)(2,1)} %param.16), channel_id=1, source_target_pairs={{0,24},{8,0},{16,8},{24,16},{32,56},{40,32},{48,40},{56,48},{64,88... | collective-permute-start | bytes 393224 | tf_op jit(solution)/shard_map/ppermute | solution.py:381
  3.9 20.4 %collective-permute-start.1 = (bf16[2,128,256]{2,1,0:T(8,128)(2,1)}, bf16[2,128,256]{2,1,0:T(8,128)(2,1)S(1)}, u32[]{:S(2)}, u32[]{:S(2)}) collective-permute-start(bf16[2,128,256]{2,1,0:T(8,128)(2,1)} %param.16), channel_id=1, source_target_pairs={{0,16},{8,24},{16,0},{24,8},{32,48},{40,56},{48,32},{56,40},{64,80... | collective-permute-start | bytes 393224 | tf_op jit(solution)/shard_map/ppermute | solution.py:381
  8.4 6.6 %copy-start.3 = (bf16[16,4,2048]{2,1,0:T(4,128)(2,1)S(1)}, bf16[16,4,2048]{2,1,0:T(4,128)(2,1)}, u32[]{:S(2)}) copy-start(bf16[16,4,2048]{2,1,0:T(4,128)(2,1)} %param.18) | copy-start | bytes 786436
  13.8 7.9 %collective-permute-start.3 = (f32[4,192,256]{2,1,0:T(8,128)}, f32[4,192,256]{2,1,0:T(8,128)S(1)}, u32[]{:S(2)}, u32[]{:S(2)}) collective-permute-start(f32[4,192,256]{2,1,0:T(8,128)} %project.3), channel_id=1, source_target_pairs={{0,1},{1,0},{2,3},{3,2},{4,5},{5,4},{6,7},{7,6},{8,9},{9,8},{10,11... | collective-permute-start | bytes 2359304 | tf_op jit(solution)/shard_map/ppermute | solution.py:389
  15.8 8.5 %copy-start.4 = (bf16[2,128,256]{2,1,0:T(8,128)(2,1)S(1)}, bf16[2,128,256]{2,1,0:T(8,128)(2,1)}, u32[]{:S(2)}) copy-start(bf16[2,128,256]{2,1,0:T(8,128)(2,1)} %param.16) | copy-start | bytes 393220
  15.9 41.1 %copy-start = (bf16[16,2,256,256]{3,2,1,0:T(8,128)(2,1)S(1)}, bf16[16,2,256,256]{3,2,1,0:T(8,128)(2,1)}, u32[]{:S(2)}) copy-start(bf16[16,2,256,256]{3,2,1,0:T(8,128)(2,1)} %cache_ref.1) | copy-start | bytes 12582916
  15.9 41.1 %copy-start.2 = (s32[16]{0:T(128)S(1)}, s32[16]{0:T(128)}, u32[]{:S(2)}) copy-start(s32[16]{0:T(128)} %length_ref.1) | copy-start | bytes 196
  22.7 8.8 %collective-permute-start.4 = (f32[2,128,256]{2,1,0:T(8,128)S(1)}, f32[2,128,256]{2,1,0:T(8,128)S(1)}, u32[]{:S(2)}, u32[]{:S(2)}) collective-permute-start(f32[2,128,256]{2,1,0:T(8,128)S(1)} %slice_add_fusion), channel_id=1, source_target_pairs={{0,2},{1,3},{2,0},{3,1},{4,6},{5,7},{6,4},{7,5},{8,10},{9,11},{10,... | collective-permute-start | bytes 786440 | tf_op jit(solution)/shard_map/ppermute | solution.py:389
  24.4 47.0 %collective-permute-start.13 = (bf16[4,2,128,256]{3,2,1,0:T(8,128)(2,1)S(1)}, bf16[4,2,128,256]{3,2,1,0:T(8,128)(2,1)S(1)}, u32[]{:S(2)}, u32[]{:S(2)}) collective-permute-start(bf16[4,2,128,256]{3,2,1,0:T(8,128)(2,1)S(1)} %pad_maximum_fusion.refs_0_.known_ref), channel_id=1, source_target_pairs={{0,96},{8,104},{16,112},{24,120},{32,0},{40,8},{48,16},{56,24},{64... | collective-permute-start | bytes 1572872 | tf_op jit(solution)/shard_map/ppermute | solution.py:381
  28.5 44.6 %collective-permute-start.12 = (bf16[4,2,128,256]{3,2,1,0:T(8,128)(2,1)S(1)}, bf16[4,2,128,256]{3,2,1,0:T(8,128)(2,1)S(1)}, u32[]{:S(2)}, u32[]{:S(2)}) collective-permute-start(bf16[4,2,128,256]{3,2,1,0:T(8,128)(2,1)S(1)} %pad_maximum_fusion.refs_0_.known_ref), channel_id=1, source_target_pairs={{0,64},{8,72},{16,80},{24,88},{32,96},{40,104},{48,112},{56,120},{... | collective-permute-start | bytes 1572872 | tf_op jit(solution)/shard_map/ppermute | solution.py:381
  28.5 44.8 %collective-permute-start.11 = (bf16[4,2,128,256]{3,2,1,0:T(8,128)(2,1)S(1)}, bf16[4,2,128,256]{3,2,1,0:T(8,128)(2,1)S(1)}, u32[]{:S(2)}, u32[]{:S(2)}) collective-permute-start(bf16[4,2,128,256]{3,2,1,0:T(8,128)(2,1)S(1)} %pad_maximum_fusion.refs_0_.known_ref), channel_id=1, source_target_pairs={{0,32},{8,40},{16,48},{24,56},{32,64},{40,72},{48,80},{56,88},{64,... | collective-permute-start | bytes 1572872 | tf_op jit(solution)/shard_map/ppermute | solution.py:381
  30.7 6.3 %collective-permute-start.15 = (f32[2,64,256]{2,1,0:T(8,128)S(1)}, f32[2,64,256]{2,1,0:T(8,128)S(1)}, u32[]{:S(2)}, u32[]{:S(2)}) collective-permute-start(f32[2,64,256]{2,1,0:T(8,128)S(1)} %slice_add_fusion.2), channel_id=1, source_target_pairs={{0,2},{1,3},{2,0},{3,1},{4,6},{5,7},{6,4},{7,5},{8,10},{9,11},{10,... | collective-permute-start | bytes 393224 | tf_op jit(solution)/shard_map/ppermute | solution.py:389
  32.5 24.4 %collective-permute-start.7 = (bf16[2,128,256]{2,1,0:T(8,128)(2,1)S(1)}, bf16[2,128,256]{2,1,0:T(8,128)(2,1)S(1)}, u32[]{:S(2)}, u32[]{:S(2)}) collective-permute-start(bf16[2,128,256]{2,1,0:T(8,128)(2,1)S(1)} %fusion.1), channel_id=1, source_target_pairs={{0,96},{8,104},{16,112},{24,120},{32,0},{40,8},{48,16},{56,24},{64... | collective-permute-start | bytes 393224 | tf_op jit(solution)/shard_map/ppermute | solution.py:381
  38.0 28.6 %collective-permute-start.6 = (bf16[2,128,256]{2,1,0:T(8,128)(2,1)S(1)}, bf16[2,128,256]{2,1,0:T(8,128)(2,1)S(1)}, u32[]{:S(2)}, u32[]{:S(2)}) collective-permute-start(bf16[2,128,256]{2,1,0:T(8,128)(2,1)S(1)} %fusion.1), channel_id=1, source_target_pairs={{0,64},{8,72},{16,80},{24,88},{32,96},{40,104},{48,112},{56,120},{... | collective-permute-start | bytes 393224 | tf_op jit(solution)/shard_map/ppermute | solution.py:381
  56.9 12.4 %collective-permute-start.5 = (bf16[2,128,256]{2,1,0:T(8,128)(2,1)S(1)}, bf16[2,128,256]{2,1,0:T(8,128)(2,1)}, u32[]{:S(2)}, u32[]{:S(2)}) collective-permute-start(bf16[2,128,256]{2,1,0:T(8,128)(2,1)S(1)} %fusion.1), channel_id=1, source_target_pairs={{0,32},{8,40},{16,48},{24,56},{32,64},{40,72},{48,80},{56,88},{64,... | collective-permute-start | bytes 393224 | tf_op jit(solution)/shard_map/ppermute | solution.py:381
  56.9 9.6 %copy-start.1 = (bf16[128,2048]{1,0:T(8,128)(2,1)S(1)}, bf16[128,2048]{1,0:T(8,128)(2,1)}, u32[]{:S(2)}) copy-start(bf16[128,2048]{1,0:T(8,128)(2,1)} %q_ref.5) | copy-start | bytes 1572868
  66.6 14.7 %collective-permute-start.14 = (bf16[128,2048]{1,0:T(8,128)(2,1)S(1)}, bf16[128,2048]{1,0:T(8,128)(2,1)S(1)}, u32[]{:S(2)}, u32[]{:S(2)}) collective-permute-start(bf16[128,2048]{1,0:T(8,128)(2,1)S(1)} %copy-done.1), channel_id=1, source_target_pairs={{0,4},{4,0},{1,5},{5,1},{2,6},{6,2},{3,7},{7,3},{8,12},{12,8},{9,1... | collective-permute-start | bytes 1572872 | tf_op jit(solution)/shard_map/ppermute | solution.py:385
  70.3 17.8 %collective-permute-start.10 = (bf16[4,2,128,256]{3,2,1,0:T(8,128)(2,1)S(1)}, bf16[4,2,128,256]{3,2,1,0:T(8,128)(2,1)S(1)}, u32[]{:S(2)}, u32[]{:S(2)}) collective-permute-start(bf16[4,2,128,256]{3,2,1,0:T(8,128)(2,1)S(1)} %pad_maximum_fusion.1.refs_4_.refs_0_), channel_id=1, source_target_pairs={{0,24},{8,0},{16,8},{24,16},{32,56},{40,32},{48,40},{56,48},{64,88... | collective-permute-start | bytes 1572872 | tf_op jit(solution)/shard_map/ppermute | solution.py:381
  71.4 16.6 %collective-permute-start.9 = (bf16[4,2,128,256]{3,2,1,0:T(8,128)(2,1)S(1)}, bf16[4,2,128,256]{3,2,1,0:T(8,128)(2,1)S(1)}, u32[]{:S(2)}, u32[]{:S(2)}) collective-permute-start(bf16[4,2,128,256]{3,2,1,0:T(8,128)(2,1)S(1)} %pad_maximum_fusion.1.refs_4_.refs_0_), channel_id=1, source_target_pairs={{0,16},{8,24},{16,0},{24,8},{32,48},{40,56},{48,32},{56,40},{64,80... | collective-permute-start | bytes 1572872 | tf_op jit(solution)/shard_map/ppermute | solution.py:381
  73.1 23.7 %collective-permute-start.8 = (bf16[4,2,128,256]{3,2,1,0:T(8,128)(2,1)S(1)}, bf16[4,2,128,256]{3,2,1,0:T(8,128)(2,1)S(1)}, u32[]{:S(2)}, u32[]{:S(2)}) collective-permute-start(bf16[4,2,128,256]{3,2,1,0:T(8,128)(2,1)S(1)} %pad_maximum_fusion.1.refs_4_.refs_0_), channel_id=1, source_target_pairs={{0,8},{8,16},{16,24},{24,0},{32,40},{40,48},{48,56},{56,32},{64,72... | collective-permute-start | bytes 1572872 | tf_op jit(solution)/shard_map/ppermute | solution.py:381
  97.5 20.7 %collective-permute-start.18 = (bf16[8,2,16,256]{3,2,1,0:T(8,128)(2,1)S(1)}, bf16[8,2,16,256]{3,2,1,0:T(8,128)(2,1)S(1)}, u32[]{:S(2)}, u32[]{:S(2)}) collective-permute-start(bf16[8,2,16,256]{3,2,1,0:T(8,128)(2,1)S(1)} %slice.43), channel_id=1, source_target_pairs={{0,4},{4,0},{1,5},{5,1},{2,6},{6,2},{3,7},{7,3},{8,12},{12,8},{9,1... | collective-permute-start | bytes 393224 | tf_op jit(solution)/shard_map/ppermute | solution.py:385
  102.4 16.6 %collective-permute-start.16 = (bf16[128,1152]{1,0:T(8,128)(2,1)S(1)}, bf16[128,1152]{1,0:T(8,128)(2,1)S(1)}, u32[]{:S(2)}, u32[]{:S(2)}) collective-permute-start(bf16[128,1152]{1,0:T(8,128)(2,1)S(1)} %attend_partner.2), channel_id=1, source_target_pairs={{0,4},{4,0},{1,5},{5,1},{2,6},{6,2},{3,7},{7,3},{8,12},{12,8},{9,1... | collective-permute-start | bytes 884744 | tf_op jit(solution)/shard_map/ppermute | solution.py:385
  109.4 10.0 %collective-permute-start.17 = (bf16[128,1152]{1,0:T(8,128)(2,1)S(1)}, bf16[128,1152]{1,0:T(8,128)(2,1)S(1)}, u32[]{:S(2)}, u32[]{:S(2)}) collective-permute-start(bf16[128,1152]{1,0:T(8,128)(2,1)S(1)} %attend_partner.3), channel_id=1, source_target_pairs={{0,4},{4,0},{1,5},{5,1},{2,6},{6,2},{3,7},{7,3},{8,12},{12,8},{9,1... | collective-permute-start | bytes 884744 | tf_op jit(solution)/shard_map/ppermute | solution.py:385
  (1 other events, 6.2 us)

commit v3 on v2

v3 whole, which is shorter than its diff:
```python
import functools
import math

import jax
import jax.numpy as jnp
from jax import lax
from jax.experimental import pallas as pl
from jax.experimental.pallas import tpu as pltpu
from jax.sharding import PartitionSpec as P

HQ = 64
KEY_VALUE_HEADS = 8
HEAD_SIZE = 128
ADAPTER_RANK = 16
BLK = 16
STEPS = 4
GROUP = HQ // KEY_VALUE_HEADS
SHARDS = 16
SIDE = 4
TOKENS = 128
ROWS = 16
DECODE = ROWS * STEPS
ALL_ROWS = TOKENS + DECODE
LOG2_SCALE = math.log2(math.e) / math.sqrt(HEAD_SIZE)
neg_large = -1e30
MIB = 2**20
WIDTH = 2 * HEAD_SIZE


def estimate(us):
    return pl.CostEstimate(flops=int(us * 1.1e9), bytes_accessed=MIB, transcendentals=0)


def split3(x):
    hi = x.astype(jnp.bfloat16)
    rest = x - hi.astype(jnp.float32)
    mid = rest.astype(jnp.bfloat16)
    low = (rest - mid.astype(jnp.float32)).astype(jnp.bfloat16)
    return hi, mid, low

PROJECT_US, ATTEND_US, DECODE_US = 1, 1, 1


def project_kernel(
    tp_ref, row_adapter_ref, span_ref, decode_ref, weight_ref, down_ref, up_ref, adapter_ref, after_ref, out_ref, rank_ref
):
    hidden = jnp.concatenate([span_ref[...], decode_ref[...].reshape(DECODE, decode_ref.shape[2])], axis=0)

    @pl.when(pl.program_id(0) == 0)
    def _():
        narrow = jnp.dot(hidden, down_ref[...], preferred_element_type=jnp.float32)
        span_owner = jnp.transpose(jnp.broadcast_to(adapter_ref[...], (TOKENS, TOKENS)))
        row = lax.broadcasted_iota(jnp.int32, (DECODE, TOKENS), 0) // STEPS
        decode_owner = jnp.zeros((DECODE, TOKENS), jnp.int32)
        for r in range(ROWS):
            decode_owner = jnp.where(row == r, row_adapter_ref[r], decode_owner)
        owner = jnp.concatenate([span_owner, decode_owner], axis=0)
        column = lax.broadcasted_iota(jnp.int32, (ALL_ROWS, TOKENS), 1) // ADAPTER_RANK
        hi, mid, low = split3(jnp.where(column == owner, narrow, 0.0))
        rank_ref[:, :TOKENS] = hi
        rank_ref[:, TOKENS : 2 * TOKENS] = mid
        rank_ref[:, 2 * TOKENS :] = low

    up = up_ref[...]
    out = jnp.dot(hidden, weight_ref[...], preferred_element_type=jnp.float32) + jnp.dot(
        rank_ref[...], jnp.concatenate([up, up, up], axis=0), preferred_element_type=jnp.float32
    )
    out_ref[0] = out[:, :WIDTH]
    out_ref[1] = out[:, WIDTH:]


def project(first, tp, row_adapter, span, decode, weight, down, up, adapter, after):
    count = 2
    depth = span.shape[1]
    whole = lambda i, *_: (0, 0)
    return pl.pallas_call(
        project_kernel,
        grid_spec=pltpu.PrefetchScalarGridSpec(
            num_scalar_prefetch=2,
            grid=(count,),
            in_specs=[
                pl.BlockSpec((TOKENS, depth), whole),
                pl.BlockSpec((ROWS, STEPS, depth), lambda i, *_: (0, 0, 0)),
                pl.BlockSpec((depth, 2 * WIDTH), lambda i, tp, rows: (0, jnp.bitwise_xor(tp[0], first + 2 * i))),
                pl.BlockSpec((depth, TOKENS), whole),
                pl.BlockSpec((TOKENS, 2 * WIDTH), lambda i, tp, rows: (0, jnp.bitwise_xor(tp[0], first + 2 * i))),
                pl.BlockSpec((1, TOKENS), whole),
                pl.BlockSpec(memory_space=pl.ANY),
            ],
            out_specs=pl.BlockSpec((2, ALL_ROWS, WIDTH), lambda i, *_: (i, 0, 0)),
            scratch_shapes=[pltpu.VMEM((ALL_ROWS, 3 * TOKENS), jnp.bfloat16)],
        ),
        out_shape=jax.ShapeDtypeStruct((2 * count, ALL_ROWS, WIDTH), jnp.float32),
        compiler_params=pltpu.CompilerParams(vmem_limit_bytes=56 * MIB),
        cost_estimate=estimate(PROJECT_US),
        name="project",
    )(tp, row_adapter, span, decode, weight, down, up, adapter, after)


def finish_kernel(kept_ref, core_ref, chip_ref, *refs):
    out_ref = refs[-1]
    out_ref[...] = (kept_ref[...] + core_ref[...] + chip_ref[...]).astype(jnp.bfloat16)


def finish(kept, from_core, from_chip, after):
    heads, rows, width = from_chip.shape
    block = pl.BlockSpec((heads, rows, width), lambda i: (0, 0, 0))
    return pl.pallas_call(
        finish_kernel,
        grid=(1,),
        in_specs=[block] * 3 + [pl.BlockSpec(memory_space=pl.ANY)] * len(after),
        out_specs=block,
        out_shape=jax.ShapeDtypeStruct(from_chip.shape, jnp.bfloat16),
        compiler_params=pltpu.CompilerParams(vmem_limit_bytes=8 * MIB),
        cost_estimate=estimate(0.5),
        name="finish",
    )(kept, from_core, from_chip, *after)


TILE = 2
TILE_ROWS = TILE * TOKENS
TILES = GROUP // TILE
HEAD_ROWS = GROUP * TOKENS
HEAD_COLUMNS = GROUP * HEAD_SIZE


def attend_kernel(blocks, diagonal, has_state, final, partner, visible_ref, q_ref, known_ref, *refs):
    pieces, refs = refs[: blocks[-1][-1][0] + 1], refs[blocks[-1][-1][0] + 1 :]
    if has_state:
        state_ref, refs = refs[0], refs[1:]
    else:
        refs = refs[1:]
    out_ref, top_ref, acc_ref, ext_ref, key_ref = refs
    queries = [
        jnp.concatenate(
            [q_ref[:, (i * TILE + j) * HEAD_SIZE : (i * TILE + j + 1) * HEAD_SIZE] for j in range(TILE)], axis=0
        )
        for i in range(TILES)
    ]
    wide = lax.broadcasted_iota(jnp.int32, (TILE_ROWS, HEAD_SIZE), 1)
    lane = wide[:TOKENS]
    one = jnp.ones((TOKENS, HEAD_SIZE), jnp.bfloat16)
    zero = jnp.zeros((TOKENS, HEAD_SIZE), jnp.bfloat16)
    if final:
        stats = jnp.zeros((TOKENS, HEAD_SIZE), out_ref.dtype)
    start = 0
    for b, shards in enumerate(blocks):
        stop = start + len(shards) * TOKENS
        block = slice(start, stop)
        for n, (piece, index, place) in enumerate(shards):
            kv = pieces[piece][index, 0]
            keys, values, ones = kv[:, :HEAD_SIZE], kv[:, HEAD_SIZE:], one
            if place is not None:
                seen = visible_ref[place] != 0
                keys = jnp.where(seen, keys, known_ref[0, 0, :, :HEAD_SIZE])
                values = jnp.where(seen, values, zero)
                ones = jnp.where(seen, one, zero)
            here = slice(start + n * TOKENS, start + (n + 1) * TOKENS)
            key_ref[here, :] = keys
            ext_ref[here, :HEAD_SIZE] = values
            ext_ref[here, HEAD_SIZE:] = ones
        for i in range(TILES):
            here = slice(i * TILE_ROWS, (i + 1) * TILE_ROWS)
            scores = lax.dot_general(
                queries[i], key_ref[block, :], (((1,), (1,)), ((), ())), preferred_element_type=jnp.float32
            )
            if diagonal is not None and diagonal in shards:
                at = shards.index(diagonal) * TOKENS
                token = lax.broadcasted_iota(jnp.int32, (TILE_ROWS, TOKENS), 0) % TOKENS
                parts = [scores[:, :at]] if at else []
                parts.append(jnp.where(wide <= token, scores[:, at : at + TOKENS], neg_large))
                if at + TOKENS < scores.shape[1]:
                    parts.append(scores[:, at + TOKENS :])
                scores = jnp.concatenate(parts, axis=1)
            top = jnp.max(scores, axis=1, keepdims=True) * LOG2_SCALE
            if b or has_state:
                if b:
                    top_before, before = top_ref[here, :1], acc_ref[here]
                else:
                    top_before = state_ref[0, here, HEAD_SIZE : HEAD_SIZE + 1]
                    total_before = state_ref[0, here, WIDTH - 1 :]
                    before = jnp.concatenate(
                        [state_ref[0, here, :HEAD_SIZE], jnp.broadcast_to(total_before, (TILE_ROWS, HEAD_SIZE))],
                        axis=1,
                    )
                top = jnp.maximum(top_before, top)
            weights = jnp.exp2(scores * LOG2_SCALE - top).astype(jnp.bfloat16)
            total = jnp.dot(weights, ext_ref[block, :], preferred_element_type=jnp.float32)
            if b or has_state:
                total = before * jnp.exp2(top_before - top) + total
            if b < len(blocks) - 1:
                acc_ref[here] = total
                top_ref[here] = jnp.broadcast_to(top, (TILE_ROWS, HEAD_SIZE))
                continue
            if not final:
                out_ref[0, here, :HEAD_SIZE] = total[:, :HEAD_SIZE]
                out_ref[0, here, HEAD_SIZE:] = jnp.where(wide < HEAD_SIZE // 2, top, total[:, HEAD_SIZE:])
                continue
            out = total[:, :HEAD_SIZE] / total[:, HEAD_SIZE:]
            level = top + jnp.log2(total[:, HEAD_SIZE:])
            for j in range(TILE):
                g = i * TILE + j
                own = slice(j * TOKENS, (j + 1) * TOKENS)
                out_ref[0, :, g * HEAD_SIZE : (g + 1) * HEAD_SIZE] = out[own].astype(out_ref.dtype)
                parts = split3(level[own]) if partner else (level[own],)
                for part, piece in enumerate(parts):
                    stats = jnp.where(lane == part * GROUP + g, piece, stats)
        start = stop
    if final:
        out_ref[0, :, HEAD_COLUMNS:] = stats


def attend(visible, queries, known, pieces, blocks, after, heads, diagonal=None, state=None, final=False, partner=False):
    first, count = heads
    head = lambda h: first + h
    shards = sum(len(block) for block in blocks)
    if final:
        out_shape = (count, TOKENS, HEAD_COLUMNS + HEAD_SIZE)
    else:
        out_shape = (count, HEAD_ROWS, WIDTH)
    in_specs = [
        pl.BlockSpec((TOKENS, HEAD_COLUMNS), lambda h, *_: (0, head(h))),
        pl.BlockSpec((1, 1, TOKENS, WIDTH), lambda h, *_: (0, head(h), 0, 0)),
    ] + [pl.BlockSpec((SIDE, 1, TOKENS, WIDTH), lambda h, *_: (0, head(h), 0, 0))] * len(pieces)
    if state is None:
        in_specs.append(pl.BlockSpec(memory_space=pl.ANY))
    else:
        in_specs.append(pl.BlockSpec((1, HEAD_ROWS, WIDTH), lambda h, *_: (head(h), 0, 0)))
    return pl.pallas_call(
        functools.partial(attend_kernel, blocks, diagonal, state is not None, final, partner),
        grid_spec=pltpu.PrefetchScalarGridSpec(
            num_scalar_prefetch=1,
            grid=(count,),
            in_specs=in_specs,
            out_specs=pl.BlockSpec((1,) + out_shape[1:], lambda h, *_: (h, 0, 0)),
            scratch_shapes=[
                pltpu.VMEM((HEAD_ROWS, HEAD_SIZE), jnp.float32),
                pltpu.VMEM((HEAD_ROWS, WIDTH), jnp.float32),
                pltpu.VMEM((shards * TOKENS, WIDTH), jnp.bfloat16),
                pltpu.VMEM((shards * TOKENS, HEAD_SIZE), jnp.bfloat16),
            ],
        ),
        out_shape=jax.ShapeDtypeStruct(out_shape, jnp.bfloat16 if partner and final else jnp.float32),
        compiler_params=pltpu.CompilerParams(vmem_limit_bytes=24 * MIB),
        cost_estimate=estimate(ATTEND_US * count * shards / 16),
        name="attend_last" if final else "attend_first",
    )(visible, queries, known, *pieces, after if state is None else state)


def combine_kernel(*refs):
    own_ref, out_ref = refs[0], refs[3]
    for h in range(2):
        other_ref = refs[1 + h]
        own_level = own_ref[h, :, HEAD_COLUMNS:]
        other_parts = other_ref[0, :, HEAD_COLUMNS:].astype(jnp.float32)
        for g in range(GROUP):
            mine = own_level[:, g : g + 1]
            theirs = (
                other_parts[:, g : g + 1]
                + other_parts[:, GROUP + g : GROUP + g + 1]
                + other_parts[:, 2 * GROUP + g : 2 * GROUP + g + 1]
            )
            peak = jnp.maximum(mine, theirs)
            mine = jnp.exp2(mine - peak)
            theirs = jnp.exp2(theirs - peak)
            whole = mine + theirs
            columns = slice(g * HEAD_SIZE, (g + 1) * HEAD_SIZE)
            mixed = (mine / whole) * own_ref[h, :, columns] + (theirs / whole) * other_ref[0, :, columns].astype(
                jnp.float32
            )
            out_ref[:, h * HEAD_COLUMNS + g * HEAD_SIZE : h * HEAD_COLUMNS + (g + 1) * HEAD_SIZE] = mixed.astype(
                jnp.bfloat16
            )


def combine(own, other):
    return pl.pallas_call(
        combine_kernel,
        out_shape=jax.ShapeDtypeStruct((TOKENS, 2 * HEAD_COLUMNS), jnp.bfloat16),
        compiler_params=pltpu.CompilerParams(vmem_limit_bytes=16 * MIB),
        cost_estimate=estimate(1),
        name="combine",
    )(own, *other)


ROW_BLOCK = 8


def decode_kernel(length_ref, live_ref, q_ref, cache_ref, fresh_ref, after_ref, out_ref):
    first = pl.program_id(0) * ROW_BLOCK
    query_rows = STEPS * GROUP
    rows = ROW_BLOCK * query_rows
    contract = (((1,), (1,)), ((), ()))
    slot = lax.broadcasted_iota(jnp.int32, (query_rows, cache_ref.shape[2]), 1)
    fresh_row = lax.broadcasted_iota(jnp.int32, (rows, DECODE), 1) // STEPS
    fresh_step = lax.broadcasted_iota(jnp.int32, (rows, DECODE), 1) % STEPS
    row = lax.broadcasted_iota(jnp.int32, (rows, DECODE), 0) // query_rows
    step = lax.broadcasted_iota(jnp.int32, (rows, DECODE), 0) % query_rows // GROUP
    fresh_seen = (fresh_row == row + first) & (fresh_step <= step)
    cached, fresh = [], []
    for h in range(2):
        scores = lax.dot_general(
            q_ref[:, h].reshape(rows, HEAD_SIZE),
            fresh_ref[h, :, :HEAD_SIZE],
            contract,
            preferred_element_type=jnp.float32,
        )
        fresh.append(jnp.where(fresh_seen, scores, neg_large))
        for n in range(ROW_BLOCK):
            scores = lax.dot_general(
                q_ref[n, h], cache_ref[n, h, :, :HEAD_SIZE], contract, preferred_element_type=jnp.float32
            )
            cached.append(jnp.where(slot < length_ref[first + n], scores, neg_large))
    cached = jnp.concatenate(cached, axis=0)
    fresh = jnp.concatenate(fresh, axis=0)
    top = jnp.maximum(jnp.max(cached, axis=1, keepdims=True), jnp.max(fresh, axis=1, keepdims=True))
    cached = jnp.exp2((cached - top) * LOG2_SCALE)
    fresh = jnp.exp2((fresh - top) * LOG2_SCALE)
    total = jnp.sum(cached, axis=1, keepdims=True) + jnp.sum(fresh, axis=1, keepdims=True)
    cached = cached.astype(jnp.bfloat16)
    fresh = fresh.astype(jnp.bfloat16)
    for h in range(2):
        of_fresh = jnp.dot(
            fresh[h * rows : (h + 1) * rows], fresh_ref[h, :, HEAD_SIZE:], preferred_element_type=jnp.float32
        )
        for n in range(ROW_BLOCK):
            here = slice(h * rows + n * query_rows, h * rows + (n + 1) * query_rows)
            out = jnp.dot(cached[here], cache_ref[n, h, :, HEAD_SIZE:], preferred_element_type=jnp.float32)
            out = (out + of_fresh[n * query_rows : (n + 1) * query_rows]) / total[here]
            out_ref[n, h] = jnp.where(first + n < live_ref[0], out, 0.0).astype(jnp.bfloat16)


def decode_attend(lengths, live, queries, cache, fresh, after):
    rows, heads, query_rows, _ = queries.shape
    cache_size = cache.shape[2]
    return pl.pallas_call(
        decode_kernel,
        grid_spec=pltpu.PrefetchScalarGridSpec(
            num_scalar_prefetch=2,
            grid=(rows // ROW_BLOCK,),
            in_specs=[
                pl.BlockSpec((ROW_BLOCK, heads, query_rows, HEAD_SIZE), lambda i, *_: (i, 0, 0, 0)),
                pl.BlockSpec((ROW_BLOCK, heads, cache_size, 2 * HEAD_SIZE), lambda i, *_: (i, 0, 0, 0)),
                pl.BlockSpec((heads, DECODE, 2 * HEAD_SIZE), lambda i, *_: (0, 0, 0)),
                pl.BlockSpec(memory_space=pl.ANY),
            ],
            out_specs=pl.BlockSpec((ROW_BLOCK, heads, query_rows, HEAD_SIZE), lambda i, *_: (i, 0, 0, 0)),
        ),
        out_shape=jax.ShapeDtypeStruct(queries.shape, jnp.bfloat16),
        compiler_params=pltpu.CompilerParams(vmem_limit_bytes=24 * MIB),
        cost_estimate=estimate(DECODE_US),
        name="decode",
    )(lengths, live, queries, cache, fresh, after)


def pages_kernel(where_ref, *refs):
    pieces = refs[:SIDE]
    out_ref = refs[SIDE]
    for n in range(out_ref.shape[0]):
        dz, dy = where_ref[0, n], where_ref[1, n]
        rows = pl.ds(pl.multiple_of(where_ref[2, n] * BLK, BLK), BLK)
        for h in range(2):
            page = pieces[0][dy, h, rows, :]
            for k in range(1, SIDE):
                page = jnp.where(dz == k, pieces[k][dy, h, rows, :], page)
            out_ref[n, h] = page


def pick_pages(where, pieces):
    count = where.shape[1]
    return pl.pallas_call(
        pages_kernel,
        grid_spec=pltpu.PrefetchScalarGridSpec(
            num_scalar_prefetch=1,
            grid=(1,),
            in_specs=[pl.BlockSpec((SIDE, 2, TOKENS, WIDTH), lambda i, *_: (0, 0, 0, 0))] * SIDE,
            out_specs=pl.BlockSpec((count, 2, BLK, WIDTH), lambda i, *_: (0, 0, 0, 0)),
        ),
        out_shape=jax.ShapeDtypeStruct((count, 2, BLK, WIDTH), jnp.bfloat16),
        compiler_params=pltpu.CompilerParams(vmem_limit_bytes=16 * MIB),
        cost_estimate=estimate(1.5),
        name="pages",
    )(where, *pieces)


def shift(x, dz, dy):
    perm = [
        (z * SIDE + y, ((z + dz) % SIDE) * SIDE + (y + dy) % SIDE) for z in range(SIDE) for y in range(SIDE)
    ]
    return lax.ppermute(x, "ctx", perm)


def swap_pool(x):
    return lax.ppermute(x, "pool", [(0, 1), (1, 0)])


def swap_tp(x, bit):
    return lax.ppermute(x, "tp", [(i, i ^ bit) for i in range(4)])


def ring(x, along_z):
    move = (lambda d: shift(x, d, 0)) if along_z else (lambda d: shift(x, 0, d))
    far = {1: move(1), 3: move(3), 2: move(2)}
    return [x, far[1], far[2], far[3]]


def per_device(
    span_hidden_states,
    span_token_queries,
    earlier_key_values,
    decode_hidden_states,
    decode_token_queries,
    decode_row_cache,
    key_value_weight,
    adapter_down_weight,
    adapter_up_weight,
    prompt_adapter,
    row_adapter_index,
    group_live_rows,
    cached_row_lengths,
    block_target_page,
):
    tp = lax.axis_index("tp")
    ctx = lax.axis_index("ctx")
    pool = lax.axis_index("pool")
    my_z, my_y = ctx // SIDE, ctx % SIDE

    prior = ring(jnp.stack(ring(earlier_key_values, False)), True)

    def partial_kv(first, after):
        return project(
            first,
            tp.astype(jnp.int32).reshape(1),
            row_adapter_index,
            span_hidden_states,
            decode_hidden_states,
            key_value_weight,
            adapter_down_weight,
            adapter_up_weight,
            prompt_adapter.reshape(1, TOKENS),
            after,
        )

    from_core = swap_tp(partial_kv(1, row_adapter_index), 1)
    kept = partial_kv(0, prior[0])

    def from_chip(rows):
        return swap_tp(kept[2:, rows] + from_core[2:, rows], 2)

    span_rows, decode_rows = slice(0, TOKENS), slice(TOKENS, ALL_ROWS)
    span_kv = finish(kept, from_core, from_chip(span_rows), (prior[1], prior[3]))
    decode_kv = (kept[:2, decode_rows] + from_core[:2, decode_rows] + from_chip(decode_rows)).astype(jnp.bfloat16)

    column = jnp.stack(ring(span_kv, False))
    planes = ring(column, True)

    queries = decode_token_queries.reshape(ROWS, STEPS, 2, GROUP, HEAD_SIZE)
    queries = jnp.transpose(queries, (0, 2, 1, 3, 4)).reshape(ROWS, 2, STEPS * GROUP, HEAD_SIZE)
    decoded = decode_attend(cached_row_lengths, group_live_rows, queries, decode_row_cache, decode_kv, prior[2])
    decoded = jnp.transpose(decoded.reshape(ROWS, 2, STEPS, GROUP, HEAD_SIZE), (0, 2, 1, 3, 4))
    decode_attention = decoded.reshape(ROWS, STEPS, 2 * GROUP * HEAD_SIZE)

    far = jnp.arange(SIDE, dtype=jnp.int32)
    shard_z, shard_y = jnp.mod(my_z - far, SIDE), jnp.mod(my_y - far, SIDE)
    place = shard_z[:, None] * SIDE + shard_y[None, :]
    partner_sees = ((place < ctx) | ((place == ctx) & (pool == 0))).astype(jnp.int32).reshape(-1)
    own_sees = (place <= ctx).astype(jnp.int32).reshape(-1)
    earlier = [(p, k, None) for p in range(SIDE) for k in range(SIDE)]
    first_blocks = (tuple(earlier[:8]), tuple(earlier[8:]), tuple((SIDE, k, k) for k in range(SIDE)))
    others = [(p, k, (p + 1) * SIDE + k) for p in range(SIDE - 1) for k in range(SIDE)]
    last_blocks = (tuple(others[:6]), tuple(others[6:]))
    both = (0, 2)
    first_pieces = prior + [column]
    partner_queries = swap_pool(span_token_queries)
    own_state = attend(
        own_sees, span_token_queries, prior[0], first_pieces, first_blocks, column, both, diagonal=(SIDE, 0, 0)
    )
    partner_state = attend(partner_sees, partner_queries, prior[0], first_pieces, first_blocks, column, both)

    pages = TOKENS // BLK
    shard = ctx * 2 + pool
    partner_shard = ctx * 2 + 1 - pool
    page_ids = jnp.concatenate([shard * pages + jnp.arange(pages), partner_shard * pages + jnp.arange(pages)])
    block_ids = jnp.arange(block_target_page.shape[0], dtype=jnp.int32)
    source = jnp.sum(
        jnp.where(block_target_page[None, :] == page_ids[:, None], block_ids[None, :], 0), axis=1
    )
    source_shard = source // pages
    source_ctx = source_shard // 2
    where = jnp.stack(
        [
            jnp.mod(my_z - source_ctx // SIDE, SIDE),
            jnp.mod(my_y - source_ctx % SIDE, SIDE),
            source % pages,
        ]
    ).astype(jnp.int32)
    found = pick_pages(where, planes)
    from_partner = swap_pool(found[pages:])
    mine = (source_shard % 2 == pool)[:pages]
    handoff_pages = jnp.where(mine[:, None, None, None], found[:pages], from_partner)

    other = [
        swap_pool(
            attend(
                partner_sees,
                partner_queries,
                prior[0],
                planes[1:],
                last_blocks,
                None,
                (h, 1),
                state=partner_state,
                final=True,
                partner=True,
            )
        )
        for h in range(2)
    ]
    own = attend(
        own_sees, span_token_queries, prior[0], planes[1:], last_blocks, None, both, state=own_state, final=True
    )
    span_attention = combine(own, other)
    return (span_attention, handoff_pages, decode_attention)


def solution(mesh):
    in_specs = (
        P(("ctx", "pool"), "tp"),
        P(("ctx", "pool"), "tp"),
        P("tp", ("ctx", "pool"), None),
        P(("ctx", "pool"), None, "tp"),
        P(("ctx", "pool"), None, "tp"),
        P(("ctx", "pool"), "tp", None, None),
        P("tp", None),
        P("tp", None),
        P(),
        P(("ctx", "pool")),
        P(("ctx", "pool")),
        P(("ctx", "pool")),
        P(("ctx", "pool")),
        P(),
    )
    out_specs = (
        P(("ctx", "pool"), "tp"),
        P(("ctx", "pool"), "tp", None, None),
        P(("ctx", "pool"), None, "tp"),
    )
    return jax.shard_map(
        per_device, mesh=mesh, in_specs=in_specs, out_specs=out_specs, check_vma=False
    )
```

time: 122 us -> 110 us (0.902)
  waiting for transfers between devices: 28.3 us -> 14.1 us
  starting transfers between devices: 29.2 us -> 33 us
  other arithmetic: 7.26 us -> 4.92 us
  local copies, waits for them, and re-layouts: 2.94 us -> 4.64 us
    ppermute x12, waiting for transfers between devices: 26.5 us -> 14.1 us  [shift(): return lax.ppermute(x, 'ctx', perm)]
    pallas_call x1, Pallas kernels: 8.8 us -> 2.08 us  [decode_attend(): pl.pallas_call(decode_kernel, grid_spec=pltpu.PrefetchScalarGridSpec(num_...]
    pallas_call x6, Pallas kernels: 29.3 us -> 34.5 us  [the longest x5 34.4 us: attend(): pl.pallas_call(functools.partial(attend_kernel, blocks, diagonal, state i...]
    unnamed x12 -> x26, local copies, waits for them, and re-layouts: 0.03 us -> 3.45 us
    ppermute x12, starting transfers between devices: 19.5 us -> 22.2 us  [shift(): return lax.ppermute(x, 'ctx', perm)]
    reshape x1 -> x0, local copies, waits for them, and re-layouts: 1.71 us -> none  [per_device(): decode_hidden = decode_hidden_states.reshape(DECODE, depth)]
    ppermute x4, waiting for transfers between devices: 1.62 us -> 0.01 us  [swap_pool(): return lax.ppermute(x, 'pool', [(0, 1), (1, 0)])]
    another operation x4 -> x2, other arithmetic: 2.2 us -> 0.87 us  [the longest x1 0.86 us: per_device(): column = jnp.stack(ring(span_kv, False))]
  transfers between devices with their start and end apart: 19 -> 19, of which waited for: 5 -> 4; matrix products, arithmetic and copies ran while one was open for 8% -> 6% of each run, Pallas kernels for 41% -> 43%
where the time goes in v3:
time: 110 us; the launch traced here: 109 us
  Pallas kernels  50.8 us (46%)
  starting transfers between devices  33 us (30%)
  waiting for transfers between devices  14.1 us (13%)
  other arithmetic  4.92 us (4%)
  local copies, waits for them, and re-layouts  4.64 us (4%)
  between operations  1.52 us (1%)
    pallas_call x5, Pallas kernels, attend(): pl.pallas_call(functools.partial(attend_kernel, blocks, diagonal, state i...  34.4 us
    ppermute x12, starting transfers between devices, shift(): return lax.ppermute(x, 'ctx', perm)  22.2 us
    ppermute x12, waiting for transfers between devices, shift(): return lax.ppermute(x, 'ctx', perm)  14.1 us
    pallas_call x2, Pallas kernels, project(): pl.pallas_call(project_kernel, grid_spec=pltpu.PrefetchScalarGridSpec(num...  10.7 us
    ppermute x4, starting transfers between devices, swap_pool(): return lax.ppermute(x, 'pool', [(0, 1), (1, 0)])  8.58 us
    unnamed x26, local copies, waits for them, and re-layouts  3.45 us
  transfers between devices with their start and end apart: 19, of which 4 were waited for; matrix products, arithmetic and copies ran while one was open for 6% of the time, Pallas kernels for 43%

profile of v3, /device:TPU:0, one launch (start us, length us, event | category | flops | bytes accessed | tf_op | source)
XLA Modules:
  0.0 109.0 jit_solution(7148329258831234600)
XLA Ops:
  0.6 1.7 %collective-permute-start = (bf16[2,128,256]{2,1,0:T(8,128)(2,1)}, bf16[2,128,256]{2,1,0:T(8,128)(2,1)S(1)}, u32[]{:S(2)}, u32[]{:S(2)}) collective-permute-start(bf16[2,128,256]{2,1,0:T(8,128)(2,1)} %param.16), channel_id=1, source_target_pairs={{0,8},{8,16},{16,24},{24,0},{32,40},{40,48},{48,56},{56,32},{64,72... | collective-permute-start | bytes 393224 | tf_op jit(solution)/shard_map/ppermute | solution.py:390
  2.4 2.9 %collective-permute-start.1 = (bf16[2,128,256]{2,1,0:T(8,128)(2,1)}, bf16[2,128,256]{2,1,0:T(8,128)(2,1)S(1)}, u32[]{:S(2)}, u32[]{:S(2)}) collective-permute-start(bf16[2,128,256]{2,1,0:T(8,128)(2,1)} %param.16), channel_id=1, source_target_pairs={{0,16},{8,24},{16,0},{24,8},{32,48},{40,56},{48,32},{56,40},{64,80... | collective-permute-start | bytes 393224 | tf_op jit(solution)/shard_map/ppermute | solution.py:390
  6.6 5.4 %project.3 = f32[4,192,256]{2,1,0:T(8,128)} custom-call(s32[1]{0:T(128)} %bitcast.4.tp_ref, s32[16]{0:T(128)} %after_ref.1, bf16[128,2048]{1,0:T(8,128)(2,1)} %span_ref.3, bf16[16,4,2048]{2,1,0:T(4,128)(2,1)} %decode_ref.3, bf16[2048,2048]{1,0:T(8,128)(2,1)} %weight_ref.3, bf16[2048,128]{1,0:T(8,128)(2,1)} %down_ref.3, bf16[128,2048]{1,0:T(8,128)(2,1)} %up_ref.3, ...), custom_call_target="tpu_custom_call" | custom-call | flops 1100000000 | bytes 1048576 | tf_op jit(solution)/shard_map/project/pallas_call | solution.py:76
  13.6 2.0 %collective-permute-start.5 = (bf16[4,2,128,256]{3,2,1,0:T(8,128)(2,1)S(1)}, bf16[4,2,128,256]{3,2,1,0:T(8,128)(2,1)S(1)}, u32[]{:S(2)}, u32[]{:S(2)}) collective-permute-start(bf16[4,2,128,256]{3,2,1,0:T(8,128)(2,1)S(1)} %pad_maximum_fusion.after_ref.known_ref.refs_0_), channel_id=1, source_target_pairs={{0,32},{8,40},{16,48},{24,56},{32,64},{40,72},{48,80},{56,88},{64,... | collective-permute-start | bytes 1572872 | tf_op jit(solution)/shard_map/ppermute | solution.py:390
  15.6 2.2 %collective-permute-start.6 = (bf16[4,2,128,256]{3,2,1,0:T(8,128)(2,1)S(1)}, bf16[4,2,128,256]{3,2,1,0:T(8,128)(2,1)S(1)}, u32[]{:S(2)}, u32[]{:S(2)}) collective-permute-start(bf16[4,2,128,256]{3,2,1,0:T(8,128)(2,1)S(1)} %pad_maximum_fusion.after_ref.known_ref.refs_0_), channel_id=1, source_target_pairs={{0,96},{8,104},{16,112},{24,120},{32,0},{40,8},{48,16},{56,24},{64... | collective-permute-start | bytes 1572872 | tf_op jit(solution)/shard_map/ppermute | solution.py:390
  17.8 1.8 %collective-permute-start.13 = (bf16[4,2,128,256]{3,2,1,0:T(8,128)(2,1)S(1)}, bf16[4,2,128,256]{3,2,1,0:T(8,128)(2,1)S(1)}, u32[]{:S(2)}, u32[]{:S(2)}) collective-permute-start(bf16[4,2,128,256]{3,2,1,0:T(8,128)(2,1)S(1)} %pad_maximum_fusion.after_ref.known_ref.refs_0_), channel_id=1, source_target_pairs={{0,64},{8,72},{16,80},{24,88},{32,96},{40,104},{48,112},{56,120},{... | collective-permute-start | bytes 1572872 | tf_op jit(solution)/shard_map/ppermute | solution.py:390
  19.6 5.3 %project.2.kept_ref = f32[4,192,256]{2,1,0:T(8,128)} custom-call(s32[1]{0:T(128)} %bitcast.4.tp_ref, s32[16]{0:T(128)} %after_ref.1, bf16[128,2048]{1,0:T(8,128)(2,1)} %span_ref.3, bf16[16,4,2048]{2,1,0:T(4,128)(2,1)} %decode_ref.3, bf16[2048,2048]{1,0:T(8,128)(2,1)} %weight_ref.3, bf16[2048,128]{1,0:T(8,128)(2,1)} %down_ref.3, bf16[128,2048]{1,0:T(8,128)(2,1)} %up_ref.3, ...), custom_call_target="tpu_custom_call" | custom-call | flops 1100000000 | bytes 1048576 | tf_op jit(solution)/shard_map/project/pallas_call | solution.py:76
  30.3 3.0 %collective-permute-start.14 = (bf16[128,2048]{1,0:T(8,128)(2,1)}, bf16[128,2048]{1,0:T(8,128)(2,1)S(1)}, u32[]{:S(2)}, u32[]{:S(2)}) collective-permute-start(bf16[128,2048]{1,0:T(8,128)(2,1)} %q_ref.3), channel_id=1, source_target_pairs={{0,4},{4,0},{1,5},{5,1},{2,6},{6,2},{3,7},{7,3},{8,12},{12,8},{9,1... | collective-permute-start | bytes 1572872 | tf_op jit(solution)/shard_map/ppermute | solution.py:394
  33.4 7.6 %collective-permute-done.6.refs_1_.refs_3_ = bf16[4,2,128,256]{3,2,1,0:T(8,128)(2,1)S(1)} collective-permute-done((bf16[4,2,128,256]{3,2,1,0:T(8,128)(2,1)S(1)}, bf16[4,2,128,256]{3,2,1,0:T(8,128)(2,1)S(1)}, u32[]{:S(2)}, u32[]{:S(2)}) %collective-permute-start.6) | collective-permute-done | bytes 524320 | tf_op jit(solution)/shard_map/ppermute | solution.py:390
  43.9 1.9 %collective-permute-start.9 = (bf16[2,128,256]{2,1,0:T(8,128)(2,1)S(1)}, bf16[2,128,256]{2,1,0:T(8,128)(2,1)S(1)}, u32[]{:S(2)}, u32[]{:S(2)}) collective-permute-start(bf16[2,128,256]{2,1,0:T(8,128)(2,1)S(1)} %finish.1), channel_id=1, source_target_pairs={{0,24},{8,0},{16,8},{24,16},{32,56},{40,32},{48,40},{56,48},{64,88... | collective-permute-start | bytes 393224 | tf_op jit(solution)/shard_map/ppermute | solution.py:390
  46.8 4.6 %collective-permute-done.7 = bf16[2,128,256]{2,1,0:T(8,128)(2,1)S(1)} collective-permute-done((bf16[2,128,256]{2,1,0:T(8,128)(2,1)S(1)}, bf16[2,128,256]{2,1,0:T(8,128)(2,1)S(1)}, u32[]{:S(2)}, u32[]{:S(2)}) %collective-permute-start.7) | collective-permute-done | bytes 131104 | tf_op jit(solution)/shard_map/ppermute | solution.py:390
  52.8 1.6 %collective-permute-start.10 = (bf16[4,2,128,256]{3,2,1,0:T(8,128)(2,1)}, bf16[4,2,128,256]{3,2,1,0:T(8,128)(2,1)S(1)}, u32[]{:S(2)}, u32[]{:S(2)}) collective-permute-start(bf16[4,2,128,256]{3,2,1,0:T(8,128)(2,1)} %pad_maximum_fusion.1.refs_4_.refs_5_.refs_0_), channel_id=1, source_target_pairs={{0,32},{8,40},{16,48},{24,56},{32,64},{40,72},{48,80},{56,88},{64,... | collective-permute-start | bytes 1572872 | tf_op jit(solution)/shard_map/ppermute | solution.py:390
  54.5 3.7 %collective-permute-start.11 = (bf16[4,2,128,256]{3,2,1,0:T(8,128)(2,1)}, bf16[4,2,128,256]{3,2,1,0:T(8,128)(2,1)S(1)}, u32[]{:S(2)}, u32[]{:S(2)}) collective-permute-start(bf16[4,2,128,256]{3,2,1,0:T(8,128)(2,1)} %pad_maximum_fusion.1.refs_4_.refs_5_.refs_0_), channel_id=1, source_target_pairs={{0,64},{8,72},{16,80},{24,88},{32,96},{40,104},{48,112},{56,120},{... | collective-permute-start | bytes 1572872 | tf_op jit(solution)/shard_map/ppermute | solution.py:390
  59.6 2.1 %decode.1 = bf16[16,2,32,128]{3,2,1,0:T(8,128)(2,1)S(1)} custom-call(s32[16]{0:T(128)S(1)} %copy-done.9, s32[1]{0:T(128)S(6)} %copy.23.live_ref, bf16[16,2,32,128]{3,2,1,0:T(8,128)(2,1)S(1)} %bitcast.46, bf16[16,2,256,256]{3,2,1,0:T(8,128)(2,1)S(1)} %copy-done.3, bf16[2,64,256]{2,1,0:T(8,128)(2,1)S(1)} %fusion.1.fresh_ref, ...), custom_call_target="tpu_custom_call" | custom-call | flops 1100000000 | bytes 1048576 | tf_op jit(solution)/shard_map/decode/pallas_call | solution.py:336
  64.6 10.3 %attend_first.2.refs_3_ = f32[2,1024,256]{2,1,0:T(8,128)S(1)} custom-call(s32[16]{0:T(128)S(1)} %reshape.342.visible_ref, bf16[128,2048]{1,0:T(8,128)(2,1)} %q_ref.3, bf16[4,2,128,256]{3,2,1,0:T(8,128)(2,1)S(1)} %copy-done.1, bf16[4,2,128,256]{3,2,1,0:T(8,128)(2,1)S(1)} %copy-done.1, bf16[4,2,128,256]{3,2,1,0:T(8,128)(2,1)S(1)} %copy-done.5, ...), custom_call_target="tpu_custom_call" | custom-call | flops 2750000128 | bytes 1048576 | tf_op jit(solution)/shard_map/attend_first/pallas_call | solution.py:229
  74.9 10.3 %attend_first.3.refs_3_ = f32[2,1024,256]{2,1,0:T(8,128)S(1)} custom-call(s32[16]{0:T(128)S(1)} %reshape.343.visible_ref, bf16[128,2048]{1,0:T(8,128)(2,1)S(1)} %collective-permute-done.14.q_ref, bf16[4,2,128,256]{3,2,1,0:T(8,128)(2,1)S(1)} %copy-done.1, bf16[4,2,128,256]{3,2,1,0:T(8,128)(2,1)S(1)} %copy-done.1, bf16[4,2,128,256]{3,2,1,0:T(8,128)(2,1)S(1)} %copy-done.6, ...), custom_call_target="tpu_custom_call" | custom-call | flops 2750000128 | bytes 1048576 | tf_op jit(solution)/shard_map/attend_first/pallas_call | solution.py:229
  85.2 1.7 %pages.1 = bf16[16,2,16,256]{3,2,1,0:T(8,128)(2,1)S(1)} custom-call(s32[3,16]{1,0:T(4,128)S(1)} %pad_add_fusion.where_ref, bf16[4,2,128,256]{3,2,1,0:T(8,128)(2,1)} %pad_maximum_fusion.1.refs_4_.refs_5_.refs_0_, bf16[4,2,128,256]{3,2,1,0:T(8,128)(2,1)S(1)} %collective-permute-done.10.refs_0_.refs_1_, ...), custom_call_target="tpu_custom_call" | custom-call | flops 1650000000 | bytes 1048576 | tf_op jit(solution)/shard_map/pages/pallas_call | solution.py:371
  86.9 1.9 %collective-permute-start.17 = (bf16[8,2,16,256]{3,2,1,0:T(8,128)(2,1)S(1)}, bf16[8,2,16,256]{3,2,1,0:T(8,128)(2,1)S(1)}, u32[]{:S(2)}, u32[]{:S(2)}) collective-permute-start(bf16[8,2,16,256]{3,2,1,0:T(8,128)(2,1)S(1)} %slice.39), channel_id=1, source_target_pairs={{0,4},{4,0},{1,5},{5,1},{2,6},{6,2},{3,7},{7,3},{8,12},{12,8},{9,1... | collective-permute-start | bytes 393224 | tf_op jit(solution)/shard_map/ppermute | solution.py:394
  88.8 3.4 %attend_last.5 = bf16[1,128,1152]{2,1,0:T(8,128)(2,1)S(1)} custom-call(s32[16]{0:T(128)S(1)} %reshape.343.visible_ref, bf16[128,2048]{1,0:T(8,128)(2,1)S(1)} %collective-permute-done.14.q_ref, bf16[4,2,128,256]{3,2,1,0:T(8,128)(2,1)S(1)} %copy-done.1, bf16[4,2,128,256]{3,2,1,0:T(8,128)(2,1)S(1)} %collective-permute-done.10.refs_0_.refs_1_, ...), custom_call_target="tpu_custom_call" | custom-call | flops 825000000 | bytes 1048576 | tf_op jit(solution)/shard_map/attend_last/pallas_call | solution.py:229
  92.2 2.0 %collective-permute-start.16 = (bf16[1,128,1152]{2,1,0:T(8,128)(2,1)S(1)}, bf16[1,128,1152]{2,1,0:T(8,128)(2,1)S(1)}, u32[]{:S(2)}, u32[]{:S(2)}) collective-permute-start(bf16[1,128,1152]{2,1,0:T(8,128)(2,1)S(1)} %attend_last.5), channel_id=1, source_target_pairs={{0,4},{4,0},{1,5},{5,1},{2,6},{6,2},{3,7},{7,3},{8,12},{12,8},{9,1... | collective-permute-start | bytes 884744 | tf_op jit(solution)/shard_map/ppermute | solution.py:394
  94.2 3.4 %attend_last.4 = bf16[1,128,1152]{2,1,0:T(8,128)(2,1)S(1)} custom-call(s32[16]{0:T(128)S(1)} %reshape.343.visible_ref, bf16[128,2048]{1,0:T(8,128)(2,1)S(1)} %collective-permute-done.14.q_ref, bf16[4,2,128,256]{3,2,1,0:T(8,128)(2,1)S(1)} %copy-done.1, bf16[4,2,128,256]{3,2,1,0:T(8,128)(2,1)S(1)} %collective-permute-done.10.refs_0_.refs_1_, ...), custom_call_target="tpu_custom_call" | custom-call | flops 825000000 | bytes 1048576 | tf_op jit(solution)/shard_map/attend_last/pallas_call | solution.py:229
  97.6 1.7 %collective-permute-start.15 = (bf16[1,128,1152]{2,1,0:T(8,128)(2,1)S(1)}, bf16[1,128,1152]{2,1,0:T(8,128)(2,1)S(1)}, u32[]{:S(2)}, u32[]{:S(2)}) collective-permute-start(bf16[1,128,1152]{2,1,0:T(8,128)(2,1)S(1)} %attend_last.4), channel_id=1, source_target_pairs={{0,4},{4,0},{1,5},{5,1},{2,6},{6,2},{3,7},{7,3},{8,12},{12,8},{9,1... | collective-permute-start | bytes 884744 | tf_op jit(solution)/shard_map/ppermute | solution.py:394
  99.3 7.1 %attend_last.3.refs_0_ = f32[2,128,1152]{2,1,0:T(8,128)S(1)} custom-call(s32[16]{0:T(128)S(1)} %reshape.342.visible_ref, bf16[128,2048]{1,0:T(8,128)(2,1)} %q_ref.3, bf16[4,2,128,256]{3,2,1,0:T(8,128)(2,1)S(1)} %copy-done.1, bf16[4,2,128,256]{3,2,1,0:T(8,128)(2,1)S(1)} %collective-permute-done.10.refs_0_.refs_1_, ...), custom_call_target="tpu_custom_call" | custom-call | flops 1650000000 | bytes 1048576 | tf_op jit(solution)/shard_map/attend_last/pallas_call | solution.py:229
  107.2 1.8 %combine.1 = bf16[128,2048]{1,0:T(8,128)(2,1)} custom-call(f32[2,128,1152]{2,1,0:T(8,128)S(1)} %attend_last.3.refs_0_, bf16[1,128,1152]{2,1,0:T(8,128)(2,1)S(1)} %collective-permute-done.15.refs_1_, bf16[1,128,1152]{2,1,0:T(8,128)(2,1)S(1)} %collective-permute-done.16.refs_2_), custom_call_target="tpu_custom_call" | custom-call | flops 1100000000 | bytes 1048576 | tf_op jit(solution)/shard_map/combine/pallas_call | solution.py:277
  (72 shorter events, 18.1 us)
Async XLA Ops:
  0.6 12.9 %collective-permute-start = (bf16[2,128,256]{2,1,0:T(8,128)(2,1)}, bf16[2,128,256]{2,1,0:T(8,128)(2,1)S(1)}, u32[]{:S(2)}, u32[]{:S(2)}) collective-permute-start(bf16[2,128,256]{2,1,0:T(8,128)(2,1)} %param.16), channel_id=1, source_target_pairs={{0,8},{8,16},{16,24},{24,0},{32,40},{40,48},{48,56},{56,32},{64,72... | collective-permute-start | bytes 393224 | tf_op jit(solution)/shard_map/ppermute | solution.py:390
  2.4 11.2 %collective-permute-start.1 = (bf16[2,128,256]{2,1,0:T(8,128)(2,1)}, bf16[2,128,256]{2,1,0:T(8,128)(2,1)S(1)}, u32[]{:S(2)}, u32[]{:S(2)}) collective-permute-start(bf16[2,128,256]{2,1,0:T(8,128)(2,1)} %param.16), channel_id=1, source_target_pairs={{0,16},{8,24},{16,0},{24,8},{32,48},{40,56},{48,32},{56,40},{64,80... | collective-permute-start | bytes 393224 | tf_op jit(solution)/shard_map/ppermute | solution.py:390
  5.3 8.3 %collective-permute-start.2 = (bf16[2,128,256]{2,1,0:T(8,128)(2,1)}, bf16[2,128,256]{2,1,0:T(8,128)(2,1)S(1)}, u32[]{:S(2)}, u32[]{:S(2)}) collective-permute-start(bf16[2,128,256]{2,1,0:T(8,128)(2,1)} %param.16), channel_id=1, source_target_pairs={{0,24},{8,0},{16,8},{24,16},{32,56},{40,32},{48,40},{56,48},{64,88... | collective-permute-start | bytes 393224 | tf_op jit(solution)/shard_map/ppermute | solution.py:390
  12.0 12.9 %collective-permute-start.3 = (f32[4,192,256]{2,1,0:T(8,128)}, f32[4,192,256]{2,1,0:T(8,128)S(1)}, u32[]{:S(2)}, u32[]{:S(2)}) collective-permute-start(f32[4,192,256]{2,1,0:T(8,128)} %project.3), channel_id=1, source_target_pairs={{0,1},{1,0},{2,3},{3,2},{4,5},{5,4},{6,7},{7,6},{8,9},{9,8},{10,11... | collective-permute-start | bytes 2359304 | tf_op jit(solution)/shard_map/ppermute | solution.py:398
  13.6 16.7 %collective-permute-start.5 = (bf16[4,2,128,256]{3,2,1,0:T(8,128)(2,1)S(1)}, bf16[4,2,128,256]{3,2,1,0:T(8,128)(2,1)S(1)}, u32[]{:S(2)}, u32[]{:S(2)}) collective-permute-start(bf16[4,2,128,256]{3,2,1,0:T(8,128)(2,1)S(1)} %pad_maximum_fusion.after_ref.known_ref.refs_0_), channel_id=1, source_target_pairs={{0,32},{8,40},{16,48},{24,56},{32,64},{40,72},{48,80},{56,88},{64,... | collective-permute-start | bytes 1572872 | tf_op jit(solution)/shard_map/ppermute | solution.py:390
  15.6 25.3 %collective-permute-start.6 = (bf16[4,2,128,256]{3,2,1,0:T(8,128)(2,1)S(1)}, bf16[4,2,128,256]{3,2,1,0:T(8,128)(2,1)S(1)}, u32[]{:S(2)}, u32[]{:S(2)}) collective-permute-start(bf16[4,2,128,256]{3,2,1,0:T(8,128)(2,1)S(1)} %pad_maximum_fusion.after_ref.known_ref.refs_0_), channel_id=1, source_target_pairs={{0,96},{8,104},{16,112},{24,120},{32,0},{40,8},{48,16},{56,24},{64... | collective-permute-start | bytes 1572872 | tf_op jit(solution)/shard_map/ppermute | solution.py:390
  17.8 41.8 %collective-permute-start.13 = (bf16[4,2,128,256]{3,2,1,0:T(8,128)(2,1)S(1)}, bf16[4,2,128,256]{3,2,1,0:T(8,128)(2,1)S(1)}, u32[]{:S(2)}, u32[]{:S(2)}) collective-permute-start(bf16[4,2,128,256]{3,2,1,0:T(8,128)(2,1)S(1)} %pad_maximum_fusion.after_ref.known_ref.refs_0_), channel_id=1, source_target_pairs={{0,64},{8,72},{16,80},{24,88},{32,96},{40,104},{48,112},{56,120},{... | collective-permute-start | bytes 1572872 | tf_op jit(solution)/shard_map/ppermute | solution.py:390
  25.9 15.1 %collective-permute-start.4 = (f32[2,128,256]{2,1,0:T(8,128)S(1)}, f32[2,128,256]{2,1,0:T(8,128)S(1)}, u32[]{:S(2)}, u32[]{:S(2)}) collective-permute-start(f32[2,128,256]{2,1,0:T(8,128)S(1)} %slice_add_fusion), channel_id=1, source_target_pairs={{0,2},{1,3},{2,0},{3,1},{4,6},{5,7},{6,4},{7,5},{8,10},{9,11},{10,... | collective-permute-start | bytes 786440 | tf_op jit(solution)/shard_map/ppermute | solution.py:398
  28.4 15.5 %collective-permute-start.18 = (f32[2,64,256]{2,1,0:T(8,128)S(1)}, f32[2,64,256]{2,1,0:T(8,128)S(1)}, u32[]{:S(2)}, u32[]{:S(2)}) collective-permute-start(f32[2,64,256]{2,1,0:T(8,128)S(1)} %slice_add_fusion.1), channel_id=1, source_target_pairs={{0,2},{1,3},{2,0},{3,1},{4,6},{5,7},{6,4},{7,5},{8,10},{9,11},{10,... | collective-permute-start | bytes 393224 | tf_op jit(solution)/shard_map/ppermute | solution.py:398
  29.0 30.6 %copy-start.9 = (s32[16]{0:T(128)S(1)}, s32[16]{0:T(128)}, u32[]{:S(2)}) copy-start(s32[16]{0:T(128)} %length_ref.1) | copy-start | bytes 196
  30.3 22.5 %copy-start.4 = (bf16[4,2,128,256]{3,2,1,0:T(8,128)(2,1)}, bf16[4,2,128,256]{3,2,1,0:T(8,128)(2,1)S(1)}, u32[]{:S(2)}) copy-start(bf16[4,2,128,256]{3,2,1,0:T(8,128)(2,1)S(1)} %collective-permute-done.5.refs_0_.refs_1_) | copy-start | bytes 1572868
  30.3 44.5 %collective-permute-start.14 = (bf16[128,2048]{1,0:T(8,128)(2,1)}, bf16[128,2048]{1,0:T(8,128)(2,1)S(1)}, u32[]{:S(2)}, u32[]{:S(2)}) collective-permute-start(bf16[128,2048]{1,0:T(8,128)(2,1)} %q_ref.3), channel_id=1, source_target_pairs={{0,4},{4,0},{1,5},{5,1},{2,6},{6,2},{3,7},{7,3},{8,12},{12,8},{9,1... | collective-permute-start | bytes 1572872 | tf_op jit(solution)/shard_map/ppermute | solution.py:394
  40.9 11.9 %copy-start.7 = (bf16[4,2,128,256]{3,2,1,0:T(8,128)(2,1)}, bf16[4,2,128,256]{3,2,1,0:T(8,128)(2,1)S(1)}, u32[]{:S(2)}) copy-start(bf16[4,2,128,256]{3,2,1,0:T(8,128)(2,1)S(1)} %collective-permute-done.6.refs_1_.refs_3_) | copy-start | bytes 1572868
  42.3 17.3 %copy-start.3 = (bf16[16,2,256,256]{3,2,1,0:T(8,128)(2,1)S(1)}, bf16[16,2,256,256]{3,2,1,0:T(8,128)(2,1)}, u32[]{:S(2)}) copy-start(bf16[16,2,256,256]{3,2,1,0:T(8,128)(2,1)} %cache_ref.1) | copy-start | bytes 12582916
  42.3 9.0 %collective-permute-start.7 = (bf16[2,128,256]{2,1,0:T(8,128)(2,1)S(1)}, bf16[2,128,256]{2,1,0:T(8,128)(2,1)S(1)}, u32[]{:S(2)}, u32[]{:S(2)}) collective-permute-start(bf16[2,128,256]{2,1,0:T(8,128)(2,1)S(1)} %finish.1), channel_id=1, source_target_pairs={{0,8},{8,16},{16,24},{24,0},{32,40},{40,48},{48,56},{56,32},{64,72... | collective-permute-start | bytes 393224 | tf_op jit(solution)/shard_map/ppermute | solution.py:390
  43.1 8.3 %collective-permute-start.8 = (bf16[2,128,256]{2,1,0:T(8,128)(2,1)S(1)}, bf16[2,128,256]{2,1,0:T(8,128)(2,1)S(1)}, u32[]{:S(2)}, u32[]{:S(2)}) collective-permute-start(bf16[2,128,256]{2,1,0:T(8,128)(2,1)S(1)} %finish.1), channel_id=1, source_target_pairs={{0,16},{8,24},{16,0},{24,8},{32,48},{40,56},{48,32},{56,40},{64,80... | collective-permute-start | bytes 393224 | tf_op jit(solution)/shard_map/ppermute | solution.py:390
  43.9 8.1 %collective-permute-start.9 = (bf16[2,128,256]{2,1,0:T(8,128)(2,1)S(1)}, bf16[2,128,256]{2,1,0:T(8,128)(2,1)S(1)}, u32[]{:S(2)}, u32[]{:S(2)}) collective-permute-start(bf16[2,128,256]{2,1,0:T(8,128)(2,1)S(1)} %finish.1), channel_id=1, source_target_pairs={{0,24},{8,0},{16,8},{24,16},{32,56},{40,32},{48,40},{56,48},{64,88... | collective-permute-start | bytes 393224 | tf_op jit(solution)/shard_map/ppermute | solution.py:390
  52.8 32.3 %collective-permute-start.10 = (bf16[4,2,128,256]{3,2,1,0:T(8,128)(2,1)}, bf16[4,2,128,256]{3,2,1,0:T(8,128)(2,1)S(1)}, u32[]{:S(2)}, u32[]{:S(2)}) collective-permute-start(bf16[4,2,128,256]{3,2,1,0:T(8,128)(2,1)} %pad_maximum_fusion.1.refs_4_.refs_5_.refs_0_), channel_id=1, source_target_pairs={{0,32},{8,40},{16,48},{24,56},{32,64},{40,72},{48,80},{56,88},{64,... | collective-permute-start | bytes 1572872 | tf_op jit(solution)/shard_map/ppermute | solution.py:390
  54.5 30.7 %collective-permute-start.11 = (bf16[4,2,128,256]{3,2,1,0:T(8,128)(2,1)}, bf16[4,2,128,256]{3,2,1,0:T(8,128)(2,1)S(1)}, u32[]{:S(2)}, u32[]{:S(2)}) collective-permute-start(bf16[4,2,128,256]{3,2,1,0:T(8,128)(2,1)} %pad_maximum_fusion.1.refs_4_.refs_5_.refs_0_), channel_id=1, source_target_pairs={{0,64},{8,72},{16,80},{24,88},{32,96},{40,104},{48,112},{56,120},{... | collective-permute-start | bytes 1572872 | tf_op jit(solution)/shard_map/ppermute | solution.py:390
  58.1 27.1 %collective-permute-start.12 = (bf16[4,2,128,256]{3,2,1,0:T(8,128)(2,1)}, bf16[4,2,128,256]{3,2,1,0:T(8,128)(2,1)S(1)}, u32[]{:S(2)}, u32[]{:S(2)}) collective-permute-start(bf16[4,2,128,256]{3,2,1,0:T(8,128)(2,1)} %pad_maximum_fusion.1.refs_4_.refs_5_.refs_0_), channel_id=1, source_target_pairs={{0,96},{8,104},{16,112},{24,120},{32,0},{40,8},{48,16},{56,24},{64... | collective-permute-start | bytes 1572872 | tf_op jit(solution)/shard_map/ppermute | solution.py:390
  64.6 10.3 %copy-start.6 = (bf16[4,2,128,256]{3,2,1,0:T(8,128)(2,1)S(1)}, bf16[4,2,128,256]{3,2,1,0:T(8,128)(2,1)}, u32[]{:S(2)}) copy-start(bf16[4,2,128,256]{3,2,1,0:T(8,128)(2,1)} %copy-done.4) | copy-start | bytes 1572868
  86.9 19.5 %collective-permute-start.17 = (bf16[8,2,16,256]{3,2,1,0:T(8,128)(2,1)S(1)}, bf16[8,2,16,256]{3,2,1,0:T(8,128)(2,1)S(1)}, u32[]{:S(2)}, u32[]{:S(2)}) collective-permute-start(bf16[8,2,16,256]{3,2,1,0:T(8,128)(2,1)S(1)} %slice.39), channel_id=1, source_target_pairs={{0,4},{4,0},{1,5},{5,1},{2,6},{6,2},{3,7},{7,3},{8,12},{12,8},{9,1... | collective-permute-start | bytes 393224 | tf_op jit(solution)/shard_map/ppermute | solution.py:394
  92.2 15.0 %collective-permute-start.16 = (bf16[1,128,1152]{2,1,0:T(8,128)(2,1)S(1)}, bf16[1,128,1152]{2,1,0:T(8,128)(2,1)S(1)}, u32[]{:S(2)}, u32[]{:S(2)}) collective-permute-start(bf16[1,128,1152]{2,1,0:T(8,128)(2,1)S(1)} %attend_last.5), channel_id=1, source_target_pairs={{0,4},{4,0},{1,5},{5,1},{2,6},{6,2},{3,7},{7,3},{8,12},{12,8},{9,1... | collective-permute-start | bytes 884744 | tf_op jit(solution)/shard_map/ppermute | solution.py:394
  97.6 9.5 %collective-permute-start.15 = (bf16[1,128,1152]{2,1,0:T(8,128)(2,1)S(1)}, bf16[1,128,1152]{2,1,0:T(8,128)(2,1)S(1)}, u32[]{:S(2)}, u32[]{:S(2)}) collective-permute-start(bf16[1,128,1152]{2,1,0:T(8,128)(2,1)S(1)} %attend_last.4), channel_id=1, source_target_pairs={{0,4},{4,0},{1,5},{5,1},{2,6},{6,2},{3,7},{7,3},{8,12},{12,8},{9,1... | collective-permute-start | bytes 884744 | tf_op jit(solution)/shard_map/ppermute | solution.py:394
  (8 other events, 31.6 us)

commit v4 on v3

--- a/solution.py
+++ b/solution.py
@@ -442,13 +442,13 @@
         )
 
     from_core = swap_tp(partial_kv(1, row_adapter_index), 1)
-    kept = partial_kv(0, prior[0])
+    kept = partial_kv(0, row_adapter_index)
 
     def from_chip(rows):
         return swap_tp(kept[2:, rows] + from_core[2:, rows], 2)
 
     span_rows, decode_rows = slice(0, TOKENS), slice(TOKENS, ALL_ROWS)
-    span_kv = finish(kept, from_core, from_chip(span_rows), (prior[1], prior[3]))
+    span_kv = finish(kept, from_core, from_chip(span_rows), ())
     decode_kv = (kept[:2, decode_rows] + from_core[:2, decode_rows] + from_chip(decode_rows)).astype(jnp.bfloat16)
 
     column = jnp.stack(ring(span_kv, False))
@@ -456,7 +456,7 @@
 
     queries = decode_token_queries.reshape(ROWS, STEPS, 2, GROUP, HEAD_SIZE)
     queries = jnp.transpose(queries, (0, 2, 1, 3, 4)).reshape(ROWS, 2, STEPS * GROUP, HEAD_SIZE)
-    decoded = decode_attend(cached_row_lengths, group_live_rows, queries, decode_row_cache, decode_kv, prior[2])
+    decoded = decode_attend(cached_row_lengths, group_live_rows, queries, decode_row_cache, decode_kv, row_adapter_index)
     decoded = jnp.transpose(decoded.reshape(ROWS, 2, STEPS, GROUP, HEAD_SIZE), (0, 2, 1, 3, 4))
     decode_attention = decoded.reshape(ROWS, STEPS, 2 * GROUP * HEAD_SIZE)
 
@@ -466,9 +466,10 @@
     partner_sees = ((place < ctx) | ((place == ctx) & (pool == 0))).astype(jnp.int32).reshape(-1)
     own_sees = (place <= ctx).astype(jnp.int32).reshape(-1)
     earlier = [(p, k, None) for p in range(SIDE) for k in range(SIDE)]
-    first_blocks = (tuple(earlier[:8]), tuple(earlier[8:]), tuple((SIDE, k, k) for k in range(SIDE)))
+    seen_first = earlier + [(SIDE, k, k) for k in range(SIDE)]
+    first_blocks = (tuple(seen_first[:10]), tuple(seen_first[10:]))
     others = [(p, k, (p + 1) * SIDE + k) for p in range(SIDE - 1) for k in range(SIDE)]
-    last_blocks = (tuple(others[:6]), tuple(others[6:]))
+    last_blocks = (tuple(others),)
     both = (0, 2)
     first_pieces = prior + [column]
     partner_queries = swap_pool(span_token_queries)

time: 110 us -> 101 us (0.918)
  waiting for transfers between devices: 14.1 us -> 9.22 us
  Pallas kernels: 50.8 us -> 49.1 us
  starting transfers between devices: 33 us -> 31.8 us
    ppermute x12, waiting for transfers between devices: 14.1 us -> 7.14 us  [shift(): return lax.ppermute(x, 'ctx', perm)]
    ppermute x3, waiting for transfers between devices: 0.01 us -> 1.87 us  [swap_tp(): return lax.ppermute(x, 'tp', [(i, i ^ bit) for i in range(4)])]
    unnamed x26 -> x16, local copies, waits for them, and re-layouts: 3.45 us -> 2.22 us
  transfers between devices with their start and end apart: 19 -> 19, of which waited for: 4 -> 4; matrix products, arithmetic and copies ran while one was open for 6% -> 7% of each run, Pallas kernels for 43% -> 46%
where the time goes in v4:
time: 101 us
  Pallas kernels  49.1 us (49%)
  starting transfers between devices  31.8 us (31%)
  waiting for transfers between devices  9.22 us (9%)
  local copies, waits for them, and re-layouts  5.06 us (5%)
  other arithmetic  4.23 us (4%)
  between operations  1.52 us (2%)
    pallas_call x5, Pallas kernels, attend(): pl.pallas_call(functools.partial(attend_kernel, blocks, diagonal, state i...  33.8 us
    ppermute x12, starting transfers between devices, shift(): return lax.ppermute(x, 'ctx', perm)  21.7 us
    pallas_call x2, Pallas kernels, project(): pl.pallas_call(project_kernel, grid_spec=pltpu.PrefetchScalarGridSpec(num...  10.7 us
    ppermute x4, starting transfers between devices, swap_pool(): return lax.ppermute(x, 'pool', [(0, 1), (1, 0)])  7.89 us
    ppermute x12, waiting for transfers between devices, shift(): return lax.ppermute(x, 'ctx', perm)  7.14 us
    unnamed x16, local copies, waits for them, and re-layouts  2.22 us
    ppermute x3, starting transfers between devices, swap_tp(): return lax.ppermute(x, 'tp', [(i, i ^ bit) for i in range(4)])  2.18 us
    pallas_call x1, Pallas kernels, decode_attend(): pl.pallas_call(decode_kernel, grid_spec=pltpu.PrefetchScalarGridSpec(num_...  2.09 us
  transfers between devices with their start and end apart: 19, of which 4 were waited for; matrix products, arithmetic and copies ran while one was open for 7% of the time, Pallas kernels for 46%

profile of v4, /device:TPU:0, one launch (start us, length us, event | category | flops | bytes accessed | tf_op | source)
XLA Modules:
  0.0 101.0 jit_solution(3554281646897950079)
XLA Ops:
  0.6 1.7 %collective-permute-start = (bf16[2,128,256]{2,1,0:T(8,128)(2,1)}, bf16[2,128,256]{2,1,0:T(8,128)(2,1)S(1)}, u32[]{:S(2)}, u32[]{:S(2)}) collective-permute-start(bf16[2,128,256]{2,1,0:T(8,128)(2,1)} %param.16), channel_id=1, source_target_pairs={{0,8},{8,16},{16,24},{24,0},{32,40},{40,48},{48,56},{56,32},{64,72... | collective-permute-start | bytes 393224 | tf_op jit(solution)/shard_map/ppermute | solution.py:390
  2.4 2.9 %collective-permute-start.1 = (bf16[2,128,256]{2,1,0:T(8,128)(2,1)}, bf16[2,128,256]{2,1,0:T(8,128)(2,1)S(1)}, u32[]{:S(2)}, u32[]{:S(2)}) collective-permute-start(bf16[2,128,256]{2,1,0:T(8,128)(2,1)} %param.16), channel_id=1, source_target_pairs={{0,16},{8,24},{16,0},{24,8},{32,48},{40,56},{48,32},{56,40},{64,80... | collective-permute-start | bytes 393224 | tf_op jit(solution)/shard_map/ppermute | solution.py:390
  6.6 5.3 %project.3 = f32[4,192,256]{2,1,0:T(8,128)} custom-call(s32[1]{0:T(128)} %bitcast.4.tp_ref, s32[16]{0:T(128)} %after_ref.5, bf16[128,2048]{1,0:T(8,128)(2,1)} %span_ref.3, bf16[16,4,2048]{2,1,0:T(4,128)(2,1)} %decode_ref.3, bf16[2048,2048]{1,0:T(8,128)(2,1)} %weight_ref.3, bf16[2048,128]{1,0:T(8,128)(2,1)} %down_ref.3, bf16[128,2048]{1,0:T(8,128)(2,1)} %up_ref.3, ...), custom_call_target="tpu_custom_call" | custom-call | flops 1100000000 | bytes 1048576 | tf_op jit(solution)/shard_map/project/pallas_call | solution.py:76
  11.9 5.4 %project.2.kept_ref = f32[4,192,256]{2,1,0:T(8,128)} custom-call(s32[1]{0:T(128)} %bitcast.4.tp_ref, s32[16]{0:T(128)} %after_ref.5, bf16[128,2048]{1,0:T(8,128)(2,1)} %span_ref.3, bf16[16,4,2048]{2,1,0:T(4,128)(2,1)} %decode_ref.3, bf16[2048,2048]{1,0:T(8,128)(2,1)} %weight_ref.3, bf16[2048,128]{1,0:T(8,128)(2,1)} %down_ref.3, bf16[128,2048]{1,0:T(8,128)(2,1)} %up_ref.3, ...), custom_call_target="tpu_custom_call" | custom-call | flops 1100000000 | bytes 1048576 | tf_op jit(solution)/shard_map/project/pallas_call | solution.py:76
  18.8 1.6 %collective-permute-start.4 = (f32[2,128,256]{2,1,0:T(8,128)S(1)}, f32[2,128,256]{2,1,0:T(8,128)S(1)}, u32[]{:S(2)}, u32[]{:S(2)}) collective-permute-start(f32[2,128,256]{2,1,0:T(8,128)S(1)} %slice_add_fusion), channel_id=1, source_target_pairs={{0,2},{1,3},{2,0},{3,1},{4,6},{5,7},{6,4},{7,5},{8,10},{9,11},{10,... | collective-permute-start | bytes 786440 | tf_op jit(solution)/shard_map/ppermute | solution.py:398
  20.5 2.0 %collective-permute-start.11 = (bf16[4,2,128,256]{3,2,1,0:T(8,128)(2,1)S(1)}, bf16[4,2,128,256]{3,2,1,0:T(8,128)(2,1)}, u32[]{:S(2)}, u32[]{:S(2)}) collective-permute-start(bf16[4,2,128,256]{3,2,1,0:T(8,128)(2,1)S(1)} %pad_maximum_fusion.known_ref.refs_0_), channel_id=1, source_target_pairs={{0,32},{8,40},{16,48},{24,56},{32,64},{40,72},{48,80},{56,88},{64,... | collective-permute-start | bytes 1572872 | tf_op jit(solution)/shard_map/ppermute | solution.py:390
  22.4 3.6 %collective-permute-start.12 = (bf16[4,2,128,256]{3,2,1,0:T(8,128)(2,1)S(1)}, bf16[4,2,128,256]{3,2,1,0:T(8,128)(2,1)}, u32[]{:S(2)}, u32[]{:S(2)}) collective-permute-start(bf16[4,2,128,256]{3,2,1,0:T(8,128)(2,1)S(1)} %pad_maximum_fusion.known_ref.refs_0_), channel_id=1, source_target_pairs={{0,64},{8,72},{16,80},{24,88},{32,96},{40,104},{48,112},{56,120},{... | collective-permute-start | bytes 1572872 | tf_op jit(solution)/shard_map/ppermute | solution.py:390
  30.2 1.9 %collective-permute-done.18 = f32[2,64,256]{2,1,0:T(8,128)S(1)} collective-permute-done((f32[2,64,256]{2,1,0:T(8,128)S(1)}, f32[2,64,256]{2,1,0:T(8,128)S(1)}, u32[]{:S(2)}, u32[]{:S(2)}) %collective-permute-start.18) | collective-permute-done | bytes 131104 | tf_op jit(solution)/shard_map/ppermute | solution.py:398
  32.1 2.6 %collective-permute-start.13 = (bf16[4,2,128,256]{3,2,1,0:T(8,128)(2,1)S(1)}, bf16[4,2,128,256]{3,2,1,0:T(8,128)(2,1)}, u32[]{:S(2)}, u32[]{:S(2)}) collective-permute-start(bf16[4,2,128,256]{3,2,1,0:T(8,128)(2,1)S(1)} %pad_maximum_fusion.known_ref.refs_0_), channel_id=1, source_target_pairs={{0,96},{8,104},{16,112},{24,120},{32,0},{40,8},{48,16},{56,24},{64... | collective-permute-start | bytes 1572872 | tf_op jit(solution)/shard_map/ppermute | solution.py:390
  34.7 2.2 %collective-permute-done.5 = bf16[2,128,256]{2,1,0:T(8,128)(2,1)S(1)} collective-permute-done((bf16[2,128,256]{2,1,0:T(8,128)(2,1)S(1)}, bf16[2,128,256]{2,1,0:T(8,128)(2,1)S(1)}, u32[]{:S(2)}, u32[]{:S(2)}) %collective-permute-start.5) | collective-permute-done | bytes 131104 | tf_op jit(solution)/shard_map/ppermute | solution.py:390
  36.9 3.0 %collective-permute-start.14 = (bf16[128,2048]{1,0:T(8,128)(2,1)}, bf16[128,2048]{1,0:T(8,128)(2,1)S(1)}, u32[]{:S(2)}, u32[]{:S(2)}) collective-permute-start(bf16[128,2048]{1,0:T(8,128)(2,1)} %q_ref.3), channel_id=1, source_target_pairs={{0,4},{4,0},{1,5},{5,1},{2,6},{6,2},{3,7},{7,3},{8,12},{12,8},{9,1... | collective-permute-start | bytes 1572872 | tf_op jit(solution)/shard_map/ppermute | solution.py:394
  40.0 4.9 %collective-permute-done.7 = bf16[2,128,256]{2,1,0:T(8,128)(2,1)S(1)} collective-permute-done((bf16[2,128,256]{2,1,0:T(8,128)(2,1)S(1)}, bf16[2,128,256]{2,1,0:T(8,128)(2,1)S(1)}, u32[]{:S(2)}, u32[]{:S(2)}) %collective-permute-start.7) | collective-permute-done | bytes 131104 | tf_op jit(solution)/shard_map/ppermute | solution.py:390
  45.9 4.1 %collective-permute-start.10 = (bf16[4,2,128,256]{3,2,1,0:T(8,128)(2,1)S(1)}, bf16[4,2,128,256]{3,2,1,0:T(8,128)(2,1)S(1)}, u32[]{:S(2)}, u32[]{:S(2)}) collective-permute-start(bf16[4,2,128,256]{3,2,1,0:T(8,128)(2,1)S(1)} %pad_maximum_fusion.1.refs_4_.refs_5_.refs_0_), channel_id=1, source_target_pairs={{0,96},{8,104},{16,112},{24,120},{32,0},{40,8},{48,16},{56,24},{64... | collective-permute-start | bytes 1572872 | tf_op jit(solution)/shard_map/ppermute | solution.py:390
  50.0 1.9 %collective-permute-start.9 = (bf16[4,2,128,256]{3,2,1,0:T(8,128)(2,1)S(1)}, bf16[4,2,128,256]{3,2,1,0:T(8,128)(2,1)S(1)}, u32[]{:S(2)}, u32[]{:S(2)}) collective-permute-start(bf16[4,2,128,256]{3,2,1,0:T(8,128)(2,1)S(1)} %pad_maximum_fusion.1.refs_4_.refs_5_.refs_0_), channel_id=1, source_target_pairs={{0,64},{8,72},{16,80},{24,88},{32,96},{40,104},{48,112},{56,120},{... | collective-permute-start | bytes 1572872 | tf_op jit(solution)/shard_map/ppermute | solution.py:390
  52.0 2.2 %copy-done = bf16[16,2,256,256]{3,2,1,0:T(8,128)(2,1)S(1)} copy-done((bf16[16,2,256,256]{3,2,1,0:T(8,128)(2,1)S(1)}, bf16[16,2,256,256]{3,2,1,0:T(8,128)(2,1)}, u32[]{:S(2)}) %copy-start) | copy-done | bytes 4194328
  54.1 2.1 %decode.1 = bf16[16,2,32,128]{3,2,1,0:T(8,128)(2,1)S(1)} custom-call(s32[16]{0:T(128)S(1)} %copy-done.3, s32[1]{0:T(128)S(6)} %copy.23.live_ref, bf16[16,2,32,128]{3,2,1,0:T(8,128)(2,1)S(1)} %bitcast.46, bf16[16,2,256,256]{3,2,1,0:T(8,128)(2,1)S(1)} %copy-done, bf16[2,64,256]{2,1,0:T(8,128)(2,1)S(1)} %fusion.1.fresh_ref, s32[16]{0:T(128)S(1)} %copy-done.2), custom_call_target="tpu_custom_call" | custom-call | flops 1100000000 | bytes 1048576 | tf_op jit(solution)/shard_map/decode/pallas_call | solution.py:336
  57.0 1.7 %reshape.341 = bf16[16,4,2048]{2,1,0:T(4,128)(2,1)} reshape(bf16[16,4,2,8,128]{4,3,2,1,0:T(8,128)(2,1)} %copy.20) | data formatting | bytes 524288 | tf_op jit(solution)/shard_map/reshape | solution.py:461
  58.7 9.9 %attend_first.2.refs_3_ = f32[2,1024,256]{2,1,0:T(8,128)S(1)} custom-call(s32[16]{0:T(128)S(1)} %reshape.342.visible_ref, bf16[128,2048]{1,0:T(8,128)(2,1)} %q_ref.3, bf16[4,2,128,256]{3,2,1,0:T(8,128)(2,1)S(1)} %pad_maximum_fusion.known_ref.refs_0_, bf16[4,2,128,256]{3,2,1,0:T(8,128)(2,1)S(1)} %pad_maximum_fusion.known_ref.refs_0_, ...), custom_call_target="tpu_custom_call" | custom-call | flops 2750000128 | bytes 1048576 | tf_op jit(solution)/shard_map/attend_first/pallas_call | solution.py:229
  68.7 9.9 %attend_first.3.refs_3_ = f32[2,1024,256]{2,1,0:T(8,128)S(1)} custom-call(s32[16]{0:T(128)S(1)} %reshape.343.visible_ref, bf16[128,2048]{1,0:T(8,128)(2,1)S(1)} %collective-permute-done.14.q_ref, bf16[4,2,128,256]{3,2,1,0:T(8,128)(2,1)S(1)} %pad_maximum_fusion.known_ref.refs_0_, bf16[4,2,128,256]{3,2,1,0:T(8,128)(2,1)S(1)} %pad_maximum_fusion.known_ref.refs_0_, ...), custom_call_target="tpu_custom_call" | custom-call | flops 2750000128 | bytes 1048576 | tf_op jit(solution)/shard_map/attend_first/pallas_call | solution.py:229
  80.5 3.4 %attend_last.5 = bf16[1,128,1152]{2,1,0:T(8,128)(2,1)S(1)} custom-call(s32[16]{0:T(128)S(1)} %reshape.343.visible_ref, bf16[128,2048]{1,0:T(8,128)(2,1)S(1)} %collective-permute-done.14.q_ref, bf16[4,2,128,256]{3,2,1,0:T(8,128)(2,1)S(1)} %pad_maximum_fusion.known_ref.refs_0_, bf16[4,2,128,256]{3,2,1,0:T(8,128)(2,1)S(1)} %collective-permute-done.8.refs_0_.refs_1_, ...), custom_call_target="tpu_custom_call" | custom-call | flops 825000000 | bytes 1048576 | tf_op jit(solution)/shard_map/attend_last/pallas_call | solution.py:229
  83.9 2.7 %collective-permute-start.16 = (bf16[1,128,1152]{2,1,0:T(8,128)(2,1)S(1)}, bf16[1,128,1152]{2,1,0:T(8,128)(2,1)S(1)}, u32[]{:S(2)}, u32[]{:S(2)}) collective-permute-start(bf16[1,128,1152]{2,1,0:T(8,128)(2,1)S(1)} %attend_last.5), channel_id=1, source_target_pairs={{0,4},{4,0},{1,5},{5,1},{2,6},{6,2},{3,7},{7,3},{8,12},{12,8},{9,1... | collective-permute-start | bytes 884744 | tf_op jit(solution)/shard_map/ppermute | solution.py:394
  86.6 3.4 %attend_last.4 = bf16[1,128,1152]{2,1,0:T(8,128)(2,1)S(1)} custom-call(s32[16]{0:T(128)S(1)} %reshape.343.visible_ref, bf16[128,2048]{1,0:T(8,128)(2,1)S(1)} %collective-permute-done.14.q_ref, bf16[4,2,128,256]{3,2,1,0:T(8,128)(2,1)S(1)} %pad_maximum_fusion.known_ref.refs_0_, bf16[4,2,128,256]{3,2,1,0:T(8,128)(2,1)S(1)} %collective-permute-done.8.refs_0_.refs_1_, ...), custom_call_target="tpu_custom_call" | custom-call | flops 825000000 | bytes 1048576 | tf_op jit(solution)/shard_map/attend_last/pallas_call | solution.py:229
  91.0 7.1 %attend_last.3.refs_0_ = f32[2,128,1152]{2,1,0:T(8,128)S(1)} custom-call(s32[16]{0:T(128)S(1)} %reshape.342.visible_ref, bf16[128,2048]{1,0:T(8,128)(2,1)} %q_ref.3, bf16[4,2,128,256]{3,2,1,0:T(8,128)(2,1)S(1)} %pad_maximum_fusion.known_ref.refs_0_, bf16[4,2,128,256]{3,2,1,0:T(8,128)(2,1)S(1)} %collective-permute-done.8.refs_0_.refs_1_, ...), custom_call_target="tpu_custom_call" | custom-call | flops 1650000000 | bytes 1048576 | tf_op jit(solution)/shard_map/attend_last/pallas_call | solution.py:229
  99.1 1.8 %combine.1 = bf16[128,2048]{1,0:T(8,128)(2,1)} custom-call(f32[2,128,1152]{2,1,0:T(8,128)S(1)} %attend_last.3.refs_0_, bf16[1,128,1152]{2,1,0:T(8,128)(2,1)S(1)} %collective-permute-done.15.refs_1_, bf16[1,128,1152]{2,1,0:T(8,128)(2,1)S(1)} %collective-permute-done.16.refs_2_), custom_call_target="tpu_custom_call" | custom-call | flops 1100000000 | bytes 1048576 | tf_op jit(solution)/shard_map/combine/pallas_call | solution.py:277
  (62 shorter events, 12.0 us)
Async XLA Ops:
  0.6 19.7 %collective-permute-start = (bf16[2,128,256]{2,1,0:T(8,128)(2,1)}, bf16[2,128,256]{2,1,0:T(8,128)(2,1)S(1)}, u32[]{:S(2)}, u32[]{:S(2)}) collective-permute-start(bf16[2,128,256]{2,1,0:T(8,128)(2,1)} %param.16), channel_id=1, source_target_pairs={{0,8},{8,16},{16,24},{24,0},{32,40},{40,48},{48,56},{56,32},{64,72... | collective-permute-start | bytes 393224 | tf_op jit(solution)/shard_map/ppermute | solution.py:390
  2.4 18.0 %collective-permute-start.1 = (bf16[2,128,256]{2,1,0:T(8,128)(2,1)}, bf16[2,128,256]{2,1,0:T(8,128)(2,1)S(1)}, u32[]{:S(2)}, u32[]{:S(2)}) collective-permute-start(bf16[2,128,256]{2,1,0:T(8,128)(2,1)} %param.16), channel_id=1, source_target_pairs={{0,16},{8,24},{16,0},{24,8},{32,48},{40,56},{48,32},{56,40},{64,80... | collective-permute-start | bytes 393224 | tf_op jit(solution)/shard_map/ppermute | solution.py:390
  5.3 15.1 %collective-permute-start.2 = (bf16[2,128,256]{2,1,0:T(8,128)(2,1)}, bf16[2,128,256]{2,1,0:T(8,128)(2,1)S(1)}, u32[]{:S(2)}, u32[]{:S(2)}) collective-permute-start(bf16[2,128,256]{2,1,0:T(8,128)(2,1)} %param.16), channel_id=1, source_target_pairs={{0,24},{8,0},{16,8},{24,16},{32,56},{40,32},{48,40},{56,48},{64,88... | collective-permute-start | bytes 393224 | tf_op jit(solution)/shard_map/ppermute | solution.py:390
  11.9 5.9 %collective-permute-start.3 = (f32[4,192,256]{2,1,0:T(8,128)}, f32[4,192,256]{2,1,0:T(8,128)S(1)}, u32[]{:S(2)}, u32[]{:S(2)}) collective-permute-start(f32[4,192,256]{2,1,0:T(8,128)} %project.3), channel_id=1, source_target_pairs={{0,1},{1,0},{2,3},{3,2},{4,5},{5,4},{6,7},{7,6},{8,9},{9,8},{10,11... | collective-permute-start | bytes 2359304 | tf_op jit(solution)/shard_map/ppermute | solution.py:398
  11.9 8.5 %copy-start.5 = (bf16[2,128,256]{2,1,0:T(8,128)(2,1)S(1)}, bf16[2,128,256]{2,1,0:T(8,128)(2,1)}, u32[]{:S(2)}) copy-start(bf16[2,128,256]{2,1,0:T(8,128)(2,1)} %param.16) | copy-start | bytes 393220
  17.3 10.3 %copy-start.1 = (f32[4,192,256]{2,1,0:T(8,128)S(1)}, f32[4,192,256]{2,1,0:T(8,128)}, u32[]{:S(2)}) copy-start(f32[4,192,256]{2,1,0:T(8,128)} %project.2.kept_ref) | copy-start | bytes 2359300
  17.8 11.6 %copy-start.4 = (bf16[16,4,2048]{2,1,0:T(4,128)(2,1)S(1)}, bf16[16,4,2048]{2,1,0:T(4,128)(2,1)}, u32[]{:S(2)}) copy-start(bf16[16,4,2048]{2,1,0:T(4,128)(2,1)} %param.18) | copy-start | bytes 786436
  18.8 8.8 %collective-permute-start.4 = (f32[2,128,256]{2,1,0:T(8,128)S(1)}, f32[2,128,256]{2,1,0:T(8,128)S(1)}, u32[]{:S(2)}, u32[]{:S(2)}) collective-permute-start(f32[2,128,256]{2,1,0:T(8,128)S(1)} %slice_add_fusion), channel_id=1, source_target_pairs={{0,2},{1,3},{2,0},{3,1},{4,6},{5,7},{6,4},{7,5},{8,10},{9,11},{10,... | collective-permute-start | bytes 786440 | tf_op jit(solution)/shard_map/ppermute | solution.py:398
  20.5 29.6 %collective-permute-start.11 = (bf16[4,2,128,256]{3,2,1,0:T(8,128)(2,1)S(1)}, bf16[4,2,128,256]{3,2,1,0:T(8,128)(2,1)}, u32[]{:S(2)}, u32[]{:S(2)}) collective-permute-start(bf16[4,2,128,256]{3,2,1,0:T(8,128)(2,1)S(1)} %pad_maximum_fusion.known_ref.refs_0_), channel_id=1, source_target_pairs={{0,32},{8,40},{16,48},{24,56},{32,64},{40,72},{48,80},{56,88},{64,... | collective-permute-start | bytes 1572872 | tf_op jit(solution)/shard_map/ppermute | solution.py:390
  22.4 27.6 %collective-permute-start.12 = (bf16[4,2,128,256]{3,2,1,0:T(8,128)(2,1)S(1)}, bf16[4,2,128,256]{3,2,1,0:T(8,128)(2,1)}, u32[]{:S(2)}, u32[]{:S(2)}) collective-permute-start(bf16[4,2,128,256]{3,2,1,0:T(8,128)(2,1)S(1)} %pad_maximum_fusion.known_ref.refs_0_), channel_id=1, source_target_pairs={{0,64},{8,72},{16,80},{24,88},{32,96},{40,104},{48,112},{56,120},{... | collective-permute-start | bytes 1572872 | tf_op jit(solution)/shard_map/ppermute | solution.py:390
  27.0 25.0 %copy-start.2 = (s32[16]{0:T(128)S(1)}, s32[16]{0:T(128)}, u32[]{:S(2)}) copy-start(s32[16]{0:T(128)} %after_ref.5) | copy-start | bytes 196
  27.0 25.0 %copy-start.3 = (s32[16]{0:T(128)S(1)}, s32[16]{0:T(128)}, u32[]{:S(2)}) copy-start(s32[16]{0:T(128)} %length_ref.1) | copy-start | bytes 196
  27.0 5.1 %collective-permute-start.18 = (f32[2,64,256]{2,1,0:T(8,128)S(1)}, f32[2,64,256]{2,1,0:T(8,128)S(1)}, u32[]{:S(2)}, u32[]{:S(2)}) collective-permute-start(f32[2,64,256]{2,1,0:T(8,128)S(1)} %slice_add_fusion.1), channel_id=1, source_target_pairs={{0,2},{1,3},{2,0},{3,1},{4,6},{5,7},{6,4},{7,5},{8,10},{9,11},{10,... | collective-permute-start | bytes 393224 | tf_op jit(solution)/shard_map/ppermute | solution.py:398
  27.6 9.3 %collective-permute-start.5 = (bf16[2,128,256]{2,1,0:T(8,128)(2,1)S(1)}, bf16[2,128,256]{2,1,0:T(8,128)(2,1)S(1)}, u32[]{:S(2)}, u32[]{:S(2)}) collective-permute-start(bf16[2,128,256]{2,1,0:T(8,128)(2,1)S(1)} %finish.1), channel_id=1, source_target_pairs={{0,8},{8,16},{16,24},{24,0},{32,40},{40,48},{48,56},{56,32},{64,72... | collective-permute-start | bytes 393224 | tf_op jit(solution)/shard_map/ppermute | solution.py:390
  28.4 11.5 %collective-permute-start.6 = (bf16[2,128,256]{2,1,0:T(8,128)(2,1)S(1)}, bf16[2,128,256]{2,1,0:T(8,128)(2,1)}, u32[]{:S(2)}, u32[]{:S(2)}) collective-permute-start(bf16[2,128,256]{2,1,0:T(8,128)(2,1)S(1)} %finish.1), channel_id=1, source_target_pairs={{0,16},{8,24},{16,0},{24,8},{32,48},{40,56},{48,32},{56,40},{64,80... | collective-permute-start | bytes 393224 | tf_op jit(solution)/shard_map/ppermute | solution.py:390
  32.1 26.6 %collective-permute-start.13 = (bf16[4,2,128,256]{3,2,1,0:T(8,128)(2,1)S(1)}, bf16[4,2,128,256]{3,2,1,0:T(8,128)(2,1)}, u32[]{:S(2)}, u32[]{:S(2)}) collective-permute-start(bf16[4,2,128,256]{3,2,1,0:T(8,128)(2,1)S(1)} %pad_maximum_fusion.known_ref.refs_0_), channel_id=1, source_target_pairs={{0,96},{8,104},{16,112},{24,120},{32,0},{40,8},{48,16},{56,24},{64... | collective-permute-start | bytes 1572872 | tf_op jit(solution)/shard_map/ppermute | solution.py:390
  36.9 31.7 %collective-permute-start.14 = (bf16[128,2048]{1,0:T(8,128)(2,1)}, bf16[128,2048]{1,0:T(8,128)(2,1)S(1)}, u32[]{:S(2)}, u32[]{:S(2)}) collective-permute-start(bf16[128,2048]{1,0:T(8,128)(2,1)} %q_ref.3), channel_id=1, source_target_pairs={{0,4},{4,0},{1,5},{5,1},{2,6},{6,2},{3,7},{7,3},{8,12},{12,8},{9,1... | collective-permute-start | bytes 1572872 | tf_op jit(solution)/shard_map/ppermute | solution.py:394
  39.9 5.0 %collective-permute-start.7 = (bf16[2,128,256]{2,1,0:T(8,128)(2,1)S(1)}, bf16[2,128,256]{2,1,0:T(8,128)(2,1)S(1)}, u32[]{:S(2)}, u32[]{:S(2)}) collective-permute-start(bf16[2,128,256]{2,1,0:T(8,128)(2,1)S(1)} %finish.1), channel_id=1, source_target_pairs={{0,24},{8,0},{16,8},{24,16},{32,56},{40,32},{48,40},{56,48},{64,88... | collective-permute-start | bytes 393224 | tf_op jit(solution)/shard_map/ppermute | solution.py:390
  45.9 32.6 %collective-permute-start.10 = (bf16[4,2,128,256]{3,2,1,0:T(8,128)(2,1)S(1)}, bf16[4,2,128,256]{3,2,1,0:T(8,128)(2,1)S(1)}, u32[]{:S(2)}, u32[]{:S(2)}) collective-permute-start(bf16[4,2,128,256]{3,2,1,0:T(8,128)(2,1)S(1)} %pad_maximum_fusion.1.refs_4_.refs_5_.refs_0_), channel_id=1, source_target_pairs={{0,96},{8,104},{16,112},{24,120},{32,0},{40,8},{48,16},{56,24},{64... | collective-permute-start | bytes 1572872 | tf_op jit(solution)/shard_map/ppermute | solution.py:390
  50.0 28.5 %collective-permute-start.8 = (bf16[4,2,128,256]{3,2,1,0:T(8,128)(2,1)S(1)}, bf16[4,2,128,256]{3,2,1,0:T(8,128)(2,1)S(1)}, u32[]{:S(2)}, u32[]{:S(2)}) collective-permute-start(bf16[4,2,128,256]{3,2,1,0:T(8,128)(2,1)S(1)} %pad_maximum_fusion.1.refs_4_.refs_5_.refs_0_), channel_id=1, source_target_pairs={{0,32},{8,40},{16,48},{24,56},{32,64},{40,72},{48,80},{56,88},{64,... | collective-permute-start | bytes 1572872 | tf_op jit(solution)/shard_map/ppermute | solution.py:390
  50.0 28.5 %collective-permute-start.9 = (bf16[4,2,128,256]{3,2,1,0:T(8,128)(2,1)S(1)}, bf16[4,2,128,256]{3,2,1,0:T(8,128)(2,1)S(1)}, u32[]{:S(2)}, u32[]{:S(2)}) collective-permute-start(bf16[4,2,128,256]{3,2,1,0:T(8,128)(2,1)S(1)} %pad_maximum_fusion.1.refs_4_.refs_5_.refs_0_), channel_id=1, source_target_pairs={{0,64},{8,72},{16,80},{24,88},{32,96},{40,104},{48,112},{56,120},{... | collective-permute-start | bytes 1572872 | tf_op jit(solution)/shard_map/ppermute | solution.py:390
  79.3 18.9 %collective-permute-start.17 = (bf16[8,2,16,256]{3,2,1,0:T(8,128)(2,1)S(1)}, bf16[8,2,16,256]{3,2,1,0:T(8,128)(2,1)S(1)}, u32[]{:S(2)}, u32[]{:S(2)}) collective-permute-start(bf16[8,2,16,256]{3,2,1,0:T(8,128)(2,1)S(1)} %slice.39), channel_id=1, source_target_pairs={{0,4},{4,0},{1,5},{5,1},{2,6},{6,2},{3,7},{7,3},{8,12},{12,8},{9,1... | collective-permute-start | bytes 393224 | tf_op jit(solution)/shard_map/ppermute | solution.py:394
  83.9 15.0 %collective-permute-start.16 = (bf16[1,128,1152]{2,1,0:T(8,128)(2,1)S(1)}, bf16[1,128,1152]{2,1,0:T(8,128)(2,1)S(1)}, u32[]{:S(2)}, u32[]{:S(2)}) collective-permute-start(bf16[1,128,1152]{2,1,0:T(8,128)(2,1)S(1)} %attend_last.5), channel_id=1, source_target_pairs={{0,4},{4,0},{1,5},{5,1},{2,6},{6,2},{3,7},{7,3},{8,12},{12,8},{9,1... | collective-permute-start | bytes 884744 | tf_op jit(solution)/shard_map/ppermute | solution.py:394
  90.1 9.1 %collective-permute-start.15 = (bf16[1,128,1152]{2,1,0:T(8,128)(2,1)S(1)}, bf16[1,128,1152]{2,1,0:T(8,128)(2,1)S(1)}, u32[]{:S(2)}, u32[]{:S(2)}) collective-permute-start(bf16[1,128,1152]{2,1,0:T(8,128)(2,1)S(1)} %attend_last.4), channel_id=1, source_target_pairs={{0,4},{4,0},{1,5},{5,1},{2,6},{6,2},{3,7},{7,3},{8,12},{12,8},{9,1... | collective-permute-start | bytes 884744 | tf_op jit(solution)/shard_map/ppermute | solution.py:394
  (3 other events, 15.7 us)

commit v5 on v4

--- a/solution.py
+++ b/solution.py
@@ -39,6 +39,7 @@
     return hi, mid, low
 
 PROJECT_US, ATTEND_US, DECODE_US = 1, 1, 1
+ATTEND_VMEM = 24
 
 
 def project_kernel(
@@ -124,124 +125,124 @@
 HEAD_COLUMNS = GROUP * HEAD_SIZE
 
 
-def attend_kernel(blocks, diagonal, has_state, final, partner, visible_ref, q_ref, known_ref, *refs):
+def attend_kernel(heads, blocks, diagonal, has_state, final, partner, visible_ref, q_ref, known_ref, *refs):
     pieces, refs = refs[: blocks[-1][-1][0] + 1], refs[blocks[-1][-1][0] + 1 :]
-    if has_state:
-        state_ref, refs = refs[0], refs[1:]
-    else:
-        refs = refs[1:]
-    out_ref, top_ref, acc_ref, ext_ref, key_ref = refs
-    queries = [
-        jnp.concatenate(
-            [q_ref[:, (i * TILE + j) * HEAD_SIZE : (i * TILE + j + 1) * HEAD_SIZE] for j in range(TILE)], axis=0
-        )
-        for i in range(TILES)
-    ]
+    state_ref, out_ref, key_ref, ext_ref = refs
     wide = lax.broadcasted_iota(jnp.int32, (TILE_ROWS, HEAD_SIZE), 1)
     lane = wide[:TOKENS]
     one = jnp.ones((TOKENS, HEAD_SIZE), jnp.bfloat16)
     zero = jnp.zeros((TOKENS, HEAD_SIZE), jnp.bfloat16)
-    if final:
-        stats = jnp.zeros((TOKENS, HEAD_SIZE), out_ref.dtype)
-    start = 0
-    for b, shards in enumerate(blocks):
-        stop = start + len(shards) * TOKENS
-        block = slice(start, stop)
-        for n, (piece, index, place) in enumerate(shards):
-            kv = pieces[piece][index, 0]
-            keys, values, ones = kv[:, :HEAD_SIZE], kv[:, HEAD_SIZE:], one
-            if place is not None:
-                seen = visible_ref[place] != 0
-                keys = jnp.where(seen, keys, known_ref[0, 0, :, :HEAD_SIZE])
-                values = jnp.where(seen, values, zero)
-                ones = jnp.where(seen, one, zero)
-            here = slice(start + n * TOKENS, start + (n + 1) * TOKENS)
-            key_ref[here, :] = keys
-            ext_ref[here, :HEAD_SIZE] = values
-            ext_ref[here, HEAD_SIZE:] = ones
-        for i in range(TILES):
-            here = slice(i * TILE_ROWS, (i + 1) * TILE_ROWS)
+    bounds = [0]
+    for shards in blocks:
+        bounds.append(bounds[-1] + len(shards) * TOKENS)
+    for slot, h in enumerate(heads):
+        for b, shards in enumerate(blocks):
+            for n, (piece, index, place) in enumerate(shards):
+                kv = pieces[piece][index, h]
+                keys, values, ones = kv[:, :HEAD_SIZE], kv[:, HEAD_SIZE:], one
+                if place is not None:
+                    seen = visible_ref[place] != 0
+                    keys = jnp.where(seen, keys, known_ref[0, h, :, :HEAD_SIZE])
+                    values = jnp.where(seen, values, zero)
+                    ones = jnp.where(seen, one, zero)
+                here = slice(bounds[b] + n * TOKENS, bounds[b] + (n + 1) * TOKENS)
+                key_ref[slot, here, :] = keys
+                ext_ref[slot, here, :HEAD_SIZE] = values
+                ext_ref[slot, here, HEAD_SIZE:] = ones
+        queries = [
+            jnp.concatenate(
+                [
+                    q_ref[:, h * HEAD_COLUMNS + g * HEAD_SIZE : h * HEAD_COLUMNS + (g + 1) * HEAD_SIZE]
+                    for g in range(i * TILE, (i + 1) * TILE)
+                ],
+                axis=0,
+            )
+            for i in range(TILES)
+        ]
+
+        def score(i, b):
             scores = lax.dot_general(
-                queries[i], key_ref[block, :], (((1,), (1,)), ((), ())), preferred_element_type=jnp.float32
-            )
-            if diagonal is not None and diagonal in shards:
-                at = shards.index(diagonal) * TOKENS
+                queries[i],
+                key_ref[slot, bounds[b] : bounds[b + 1], :],
+                (((1,), (1,)), ((), ())),
+                preferred_element_type=jnp.float32,
+            )
+            if diagonal is not None and diagonal in blocks[b]:
+                at = blocks[b].index(diagonal) * TOKENS
                 token = lax.broadcasted_iota(jnp.int32, (TILE_ROWS, TOKENS), 0) % TOKENS
                 parts = [scores[:, :at]] if at else []
                 parts.append(jnp.where(wide <= token, scores[:, at : at + TOKENS], neg_large))
                 if at + TOKENS < scores.shape[1]:
                     parts.append(scores[:, at + TOKENS :])
                 scores = jnp.concatenate(parts, axis=1)
-            top = jnp.max(scores, axis=1, keepdims=True) * LOG2_SCALE
+            return scores, jnp.max(scores, axis=1, keepdims=True) * LOG2_SCALE
+
+        steps = [(i, b) for i in range(TILES) for b in range(len(blocks))]
+        if final:
+            stats = jnp.zeros((TOKENS, HEAD_SIZE), out_ref.dtype)
+        coming = score(*steps[0])
+        for n, (i, b) in enumerate(steps):
+            scores, top = coming
+            if n + 1 < len(steps):
+                coming = score(*steps[n + 1])
+            here = slice(i * TILE_ROWS, (i + 1) * TILE_ROWS)
             if b or has_state:
-                if b:
-                    top_before, before = top_ref[here, :1], acc_ref[here]
-                else:
-                    top_before = state_ref[0, here, HEAD_SIZE : HEAD_SIZE + 1]
-                    total_before = state_ref[0, here, WIDTH - 1 :]
-                    before = jnp.concatenate(
-                        [state_ref[0, here, :HEAD_SIZE], jnp.broadcast_to(total_before, (TILE_ROWS, HEAD_SIZE))],
+                if not b:
+                    top_before = state_ref[h, here, HEAD_SIZE : HEAD_SIZE + 1]
+                    total = jnp.concatenate(
+                        [
+                            state_ref[h, here, :HEAD_SIZE],
+                            jnp.broadcast_to(state_ref[h, here, WIDTH - 1 :], (TILE_ROWS, HEAD_SIZE)),
+                        ],
                         axis=1,
                     )
                 top = jnp.maximum(top_before, top)
+                total = total * jnp.exp2(top_before - top)
             weights = jnp.exp2(scores * LOG2_SCALE - top).astype(jnp.bfloat16)
-            total = jnp.dot(weights, ext_ref[block, :], preferred_element_type=jnp.float32)
-            if b or has_state:
-                total = before * jnp.exp2(top_before - top) + total
+            added = jnp.dot(
+                weights, ext_ref[slot, bounds[b] : bounds[b + 1], :], preferred_element_type=jnp.float32
+            )
+            total = total + added if b or has_state else added
+            top_before = top
             if b < len(blocks) - 1:
-                acc_ref[here] = total
-                top_ref[here] = jnp.broadcast_to(top, (TILE_ROWS, HEAD_SIZE))
                 continue
             if not final:
-                out_ref[0, here, :HEAD_SIZE] = total[:, :HEAD_SIZE]
-                out_ref[0, here, HEAD_SIZE:] = jnp.where(wide < HEAD_SIZE // 2, top, total[:, HEAD_SIZE:])
+                out_ref[slot, here, :HEAD_SIZE] = total[:, :HEAD_SIZE]
+                out_ref[slot, here, HEAD_SIZE:] = jnp.where(wide < HEAD_SIZE // 2, top, total[:, HEAD_SIZE:])
                 continue
             out = total[:, :HEAD_SIZE] / total[:, HEAD_SIZE:]
             level = top + jnp.log2(total[:, HEAD_SIZE:])
             for j in range(TILE):
                 g = i * TILE + j
                 own = slice(j * TOKENS, (j + 1) * TOKENS)
-                out_ref[0, :, g * HEAD_SIZE : (g + 1) * HEAD_SIZE] = out[own].astype(out_ref.dtype)
+                out_ref[slot, :, g * HEAD_SIZE : (g + 1) * HEAD_SIZE] = out[own].astype(out_ref.dtype)
                 parts = split3(level[own]) if partner else (level[own],)
                 for part, piece in enumerate(parts):
                     stats = jnp.where(lane == part * GROUP + g, piece, stats)
-        start = stop
-    if final:
-        out_ref[0, :, HEAD_COLUMNS:] = stats
+        if final:
+            out_ref[slot, :, HEAD_COLUMNS:] = stats
 
 
 def attend(visible, queries, known, pieces, blocks, after, heads, diagonal=None, state=None, final=False, partner=False):
-    first, count = heads
-    head = lambda h: first + h
     shards = sum(len(block) for block in blocks)
+    count = len(heads)
     if final:
         out_shape = (count, TOKENS, HEAD_COLUMNS + HEAD_SIZE)
     else:
         out_shape = (count, HEAD_ROWS, WIDTH)
-    in_specs = [
-        pl.BlockSpec((TOKENS, HEAD_COLUMNS), lambda h, *_: (0, head(h))),
-        pl.BlockSpec((1, 1, TOKENS, WIDTH), lambda h, *_: (0, head(h), 0, 0)),
-    ] + [pl.BlockSpec((SIDE, 1, TOKENS, WIDTH), lambda h, *_: (0, head(h), 0, 0))] * len(pieces)
-    if state is None:
-        in_specs.append(pl.BlockSpec(memory_space=pl.ANY))
-    else:
-        in_specs.append(pl.BlockSpec((1, HEAD_ROWS, WIDTH), lambda h, *_: (head(h), 0, 0)))
+    local = pl.BlockSpec(memory_space=pltpu.VMEM)
     return pl.pallas_call(
-        functools.partial(attend_kernel, blocks, diagonal, state is not None, final, partner),
-        grid_spec=pltpu.PrefetchScalarGridSpec(
-            num_scalar_prefetch=1,
-            grid=(count,),
-            in_specs=in_specs,
-            out_specs=pl.BlockSpec((1,) + out_shape[1:], lambda h, *_: (h, 0, 0)),
-            scratch_shapes=[
-                pltpu.VMEM((HEAD_ROWS, HEAD_SIZE), jnp.float32),
-                pltpu.VMEM((HEAD_ROWS, WIDTH), jnp.float32),
-                pltpu.VMEM((shards * TOKENS, WIDTH), jnp.bfloat16),
-                pltpu.VMEM((shards * TOKENS, HEAD_SIZE), jnp.bfloat16),
-            ],
-        ),
+        functools.partial(attend_kernel, heads, blocks, diagonal, state is not None, final, partner),
+        in_specs=[pl.BlockSpec(memory_space=pltpu.SMEM)]
+        + [local] * (2 + len(pieces))
+        + [pl.BlockSpec(memory_space=pl.ANY) if state is None else local],
+        out_specs=local,
+        scratch_shapes=[
+            pltpu.VMEM((count, shards * TOKENS, HEAD_SIZE), jnp.bfloat16),
+            pltpu.VMEM((count, shards * TOKENS, WIDTH), jnp.bfloat16),
+        ],
         out_shape=jax.ShapeDtypeStruct(out_shape, jnp.bfloat16 if partner and final else jnp.float32),
-        compiler_params=pltpu.CompilerParams(vmem_limit_bytes=24 * MIB),
+        compiler_params=pltpu.CompilerParams(vmem_limit_bytes=ATTEND_VMEM * MIB),
         cost_estimate=estimate(ATTEND_US * count * shards / 16),
         name="attend_last" if final else "attend_first",
     )(visible, queries, known, *pieces, after if state is None else state)
@@ -470,7 +471,7 @@
     first_blocks = (tuple(seen_first[:10]), tuple(seen_first[10:]))
     others = [(p, k, (p + 1) * SIDE + k) for p in range(SIDE - 1) for k in range(SIDE)]
     last_blocks = (tuple(others),)
-    both = (0, 2)
+    both = (0, 1)
     first_pieces = prior + [column]
     partner_queries = swap_pool(span_token_queries)
     own_state = attend(
@@ -509,7 +510,7 @@
                 planes[1:],
                 last_blocks,
                 None,
-                (h, 1),
+                (h,),
                 state=partner_state,
                 final=True,
                 partner=True,

time: 101 us -> 98.3 us (0.973)
  Pallas kernels: 49.1 us -> 44.9 us
  waiting for transfers between devices: 9.22 us -> 10.4 us
    pallas_call x5, Pallas kernels: 33.8 us -> 29.3 us  [attend(): pl.pallas_call(functools.partial(attend_kernel, heads, blocks, diagonal,...]
    ppermute x4, waiting for transfers between devices: 0.21 us -> 1.41 us  [swap_pool(): return lax.ppermute(x, 'pool', [(0, 1), (1, 0)])]
  transfers between devices with their start and end apart: 19 -> 19, of which waited for: 4 -> 4; matrix products, arithmetic and copies ran while one was open for 7% -> 7% of each run, Pallas kernels for 46% -> 43%
where the time goes in v5:
time: 98.3 us; the launch traced here: 97.9 us
  Pallas kernels  44.9 us (46%)
  starting transfers between devices  31.8 us (32%)
  waiting for transfers between devices  10.4 us (11%)
  local copies, waits for them, and re-layouts  5.06 us (5%)
  other arithmetic  4.23 us (4%)
  between operations  1.52 us (2%)
    pallas_call x5, Pallas kernels, attend(): pl.pallas_call(functools.partial(attend_kernel, heads, blocks, diagonal,...  29.3 us
    ppermute x12, starting transfers between devices, shift(): return lax.ppermute(x, 'ctx', perm)  21.7 us
    pallas_call x2, Pallas kernels, project(): pl.pallas_call(project_kernel, grid_spec=pltpu.PrefetchScalarGridSpec(num...  10.7 us
    ppermute x4, starting transfers between devices, swap_pool(): return lax.ppermute(x, 'pool', [(0, 1), (1, 0)])  7.93 us
    ppermute x12, waiting for transfers between devices, shift(): return lax.ppermute(x, 'ctx', perm)  7.14 us
    pallas_call x1, Pallas kernels, decode_attend(): pl.pallas_call(decode_kernel, grid_spec=pltpu.PrefetchScalarGridSpec(num_...  2.27 us
    unnamed x16, local copies, waits for them, and re-layouts  2.22 us
    ppermute x3, starting transfers between devices, swap_tp(): return lax.ppermute(x, 'tp', [(i, i ^ bit) for i in range(4)])  2.18 us
  transfers between devices with their start and end apart: 19, of which 4 were waited for; matrix products, arithmetic and copies ran while one was open for 7% of the time, Pallas kernels for 43%

profile of v5, /device:TPU:0, one launch (start us, length us, event | category | flops | bytes accessed | tf_op | source)
XLA Modules:
  0.0 97.9 jit_solution(13309465211152674369)
XLA Ops:
  0.6 1.7 %collective-permute-start = (bf16[2,128,256]{2,1,0:T(8,128)(2,1)}, bf16[2,128,256]{2,1,0:T(8,128)(2,1)S(1)}, u32[]{:S(2)}, u32[]{:S(2)}) collective-permute-start(bf16[2,128,256]{2,1,0:T(8,128)(2,1)} %param.16), channel_id=1, source_target_pairs={{0,8},{8,16},{16,24},{24,0},{32,40},{40,48},{48,56},{56,32},{64,72... | collective-permute-start | bytes 393224 | tf_op jit(solution)/shard_map/ppermute | solution.py:391
  2.4 2.9 %collective-permute-start.1 = (bf16[2,128,256]{2,1,0:T(8,128)(2,1)}, bf16[2,128,256]{2,1,0:T(8,128)(2,1)S(1)}, u32[]{:S(2)}, u32[]{:S(2)}) collective-permute-start(bf16[2,128,256]{2,1,0:T(8,128)(2,1)} %param.16), channel_id=1, source_target_pairs={{0,16},{8,24},{16,0},{24,8},{32,48},{40,56},{48,32},{56,40},{64,80... | collective-permute-start | bytes 393224 | tf_op jit(solution)/shard_map/ppermute | solution.py:391
  6.6 5.3 %project.3 = f32[4,192,256]{2,1,0:T(8,128)} custom-call(s32[1]{0:T(128)} %bitcast.4.tp_ref, s32[16]{0:T(128)} %after_ref.5, bf16[128,2048]{1,0:T(8,128)(2,1)} %span_ref.3, bf16[16,4,2048]{2,1,0:T(4,128)(2,1)} %decode_ref.3, bf16[2048,2048]{1,0:T(8,128)(2,1)} %weight_ref.3, bf16[2048,128]{1,0:T(8,128)(2,1)} %down_ref.3, bf16[128,2048]{1,0:T(8,128)(2,1)} %up_ref.3, ...), custom_call_target="tpu_custom_call" | custom-call | flops 1100000000 | bytes 1048576 | tf_op jit(solution)/shard_map/project/pallas_call | solution.py:77
  11.9 5.4 %project.2.kept_ref = f32[4,192,256]{2,1,0:T(8,128)} custom-call(s32[1]{0:T(128)} %bitcast.4.tp_ref, s32[16]{0:T(128)} %after_ref.5, bf16[128,2048]{1,0:T(8,128)(2,1)} %span_ref.3, bf16[16,4,2048]{2,1,0:T(4,128)(2,1)} %decode_ref.3, bf16[2048,2048]{1,0:T(8,128)(2,1)} %weight_ref.3, bf16[2048,128]{1,0:T(8,128)(2,1)} %down_ref.3, bf16[128,2048]{1,0:T(8,128)(2,1)} %up_ref.3, ...), custom_call_target="tpu_custom_call" | custom-call | flops 1100000000 | bytes 1048576 | tf_op jit(solution)/shard_map/project/pallas_call | solution.py:77
  18.8 1.6 %collective-permute-start.4 = (f32[2,128,256]{2,1,0:T(8,128)S(1)}, f32[2,128,256]{2,1,0:T(8,128)S(1)}, u32[]{:S(2)}, u32[]{:S(2)}) collective-permute-start(f32[2,128,256]{2,1,0:T(8,128)S(1)} %slice_add_fusion), channel_id=1, source_target_pairs={{0,2},{1,3},{2,0},{3,1},{4,6},{5,7},{6,4},{7,5},{8,10},{9,11},{10,... | collective-permute-start | bytes 786440 | tf_op jit(solution)/shard_map/ppermute | solution.py:399
  20.5 2.0 %collective-permute-start.11 = (bf16[4,2,128,256]{3,2,1,0:T(8,128)(2,1)S(1)}, bf16[4,2,128,256]{3,2,1,0:T(8,128)(2,1)}, u32[]{:S(2)}, u32[]{:S(2)}) collective-permute-start(bf16[4,2,128,256]{3,2,1,0:T(8,128)(2,1)S(1)} %pad_maximum_fusion.known_ref.refs_0_), channel_id=1, source_target_pairs={{0,32},{8,40},{16,48},{24,56},{32,64},{40,72},{48,80},{56,88},{64,... | collective-permute-start | bytes 1572872 | tf_op jit(solution)/shard_map/ppermute | solution.py:391
  22.4 3.6 %collective-permute-start.12 = (bf16[4,2,128,256]{3,2,1,0:T(8,128)(2,1)S(1)}, bf16[4,2,128,256]{3,2,1,0:T(8,128)(2,1)}, u32[]{:S(2)}, u32[]{:S(2)}) collective-permute-start(bf16[4,2,128,256]{3,2,1,0:T(8,128)(2,1)S(1)} %pad_maximum_fusion.known_ref.refs_0_), channel_id=1, source_target_pairs={{0,64},{8,72},{16,80},{24,88},{32,96},{40,104},{48,112},{56,120},{... | collective-permute-start | bytes 1572872 | tf_op jit(solution)/shard_map/ppermute | solution.py:391
  30.2 1.9 %collective-permute-done.18 = f32[2,64,256]{2,1,0:T(8,128)S(1)} collective-permute-done((f32[2,64,256]{2,1,0:T(8,128)S(1)}, f32[2,64,256]{2,1,0:T(8,128)S(1)}, u32[]{:S(2)}, u32[]{:S(2)}) %collective-permute-start.18) | collective-permute-done | bytes 131104 | tf_op jit(solution)/shard_map/ppermute | solution.py:399
  32.1 2.6 %collective-permute-start.13 = (bf16[4,2,128,256]{3,2,1,0:T(8,128)(2,1)S(1)}, bf16[4,2,128,256]{3,2,1,0:T(8,128)(2,1)}, u32[]{:S(2)}, u32[]{:S(2)}) collective-permute-start(bf16[4,2,128,256]{3,2,1,0:T(8,128)(2,1)S(1)} %pad_maximum_fusion.known_ref.refs_0_), channel_id=1, source_target_pairs={{0,96},{8,104},{16,112},{24,120},{32,0},{40,8},{48,16},{56,24},{64... | collective-permute-start | bytes 1572872 | tf_op jit(solution)/shard_map/ppermute | solution.py:391
  34.7 2.2 %collective-permute-done.5 = bf16[2,128,256]{2,1,0:T(8,128)(2,1)S(1)} collective-permute-done((bf16[2,128,256]{2,1,0:T(8,128)(2,1)S(1)}, bf16[2,128,256]{2,1,0:T(8,128)(2,1)S(1)}, u32[]{:S(2)}, u32[]{:S(2)}) %collective-permute-start.5) | collective-permute-done | bytes 131104 | tf_op jit(solution)/shard_map/ppermute | solution.py:391
  36.9 3.0 %collective-permute-start.14 = (bf16[128,2048]{1,0:T(8,128)(2,1)}, bf16[128,2048]{1,0:T(8,128)(2,1)S(1)}, u32[]{:S(2)}, u32[]{:S(2)}) collective-permute-start(bf16[128,2048]{1,0:T(8,128)(2,1)} %q_ref.3), channel_id=1, source_target_pairs={{0,4},{4,0},{1,5},{5,1},{2,6},{6,2},{3,7},{7,3},{8,12},{12,8},{9,1... | collective-permute-start | bytes 1572872 | tf_op jit(solution)/shard_map/ppermute | solution.py:395
  40.0 4.9 %collective-permute-done.7 = bf16[2,128,256]{2,1,0:T(8,128)(2,1)S(1)} collective-permute-done((bf16[2,128,256]{2,1,0:T(8,128)(2,1)S(1)}, bf16[2,128,256]{2,1,0:T(8,128)(2,1)S(1)}, u32[]{:S(2)}, u32[]{:S(2)}) %collective-permute-start.7) | collective-permute-done | bytes 131104 | tf_op jit(solution)/shard_map/ppermute | solution.py:391
  45.9 4.1 %collective-permute-start.10 = (bf16[4,2,128,256]{3,2,1,0:T(8,128)(2,1)S(1)}, bf16[4,2,128,256]{3,2,1,0:T(8,128)(2,1)S(1)}, u32[]{:S(2)}, u32[]{:S(2)}) collective-permute-start(bf16[4,2,128,256]{3,2,1,0:T(8,128)(2,1)S(1)} %pad_maximum_fusion.1.refs_4_.refs_5_.refs_0_), channel_id=1, source_target_pairs={{0,96},{8,104},{16,112},{24,120},{32,0},{40,8},{48,16},{56,24},{64... | collective-permute-start | bytes 1572872 | tf_op jit(solution)/shard_map/ppermute | solution.py:391
  50.0 1.9 %collective-permute-start.9 = (bf16[4,2,128,256]{3,2,1,0:T(8,128)(2,1)S(1)}, bf16[4,2,128,256]{3,2,1,0:T(8,128)(2,1)S(1)}, u32[]{:S(2)}, u32[]{:S(2)}) collective-permute-start(bf16[4,2,128,256]{3,2,1,0:T(8,128)(2,1)S(1)} %pad_maximum_fusion.1.refs_4_.refs_5_.refs_0_), channel_id=1, source_target_pairs={{0,64},{8,72},{16,80},{24,88},{32,96},{40,104},{48,112},{56,120},{... | collective-permute-start | bytes 1572872 | tf_op jit(solution)/shard_map/ppermute | solution.py:391
  52.0 2.2 %copy-done = bf16[16,2,256,256]{3,2,1,0:T(8,128)(2,1)S(1)} copy-done((bf16[16,2,256,256]{3,2,1,0:T(8,128)(2,1)S(1)}, bf16[16,2,256,256]{3,2,1,0:T(8,128)(2,1)}, u32[]{:S(2)}) %copy-start) | copy-done | bytes 4194328
  54.1 2.3 %decode.1 = bf16[16,2,32,128]{3,2,1,0:T(8,128)(2,1)S(1)} custom-call(s32[16]{0:T(128)S(1)} %copy-done.3, s32[1]{0:T(128)S(6)} %copy.23.live_ref, bf16[16,2,32,128]{3,2,1,0:T(8,128)(2,1)S(1)} %bitcast.46, bf16[16,2,256,256]{3,2,1,0:T(8,128)(2,1)S(1)} %copy-done, bf16[2,64,256]{2,1,0:T(8,128)(2,1)S(1)} %fusion.1.fresh_ref, s32[16]{0:T(128)S(1)} %copy-done.2), custom_call_target="tpu_custom_call" | custom-call | flops 1100000000 | bytes 1048576 | tf_op jit(solution)/shard_map/decode/pallas_call | solution.py:337
  57.2 1.7 %reshape.341 = bf16[16,4,2048]{2,1,0:T(4,128)(2,1)} reshape(bf16[16,4,2,8,128]{4,3,2,1,0:T(8,128)(2,1)} %copy.20) | data formatting | bytes 524288 | tf_op jit(solution)/shard_map/reshape | solution.py:462
  58.9 8.5 %attend_first.2.refs_3_ = f32[2,1024,256]{2,1,0:T(8,128)S(1)} custom-call(s32[16]{0:T(128)S(1)} %reshape.342.visible_ref, bf16[128,2048]{1,0:T(8,128)(2,1)} %q_ref.3, bf16[4,2,128,256]{3,2,1,0:T(8,128)(2,1)S(1)} %pad_maximum_fusion.known_ref.refs_0_, bf16[4,2,128,256]{3,2,1,0:T(8,128)(2,1)S(1)} %pad_maximum_fusion.known_ref.refs_0_, ...), custom_call_target="tpu_custom_call" | custom-call | flops 2750000128 | bytes 1048576 | tf_op jit(solution)/shard_map/attend_first/pallas_call | solution.py:234
  67.4 8.6 %attend_first.3.refs_3_ = f32[2,1024,256]{2,1,0:T(8,128)S(1)} custom-call(s32[16]{0:T(128)S(1)} %reshape.343.visible_ref, bf16[128,2048]{1,0:T(8,128)(2,1)S(1)} %collective-permute-done.14.q_ref, bf16[4,2,128,256]{3,2,1,0:T(8,128)(2,1)S(1)} %pad_maximum_fusion.known_ref.refs_0_, bf16[4,2,128,256]{3,2,1,0:T(8,128)(2,1)S(1)} %pad_maximum_fusion.known_ref.refs_0_, ...), custom_call_target="tpu_custom_call" | custom-call | flops 2750000128 | bytes 1048576 | tf_op jit(solution)/shard_map/attend_first/pallas_call | solution.py:234
  77.7 3.1 %attend_last.5 = bf16[1,128,1152]{2,1,0:T(8,128)(2,1)S(1)} custom-call(s32[16]{0:T(128)S(1)} %reshape.343.visible_ref, bf16[128,2048]{1,0:T(8,128)(2,1)S(1)} %collective-permute-done.14.q_ref, bf16[4,2,128,256]{3,2,1,0:T(8,128)(2,1)S(1)} %pad_maximum_fusion.known_ref.refs_0_, bf16[4,2,128,256]{3,2,1,0:T(8,128)(2,1)S(1)} %collective-permute-done.8.refs_0_.refs_1_, ...), custom_call_target="tpu_custom_call" | custom-call | flops 825000000 | bytes 1048576 | tf_op jit(solution)/shard_map/attend_last/pallas_call | solution.py:234
  80.9 2.7 %collective-permute-start.16 = (bf16[1,128,1152]{2,1,0:T(8,128)(2,1)S(1)}, bf16[1,128,1152]{2,1,0:T(8,128)(2,1)S(1)}, u32[]{:S(2)}, u32[]{:S(2)}) collective-permute-start(bf16[1,128,1152]{2,1,0:T(8,128)(2,1)S(1)} %attend_last.5), channel_id=1, source_target_pairs={{0,4},{4,0},{1,5},{5,1},{2,6},{6,2},{3,7},{7,3},{8,12},{12,8},{9,1... | collective-permute-start | bytes 884744 | tf_op jit(solution)/shard_map/ppermute | solution.py:395
  83.6 3.1 %attend_last.4 = bf16[1,128,1152]{2,1,0:T(8,128)(2,1)S(1)} custom-call(s32[16]{0:T(128)S(1)} %reshape.343.visible_ref, bf16[128,2048]{1,0:T(8,128)(2,1)S(1)} %collective-permute-done.14.q_ref, bf16[4,2,128,256]{3,2,1,0:T(8,128)(2,1)S(1)} %pad_maximum_fusion.known_ref.refs_0_, bf16[4,2,128,256]{3,2,1,0:T(8,128)(2,1)S(1)} %collective-permute-done.8.refs_0_.refs_1_, ...), custom_call_target="tpu_custom_call" | custom-call | flops 825000000 | bytes 1048576 | tf_op jit(solution)/shard_map/attend_last/pallas_call | solution.py:234
  88.0 6.0 %attend_last.3.refs_0_ = f32[2,128,1152]{2,1,0:T(8,128)S(1)} custom-call(s32[16]{0:T(128)S(1)} %reshape.342.visible_ref, bf16[128,2048]{1,0:T(8,128)(2,1)} %q_ref.3, bf16[4,2,128,256]{3,2,1,0:T(8,128)(2,1)S(1)} %pad_maximum_fusion.known_ref.refs_0_, bf16[4,2,128,256]{3,2,1,0:T(8,128)(2,1)S(1)} %collective-permute-done.8.refs_0_.refs_1_, ...), custom_call_target="tpu_custom_call" | custom-call | flops 1650000000 | bytes 1048576 | tf_op jit(solution)/shard_map/attend_last/pallas_call | solution.py:234
  96.1 1.8 %combine.1 = bf16[128,2048]{1,0:T(8,128)(2,1)} custom-call(f32[2,128,1152]{2,1,0:T(8,128)S(1)} %attend_last.3.refs_0_, bf16[1,128,1152]{2,1,0:T(8,128)(2,1)S(1)} %collective-permute-done.15.refs_1_, bf16[1,128,1152]{2,1,0:T(8,128)(2,1)S(1)} %collective-permute-done.16.refs_2_), custom_call_target="tpu_custom_call" | custom-call | flops 1100000000 | bytes 1048576 | tf_op jit(solution)/shard_map/combine/pallas_call | solution.py:278
  (62 shorter events, 13.3 us)
Async XLA Ops:
  0.6 19.7 %collective-permute-start = (bf16[2,128,256]{2,1,0:T(8,128)(2,1)}, bf16[2,128,256]{2,1,0:T(8,128)(2,1)S(1)}, u32[]{:S(2)}, u32[]{:S(2)}) collective-permute-start(bf16[2,128,256]{2,1,0:T(8,128)(2,1)} %param.16), channel_id=1, source_target_pairs={{0,8},{8,16},{16,24},{24,0},{32,40},{40,48},{48,56},{56,32},{64,72... | collective-permute-start | bytes 393224 | tf_op jit(solution)/shard_map/ppermute | solution.py:391
  2.4 18.0 %collective-permute-start.1 = (bf16[2,128,256]{2,1,0:T(8,128)(2,1)}, bf16[2,128,256]{2,1,0:T(8,128)(2,1)S(1)}, u32[]{:S(2)}, u32[]{:S(2)}) collective-permute-start(bf16[2,128,256]{2,1,0:T(8,128)(2,1)} %param.16), channel_id=1, source_target_pairs={{0,16},{8,24},{16,0},{24,8},{32,48},{40,56},{48,32},{56,40},{64,80... | collective-permute-start | bytes 393224 | tf_op jit(solution)/shard_map/ppermute | solution.py:391
  5.3 15.1 %collective-permute-start.2 = (bf16[2,128,256]{2,1,0:T(8,128)(2,1)}, bf16[2,128,256]{2,1,0:T(8,128)(2,1)S(1)}, u32[]{:S(2)}, u32[]{:S(2)}) collective-permute-start(bf16[2,128,256]{2,1,0:T(8,128)(2,1)} %param.16), channel_id=1, source_target_pairs={{0,24},{8,0},{16,8},{24,16},{32,56},{40,32},{48,40},{56,48},{64,88... | collective-permute-start | bytes 393224 | tf_op jit(solution)/shard_map/ppermute | solution.py:391
  11.9 5.9 %collective-permute-start.3 = (f32[4,192,256]{2,1,0:T(8,128)}, f32[4,192,256]{2,1,0:T(8,128)S(1)}, u32[]{:S(2)}, u32[]{:S(2)}) collective-permute-start(f32[4,192,256]{2,1,0:T(8,128)} %project.3), channel_id=1, source_target_pairs={{0,1},{1,0},{2,3},{3,2},{4,5},{5,4},{6,7},{7,6},{8,9},{9,8},{10,11... | collective-permute-start | bytes 2359304 | tf_op jit(solution)/shard_map/ppermute | solution.py:399
  11.9 8.5 %copy-start.5 = (bf16[2,128,256]{2,1,0:T(8,128)(2,1)S(1)}, bf16[2,128,256]{2,1,0:T(8,128)(2,1)}, u32[]{:S(2)}) copy-start(bf16[2,128,256]{2,1,0:T(8,128)(2,1)} %param.16) | copy-start | bytes 393220
  17.3 10.3 %copy-start.1 = (f32[4,192,256]{2,1,0:T(8,128)S(1)}, f32[4,192,256]{2,1,0:T(8,128)}, u32[]{:S(2)}) copy-start(f32[4,192,256]{2,1,0:T(8,128)} %project.2.kept_ref) | copy-start | bytes 2359300
  17.8 11.6 %copy-start.4 = (bf16[16,4,2048]{2,1,0:T(4,128)(2,1)S(1)}, bf16[16,4,2048]{2,1,0:T(4,128)(2,1)}, u32[]{:S(2)}) copy-start(bf16[16,4,2048]{2,1,0:T(4,128)(2,1)} %param.18) | copy-start | bytes 786436
  18.8 8.8 %collective-permute-start.4 = (f32[2,128,256]{2,1,0:T(8,128)S(1)}, f32[2,128,256]{2,1,0:T(8,128)S(1)}, u32[]{:S(2)}, u32[]{:S(2)}) collective-permute-start(f32[2,128,256]{2,1,0:T(8,128)S(1)} %slice_add_fusion), channel_id=1, source_target_pairs={{0,2},{1,3},{2,0},{3,1},{4,6},{5,7},{6,4},{7,5},{8,10},{9,11},{10,... | collective-permute-start | bytes 786440 | tf_op jit(solution)/shard_map/ppermute | solution.py:399
  20.5 29.6 %collective-permute-start.11 = (bf16[4,2,128,256]{3,2,1,0:T(8,128)(2,1)S(1)}, bf16[4,2,128,256]{3,2,1,0:T(8,128)(2,1)}, u32[]{:S(2)}, u32[]{:S(2)}) collective-permute-start(bf16[4,2,128,256]{3,2,1,0:T(8,128)(2,1)S(1)} %pad_maximum_fusion.known_ref.refs_0_), channel_id=1, source_target_pairs={{0,32},{8,40},{16,48},{24,56},{32,64},{40,72},{48,80},{56,88},{64,... | collective-permute-start | bytes 1572872 | tf_op jit(solution)/shard_map/ppermute | solution.py:391
  22.4 27.6 %collective-permute-start.12 = (bf16[4,2,128,256]{3,2,1,0:T(8,128)(2,1)S(1)}, bf16[4,2,128,256]{3,2,1,0:T(8,128)(2,1)}, u32[]{:S(2)}, u32[]{:S(2)}) collective-permute-start(bf16[4,2,128,256]{3,2,1,0:T(8,128)(2,1)S(1)} %pad_maximum_fusion.known_ref.refs_0_), channel_id=1, source_target_pairs={{0,64},{8,72},{16,80},{24,88},{32,96},{40,104},{48,112},{56,120},{... | collective-permute-start | bytes 1572872 | tf_op jit(solution)/shard_map/ppermute | solution.py:391
  27.0 25.0 %copy-start.2 = (s32[16]{0:T(128)S(1)}, s32[16]{0:T(128)}, u32[]{:S(2)}) copy-start(s32[16]{0:T(128)} %after_ref.5) | copy-start | bytes 196
  27.0 25.0 %copy-start.3 = (s32[16]{0:T(128)S(1)}, s32[16]{0:T(128)}, u32[]{:S(2)}) copy-start(s32[16]{0:T(128)} %length_ref.1) | copy-start | bytes 196
  27.0 5.1 %collective-permute-start.18 = (f32[2,64,256]{2,1,0:T(8,128)S(1)}, f32[2,64,256]{2,1,0:T(8,128)S(1)}, u32[]{:S(2)}, u32[]{:S(2)}) collective-permute-start(f32[2,64,256]{2,1,0:T(8,128)S(1)} %slice_add_fusion.1), channel_id=1, source_target_pairs={{0,2},{1,3},{2,0},{3,1},{4,6},{5,7},{6,4},{7,5},{8,10},{9,11},{10,... | collective-permute-start | bytes 393224 | tf_op jit(solution)/shard_map/ppermute | solution.py:399
  27.6 9.3 %collective-permute-start.5 = (bf16[2,128,256]{2,1,0:T(8,128)(2,1)S(1)}, bf16[2,128,256]{2,1,0:T(8,128)(2,1)S(1)}, u32[]{:S(2)}, u32[]{:S(2)}) collective-permute-start(bf16[2,128,256]{2,1,0:T(8,128)(2,1)S(1)} %finish.1), channel_id=1, source_target_pairs={{0,8},{8,16},{16,24},{24,0},{32,40},{40,48},{48,56},{56,32},{64,72... | collective-permute-start | bytes 393224 | tf_op jit(solution)/shard_map/ppermute | solution.py:391
  28.4 11.5 %collective-permute-start.6 = (bf16[2,128,256]{2,1,0:T(8,128)(2,1)S(1)}, bf16[2,128,256]{2,1,0:T(8,128)(2,1)}, u32[]{:S(2)}, u32[]{:S(2)}) collective-permute-start(bf16[2,128,256]{2,1,0:T(8,128)(2,1)S(1)} %finish.1), channel_id=1, source_target_pairs={{0,16},{8,24},{16,0},{24,8},{32,48},{40,56},{48,32},{56,40},{64,80... | collective-permute-start | bytes 393224 | tf_op jit(solution)/shard_map/ppermute | solution.py:391
  32.1 26.8 %collective-permute-start.13 = (bf16[4,2,128,256]{3,2,1,0:T(8,128)(2,1)S(1)}, bf16[4,2,128,256]{3,2,1,0:T(8,128)(2,1)}, u32[]{:S(2)}, u32[]{:S(2)}) collective-permute-start(bf16[4,2,128,256]{3,2,1,0:T(8,128)(2,1)S(1)} %pad_maximum_fusion.known_ref.refs_0_), channel_id=1, source_target_pairs={{0,96},{8,104},{16,112},{24,120},{32,0},{40,8},{48,16},{56,24},{64... | collective-permute-start | bytes 1572872 | tf_op jit(solution)/shard_map/ppermute | solution.py:391
  36.9 30.5 %collective-permute-start.14 = (bf16[128,2048]{1,0:T(8,128)(2,1)}, bf16[128,2048]{1,0:T(8,128)(2,1)S(1)}, u32[]{:S(2)}, u32[]{:S(2)}) collective-permute-start(bf16[128,2048]{1,0:T(8,128)(2,1)} %q_ref.3), channel_id=1, source_target_pairs={{0,4},{4,0},{1,5},{5,1},{2,6},{6,2},{3,7},{7,3},{8,12},{12,8},{9,1... | collective-permute-start | bytes 1572872 | tf_op jit(solution)/shard_map/ppermute | solution.py:395
  39.9 5.0 %collective-permute-start.7 = (bf16[2,128,256]{2,1,0:T(8,128)(2,1)S(1)}, bf16[2,128,256]{2,1,0:T(8,128)(2,1)S(1)}, u32[]{:S(2)}, u32[]{:S(2)}) collective-permute-start(bf16[2,128,256]{2,1,0:T(8,128)(2,1)S(1)} %finish.1), channel_id=1, source_target_pairs={{0,24},{8,0},{16,8},{24,16},{32,56},{40,32},{48,40},{56,48},{64,88... | collective-permute-start | bytes 393224 | tf_op jit(solution)/shard_map/ppermute | solution.py:391
  45.9 30.1 %collective-permute-start.10 = (bf16[4,2,128,256]{3,2,1,0:T(8,128)(2,1)S(1)}, bf16[4,2,128,256]{3,2,1,0:T(8,128)(2,1)S(1)}, u32[]{:S(2)}, u32[]{:S(2)}) collective-permute-start(bf16[4,2,128,256]{3,2,1,0:T(8,128)(2,1)S(1)} %pad_maximum_fusion.1.refs_4_.refs_5_.refs_0_), channel_id=1, source_target_pairs={{0,96},{8,104},{16,112},{24,120},{32,0},{40,8},{48,16},{56,24},{64... | collective-permute-start | bytes 1572872 | tf_op jit(solution)/shard_map/ppermute | solution.py:391
  50.0 26.0 %collective-permute-start.8 = (bf16[4,2,128,256]{3,2,1,0:T(8,128)(2,1)S(1)}, bf16[4,2,128,256]{3,2,1,0:T(8,128)(2,1)S(1)}, u32[]{:S(2)}, u32[]{:S(2)}) collective-permute-start(bf16[4,2,128,256]{3,2,1,0:T(8,128)(2,1)S(1)} %pad_maximum_fusion.1.refs_4_.refs_5_.refs_0_), channel_id=1, source_target_pairs={{0,32},{8,40},{16,48},{24,56},{32,64},{40,72},{48,80},{56,88},{64,... | collective-permute-start | bytes 1572872 | tf_op jit(solution)/shard_map/ppermute | solution.py:391
  50.0 26.0 %collective-permute-start.9 = (bf16[4,2,128,256]{3,2,1,0:T(8,128)(2,1)S(1)}, bf16[4,2,128,256]{3,2,1,0:T(8,128)(2,1)S(1)}, u32[]{:S(2)}, u32[]{:S(2)}) collective-permute-start(bf16[4,2,128,256]{3,2,1,0:T(8,128)(2,1)S(1)} %pad_maximum_fusion.1.refs_4_.refs_5_.refs_0_), channel_id=1, source_target_pairs={{0,64},{8,72},{16,80},{24,88},{32,96},{40,104},{48,112},{56,120},{... | collective-permute-start | bytes 1572872 | tf_op jit(solution)/shard_map/ppermute | solution.py:391
  76.8 17.2 %collective-permute-start.17 = (bf16[8,2,16,256]{3,2,1,0:T(8,128)(2,1)S(1)}, bf16[8,2,16,256]{3,2,1,0:T(8,128)(2,1)S(1)}, u32[]{:S(2)}, u32[]{:S(2)}) collective-permute-start(bf16[8,2,16,256]{3,2,1,0:T(8,128)(2,1)S(1)} %slice.39), channel_id=1, source_target_pairs={{0,4},{4,0},{1,5},{5,1},{2,6},{6,2},{3,7},{7,3},{8,12},{12,8},{9,1... | collective-permute-start | bytes 393224 | tf_op jit(solution)/shard_map/ppermute | solution.py:395
  80.9 13.8 %collective-permute-start.16 = (bf16[1,128,1152]{2,1,0:T(8,128)(2,1)S(1)}, bf16[1,128,1152]{2,1,0:T(8,128)(2,1)S(1)}, u32[]{:S(2)}, u32[]{:S(2)}) collective-permute-start(bf16[1,128,1152]{2,1,0:T(8,128)(2,1)S(1)} %attend_last.5), channel_id=1, source_target_pairs={{0,4},{4,0},{1,5},{5,1},{2,6},{6,2},{3,7},{7,3},{8,12},{12,8},{9,1... | collective-permute-start | bytes 884744 | tf_op jit(solution)/shard_map/ppermute | solution.py:395
  86.7 9.4 %collective-permute-start.15 = (bf16[1,128,1152]{2,1,0:T(8,128)(2,1)S(1)}, bf16[1,128,1152]{2,1,0:T(8,128)(2,1)S(1)}, u32[]{:S(2)}, u32[]{:S(2)}) collective-permute-start(bf16[1,128,1152]{2,1,0:T(8,128)(2,1)S(1)} %attend_last.4), channel_id=1, source_target_pairs={{0,4},{4,0},{1,5},{5,1},{2,6},{6,2},{3,7},{7,3},{8,12},{12,8},{9,1... | collective-permute-start | bytes 884744 | tf_op jit(solution)/shard_map/ppermute | solution.py:395
  (3 other events, 15.7 us)

commit v6 on v5

--- a/solution.py
+++ b/solution.py
@@ -38,80 +38,168 @@
     low = (rest - mid.astype(jnp.float32)).astype(jnp.bfloat16)
     return hi, mid, low
 
-PROJECT_US, ATTEND_US, DECODE_US = 1, 1, 1
-ATTEND_VMEM = 24
-
-
-def project_kernel(
-    tp_ref, row_adapter_ref, span_ref, decode_ref, weight_ref, down_ref, up_ref, adapter_ref, after_ref, out_ref, rank_ref
+PROJECT_US, ATTEND_US, DECODE_US = 1, 3.4, 1
+ATTEND_VMEM, PROJECT_VMEM, DECODE_VMEM = 24, 56, 24
+
+
+CHUNKS = 4
+
+
+def weight_copies(first, tp, weight_ref, buffer_ref, sems):
+    depth = weight_ref.shape[0] // CHUNKS
+    copies = []
+    for i in range(2):
+        column = pl.multiple_of(jnp.bitwise_xor(tp, first + 2 * i) * 2 * WIDTH, 2 * WIDTH)
+        copies.append(
+            [
+                pltpu.make_async_copy(
+                    weight_ref.at[pl.ds(k * depth, depth), pl.ds(column, 2 * WIDTH)],
+                    buffer_ref.at[i, pl.ds(k * depth, depth)],
+                    sems.at[i, k],
+                )
+                for k in range(CHUNKS)
+            ]
+        )
+    return copies
+
+
+def project_columns(first, tp, copies, hidden_ref, rank_ref, up_ref, buffer_ref, out_ref):
+    depth = hidden_ref.shape[1] // CHUNKS
+    for i in range(2):
+        column = pl.multiple_of(jnp.bitwise_xor(tp, first + 2 * i) * 2 * WIDTH, 2 * WIDTH)
+        up = up_ref[:, pl.ds(column, 2 * WIDTH)]
+        out = jnp.dot(rank_ref[...], jnp.concatenate([up, up, up], axis=0), preferred_element_type=jnp.float32)
+        for k in range(CHUNKS):
+            copies[i][k].wait()
+            here = slice(k * depth, (k + 1) * depth)
+            out = out + jnp.dot(hidden_ref[:, here], buffer_ref[i, here, :], preferred_element_type=jnp.float32)
+        out_ref[2 * i] = out[:, :WIDTH]
+        out_ref[2 * i + 1] = out[:, WIDTH:]
+
+
+def project_first_kernel(
+    first,
+    tp_ref,
+    row_adapter_ref,
+    adapter_ref,
+    span_ref,
+    decode_ref,
+    weight_ref,
+    down_ref,
+    up_ref,
+    out_ref,
+    hidden_ref,
+    rank_ref,
+    buffer_ref,
+    decode_buffer,
+    down_buffer,
+    up_buffer,
+    sems,
+    small_sems,
 ):
-    hidden = jnp.concatenate([span_ref[...], decode_ref[...].reshape(DECODE, decode_ref.shape[2])], axis=0)
-
-    @pl.when(pl.program_id(0) == 0)
-    def _():
-        narrow = jnp.dot(hidden, down_ref[...], preferred_element_type=jnp.float32)
-        span_owner = jnp.transpose(jnp.broadcast_to(adapter_ref[...], (TOKENS, TOKENS)))
-        row = lax.broadcasted_iota(jnp.int32, (DECODE, TOKENS), 0) // STEPS
-        decode_owner = jnp.zeros((DECODE, TOKENS), jnp.int32)
-        for r in range(ROWS):
-            decode_owner = jnp.where(row == r, row_adapter_ref[r], decode_owner)
-        owner = jnp.concatenate([span_owner, decode_owner], axis=0)
-        column = lax.broadcasted_iota(jnp.int32, (ALL_ROWS, TOKENS), 1) // ADAPTER_RANK
-        hi, mid, low = split3(jnp.where(column == owner, narrow, 0.0))
-        rank_ref[:, :TOKENS] = hi
-        rank_ref[:, TOKENS : 2 * TOKENS] = mid
-        rank_ref[:, 2 * TOKENS :] = low
-
-    up = up_ref[...]
-    out = jnp.dot(hidden, weight_ref[...], preferred_element_type=jnp.float32) + jnp.dot(
-        rank_ref[...], jnp.concatenate([up, up, up], axis=0), preferred_element_type=jnp.float32
-    )
-    out_ref[0] = out[:, :WIDTH]
-    out_ref[1] = out[:, WIDTH:]
-
-
-def project(first, tp, row_adapter, span, decode, weight, down, up, adapter, after):
-    count = 2
+    tp = tp_ref[0]
+    small = [
+        pltpu.make_async_copy(span_ref, hidden_ref.at[pl.ds(0, TOKENS)], small_sems.at[0]),
+        pltpu.make_async_copy(decode_ref, decode_buffer, small_sems.at[1]),
+        pltpu.make_async_copy(down_ref, down_buffer, small_sems.at[2]),
+        pltpu.make_async_copy(up_ref, up_buffer, small_sems.at[3]),
+    ]
+    for copy in small:
+        copy.start()
+    copies = weight_copies(first, tp, weight_ref, buffer_ref, sems)
+    for i in range(2):
+        for copy in copies[i]:
+            copy.start()
+    span_owner = jnp.transpose(jnp.broadcast_to(adapter_ref[...], (TOKENS, TOKENS)))
+    row = lax.broadcasted_iota(jnp.int32, (DECODE, TOKENS), 0) // STEPS
+    decode_owner = jnp.zeros((DECODE, TOKENS), jnp.int32)
+    for r in range(ROWS):
+        decode_owner = jnp.where(row == r, row_adapter_ref[r], decode_owner)
+    owner = jnp.concatenate([span_owner, decode_owner], axis=0)
+    column = lax.broadcasted_iota(jnp.int32, (ALL_ROWS, TOKENS), 1) // ADAPTER_RANK
+    for copy in small:
+        copy.wait()
+    hidden_ref[TOKENS:, :] = decode_buffer[...].reshape(DECODE, decode_buffer.shape[2])
+    narrow = jnp.dot(hidden_ref[...], down_buffer[...], preferred_element_type=jnp.float32)
+    for part, piece in enumerate(split3(jnp.where(column == owner, narrow, 0.0))):
+        rank_ref[:, part * TOKENS : (part + 1) * TOKENS] = piece
+    project_columns(first, tp, copies, hidden_ref, rank_ref, up_buffer, buffer_ref, out_ref)
+
+
+def project_second_kernel(first, tp_ref, hidden_ref, rank_ref, up_ref, weight_ref, after_ref, out_ref, buffer_ref, sems):
+    tp = tp_ref[0]
+    copies = weight_copies(first, tp, weight_ref, buffer_ref, sems)
+    for i in range(2):
+        for copy in copies[i]:
+            copy.start()
+    project_columns(first, tp, copies, hidden_ref, rank_ref, up_ref, buffer_ref, out_ref)
+
+
+def project_first(first, tp, row_adapter, adapter, span, decode, weight, down, up):
     depth = span.shape[1]
-    whole = lambda i, *_: (0, 0)
+    scalar = pl.BlockSpec(memory_space=pltpu.SMEM)
+    local = pl.BlockSpec(memory_space=pltpu.VMEM)
+    far = pl.BlockSpec(memory_space=pl.ANY)
     return pl.pallas_call(
-        project_kernel,
-        grid_spec=pltpu.PrefetchScalarGridSpec(
-            num_scalar_prefetch=2,
-            grid=(count,),
-            in_specs=[
-                pl.BlockSpec((TOKENS, depth), whole),
-                pl.BlockSpec((ROWS, STEPS, depth), lambda i, *_: (0, 0, 0)),
-                pl.BlockSpec((depth, 2 * WIDTH), lambda i, tp, rows: (0, jnp.bitwise_xor(tp[0], first + 2 * i))),
-                pl.BlockSpec((depth, TOKENS), whole),
-                pl.BlockSpec((TOKENS, 2 * WIDTH), lambda i, tp, rows: (0, jnp.bitwise_xor(tp[0], first + 2 * i))),
-                pl.BlockSpec((1, TOKENS), whole),
-                pl.BlockSpec(memory_space=pl.ANY),
-            ],
-            out_specs=pl.BlockSpec((2, ALL_ROWS, WIDTH), lambda i, *_: (i, 0, 0)),
-            scratch_shapes=[pltpu.VMEM((ALL_ROWS, 3 * TOKENS), jnp.bfloat16)],
-        ),
-        out_shape=jax.ShapeDtypeStruct((2 * count, ALL_ROWS, WIDTH), jnp.float32),
-        compiler_params=pltpu.CompilerParams(vmem_limit_bytes=56 * MIB),
+        functools.partial(project_first_kernel, first),
+        in_specs=[scalar, scalar, local] + [far] * 5,
+        out_specs=[local] * 3,
+        out_shape=[
+            jax.ShapeDtypeStruct((4, ALL_ROWS, WIDTH), jnp.float32),
+            jax.ShapeDtypeStruct((ALL_ROWS, depth), jnp.bfloat16),
+            jax.ShapeDtypeStruct((ALL_ROWS, 3 * TOKENS), jnp.bfloat16),
+        ],
+        scratch_shapes=[
+            pltpu.VMEM((2, depth, 2 * WIDTH), jnp.bfloat16),
+            pltpu.VMEM(decode.shape, jnp.bfloat16),
+            pltpu.VMEM(down.shape, jnp.bfloat16),
+            pltpu.VMEM(up.shape, jnp.bfloat16),
+            pltpu.SemaphoreType.DMA((2, CHUNKS)),
+            pltpu.SemaphoreType.DMA((4,)),
+        ],
+        compiler_params=pltpu.CompilerParams(vmem_limit_bytes=PROJECT_VMEM * MIB),
         cost_estimate=estimate(PROJECT_US),
-        name="project",
-    )(tp, row_adapter, span, decode, weight, down, up, adapter, after)
+        name="project_first",
+    )(tp, row_adapter, adapter, span, decode, weight, down, up)
+
+
+def project_second(first, tp, hidden, rank, up, weight, after):
+    depth = hidden.shape[1]
+    local = pl.BlockSpec(memory_space=pltpu.VMEM)
+    far = pl.BlockSpec(memory_space=pl.ANY)
+    return pl.pallas_call(
+        functools.partial(project_second_kernel, first),
+        in_specs=[pl.BlockSpec(memory_space=pltpu.SMEM), local, local, local, far, far],
+        out_specs=local,
+        out_shape=jax.ShapeDtypeStruct((4, ALL_ROWS, WIDTH), jnp.float32),
+        scratch_shapes=[
+            pltpu.VMEM((2, depth, 2 * WIDTH), jnp.bfloat16),
+            pltpu.SemaphoreType.DMA((2, CHUNKS)),
+        ],
+        compiler_params=pltpu.CompilerParams(vmem_limit_bytes=PROJECT_VMEM * MIB),
+        cost_estimate=estimate(PROJECT_US),
+        name="project_second",
+    )(tp, hidden, rank, up, weight, after)
 
 
 def finish_kernel(kept_ref, core_ref, chip_ref, *refs):
-    out_ref = refs[-1]
-    out_ref[...] = (kept_ref[...] + core_ref[...] + chip_ref[...]).astype(jnp.bfloat16)
+    span_ref, decode_ref = refs[-2:]
+    total = (kept_ref[:2] + core_ref[:2] + chip_ref[...]).astype(jnp.bfloat16)
+    span_ref[...] = total[:, :TOKENS]
+    decode_ref[...] = total[:, TOKENS:]
 
 
 def finish(kept, from_core, from_chip, after):
-    heads, rows, width = from_chip.shape
-    block = pl.BlockSpec((heads, rows, width), lambda i: (0, 0, 0))
+    heads, _, width = from_chip.shape
+    local = pl.BlockSpec(memory_space=pltpu.VMEM)
     return pl.pallas_call(
         finish_kernel,
-        grid=(1,),
-        in_specs=[block] * 3 + [pl.BlockSpec(memory_space=pl.ANY)] * len(after),
-        out_specs=block,
-        out_shape=jax.ShapeDtypeStruct(from_chip.shape, jnp.bfloat16),
+        in_specs=[local] * 3 + [pl.BlockSpec(memory_space=pl.ANY)] * len(after),
+        out_specs=[local] * 2,
+        out_shape=[
+            jax.ShapeDtypeStruct((heads, TOKENS, width), jnp.bfloat16),
+            jax.ShapeDtypeStruct((heads, DECODE, width), jnp.bfloat16),
+        ],
         compiler_params=pltpu.CompilerParams(vmem_limit_bytes=8 * MIB),
         cost_estimate=estimate(0.5),
         name="finish",
@@ -287,7 +375,8 @@
 ROW_BLOCK = 8
 
 
-def decode_kernel(length_ref, live_ref, q_ref, cache_ref, fresh_ref, after_ref, out_ref):
+def decode_kernel(length_ref, live_ref, q_ref, cache_ref, fresh_ref, *refs):
+    out_ref = refs[-1]
     first = pl.program_id(0) * ROW_BLOCK
     query_rows = STEPS * GROUP
     rows = ROW_BLOCK * query_rows
@@ -343,15 +432,15 @@
                 pl.BlockSpec((ROW_BLOCK, heads, query_rows, HEAD_SIZE), lambda i, *_: (i, 0, 0, 0)),
                 pl.BlockSpec((ROW_BLOCK, heads, cache_size, 2 * HEAD_SIZE), lambda i, *_: (i, 0, 0, 0)),
                 pl.BlockSpec((heads, DECODE, 2 * HEAD_SIZE), lambda i, *_: (0, 0, 0)),
-                pl.BlockSpec(memory_space=pl.ANY),
-            ],
+            ]
+            + [pl.BlockSpec(memory_space=pl.ANY)] * len(after),
             out_specs=pl.BlockSpec((ROW_BLOCK, heads, query_rows, HEAD_SIZE), lambda i, *_: (i, 0, 0, 0)),
         ),
         out_shape=jax.ShapeDtypeStruct(queries.shape, jnp.bfloat16),
-        compiler_params=pltpu.CompilerParams(vmem_limit_bytes=24 * MIB),
+        compiler_params=pltpu.CompilerParams(vmem_limit_bytes=DECODE_VMEM * MIB),
         cost_estimate=estimate(DECODE_US),
         name="decode",
-    )(lengths, live, queries, cache, fresh, after)
+    )(lengths, live, queries, cache, fresh, *after)
 
 
 def pages_kernel(where_ref, *refs):
@@ -428,36 +517,29 @@
 
     prior = ring(jnp.stack(ring(earlier_key_values, False)), True)
 
-    def partial_kv(first, after):
-        return project(
-            first,
-            tp.astype(jnp.int32).reshape(1),
-            row_adapter_index,
-            span_hidden_states,
-            decode_hidden_states,
-            key_value_weight,
-            adapter_down_weight,
-            adapter_up_weight,
-            prompt_adapter.reshape(1, TOKENS),
-            after,
-        )
-
-    from_core = swap_tp(partial_kv(1, row_adapter_index), 1)
-    kept = partial_kv(0, row_adapter_index)
-
-    def from_chip(rows):
-        return swap_tp(kept[2:, rows] + from_core[2:, rows], 2)
-
-    span_rows, decode_rows = slice(0, TOKENS), slice(TOKENS, ALL_ROWS)
-    span_kv = finish(kept, from_core, from_chip(span_rows), ())
-    decode_kv = (kept[:2, decode_rows] + from_core[:2, decode_rows] + from_chip(decode_rows)).astype(jnp.bfloat16)
+    my_tp = tp.astype(jnp.int32).reshape(1)
+    for_core, hidden, rank = project_first(
+        1,
+        my_tp,
+        row_adapter_index,
+        prompt_adapter.reshape(1, TOKENS),
+        span_hidden_states,
+        decode_hidden_states,
+        key_value_weight,
+        adapter_down_weight,
+        adapter_up_weight,
+    )
+    from_core = swap_tp(for_core, 1)
+    kept = project_second(0, my_tp, hidden, rank, adapter_up_weight, key_value_weight, prior[0])
+    from_chip = swap_tp(kept[2:] + from_core[2:], 2)
+    span_kv, decode_kv = finish(kept, from_core, from_chip, (prior[1],))
 
     column = jnp.stack(ring(span_kv, False))
     planes = ring(column, True)
 
     queries = decode_token_queries.reshape(ROWS, STEPS, 2, GROUP, HEAD_SIZE)
     queries = jnp.transpose(queries, (0, 2, 1, 3, 4)).reshape(ROWS, 2, STEPS * GROUP, HEAD_SIZE)
-    decoded = decode_attend(cached_row_lengths, group_live_rows, queries, decode_row_cache, decode_kv, row_adapter_index)
+    decoded = decode_attend(cached_row_lengths, group_live_rows, queries, decode_row_cache, decode_kv, (prior[2], prior[3]))
     decoded = jnp.transpose(decoded.reshape(ROWS, 2, STEPS, GROUP, HEAD_SIZE), (0, 2, 1, 3, 4))
     decode_attention = decoded.reshape(ROWS, STEPS, 2 * GROUP * HEAD_SIZE)
 

time: 98.3 us -> 101 us (1.027)
  waiting for transfers between devices: 10.4 us -> 13.2 us
  other arithmetic: 4.23 us -> 3.1 us
    ppermute x3 -> x2, waiting for transfers between devices: 1.87 us -> 7.67 us  [swap_tp(): return lax.ppermute(x, 'tp', [(i, i ^ bit) for i in range(4)])]
    ppermute x12, waiting for transfers between devices: 7.14 us -> 3 us  [shift(): return lax.ppermute(x, 'ctx', perm)]
    ppermute x12, starting transfers between devices: 21.7 us -> 23.3 us  [shift(): return lax.ppermute(x, 'ctx', perm)]
    ppermute x4, waiting for transfers between devices: 1.41 us -> 2.55 us  [swap_pool(): return lax.ppermute(x, 'pool', [(0, 1), (1, 0)])]
    unnamed x16, local copies, waits for them, and re-layouts: 2.22 us -> 3.35 us
    ppermute x3 -> x2, starting transfers between devices: 2.18 us -> 1.56 us  [swap_tp(): return lax.ppermute(x, 'tp', [(i, i ^ bit) for i in range(4)])]
  transfers between devices with their start and end apart: 19 -> 18, of which waited for: 4 -> 4; matrix products, arithmetic and copies ran while one was open for 7% -> 5% of each run, Pallas kernels for 43% -> 42%
where the time goes in v6:
time: 101 us
  Pallas kernels  44.6 us (44%)
  starting transfers between devices  32.5 us (32%)
  waiting for transfers between devices  13.2 us (13%)
  local copies, waits for them, and re-layouts  5.5 us (5%)
  other arithmetic  3.1 us (3%)
  between operations  1.58 us (2%)
    pallas_call x5, Pallas kernels, attend(): pl.pallas_call(functools.partial(attend_kernel, heads, blocks, diagonal,...  28.4 us
    ppermute x12, starting transfers between devices, shift(): return lax.ppermute(x, 'ctx', perm)  23.3 us
    ppermute x2, waiting for transfers between devices, swap_tp(): return lax.ppermute(x, 'tp', [(i, i ^ bit) for i in range(4)])  7.67 us
    ppermute x4, starting transfers between devices, swap_pool(): return lax.ppermute(x, 'pool', [(0, 1), (1, 0)])  7.63 us
    pallas_call x1, Pallas kernels, project_first(): pl.pallas_call(functools.partial(project_first_kernel, first), in_specs=[...  6.57 us
    pallas_call x1, Pallas kernels, project_second(): pl.pallas_call(functools.partial(project_second_kernel, first), in_specs=...  5.05 us
    unnamed x16, local copies, waits for them, and re-layouts  3.35 us
    ppermute x12, waiting for transfers between devices, shift(): return lax.ppermute(x, 'ctx', perm)  3 us
  transfers between devices with their start and end apart: 18, of which 4 were waited for; matrix products, arithmetic and copies ran while one was open for 5% of the time, Pallas kernels for 42%

profile of v6, /device:TPU:0, one launch (start us, length us, event | category | flops | bytes accessed | tf_op | source)
XLA Modules:
  0.0 100.5 jit_solution(4535382389071690560)
XLA Ops:
  0.6 1.7 %collective-permute-start = (bf16[2,128,256]{2,1,0:T(8,128)(2,1)}, bf16[2,128,256]{2,1,0:T(8,128)(2,1)S(1)}, u32[]{:S(2)}, u32[]{:S(2)}) collective-permute-start(bf16[2,128,256]{2,1,0:T(8,128)(2,1)} %param.16), channel_id=1, source_target_pairs={{0,8},{8,16},{16,24},{24,0},{32,40},{40,48},{48,56},{56,32},{64,72... | collective-permute-start | bytes 393224 | tf_op jit(solution)/shard_map/ppermute | solution.py:480
  2.4 2.9 %collective-permute-start.1 = (bf16[2,128,256]{2,1,0:T(8,128)(2,1)}, bf16[2,128,256]{2,1,0:T(8,128)(2,1)S(1)}, u32[]{:S(2)}, u32[]{:S(2)}) collective-permute-start(bf16[2,128,256]{2,1,0:T(8,128)(2,1)} %param.16), channel_id=1, source_target_pairs={{0,16},{8,24},{16,0},{24,8},{32,48},{40,56},{48,32},{56,40},{64,80... | collective-permute-start | bytes 393224 | tf_op jit(solution)/shard_map/ppermute | solution.py:480
  6.6 6.6 %project_first.1 = (f32[4,192,256]{2,1,0:T(8,128)}, bf16[192,2048]{1,0:T(8,128)(2,1)}, bf16[192,384]{1,0:T(8,128)(2,1)}) custom-call(s32[1]{0:T(128)} %bitcast.4.tp_ref, s32[16]{0:T(128)} %row_adapter_ref.1, s32[1,128]{1,0:T(1,128)} %bitcast.56, bf16[128,2048]{1,0:T(8,128)(2,1)} %span_ref.1, bf16[16,4,2048]{2,1,0:T(4,128)(2,1)} %decode_ref.1, ...), custom_call_target="tpu_custom_call" | custom-call | flops 1100000000 | bytes 1048576 | tf_op jit(solution)/shard_map/project_first/pallas_call | solution.py:143
  13.8 2.0 %collective-permute-start.5 = (bf16[4,2,128,256]{3,2,1,0:T(8,128)(2,1)S(1)}, bf16[4,2,128,256]{3,2,1,0:T(8,128)(2,1)S(1)}, u32[]{:S(2)}, u32[]{:S(2)}) collective-permute-start(bf16[4,2,128,256]{3,2,1,0:T(8,128)(2,1)S(1)} %pad_maximum_fusion.after_ref.known_ref.refs_0_), channel_id=1, source_target_pairs={{0,32},{8,40},{16,48},{24,56},{32,64},{40,72},{48,80},{56,88},{64,... | collective-permute-start | bytes 1572872 | tf_op jit(solution)/shard_map/ppermute | solution.py:480
  15.7 3.6 %collective-permute-start.12 = (bf16[4,2,128,256]{3,2,1,0:T(8,128)(2,1)S(1)}, bf16[4,2,128,256]{3,2,1,0:T(8,128)(2,1)S(1)}, u32[]{:S(2)}, u32[]{:S(2)}) collective-permute-start(bf16[4,2,128,256]{3,2,1,0:T(8,128)(2,1)S(1)} %pad_maximum_fusion.after_ref.known_ref.refs_0_), channel_id=1, source_target_pairs={{0,64},{8,72},{16,80},{24,88},{32,96},{40,104},{48,112},{56,120},{... | collective-permute-start | bytes 1572872 | tf_op jit(solution)/shard_map/ppermute | solution.py:480
  20.3 5.1 %project_second.1.kept_ref = f32[4,192,256]{2,1,0:T(8,128)} custom-call(s32[1]{0:T(128)} %bitcast.4.tp_ref, bf16[192,2048]{1,0:T(8,128)(2,1)} %get-tuple-element.8.hidden_ref, bf16[192,384]{1,0:T(8,128)(2,1)} %get-tuple-element.9.rank_ref, bf16[128,2048]{1,0:T(8,128)(2,1)} %up_ref.3, bf16[2048,2048]{1,0:T(8,128)(2,1)} %weight_ref.3, ...), custom_call_target="tpu_custom_call" | custom-call | flops 1100000000 | bytes 1048576 | tf_op jit(solution)/shard_map/project_second/pallas_call | solution.py:170
  25.4 1.8 %slice_add_fusion = f32[2,192,256]{2,1,0:T(8,128)} fusion(f32[4,192,256]{2,1,0:T(8,128)S(1)} %collective-permute-done.3.core_ref, f32[4,192,256]{2,1,0:T(8,128)} %project_second.1.kept_ref), kind=kLoop, calls=%fused_computation.2 | loop fusion | flops 98304 | bytes 1179648 | tf_op jit(solution)/shard_map/add | solution.py:534
  27.2 1.5 %collective-permute-start.4 = (f32[2,192,256]{2,1,0:T(8,128)}, f32[2,192,256]{2,1,0:T(8,128)S(1)}, u32[]{:S(2)}, u32[]{:S(2)}) collective-permute-start(f32[2,192,256]{2,1,0:T(8,128)} %slice_add_fusion), channel_id=1, source_target_pairs={{0,2},{1,3},{2,0},{3,1},{4,6},{5,7},{6,4},{7,5},{8,10},{9,11},{10,... | collective-permute-start | bytes 1179656 | tf_op jit(solution)/shard_map/ppermute | solution.py:488
  28.8 1.6 %collective-permute-done.5.refs_0_.refs_1_ = bf16[4,2,128,256]{3,2,1,0:T(8,128)(2,1)S(1)} collective-permute-done((bf16[4,2,128,256]{3,2,1,0:T(8,128)(2,1)S(1)}, bf16[4,2,128,256]{3,2,1,0:T(8,128)(2,1)S(1)}, u32[]{:S(2)}, u32[]{:S(2)}) %collective-permute-start.5) | collective-permute-done | bytes 524320 | tf_op jit(solution)/shard_map/ppermute | solution.py:480
  30.4 7.7 %collective-permute-done.4.chip_ref = f32[2,192,256]{2,1,0:T(8,128)S(1)} collective-permute-done((f32[2,192,256]{2,1,0:T(8,128)}, f32[2,192,256]{2,1,0:T(8,128)S(1)}, u32[]{:S(2)}, u32[]{:S(2)}) %collective-permute-start.4) | collective-permute-done | bytes 393248 | tf_op jit(solution)/shard_map/ppermute | solution.py:488
  40.8 2.0 %collective-permute-start.8 = (bf16[2,128,256]{2,1,0:T(8,128)(2,1)S(1)}, bf16[2,128,256]{2,1,0:T(8,128)(2,1)S(1)}, u32[]{:S(2)}, u32[]{:S(2)}) collective-permute-start(bf16[2,128,256]{2,1,0:T(8,128)(2,1)S(1)} %get-tuple-element.11), channel_id=1, source_target_pairs={{0,24},{8,0},{16,8},{24,16},{32,56},{40,32},{48,40},{56,48},{64,88... | collective-permute-start | bytes 393224 | tf_op jit(solution)/shard_map/ppermute | solution.py:480
  44.8 3.1 %collective-permute-start.14 = (bf16[128,2048]{1,0:T(8,128)(2,1)}, bf16[128,2048]{1,0:T(8,128)(2,1)}, u32[]{:S(2)}, u32[]{:S(2)}) collective-permute-start(bf16[128,2048]{1,0:T(8,128)(2,1)} %q_ref.3), channel_id=1, source_target_pairs={{0,4},{4,0},{1,5},{5,1},{2,6},{6,2},{3,7},{7,3},{8,12},{12,8},{9,1... | collective-permute-start | bytes 1572872 | tf_op jit(solution)/shard_map/ppermute | solution.py:484
  48.0 2.2 %copy-done.1 = bf16[16,2,256,256]{3,2,1,0:T(8,128)(2,1)S(1)} copy-done((bf16[16,2,256,256]{3,2,1,0:T(8,128)(2,1)S(1)}, bf16[16,2,256,256]{3,2,1,0:T(8,128)(2,1)}, u32[]{:S(2)}) %copy-start.1) | copy-done | bytes 4194328
  50.1 2.0 %decode.1 = bf16[16,2,32,128]{3,2,1,0:T(8,128)(2,1)S(1)} custom-call(s32[16]{0:T(128)S(1)} %copy-done.4, s32[1]{0:T(128)S(6)} %copy.23.live_ref, bf16[16,2,32,128]{3,2,1,0:T(8,128)(2,1)S(1)} %bitcast.46, bf16[16,2,256,256]{3,2,1,0:T(8,128)(2,1)S(1)} %copy-done.1, bf16[2,64,256]{2,1,0:T(8,128)(2,1)S(1)} %get-tuple-element.12.fresh_ref, ...), custom_call_target="tpu_custom_call" | custom-call | flops 1100000000 | bytes 1048576 | tf_op jit(solution)/shard_map/decode/pallas_call | solution.py:426
  53.1 5.2 %collective-permute-start.10 = (bf16[4,2,128,256]{3,2,1,0:T(8,128)(2,1)S(1)}, bf16[4,2,128,256]{3,2,1,0:T(8,128)(2,1)S(1)}, u32[]{:S(2)}, u32[]{:S(2)}) collective-permute-start(bf16[4,2,128,256]{3,2,1,0:T(8,128)(2,1)S(1)} %pad_maximum_fusion.1.refs_4_.refs_5_.refs_0_), channel_id=1, source_target_pairs={{0,64},{8,72},{16,80},{24,88},{32,96},{40,104},{48,112},{56,120},{... | collective-permute-start | bytes 1572872 | tf_op jit(solution)/shard_map/ppermute | solution.py:480
  58.5 1.8 %collective-permute-start.9 = (bf16[4,2,128,256]{3,2,1,0:T(8,128)(2,1)S(1)}, bf16[4,2,128,256]{3,2,1,0:T(8,128)(2,1)S(1)}, u32[]{:S(2)}, u32[]{:S(2)}) collective-permute-start(bf16[4,2,128,256]{3,2,1,0:T(8,128)(2,1)S(1)} %pad_maximum_fusion.1.refs_4_.refs_5_.refs_0_), channel_id=1, source_target_pairs={{0,32},{8,40},{16,48},{24,56},{32,64},{40,72},{48,80},{56,88},{64,... | collective-permute-start | bytes 1572872 | tf_op jit(solution)/shard_map/ppermute | solution.py:480
  60.4 7.6 %attend_first.2.refs_3_ = f32[2,1024,256]{2,1,0:T(8,128)S(1)} custom-call(s32[16]{0:T(128)S(1)} %reshape.340.visible_ref, bf16[128,2048]{1,0:T(8,128)(2,1)S(1)} %copy-done.5, bf16[4,2,128,256]{3,2,1,0:T(8,128)(2,1)S(1)} %copy-done.3, bf16[4,2,128,256]{3,2,1,0:T(8,128)(2,1)S(1)} %copy-done.3, ...), custom_call_target="tpu_custom_call" | custom-call | flops 9349999616 | bytes 1048576 | tf_op jit(solution)/shard_map/attend_first/pallas_call | solution.py:322
  68.0 8.3 %attend_first.3.refs_3_ = f32[2,1024,256]{2,1,0:T(8,128)S(1)} custom-call(s32[16]{0:T(128)S(1)} %reshape.341.visible_ref, bf16[128,2048]{1,0:T(8,128)(2,1)} %collective-permute-done.14.q_ref, bf16[4,2,128,256]{3,2,1,0:T(8,128)(2,1)S(1)} %copy-done.3, bf16[4,2,128,256]{3,2,1,0:T(8,128)(2,1)S(1)} %copy-done.3, ...), custom_call_target="tpu_custom_call" | custom-call | flops 9349999616 | bytes 1048576 | tf_op jit(solution)/shard_map/attend_first/pallas_call | solution.py:322
  78.9 3.6 %attend_last.5 = bf16[1,128,1152]{2,1,0:T(8,128)(2,1)S(1)} custom-call(s32[16]{0:T(128)S(1)} %reshape.341.visible_ref, bf16[128,2048]{1,0:T(8,128)(2,1)} %collective-permute-done.14.q_ref, bf16[4,2,128,256]{3,2,1,0:T(8,128)(2,1)S(1)} %copy-done.3, bf16[4,2,128,256]{3,2,1,0:T(8,128)(2,1)S(1)} %collective-permute-done.9.refs_0_.refs_1_, ...), custom_call_target="tpu_custom_call" | custom-call | flops 2804999936 | bytes 1048576 | tf_op jit(solution)/shard_map/attend_last/pallas_call | solution.py:322
  82.5 3.1 %collective-permute-start.16 = (bf16[1,128,1152]{2,1,0:T(8,128)(2,1)S(1)}, bf16[1,128,1152]{2,1,0:T(8,128)(2,1)S(1)}, u32[]{:S(2)}, u32[]{:S(2)}) collective-permute-start(bf16[1,128,1152]{2,1,0:T(8,128)(2,1)S(1)} %attend_last.5), channel_id=1, source_target_pairs={{0,4},{4,0},{1,5},{5,1},{2,6},{6,2},{3,7},{7,3},{8,12},{12,8},{9,1... | collective-permute-start | bytes 884744 | tf_op jit(solution)/shard_map/ppermute | solution.py:484
  85.6 3.6 %attend_last.4 = bf16[1,128,1152]{2,1,0:T(8,128)(2,1)S(1)} custom-call(s32[16]{0:T(128)S(1)} %reshape.341.visible_ref, bf16[128,2048]{1,0:T(8,128)(2,1)} %collective-permute-done.14.q_ref, bf16[4,2,128,256]{3,2,1,0:T(8,128)(2,1)S(1)} %copy-done.3, bf16[4,2,128,256]{3,2,1,0:T(8,128)(2,1)S(1)} %collective-permute-done.9.refs_0_.refs_1_, ...), custom_call_target="tpu_custom_call" | custom-call | flops 2804999936 | bytes 1048576 | tf_op jit(solution)/shard_map/attend_last/pallas_call | solution.py:322
  90.1 5.3 %attend_last.3.refs_0_ = f32[2,128,1152]{2,1,0:T(8,128)S(1)} custom-call(s32[16]{0:T(128)S(1)} %reshape.340.visible_ref, bf16[128,2048]{1,0:T(8,128)(2,1)S(1)} %copy-done.5, bf16[4,2,128,256]{3,2,1,0:T(8,128)(2,1)S(1)} %copy-done.3, bf16[4,2,128,256]{3,2,1,0:T(8,128)(2,1)S(1)} %collective-permute-done.9.refs_0_.refs_1_, ...), custom_call_target="tpu_custom_call" | custom-call | flops 5609999872 | bytes 1048576 | tf_op jit(solution)/shard_map/attend_last/pallas_call | solution.py:322
  96.1 2.5 %collective-permute-done.15.refs_1_ = bf16[1,128,1152]{2,1,0:T(8,128)(2,1)S(1)} collective-permute-done((bf16[1,128,1152]{2,1,0:T(8,128)(2,1)S(1)}, bf16[1,128,1152]{2,1,0:T(8,128)(2,1)S(1)}, u32[]{:S(2)}, u32[]{:S(2)}) %collective-permute-start.15) | collective-permute-done | bytes 294944 | tf_op jit(solution)/shard_map/ppermute | solution.py:484
  98.7 1.8 %combine.1 = bf16[128,2048]{1,0:T(8,128)(2,1)} custom-call(f32[2,128,1152]{2,1,0:T(8,128)S(1)} %attend_last.3.refs_0_, bf16[1,128,1152]{2,1,0:T(8,128)(2,1)S(1)} %collective-permute-done.15.refs_1_, bf16[1,128,1152]{2,1,0:T(8,128)(2,1)S(1)} %collective-permute-done.16.refs_2_), custom_call_target="tpu_custom_call" | custom-call | flops 1100000000 | bytes 1048576 | tf_op jit(solution)/shard_map/combine/pallas_call | solution.py:366
  (58 shorter events, 12.3 us)
Async XLA Ops:
  0.6 13.0 %collective-permute-start = (bf16[2,128,256]{2,1,0:T(8,128)(2,1)}, bf16[2,128,256]{2,1,0:T(8,128)(2,1)S(1)}, u32[]{:S(2)}, u32[]{:S(2)}) collective-permute-start(bf16[2,128,256]{2,1,0:T(8,128)(2,1)} %param.16), channel_id=1, source_target_pairs={{0,8},{8,16},{16,24},{24,0},{32,40},{40,48},{48,56},{56,32},{64,72... | collective-permute-start | bytes 393224 | tf_op jit(solution)/shard_map/ppermute | solution.py:480
  2.4 11.3 %collective-permute-start.1 = (bf16[2,128,256]{2,1,0:T(8,128)(2,1)}, bf16[2,128,256]{2,1,0:T(8,128)(2,1)S(1)}, u32[]{:S(2)}, u32[]{:S(2)}) collective-permute-start(bf16[2,128,256]{2,1,0:T(8,128)(2,1)} %param.16), channel_id=1, source_target_pairs={{0,16},{8,24},{16,0},{24,8},{32,48},{40,56},{48,32},{56,40},{64,80... | collective-permute-start | bytes 393224 | tf_op jit(solution)/shard_map/ppermute | solution.py:480
  5.3 8.4 %collective-permute-start.2 = (bf16[2,128,256]{2,1,0:T(8,128)(2,1)}, bf16[2,128,256]{2,1,0:T(8,128)(2,1)S(1)}, u32[]{:S(2)}, u32[]{:S(2)}) collective-permute-start(bf16[2,128,256]{2,1,0:T(8,128)(2,1)} %param.16), channel_id=1, source_target_pairs={{0,24},{8,0},{16,8},{24,16},{32,56},{40,32},{48,40},{56,48},{64,88... | collective-permute-start | bytes 393224 | tf_op jit(solution)/shard_map/ppermute | solution.py:480
  6.6 6.8 %copy-start.7 = (s32[256]{0:T(256)S(1)}, s32[256]{0:T(256)}, u32[]{:S(2)}) copy-start(s32[256]{0:T(256)} %param.27) | copy-start | bytes 3076
  6.6 7.0 %copy-start.6 = (bf16[2,128,256]{2,1,0:T(8,128)(2,1)S(1)}, bf16[2,128,256]{2,1,0:T(8,128)(2,1)}, u32[]{:S(2)}) copy-start(bf16[2,128,256]{2,1,0:T(8,128)(2,1)} %param.16) | copy-start | bytes 393220
  13.2 12.2 %collective-permute-start.3 = (f32[4,192,256]{2,1,0:T(8,128)}, f32[4,192,256]{2,1,0:T(8,128)S(1)}, u32[]{:S(2)}, u32[]{:S(2)}) collective-permute-start(f32[4,192,256]{2,1,0:T(8,128)} %get-tuple-element.10), channel_id=1, source_target_pairs={{0,1},{1,0},{2,3},{3,2},{4,5},{5,4},{6,7},{7,6},{8,9},{9,8},{10,11... | collective-permute-start | bytes 2359304 | tf_op jit(solution)/shard_map/ppermute | solution.py:488
  13.7 6.6 %copy-start.2 = (bf16[4,2,128,256]{3,2,1,0:T(8,128)(2,1)}, bf16[4,2,128,256]{3,2,1,0:T(8,128)(2,1)S(1)}, u32[]{:S(2)}) copy-start(bf16[4,2,128,256]{3,2,1,0:T(8,128)(2,1)S(1)} %pad_maximum_fusion.after_ref.known_ref.refs_0_) | copy-start | bytes 1572868
  13.8 16.7 %collective-permute-start.5 = (bf16[4,2,128,256]{3,2,1,0:T(8,128)(2,1)S(1)}, bf16[4,2,128,256]{3,2,1,0:T(8,128)(2,1)S(1)}, u32[]{:S(2)}, u32[]{:S(2)}) collective-permute-start(bf16[4,2,128,256]{3,2,1,0:T(8,128)(2,1)S(1)} %pad_maximum_fusion.after_ref.known_ref.refs_0_), channel_id=1, source_target_pairs={{0,32},{8,40},{16,48},{24,56},{32,64},{40,72},{48,80},{56,88},{64,... | collective-permute-start | bytes 1572872 | tf_op jit(solution)/shard_map/ppermute | solution.py:480
  15.7 29.1 %collective-permute-start.12 = (bf16[4,2,128,256]{3,2,1,0:T(8,128)(2,1)S(1)}, bf16[4,2,128,256]{3,2,1,0:T(8,128)(2,1)S(1)}, u32[]{:S(2)}, u32[]{:S(2)}) collective-permute-start(bf16[4,2,128,256]{3,2,1,0:T(8,128)(2,1)S(1)} %pad_maximum_fusion.after_ref.known_ref.refs_0_), channel_id=1, source_target_pairs={{0,64},{8,72},{16,80},{24,88},{32,96},{40,104},{48,112},{56,120},{... | collective-permute-start | bytes 1572872 | tf_op jit(solution)/shard_map/ppermute | solution.py:480
  19.3 28.6 %collective-permute-start.13 = (bf16[4,2,128,256]{3,2,1,0:T(8,128)(2,1)S(1)}, bf16[4,2,128,256]{3,2,1,0:T(8,128)(2,1)S(1)}, u32[]{:S(2)}, u32[]{:S(2)}) collective-permute-start(bf16[4,2,128,256]{3,2,1,0:T(8,128)(2,1)S(1)} %pad_maximum_fusion.after_ref.known_ref.refs_0_), channel_id=1, source_target_pairs={{0,96},{8,104},{16,112},{24,120},{32,0},{40,8},{48,16},{56,24},{64... | collective-permute-start | bytes 1572872 | tf_op jit(solution)/shard_map/ppermute | solution.py:480
  25.4 22.6 %copy-start.4 = (s32[16]{0:T(128)S(1)}, s32[16]{0:T(128)}, u32[]{:S(2)}) copy-start(s32[16]{0:T(128)} %length_ref.1) | copy-start | bytes 196
  27.2 10.9 %collective-permute-start.4 = (f32[2,192,256]{2,1,0:T(8,128)}, f32[2,192,256]{2,1,0:T(8,128)S(1)}, u32[]{:S(2)}, u32[]{:S(2)}) collective-permute-start(f32[2,192,256]{2,1,0:T(8,128)} %slice_add_fusion), channel_id=1, source_target_pairs={{0,2},{1,3},{2,0},{3,1},{4,6},{5,7},{6,4},{7,5},{8,10},{9,11},{10,... | collective-permute-start | bytes 1179656 | tf_op jit(solution)/shard_map/ppermute | solution.py:488
  39.3 13.7 %collective-permute-start.6 = (bf16[2,128,256]{2,1,0:T(8,128)(2,1)S(1)}, bf16[2,128,256]{2,1,0:T(8,128)(2,1)S(1)}, u32[]{:S(2)}, u32[]{:S(2)}) collective-permute-start(bf16[2,128,256]{2,1,0:T(8,128)(2,1)S(1)} %get-tuple-element.11), channel_id=1, source_target_pairs={{0,8},{8,16},{16,24},{24,0},{32,40},{40,48},{48,56},{56,32},{64,72... | collective-permute-start | bytes 393224 | tf_op jit(solution)/shard_map/ppermute | solution.py:480
  40.1 13.0 %collective-permute-start.7 = (bf16[2,128,256]{2,1,0:T(8,128)(2,1)S(1)}, bf16[2,128,256]{2,1,0:T(8,128)(2,1)S(1)}, u32[]{:S(2)}, u32[]{:S(2)}) collective-permute-start(bf16[2,128,256]{2,1,0:T(8,128)(2,1)S(1)} %get-tuple-element.11), channel_id=1, source_target_pairs={{0,16},{8,24},{16,0},{24,8},{32,48},{40,56},{48,32},{56,40},{64,80... | collective-permute-start | bytes 393224 | tf_op jit(solution)/shard_map/ppermute | solution.py:480
  40.8 12.2 %collective-permute-start.8 = (bf16[2,128,256]{2,1,0:T(8,128)(2,1)S(1)}, bf16[2,128,256]{2,1,0:T(8,128)(2,1)S(1)}, u32[]{:S(2)}, u32[]{:S(2)}) collective-permute-start(bf16[2,128,256]{2,1,0:T(8,128)(2,1)S(1)} %get-tuple-element.11), channel_id=1, source_target_pairs={{0,24},{8,0},{16,8},{24,16},{32,56},{40,32},{48,40},{56,48},{64,88... | collective-permute-start | bytes 393224 | tf_op jit(solution)/shard_map/ppermute | solution.py:480
  44.8 23.1 %collective-permute-start.14 = (bf16[128,2048]{1,0:T(8,128)(2,1)}, bf16[128,2048]{1,0:T(8,128)(2,1)}, u32[]{:S(2)}, u32[]{:S(2)}) collective-permute-start(bf16[128,2048]{1,0:T(8,128)(2,1)} %q_ref.3), channel_id=1, source_target_pairs={{0,4},{4,0},{1,5},{5,1},{2,6},{6,2},{3,7},{7,3},{8,12},{12,8},{9,1... | collective-permute-start | bytes 1572872 | tf_op jit(solution)/shard_map/ppermute | solution.py:484
  52.2 8.2 %copy-start.3 = (bf16[4,2,128,256]{3,2,1,0:T(8,128)(2,1)S(1)}, bf16[4,2,128,256]{3,2,1,0:T(8,128)(2,1)}, u32[]{:S(2)}) copy-start(bf16[4,2,128,256]{3,2,1,0:T(8,128)(2,1)} %copy-done.2) | copy-start | bytes 1572868
  52.2 8.2 %copy-start.5 = (bf16[128,2048]{1,0:T(8,128)(2,1)S(1)}, bf16[128,2048]{1,0:T(8,128)(2,1)}, u32[]{:S(2)}) copy-start(bf16[128,2048]{1,0:T(8,128)(2,1)} %q_ref.3) | copy-start | bytes 1572868
  53.1 23.1 %collective-permute-start.10 = (bf16[4,2,128,256]{3,2,1,0:T(8,128)(2,1)S(1)}, bf16[4,2,128,256]{3,2,1,0:T(8,128)(2,1)S(1)}, u32[]{:S(2)}, u32[]{:S(2)}) collective-permute-start(bf16[4,2,128,256]{3,2,1,0:T(8,128)(2,1)S(1)} %pad_maximum_fusion.1.refs_4_.refs_5_.refs_0_), channel_id=1, source_target_pairs={{0,64},{8,72},{16,80},{24,88},{32,96},{40,104},{48,112},{56,120},{... | collective-permute-start | bytes 1572872 | tf_op jit(solution)/shard_map/ppermute | solution.py:480
  58.3 17.9 %collective-permute-start.11 = (bf16[4,2,128,256]{3,2,1,0:T(8,128)(2,1)S(1)}, bf16[4,2,128,256]{3,2,1,0:T(8,128)(2,1)S(1)}, u32[]{:S(2)}, u32[]{:S(2)}) collective-permute-start(bf16[4,2,128,256]{3,2,1,0:T(8,128)(2,1)S(1)} %pad_maximum_fusion.1.refs_4_.refs_5_.refs_0_), channel_id=1, source_target_pairs={{0,96},{8,104},{16,112},{24,120},{32,0},{40,8},{48,16},{56,24},{64... | collective-permute-start | bytes 1572872 | tf_op jit(solution)/shard_map/ppermute | solution.py:480
  58.5 19.1 %collective-permute-start.9 = (bf16[4,2,128,256]{3,2,1,0:T(8,128)(2,1)S(1)}, bf16[4,2,128,256]{3,2,1,0:T(8,128)(2,1)S(1)}, u32[]{:S(2)}, u32[]{:S(2)}) collective-permute-start(bf16[4,2,128,256]{3,2,1,0:T(8,128)(2,1)S(1)} %pad_maximum_fusion.1.refs_4_.refs_5_.refs_0_), channel_id=1, source_target_pairs={{0,32},{8,40},{16,48},{24,56},{32,64},{40,72},{48,80},{56,88},{64,... | collective-permute-start | bytes 1572872 | tf_op jit(solution)/shard_map/ppermute | solution.py:480
  78.3 17.0 %collective-permute-start.17 = (bf16[8,2,16,256]{3,2,1,0:T(8,128)(2,1)S(1)}, bf16[8,2,16,256]{3,2,1,0:T(8,128)(2,1)S(1)}, u32[]{:S(2)}, u32[]{:S(2)}) collective-permute-start(bf16[8,2,16,256]{3,2,1,0:T(8,128)(2,1)S(1)} %slice.23), channel_id=1, source_target_pairs={{0,4},{4,0},{1,5},{5,1},{2,6},{6,2},{3,7},{7,3},{8,12},{12,8},{9,1... | collective-permute-start | bytes 393224 | tf_op jit(solution)/shard_map/ppermute | solution.py:484
  82.5 13.6 %collective-permute-start.16 = (bf16[1,128,1152]{2,1,0:T(8,128)(2,1)S(1)}, bf16[1,128,1152]{2,1,0:T(8,128)(2,1)S(1)}, u32[]{:S(2)}, u32[]{:S(2)}) collective-permute-start(bf16[1,128,1152]{2,1,0:T(8,128)(2,1)S(1)} %attend_last.5), channel_id=1, source_target_pairs={{0,4},{4,0},{1,5},{5,1},{2,6},{6,2},{3,7},{7,3},{8,12},{12,8},{9,1... | collective-permute-start | bytes 884744 | tf_op jit(solution)/shard_map/ppermute | solution.py:484
  89.2 9.4 %collective-permute-start.15 = (bf16[1,128,1152]{2,1,0:T(8,128)(2,1)S(1)}, bf16[1,128,1152]{2,1,0:T(8,128)(2,1)S(1)}, u32[]{:S(2)}, u32[]{:S(2)}) collective-permute-start(bf16[1,128,1152]{2,1,0:T(8,128)(2,1)S(1)} %attend_last.4), channel_id=1, source_target_pairs={{0,4},{4,0},{1,5},{5,1},{2,6},{6,2},{3,7},{7,3},{8,12},{12,8},{9,1... | collective-permute-start | bytes 884744 | tf_op jit(solution)/shard_map/ppermute | solution.py:484
  (2 other events, 3.3 us)

commit v7 on v6

--- a/solution.py
+++ b/solution.py
@@ -43,42 +43,10 @@
 
 
 CHUNKS = 4
-
-
-def weight_copies(first, tp, weight_ref, buffer_ref, sems):
-    depth = weight_ref.shape[0] // CHUNKS
-    copies = []
-    for i in range(2):
-        column = pl.multiple_of(jnp.bitwise_xor(tp, first + 2 * i) * 2 * WIDTH, 2 * WIDTH)
-        copies.append(
-            [
-                pltpu.make_async_copy(
-                    weight_ref.at[pl.ds(k * depth, depth), pl.ds(column, 2 * WIDTH)],
-                    buffer_ref.at[i, pl.ds(k * depth, depth)],
-                    sems.at[i, k],
-                )
-                for k in range(CHUNKS)
-            ]
-        )
-    return copies
-
-
-def project_columns(first, tp, copies, hidden_ref, rank_ref, up_ref, buffer_ref, out_ref):
-    depth = hidden_ref.shape[1] // CHUNKS
-    for i in range(2):
-        column = pl.multiple_of(jnp.bitwise_xor(tp, first + 2 * i) * 2 * WIDTH, 2 * WIDTH)
-        up = up_ref[:, pl.ds(column, 2 * WIDTH)]
-        out = jnp.dot(rank_ref[...], jnp.concatenate([up, up, up], axis=0), preferred_element_type=jnp.float32)
-        for k in range(CHUNKS):
-            copies[i][k].wait()
-            here = slice(k * depth, (k + 1) * depth)
-            out = out + jnp.dot(hidden_ref[:, here], buffer_ref[i, here, :], preferred_element_type=jnp.float32)
-        out_ref[2 * i] = out[:, :WIDTH]
-        out_ref[2 * i + 1] = out[:, WIDTH:]
-
-
-def project_first_kernel(
-    first,
+OWNERS = (1, 3, 0, 2)
+
+
+def project_kernel(
     tp_ref,
     row_adapter_ref,
     adapter_ref,
@@ -87,7 +55,8 @@
     weight_ref,
     down_ref,
     up_ref,
-    out_ref,
+    core_ref,
+    kept_ref,
     hidden_ref,
     rank_ref,
     buffer_ref,
@@ -98,6 +67,7 @@
     small_sems,
 ):
     tp = tp_ref[0]
+    depth = weight_ref.shape[0] // CHUNKS
     small = [
         pltpu.make_async_copy(span_ref, hidden_ref.at[pl.ds(0, TOKENS)], small_sems.at[0]),
         pltpu.make_async_copy(decode_ref, decode_buffer, small_sems.at[1]),
@@ -106,9 +76,20 @@
     ]
     for copy in small:
         copy.start()
-    copies = weight_copies(first, tp, weight_ref, buffer_ref, sems)
-    for i in range(2):
-        for copy in copies[i]:
+    columns = [pl.multiple_of(jnp.bitwise_xor(tp, bit) * 2 * WIDTH, 2 * WIDTH) for bit in OWNERS]
+    copies = [
+        [
+            pltpu.make_async_copy(
+                weight_ref.at[pl.ds(k * depth, depth), pl.ds(column, 2 * WIDTH)],
+                buffer_ref.at[i, pl.ds(k * depth, depth)],
+                sems.at[i, k],
+            )
+            for k in range(CHUNKS)
+        ]
+        for i, column in enumerate(columns)
+    ]
+    for group in copies:
+        for copy in group:
             copy.start()
     span_owner = jnp.transpose(jnp.broadcast_to(adapter_ref[...], (TOKENS, TOKENS)))
     row = lax.broadcasted_iota(jnp.int32, (DECODE, TOKENS), 0) // STEPS
@@ -123,87 +104,68 @@
     narrow = jnp.dot(hidden_ref[...], down_buffer[...], preferred_element_type=jnp.float32)
     for part, piece in enumerate(split3(jnp.where(column == owner, narrow, 0.0))):
         rank_ref[:, part * TOKENS : (part + 1) * TOKENS] = piece
-    project_columns(first, tp, copies, hidden_ref, rank_ref, up_buffer, buffer_ref, out_ref)
-
-
-def project_second_kernel(first, tp_ref, hidden_ref, rank_ref, up_ref, weight_ref, after_ref, out_ref, buffer_ref, sems):
-    tp = tp_ref[0]
-    copies = weight_copies(first, tp, weight_ref, buffer_ref, sems)
-    for i in range(2):
-        for copy in copies[i]:
-            copy.start()
-    project_columns(first, tp, copies, hidden_ref, rank_ref, up_ref, buffer_ref, out_ref)
-
-
-def project_first(first, tp, row_adapter, adapter, span, decode, weight, down, up):
+    for i, first in enumerate(columns):
+        up = up_buffer[:, pl.ds(first, 2 * WIDTH)]
+        out = jnp.dot(rank_ref[...], jnp.concatenate([up, up, up], axis=0), preferred_element_type=jnp.float32)
+        for k in range(CHUNKS):
+            copies[i][k].wait()
+            here = slice(k * depth, (k + 1) * depth)
+            out = out + jnp.dot(hidden_ref[:, here], buffer_ref[i, here, :], preferred_element_type=jnp.float32)
+        out_ref = core_ref if i < 2 else kept_ref
+        out_ref[2 * (i % 2)] = out[:, :WIDTH]
+        out_ref[2 * (i % 2) + 1] = out[:, WIDTH:]
+
+
+def project(tp, row_adapter, adapter, span, decode, weight, down, up):
     depth = span.shape[1]
     scalar = pl.BlockSpec(memory_space=pltpu.SMEM)
     local = pl.BlockSpec(memory_space=pltpu.VMEM)
     far = pl.BlockSpec(memory_space=pl.ANY)
     return pl.pallas_call(
-        functools.partial(project_first_kernel, first),
+        project_kernel,
         in_specs=[scalar, scalar, local] + [far] * 5,
-        out_specs=[local] * 3,
-        out_shape=[
-            jax.ShapeDtypeStruct((4, ALL_ROWS, WIDTH), jnp.float32),
-            jax.ShapeDtypeStruct((ALL_ROWS, depth), jnp.bfloat16),
-            jax.ShapeDtypeStruct((ALL_ROWS, 3 * TOKENS), jnp.bfloat16),
-        ],
+        out_specs=[local] * 2,
+        out_shape=[jax.ShapeDtypeStruct((4, ALL_ROWS, WIDTH), jnp.float32)] * 2,
         scratch_shapes=[
-            pltpu.VMEM((2, depth, 2 * WIDTH), jnp.bfloat16),
+            pltpu.VMEM((ALL_ROWS, depth), jnp.bfloat16),
+            pltpu.VMEM((ALL_ROWS, 3 * TOKENS), jnp.bfloat16),
+            pltpu.VMEM((4, depth, 2 * WIDTH), jnp.bfloat16),
             pltpu.VMEM(decode.shape, jnp.bfloat16),
             pltpu.VMEM(down.shape, jnp.bfloat16),
             pltpu.VMEM(up.shape, jnp.bfloat16),
-            pltpu.SemaphoreType.DMA((2, CHUNKS)),
+            pltpu.SemaphoreType.DMA((4, CHUNKS)),
             pltpu.SemaphoreType.DMA((4,)),
         ],
         compiler_params=pltpu.CompilerParams(vmem_limit_bytes=PROJECT_VMEM * MIB),
         cost_estimate=estimate(PROJECT_US),
-        name="project_first",
+        name="project",
     )(tp, row_adapter, adapter, span, decode, weight, down, up)
 
 
-def project_second(first, tp, hidden, rank, up, weight, after):
-    depth = hidden.shape[1]
-    local = pl.BlockSpec(memory_space=pltpu.VMEM)
-    far = pl.BlockSpec(memory_space=pl.ANY)
-    return pl.pallas_call(
-        functools.partial(project_second_kernel, first),
-        in_specs=[pl.BlockSpec(memory_space=pltpu.SMEM), local, local, local, far, far],
-        out_specs=local,
-        out_shape=jax.ShapeDtypeStruct((4, ALL_ROWS, WIDTH), jnp.float32),
-        scratch_shapes=[
-            pltpu.VMEM((2, depth, 2 * WIDTH), jnp.bfloat16),
-            pltpu.SemaphoreType.DMA((2, CHUNKS)),
-        ],
-        compiler_params=pltpu.CompilerParams(vmem_limit_bytes=PROJECT_VMEM * MIB),
-        cost_estimate=estimate(PROJECT_US),
-        name="project_second",
-    )(tp, hidden, rank, up, weight, after)
-
-
-def finish_kernel(kept_ref, core_ref, chip_ref, *refs):
-    span_ref, decode_ref = refs[-2:]
-    total = (kept_ref[:2] + core_ref[:2] + chip_ref[...]).astype(jnp.bfloat16)
+def finish_kernel(own_ref, chip_ref, queries_ref, *refs):
+    span_ref, decode_ref, late_ref = refs[-3:]
+    late_ref[...] = queries_ref[...]
+    total = (own_ref[...] + chip_ref[...]).astype(jnp.bfloat16)
     span_ref[...] = total[:, :TOKENS]
     decode_ref[...] = total[:, TOKENS:]
 
 
-def finish(kept, from_core, from_chip, after):
+def finish(own_sum, from_chip, queries, after):
     heads, _, width = from_chip.shape
     local = pl.BlockSpec(memory_space=pltpu.VMEM)
     return pl.pallas_call(
         finish_kernel,
         in_specs=[local] * 3 + [pl.BlockSpec(memory_space=pl.ANY)] * len(after),
-        out_specs=[local] * 2,
+        out_specs=[local] * 3,
         out_shape=[
             jax.ShapeDtypeStruct((heads, TOKENS, width), jnp.bfloat16),
             jax.ShapeDtypeStruct((heads, DECODE, width), jnp.bfloat16),
+            jax.ShapeDtypeStruct(queries.shape, jnp.bfloat16),
         ],
         compiler_params=pltpu.CompilerParams(vmem_limit_bytes=8 * MIB),
         cost_estimate=estimate(0.5),
         name="finish",
-    )(kept, from_core, from_chip, *after)
+    )(own_sum, from_chip, queries, *after)
 
 
 TILE = 2
@@ -214,7 +176,7 @@
 
 
 def attend_kernel(heads, blocks, diagonal, has_state, final, partner, visible_ref, q_ref, known_ref, *refs):
-    pieces, refs = refs[: blocks[-1][-1][0] + 1], refs[blocks[-1][-1][0] + 1 :]
+    pieces, refs = refs[:-4], refs[-4:]
     state_ref, out_ref, key_ref, ext_ref = refs
     wide = lax.broadcasted_iota(jnp.int32, (TILE_ROWS, HEAD_SIZE), 1)
     lane = wide[:TOKENS]
@@ -443,34 +405,32 @@
     )(lengths, live, queries, cache, fresh, *after)
 
 
-def pages_kernel(where_ref, *refs):
-    pieces = refs[:SIDE]
-    out_ref = refs[SIDE]
+def pages_kernel(where_ref, column_ref, up_ref, down_ref, *refs):
+    ring_refs, out_ref = refs[:SIDE], refs[SIDE]
     for n in range(out_ref.shape[0]):
         dz, dy = where_ref[0, n], where_ref[1, n]
         rows = pl.ds(pl.multiple_of(where_ref[2, n] * BLK, BLK), BLK)
         for h in range(2):
-            page = pieces[0][dy, h, rows, :]
-            for k in range(1, SIDE):
-                page = jnp.where(dz == k, pieces[k][dy, h, rows, :], page)
+            page = column_ref[dy, h, rows, :]
+            page = jnp.where(dz == 1, up_ref[dy, h, rows, :], page)
+            page = jnp.where(dz == 3, down_ref[dy, h, rows, :], page)
+            for k in range(SIDE):
+                page = jnp.where((dz == 2) & (dy == k), ring_refs[k][1, h, rows, :], page)
             out_ref[n, h] = page
 
 
-def pick_pages(where, pieces):
+def pick_pages(where, column, up, down, rings):
     count = where.shape[1]
+    local = pl.BlockSpec(memory_space=pltpu.VMEM)
     return pl.pallas_call(
         pages_kernel,
-        grid_spec=pltpu.PrefetchScalarGridSpec(
-            num_scalar_prefetch=1,
-            grid=(1,),
-            in_specs=[pl.BlockSpec((SIDE, 2, TOKENS, WIDTH), lambda i, *_: (0, 0, 0, 0))] * SIDE,
-            out_specs=pl.BlockSpec((count, 2, BLK, WIDTH), lambda i, *_: (0, 0, 0, 0)),
-        ),
+        in_specs=[pl.BlockSpec(memory_space=pltpu.SMEM)] + [local] * (3 + SIDE),
+        out_specs=local,
         out_shape=jax.ShapeDtypeStruct((count, 2, BLK, WIDTH), jnp.bfloat16),
         compiler_params=pltpu.CompilerParams(vmem_limit_bytes=16 * MIB),
-        cost_estimate=estimate(1.5),
+        cost_estimate=estimate(1),
         name="pages",
-    )(where, *pieces)
+    )(where, column, up, down, *rings)
 
 
 def shift(x, dz, dy):
@@ -488,10 +448,12 @@
     return lax.ppermute(x, "tp", [(i, i ^ bit) for i in range(4)])
 
 
-def ring(x, along_z):
-    move = (lambda d: shift(x, d, 0)) if along_z else (lambda d: shift(x, 0, d))
-    far = {1: move(1), 3: move(3), 2: move(2)}
-    return [x, far[1], far[2], far[3]]
+def gather(x):
+    pair = jnp.stack([x, shift(x, 2, 0)])
+    far = {1: shift(pair, 0, 1), 3: shift(pair, 0, 3), 2: shift(pair, 0, 2)}
+    rings = [pair, far[1], far[2], far[3]]
+    column = jnp.stack([r[0] for r in rings])
+    return column, shift(column, 1, 0), shift(column, 3, 0), rings
 
 
 def per_device(
@@ -515,12 +477,10 @@
     pool = lax.axis_index("pool")
     my_z, my_y = ctx // SIDE, ctx % SIDE
 
-    prior = ring(jnp.stack(ring(earlier_key_values, False)), True)
-
-    my_tp = tp.astype(jnp.int32).reshape(1)
-    for_core, hidden, rank = project_first(
-        1,
-        my_tp,
+    prior_column, prior_up, prior_down, prior_rings = gather(earlier_key_values)
+
+    for_core, kept = project(
+        tp.astype(jnp.int32).reshape(1),
         row_adapter_index,
         prompt_adapter.reshape(1, TOKENS),
         span_hidden_states,
@@ -530,16 +490,16 @@
         adapter_up_weight,
     )
     from_core = swap_tp(for_core, 1)
-    kept = project_second(0, my_tp, hidden, rank, adapter_up_weight, key_value_weight, prior[0])
     from_chip = swap_tp(kept[2:] + from_core[2:], 2)
-    span_kv, decode_kv = finish(kept, from_core, from_chip, (prior[1],))
-
-    column = jnp.stack(ring(span_kv, False))
-    planes = ring(column, True)
+    span_kv, decode_kv, late_queries = finish(
+        kept[:2] + from_core[:2], from_chip, span_token_queries, (prior_rings[0],)
+    )
+
+    column, up, down, rings = gather(span_kv)
 
     queries = decode_token_queries.reshape(ROWS, STEPS, 2, GROUP, HEAD_SIZE)
     queries = jnp.transpose(queries, (0, 2, 1, 3, 4)).reshape(ROWS, 2, STEPS * GROUP, HEAD_SIZE)
-    decoded = decode_attend(cached_row_lengths, group_live_rows, queries, decode_row_cache, decode_kv, (prior[2], prior[3]))
+    decoded = decode_attend(cached_row_lengths, group_live_rows, queries, decode_row_cache, decode_kv, ())
     decoded = jnp.transpose(decoded.reshape(ROWS, 2, STEPS, GROUP, HEAD_SIZE), (0, 2, 1, 3, 4))
     decode_attention = decoded.reshape(ROWS, STEPS, 2 * GROUP * HEAD_SIZE)
 
@@ -548,18 +508,28 @@
     place = shard_z[:, None] * SIDE + shard_y[None, :]
     partner_sees = ((place < ctx) | ((place == ctx) & (pool == 0))).astype(jnp.int32).reshape(-1)
     own_sees = (place <= ctx).astype(jnp.int32).reshape(-1)
-    earlier = [(p, k, None) for p in range(SIDE) for k in range(SIDE)]
-    seen_first = earlier + [(SIDE, k, k) for k in range(SIDE)]
-    first_blocks = (tuple(seen_first[:10]), tuple(seen_first[10:]))
-    others = [(p, k, (p + 1) * SIDE + k) for p in range(SIDE - 1) for k in range(SIDE)]
-    last_blocks = (tuple(others),)
+    prior_pieces = [prior_up, prior_down] + prior_rings
+    earlier = [(p, k, None) for p in range(2) for k in range(SIDE)]
+    earlier += [(2 + k, j, None) for j in range(2) for k in range(SIDE)]
+
+    def pairs(first):
+        return [(first + k, j, 2 * j * SIDE + k) for j in range(2) for k in range(SIDE)]
+
+    sides = [(p, k, (1 + 2 * p) * SIDE + k) for p in range(2) for k in range(SIDE)]
     both = (0, 1)
-    first_pieces = prior + [column]
-    partner_queries = swap_pool(span_token_queries)
+    partner_queries = swap_pool(late_queries)
     own_state = attend(
-        own_sees, span_token_queries, prior[0], first_pieces, first_blocks, column, both, diagonal=(SIDE, 0, 0)
-    )
-    partner_state = attend(partner_sees, partner_queries, prior[0], first_pieces, first_blocks, column, both)
+        own_sees, span_token_queries, prior_up, prior_pieces, (tuple(earlier[:8]), tuple(earlier[8:])), column, both
+    )
+    partner_state = attend(
+        partner_sees,
+        partner_queries,
+        prior_up,
+        prior_pieces + rings,
+        (tuple(earlier[:12]), tuple(earlier[12:] + pairs(6))),
+        own_state,
+        both,
+    )
 
     pages = TOKENS // BLK
     shard = ctx * 2 + pool
@@ -578,7 +548,7 @@
             source % pages,
         ]
     ).astype(jnp.int32)
-    found = pick_pages(where, planes)
+    found = pick_pages(where, column, up, down, rings)
     from_partner = swap_pool(found[pages:])
     mine = (source_shard % 2 == pool)[:pages]
     handoff_pages = jnp.where(mine[:, None, None, None], found[:pages], from_partner)
@@ -588,9 +558,9 @@
             attend(
                 partner_sees,
                 partner_queries,
-                prior[0],
-                planes[1:],
-                last_blocks,
+                prior_up,
+                [up, down],
+                (tuple(sides),),
                 None,
                 (h,),
                 state=partner_state,
@@ -601,7 +571,16 @@
         for h in range(2)
     ]
     own = attend(
-        own_sees, span_token_queries, prior[0], planes[1:], last_blocks, None, both, state=own_state, final=True
+        own_sees,
+        span_token_queries,
+        prior_up,
+        [up, down] + rings,
+        (tuple(pairs(2)), tuple(sides)),
+        None,
+        both,
+        diagonal=(2, 0, 0),
+        state=own_state,
+        final=True,
     )
     span_attention = combine(own, other)
     return (span_attention, handoff_pages, decode_attention)

time: 101 us -> 100 us (0.990)
  waiting for transfers between devices: 13.2 us -> 8.72 us
  starting transfers between devices: 32.5 us -> 35.7 us
  Pallas kernels: 44.6 us -> 42.1 us
  local copies, waits for them, and re-layouts: 5.5 us -> 7.71 us
    ppermute x2, waiting for transfers between devices: 7.67 us -> 2.57 us  [swap_tp(): return lax.ppermute(x, 'tp', [(i, i ^ bit) for i in range(4)])]
    ppermute x12, waiting for transfers between devices: 3 us -> 6.14 us  [shift(): return lax.ppermute(x, 'ctx', perm)]
    ppermute x4, waiting for transfers between devices: 2.55 us -> 0.01 us  [swap_pool(): return lax.ppermute(x, 'pool', [(0, 1), (1, 0)])]
    ppermute x4, starting transfers between devices: 7.63 us -> 10 us  [swap_pool(): return lax.ppermute(x, 'pool', [(0, 1), (1, 0)])]
    pallas_call x3 -> x2, Pallas kernels: 12.3 us -> 10.2 us  [the longest x1 9.51 us: project(): pl.pallas_call(project_kernel, in_specs=[scalar, scalar, local] + [far] *...]
    reshape x2, local copies, waits for them, and re-layouts: 1.16 us -> 2.81 us  [per_device(): queries = decode_token_queries.reshape(ROWS, STEPS, 2, GROUP, HEAD_SIZE)]
    unnamed x16 -> x12, local copies, waits for them, and re-layouts: 3.35 us -> 2.21 us
  transfers between devices with their start and end apart: 18 -> 18, of which waited for: 4 -> 3; matrix products, arithmetic and copies ran while one was open for 5% -> 9% of each run, Pallas kernels for 42% -> 30%
where the time goes in v7:
time: 100 us; the launch traced here: 99.2 us
  Pallas kernels  42.1 us (42%)
  starting transfers between devices  35.7 us (36%)
  waiting for transfers between devices  8.72 us (9%)
  local copies, waits for them, and re-layouts  7.71 us (8%)
  other arithmetic  3.35 us (3%)
  between operations  1.6 us (2%)
    pallas_call x5, Pallas kernels, attend(): pl.pallas_call(functools.partial(attend_kernel, heads, blocks, diagonal,...  27.9 us
    ppermute x12, starting transfers between devices, shift(): return lax.ppermute(x, 'ctx', perm)  24.1 us
    ppermute x4, starting transfers between devices, swap_pool(): return lax.ppermute(x, 'pool', [(0, 1), (1, 0)])  10 us
    pallas_call x1, Pallas kernels, project(): pl.pallas_call(project_kernel, in_specs=[scalar, scalar, local] + [far] *...  9.51 us
    ppermute x12, waiting for transfers between devices, shift(): return lax.ppermute(x, 'ctx', perm)  6.14 us
    reshape x2, local copies, waits for them, and re-layouts, per_device(): queries = decode_token_queries.reshape(ROWS, STEPS, 2, GROUP, HEAD_SIZE)  2.81 us
    ppermute x2, waiting for transfers between devices, swap_tp(): return lax.ppermute(x, 'tp', [(i, i ^ bit) for i in range(4)])  2.57 us
    unnamed x12, local copies, waits for them, and re-layouts  2.21 us
  transfers between devices with their start and end apart: 18, of which 3 were waited for; matrix products, arithmetic and copies ran while one was open for 9% of the time, Pallas kernels for 30%

profile of v7, /device:TPU:0, one launch (start us, length us, event | category | flops | bytes accessed | tf_op | source)
XLA Modules:
  0.0 99.2 jit_solution(15682295044489680963)
XLA Ops:
  0.6 9.5 %project.1 = (f32[4,192,256]{2,1,0:T(8,128)}, f32[4,192,256]{2,1,0:T(8,128)}) custom-call(s32[1]{0:T(128)} %bitcast.2.tp_ref, s32[16]{0:T(128)} %row_adapter_ref.1, s32[1,128]{1,0:T(1,128)} %bitcast.50, bf16[128,2048]{1,0:T(8,128)(2,1)} %span_ref.1, bf16[16,4,2048]{2,1,0:T(4,128)(2,1)} %decode_ref.1, bf16[2048,2048]{1,0:T(8,128)(2,1)} %weight_ref.1, ...), custom_call_target="tpu_custom_call" | custom-call | flops 1100000000 | bytes 1048576 | tf_op jit(solution)/shard_map/project/pallas_call | solution.py:124
  10.3 4.0 %collective-permute-start = (bf16[2,128,256]{2,1,0:T(8,128)(2,1)S(1)}, bf16[2,128,256]{2,1,0:T(8,128)(2,1)S(1)}, u32[]{:S(2)}, u32[]{:S(2)}) collective-permute-start(bf16[2,128,256]{2,1,0:T(8,128)(2,1)S(1)} %copy-done.4), channel_id=1, source_target_pairs={{0,64},{8,72},{16,80},{24,88},{32,96},{40,104},{48,112},{56,120},{... | collective-permute-start | bytes 393224 | tf_op jit(solution)/shard_map/ppermute | solution.py:440
  18.4 1.6 %collective-permute-start.1 = (bf16[2,2,128,256]{3,2,1,0:T(8,128)(2,1)S(1)}, bf16[2,2,128,256]{3,2,1,0:T(8,128)(2,1)S(1)}, u32[]{:S(2)}, u32[]{:S(2)}) collective-permute-start(bf16[2,2,128,256]{3,2,1,0:T(8,128)(2,1)S(1)} %pad_maximum_fusion.2.refs_0_.refs_2_), channel_id=1, source_target_pairs={{0,8},{8,16},{16,24},{24,0},{32,40},{40,48},{48,56},{56,32},{64,72... | collective-permute-start | bytes 786440 | tf_op jit(solution)/shard_map/ppermute | solution.py:440
  20.1 2.9 %collective-permute-start.2 = (bf16[2,2,128,256]{3,2,1,0:T(8,128)(2,1)S(1)}, bf16[2,2,128,256]{3,2,1,0:T(8,128)(2,1)S(1)}, u32[]{:S(2)}, u32[]{:S(2)}) collective-permute-start(bf16[2,2,128,256]{3,2,1,0:T(8,128)(2,1)S(1)} %pad_maximum_fusion.2.refs_0_.refs_2_), channel_id=1, source_target_pairs={{0,16},{8,24},{16,0},{24,8},{32,48},{40,56},{48,32},{56,40},{64,80... | collective-permute-start | bytes 786440 | tf_op jit(solution)/shard_map/ppermute | solution.py:440
  24.3 2.6 %collective-permute-done.6.chip_ref = f32[2,192,256]{2,1,0:T(8,128)S(1)} collective-permute-done((f32[2,192,256]{2,1,0:T(8,128)S(1)}, f32[2,192,256]{2,1,0:T(8,128)S(1)}, u32[]{:S(2)}, u32[]{:S(2)}) %collective-permute-start.6) | collective-permute-done | bytes 393248 | tf_op jit(solution)/shard_map/ppermute | solution.py:448
  27.0 2.4 %collective-permute-start.7 = (bf16[2,128,256]{2,1,0:T(8,128)(2,1)S(1)}, bf16[2,128,256]{2,1,0:T(8,128)(2,1)S(1)}, u32[]{:S(2)}, u32[]{:S(2)}) collective-permute-start(bf16[2,128,256]{2,1,0:T(8,128)(2,1)S(1)} %get-tuple-element.10), channel_id=1, source_target_pairs={{0,64},{8,72},{16,80},{24,88},{32,96},{40,104},{48,112},{56,120},{... | collective-permute-start | bytes 393224 | tf_op jit(solution)/shard_map/ppermute | solution.py:440
  29.4 5.2 %collective-permute-done.2.refs_4_ = bf16[2,2,128,256]{3,2,1,0:T(8,128)(2,1)S(1)} collective-permute-done((bf16[2,2,128,256]{3,2,1,0:T(8,128)(2,1)S(1)}, bf16[2,2,128,256]{3,2,1,0:T(8,128)(2,1)S(1)}, u32[]{:S(2)}, u32[]{:S(2)}) %collective-permute-start.2) | collective-permute-done | bytes 262176 | tf_op jit(solution)/shard_map/ppermute | solution.py:440
  36.6 2.1 %collective-permute-start.13 = (bf16[4,2,128,256]{3,2,1,0:T(8,128)(2,1)}, bf16[4,2,128,256]{3,2,1,0:T(8,128)(2,1)}, u32[]{:S(2)}, u32[]{:S(2)}) collective-permute-start(bf16[4,2,128,256]{3,2,1,0:T(8,128)(2,1)} %pad_maximum_fusion), channel_id=1, source_target_pairs={{0,96},{8,104},{16,112},{24,120},{32,0},{40,8},{48,16},{56,24},{64... | collective-permute-start | bytes 1572872 | tf_op jit(solution)/shard_map/ppermute | solution.py:440
  40.1 2.4 %collective-permute-start.9 = (bf16[2,2,128,256]{3,2,1,0:T(8,128)(2,1)S(1)}, bf16[2,2,128,256]{3,2,1,0:T(8,128)(2,1)S(1)}, u32[]{:S(2)}, u32[]{:S(2)}) collective-permute-start(bf16[2,2,128,256]{3,2,1,0:T(8,128)(2,1)S(1)} %pad_maximum_fusion.3.refs_2_.refs_6_.refs_0_), channel_id=1, source_target_pairs={{0,16},{8,24},{16,0},{24,8},{32,48},{40,56},{48,32},{56,40},{64,80... | collective-permute-start | bytes 786440 | tf_op jit(solution)/shard_map/ppermute | solution.py:440
  42.5 1.6 %collective-permute-start.10 = (bf16[2,2,128,256]{3,2,1,0:T(8,128)(2,1)S(1)}, bf16[2,2,128,256]{3,2,1,0:T(8,128)(2,1)S(1)}, u32[]{:S(2)}, u32[]{:S(2)}) collective-permute-start(bf16[2,2,128,256]{3,2,1,0:T(8,128)(2,1)S(1)} %pad_maximum_fusion.3.refs_2_.refs_6_.refs_0_), channel_id=1, source_target_pairs={{0,24},{8,0},{16,8},{24,16},{32,56},{40,32},{48,40},{56,48},{64,88... | collective-permute-start | bytes 786440 | tf_op jit(solution)/shard_map/ppermute | solution.py:440
  44.2 1.8 %reshape.336 = bf16[16,4,2,8,128]{4,3,2,1,0:T(8,128)(2,1)} reshape(bf16[16,4,2048]{2,1,0:T(4,128)(2,1)} %param.18) | data formatting | bytes 524288 | tf_op jit(solution)/shard_map/reshape | solution.py:500
  47.7 2.2 %copy-done = bf16[16,2,256,256]{3,2,1,0:T(8,128)(2,1)S(1)} copy-done((bf16[16,2,256,256]{3,2,1,0:T(8,128)(2,1)S(1)}, bf16[16,2,256,256]{3,2,1,0:T(8,128)(2,1)}, u32[]{:S(2)}) %copy-start) | copy-done | bytes 4194328
  49.9 2.0 %decode.1 = bf16[16,2,32,128]{3,2,1,0:T(8,128)(2,1)S(1)} custom-call(s32[16]{0:T(128)S(1)} %copy-done.1, s32[1]{0:T(128)S(6)} %copy.23.live_ref, bf16[16,2,32,128]{3,2,1,0:T(8,128)(2,1)S(1)} %bitcast.42, bf16[16,2,256,256]{3,2,1,0:T(8,128)(2,1)S(1)} %copy-done, bf16[2,64,256]{2,1,0:T(8,128)(2,1)S(1)} %get-tuple-element.12.fresh_ref), custom_call_target="tpu_custom_call" | custom-call | flops 1100000000 | bytes 1048576 | tf_op jit(solution)/shard_map/decode/pallas_call | solution.py:388
  52.7 1.7 %reshape.339 = bf16[16,4,2048]{2,1,0:T(4,128)(2,1)} reshape(bf16[16,4,2,8,128]{4,3,2,1,0:T(8,128)(2,1)} %copy.20) | data formatting | bytes 524288 | tf_op jit(solution)/shard_map/reshape | solution.py:504
  54.4 3.0 %collective-permute-start.14 = (bf16[128,2048]{1,0:T(8,128)(2,1)}, bf16[128,2048]{1,0:T(8,128)(2,1)S(1)}, u32[]{:S(2)}, u32[]{:S(2)}) collective-permute-start(bf16[128,2048]{1,0:T(8,128)(2,1)} %copy-done.3), channel_id=1, source_target_pairs={{0,4},{4,0},{1,5},{5,1},{2,6},{6,2},{3,7},{7,3},{8,12},{12,8},{9,1... | collective-permute-start | bytes 1572872 | tf_op jit(solution)/shard_map/ppermute | solution.py:444
  57.7 3.2 %collective-permute-start.12 = (bf16[4,2,128,256]{3,2,1,0:T(8,128)(2,1)S(1)}, bf16[4,2,128,256]{3,2,1,0:T(8,128)(2,1)S(1)}, u32[]{:S(2)}, u32[]{:S(2)}) collective-permute-start(bf16[4,2,128,256]{3,2,1,0:T(8,128)(2,1)S(1)} %pad_maximum_fusion.1.refs_6_.column_ref), channel_id=1, source_target_pairs={{0,96},{8,104},{16,112},{24,120},{32,0},{40,8},{48,16},{56,24},{64... | collective-permute-start | bytes 1572872 | tf_op jit(solution)/shard_map/ppermute | solution.py:440
  60.9 6.7 %attend_first.2.refs_6_.refs_10_ = f32[2,1024,256]{2,1,0:T(8,128)S(1)} custom-call(s32[16]{0:T(128)S(1)} %reshape.340.visible_ref, bf16[128,2048]{1,0:T(8,128)(2,1)S(1)} %copy-done.2, bf16[4,2,128,256]{3,2,1,0:T(8,128)(2,1)S(1)} %collective-permute-done.4.known_ref.refs_0_, bf16[4,2,128,256]{3,2,1,0:T(8,128)(2,1)S(1)} %collective-permute-done.4.known_ref.refs_0_, ...), custom_call_target="tpu_custom_call" | custom-call | flops 7480000000 | bytes 1048576 | tf_op jit(solution)/shard_map/attend_first/pallas_call | solution.py:284
  67.6 9.3 %attend_first.3.refs_2_ = f32[2,1024,256]{2,1,0:T(8,128)S(1)} custom-call(s32[16]{0:T(128)S(1)} %reshape.341.visible_ref, bf16[128,2048]{1,0:T(8,128)(2,1)S(1)} %collective-permute-done.14.q_ref, bf16[4,2,128,256]{3,2,1,0:T(8,128)(2,1)S(1)} %collective-permute-done.4.known_ref.refs_0_, bf16[4,2,128,256]{3,2,1,0:T(8,128)(2,1)S(1)} %collective-permute-done.4.known_ref.refs_0_, ...), custom_call_target="tpu_custom_call" | custom-call | flops 11219999744 | bytes 1048576 | tf_op jit(solution)/shard_map/attend_first/pallas_call | solution.py:284
  77.7 3.0 %collective-permute-start.17 = (bf16[8,2,16,256]{3,2,1,0:T(8,128)(2,1)S(1)}, bf16[8,2,16,256]{3,2,1,0:T(8,128)(2,1)S(1)}, u32[]{:S(2)}, u32[]{:S(2)}) collective-permute-start(bf16[8,2,16,256]{3,2,1,0:T(8,128)(2,1)S(1)} %slice.61), channel_id=1, source_target_pairs={{0,4},{4,0},{1,5},{5,1},{2,6},{6,2},{3,7},{7,3},{8,12},{12,8},{9,1... | collective-permute-start | bytes 393224 | tf_op jit(solution)/shard_map/ppermute | solution.py:444
  80.8 2.5 %attend_last.5 = bf16[1,128,1152]{2,1,0:T(8,128)(2,1)S(1)} custom-call(s32[16]{0:T(128)S(1)} %reshape.341.visible_ref, bf16[128,2048]{1,0:T(8,128)(2,1)S(1)} %collective-permute-done.14.q_ref, bf16[4,2,128,256]{3,2,1,0:T(8,128)(2,1)S(1)} %collective-permute-done.4.known_ref.refs_0_, bf16[4,2,128,256]{3,2,1,0:T(8,128)(2,1)S(1)} %collective-permute-done.11.refs_0_.up_ref, ...), custom_call_target="tpu_custom_call" | custom-call | flops 1870000000 | bytes 1048576 | tf_op jit(solution)/shard_map/attend_last/pallas_call | solution.py:284
  83.9 2.5 %attend_last.4 = bf16[1,128,1152]{2,1,0:T(8,128)(2,1)S(1)} custom-call(s32[16]{0:T(128)S(1)} %reshape.341.visible_ref, bf16[128,2048]{1,0:T(8,128)(2,1)S(1)} %collective-permute-done.14.q_ref, bf16[4,2,128,256]{3,2,1,0:T(8,128)(2,1)S(1)} %collective-permute-done.4.known_ref.refs_0_, bf16[4,2,128,256]{3,2,1,0:T(8,128)(2,1)S(1)} %collective-permute-done.11.refs_0_.up_ref, ...), custom_call_target="tpu_custom_call" | custom-call | flops 1870000000 | bytes 1048576 | tf_op jit(solution)/shard_map/attend_last/pallas_call | solution.py:284
  86.3 3.3 %collective-permute-start.15 = (bf16[1,128,1152]{2,1,0:T(8,128)(2,1)S(1)}, bf16[1,128,1152]{2,1,0:T(8,128)(2,1)S(1)}, u32[]{:S(2)}, u32[]{:S(2)}) collective-permute-start(bf16[1,128,1152]{2,1,0:T(8,128)(2,1)S(1)} %attend_last.4), channel_id=1, source_target_pairs={{0,4},{4,0},{1,5},{5,1},{2,6},{6,2},{3,7},{7,3},{8,12},{12,8},{9,1... | collective-permute-start | bytes 884744 | tf_op jit(solution)/shard_map/ppermute | solution.py:444
  89.6 7.0 %attend_last.3.refs_0_ = f32[2,128,1152]{2,1,0:T(8,128)S(1)} custom-call(s32[16]{0:T(128)S(1)} %reshape.340.visible_ref, bf16[128,2048]{1,0:T(8,128)(2,1)S(1)} %copy-done.2, bf16[4,2,128,256]{3,2,1,0:T(8,128)(2,1)S(1)} %collective-permute-done.4.known_ref.refs_0_, bf16[4,2,128,256]{3,2,1,0:T(8,128)(2,1)S(1)} %collective-permute-done.11.refs_0_.up_ref, ...), custom_call_target="tpu_custom_call" | custom-call | flops 7480000000 | bytes 1048576 | tf_op jit(solution)/shard_map/attend_last/pallas_call | solution.py:284
  97.4 1.8 %combine.1 = bf16[128,2048]{1,0:T(8,128)(2,1)} custom-call(f32[2,128,1152]{2,1,0:T(8,128)S(1)} %attend_last.3.refs_0_, bf16[1,128,1152]{2,1,0:T(8,128)(2,1)S(1)} %collective-permute-done.15.refs_1_, bf16[1,128,1152]{2,1,0:T(8,128)(2,1)S(1)} %collective-permute-done.16.refs_2_), custom_call_target="tpu_custom_call" | custom-call | flops 1100000000 | bytes 1048576 | tf_op jit(solution)/shard_map/combine/pallas_call | solution.py:328
  (61 shorter events, 13.2 us)
Async XLA Ops:
  0.6 9.6 %copy-start.4 = (bf16[2,128,256]{2,1,0:T(8,128)(2,1)S(1)}, bf16[2,128,256]{2,1,0:T(8,128)(2,1)}, u32[]{:S(2)}) copy-start(bf16[2,128,256]{2,1,0:T(8,128)(2,1)} %param.16) | copy-start | bytes 393220
  10.2 7.1 %copy-start.5 = (s32[256]{0:T(256)S(1)}, s32[256]{0:T(256)}, u32[]{:S(2)}) copy-start(s32[256]{0:T(256)} %param.27) | copy-start | bytes 3076
  10.2 16.7 %copy-start.2 = (bf16[128,2048]{1,0:T(8,128)(2,1)S(1)}, bf16[128,2048]{1,0:T(8,128)(2,1)}, u32[]{:S(2)}) copy-start(bf16[128,2048]{1,0:T(8,128)(2,1)} %q_ref.3) | copy-start | bytes 1572868
  10.2 4.2 %collective-permute-start.5 = (f32[4,192,256]{2,1,0:T(8,128)}, f32[4,192,256]{2,1,0:T(8,128)S(1)}, u32[]{:S(2)}, u32[]{:S(2)}) collective-permute-start(f32[4,192,256]{2,1,0:T(8,128)} %get-tuple-element.9), channel_id=1, source_target_pairs={{0,1},{1,0},{2,3},{3,2},{4,5},{5,4},{6,7},{7,6},{8,9},{9,8},{10,11... | collective-permute-start | bytes 2359304 | tf_op jit(solution)/shard_map/ppermute | solution.py:448
  10.3 8.1 %collective-permute-start = (bf16[2,128,256]{2,1,0:T(8,128)(2,1)S(1)}, bf16[2,128,256]{2,1,0:T(8,128)(2,1)S(1)}, u32[]{:S(2)}, u32[]{:S(2)}) collective-permute-start(bf16[2,128,256]{2,1,0:T(8,128)(2,1)S(1)} %copy-done.4), channel_id=1, source_target_pairs={{0,64},{8,72},{16,80},{24,88},{32,96},{40,104},{48,112},{56,120},{... | collective-permute-start | bytes 393224 | tf_op jit(solution)/shard_map/ppermute | solution.py:440
  15.6 11.2 %collective-permute-start.6 = (f32[2,192,256]{2,1,0:T(8,128)S(1)}, f32[2,192,256]{2,1,0:T(8,128)S(1)}, u32[]{:S(2)}, u32[]{:S(2)}) collective-permute-start(f32[2,192,256]{2,1,0:T(8,128)S(1)} %get-tuple-element.13), channel_id=1, source_target_pairs={{0,2},{1,3},{2,0},{3,1},{4,6},{5,7},{6,4},{7,5},{8,10},{9,11},{10,... | collective-permute-start | bytes 1179656 | tf_op jit(solution)/shard_map/ppermute | solution.py:448
  18.4 11.0 %collective-permute-start.1 = (bf16[2,2,128,256]{3,2,1,0:T(8,128)(2,1)S(1)}, bf16[2,2,128,256]{3,2,1,0:T(8,128)(2,1)S(1)}, u32[]{:S(2)}, u32[]{:S(2)}) collective-permute-start(bf16[2,2,128,256]{3,2,1,0:T(8,128)(2,1)S(1)} %pad_maximum_fusion.2.refs_0_.refs_2_), channel_id=1, source_target_pairs={{0,8},{8,16},{16,24},{24,0},{32,40},{40,48},{48,56},{56,32},{64,72... | collective-permute-start | bytes 786440 | tf_op jit(solution)/shard_map/ppermute | solution.py:440
  20.1 14.5 %collective-permute-start.2 = (bf16[2,2,128,256]{3,2,1,0:T(8,128)(2,1)S(1)}, bf16[2,2,128,256]{3,2,1,0:T(8,128)(2,1)S(1)}, u32[]{:S(2)}, u32[]{:S(2)}) collective-permute-start(bf16[2,2,128,256]{3,2,1,0:T(8,128)(2,1)S(1)} %pad_maximum_fusion.2.refs_0_.refs_2_), channel_id=1, source_target_pairs={{0,16},{8,24},{16,0},{24,8},{32,48},{40,56},{48,32},{56,40},{64,80... | collective-permute-start | bytes 786440 | tf_op jit(solution)/shard_map/ppermute | solution.py:440
  23.0 11.6 %collective-permute-start.3 = (bf16[2,2,128,256]{3,2,1,0:T(8,128)(2,1)S(1)}, bf16[2,2,128,256]{3,2,1,0:T(8,128)(2,1)S(1)}, u32[]{:S(2)}, u32[]{:S(2)}) collective-permute-start(bf16[2,2,128,256]{3,2,1,0:T(8,128)(2,1)S(1)} %pad_maximum_fusion.2.refs_0_.refs_2_), channel_id=1, source_target_pairs={{0,24},{8,0},{16,8},{24,16},{32,56},{40,32},{48,40},{56,48},{64,88... | collective-permute-start | bytes 786440 | tf_op jit(solution)/shard_map/ppermute | solution.py:440
  27.0 7.7 %copy-start.3 = (bf16[128,2048]{1,0:T(8,128)(2,1)}, bf16[128,2048]{1,0:T(8,128)(2,1)S(1)}, u32[]{:S(2)}) copy-start(bf16[128,2048]{1,0:T(8,128)(2,1)S(1)} %get-tuple-element.11) | copy-start | bytes 1572868
  27.0 20.7 %copy-start.1 = (s32[16]{0:T(128)S(1)}, s32[16]{0:T(128)}, u32[]{:S(2)}) copy-start(s32[16]{0:T(128)} %length_ref.1) | copy-start | bytes 196
  27.0 11.8 %collective-permute-start.7 = (bf16[2,128,256]{2,1,0:T(8,128)(2,1)S(1)}, bf16[2,128,256]{2,1,0:T(8,128)(2,1)S(1)}, u32[]{:S(2)}, u32[]{:S(2)}) collective-permute-start(bf16[2,128,256]{2,1,0:T(8,128)(2,1)S(1)} %get-tuple-element.10), channel_id=1, source_target_pairs={{0,64},{8,72},{16,80},{24,88},{32,96},{40,104},{48,112},{56,120},{... | collective-permute-start | bytes 393224 | tf_op jit(solution)/shard_map/ppermute | solution.py:440
  35.5 25.4 %collective-permute-start.4 = (bf16[4,2,128,256]{3,2,1,0:T(8,128)(2,1)}, bf16[4,2,128,256]{3,2,1,0:T(8,128)(2,1)S(1)}, u32[]{:S(2)}, u32[]{:S(2)}) collective-permute-start(bf16[4,2,128,256]{3,2,1,0:T(8,128)(2,1)} %pad_maximum_fusion), channel_id=1, source_target_pairs={{0,32},{8,40},{16,48},{24,56},{32,64},{40,72},{48,80},{56,88},{64,... | collective-permute-start | bytes 1572872 | tf_op jit(solution)/shard_map/ppermute | solution.py:440
  36.6 24.2 %collective-permute-start.13 = (bf16[4,2,128,256]{3,2,1,0:T(8,128)(2,1)}, bf16[4,2,128,256]{3,2,1,0:T(8,128)(2,1)}, u32[]{:S(2)}, u32[]{:S(2)}) collective-permute-start(bf16[4,2,128,256]{3,2,1,0:T(8,128)(2,1)} %pad_maximum_fusion), channel_id=1, source_target_pairs={{0,96},{8,104},{16,112},{24,120},{32,0},{40,8},{48,16},{56,24},{64... | collective-permute-start | bytes 1572872 | tf_op jit(solution)/shard_map/ppermute | solution.py:440
  38.8 15.6 %collective-permute-start.8 = (bf16[2,2,128,256]{3,2,1,0:T(8,128)(2,1)S(1)}, bf16[2,2,128,256]{3,2,1,0:T(8,128)(2,1)S(1)}, u32[]{:S(2)}, u32[]{:S(2)}) collective-permute-start(bf16[2,2,128,256]{3,2,1,0:T(8,128)(2,1)S(1)} %pad_maximum_fusion.3.refs_2_.refs_6_.refs_0_), channel_id=1, source_target_pairs={{0,8},{8,16},{16,24},{24,0},{32,40},{40,48},{48,56},{56,32},{64,72... | collective-permute-start | bytes 786440 | tf_op jit(solution)/shard_map/ppermute | solution.py:440
  40.1 17.4 %collective-permute-start.9 = (bf16[2,2,128,256]{3,2,1,0:T(8,128)(2,1)S(1)}, bf16[2,2,128,256]{3,2,1,0:T(8,128)(2,1)S(1)}, u32[]{:S(2)}, u32[]{:S(2)}) collective-permute-start(bf16[2,2,128,256]{3,2,1,0:T(8,128)(2,1)S(1)} %pad_maximum_fusion.3.refs_2_.refs_6_.refs_0_), channel_id=1, source_target_pairs={{0,16},{8,24},{16,0},{24,8},{32,48},{40,56},{48,32},{56,40},{64,80... | collective-permute-start | bytes 786440 | tf_op jit(solution)/shard_map/ppermute | solution.py:440
  42.5 15.0 %collective-permute-start.10 = (bf16[2,2,128,256]{3,2,1,0:T(8,128)(2,1)S(1)}, bf16[2,2,128,256]{3,2,1,0:T(8,128)(2,1)S(1)}, u32[]{:S(2)}, u32[]{:S(2)}) collective-permute-start(bf16[2,2,128,256]{3,2,1,0:T(8,128)(2,1)S(1)} %pad_maximum_fusion.3.refs_2_.refs_6_.refs_0_), channel_id=1, source_target_pairs={{0,24},{8,0},{16,8},{24,16},{32,56},{40,32},{48,40},{56,48},{64,88... | collective-permute-start | bytes 786440 | tf_op jit(solution)/shard_map/ppermute | solution.py:440
  47.7 2.2 %copy-start = (bf16[16,2,256,256]{3,2,1,0:T(8,128)(2,1)S(1)}, bf16[16,2,256,256]{3,2,1,0:T(8,128)(2,1)}, u32[]{:S(2)}) copy-start(bf16[16,2,256,256]{3,2,1,0:T(8,128)(2,1)} %cache_ref.1) | copy-start | bytes 12582916
  54.4 13.2 %collective-permute-start.14 = (bf16[128,2048]{1,0:T(8,128)(2,1)}, bf16[128,2048]{1,0:T(8,128)(2,1)S(1)}, u32[]{:S(2)}, u32[]{:S(2)}) collective-permute-start(bf16[128,2048]{1,0:T(8,128)(2,1)} %copy-done.3), channel_id=1, source_target_pairs={{0,4},{4,0},{1,5},{5,1},{2,6},{6,2},{3,7},{7,3},{8,12},{12,8},{9,1... | collective-permute-start | bytes 1572872 | tf_op jit(solution)/shard_map/ppermute | solution.py:444
  57.6 19.4 %collective-permute-start.11 = (bf16[4,2,128,256]{3,2,1,0:T(8,128)(2,1)S(1)}, bf16[4,2,128,256]{3,2,1,0:T(8,128)(2,1)S(1)}, u32[]{:S(2)}, u32[]{:S(2)}) collective-permute-start(bf16[4,2,128,256]{3,2,1,0:T(8,128)(2,1)S(1)} %pad_maximum_fusion.1.refs_6_.column_ref), channel_id=1, source_target_pairs={{0,32},{8,40},{16,48},{24,56},{32,64},{40,72},{48,80},{56,88},{64,... | collective-permute-start | bytes 1572872 | tf_op jit(solution)/shard_map/ppermute | solution.py:440
  57.7 19.3 %collective-permute-start.12 = (bf16[4,2,128,256]{3,2,1,0:T(8,128)(2,1)S(1)}, bf16[4,2,128,256]{3,2,1,0:T(8,128)(2,1)S(1)}, u32[]{:S(2)}, u32[]{:S(2)}) collective-permute-start(bf16[4,2,128,256]{3,2,1,0:T(8,128)(2,1)S(1)} %pad_maximum_fusion.1.refs_6_.column_ref), channel_id=1, source_target_pairs={{0,96},{8,104},{16,112},{24,120},{32,0},{40,8},{48,16},{56,24},{64... | collective-permute-start | bytes 1572872 | tf_op jit(solution)/shard_map/ppermute | solution.py:440
  77.7 18.9 %collective-permute-start.17 = (bf16[8,2,16,256]{3,2,1,0:T(8,128)(2,1)S(1)}, bf16[8,2,16,256]{3,2,1,0:T(8,128)(2,1)S(1)}, u32[]{:S(2)}, u32[]{:S(2)}) collective-permute-start(bf16[8,2,16,256]{3,2,1,0:T(8,128)(2,1)S(1)} %slice.61), channel_id=1, source_target_pairs={{0,4},{4,0},{1,5},{5,1},{2,6},{6,2},{3,7},{7,3},{8,12},{12,8},{9,1... | collective-permute-start | bytes 393224 | tf_op jit(solution)/shard_map/ppermute | solution.py:444
  83.2 14.1 %collective-permute-start.16 = (bf16[1,128,1152]{2,1,0:T(8,128)(2,1)S(1)}, bf16[1,128,1152]{2,1,0:T(8,128)(2,1)S(1)}, u32[]{:S(2)}, u32[]{:S(2)}) collective-permute-start(bf16[1,128,1152]{2,1,0:T(8,128)(2,1)S(1)} %attend_last.5), channel_id=1, source_target_pairs={{0,4},{4,0},{1,5},{5,1},{2,6},{6,2},{3,7},{7,3},{8,12},{12,8},{9,1... | collective-permute-start | bytes 884744 | tf_op jit(solution)/shard_map/ppermute | solution.py:444
  86.3 11.0 %collective-permute-start.15 = (bf16[1,128,1152]{2,1,0:T(8,128)(2,1)S(1)}, bf16[1,128,1152]{2,1,0:T(8,128)(2,1)S(1)}, u32[]{:S(2)}, u32[]{:S(2)}) collective-permute-start(bf16[1,128,1152]{2,1,0:T(8,128)(2,1)S(1)} %attend_last.4), channel_id=1, source_target_pairs={{0,4},{4,0},{1,5},{5,1},{2,6},{6,2},{3,7},{7,3},{8,12},{12,8},{9,1... | collective-permute-start | bytes 884744 | tf_op jit(solution)/shard_map/ppermute | solution.py:444

commit v8 on v7

--- a/solution.py
+++ b/solution.py
@@ -175,9 +175,41 @@
 HEAD_COLUMNS = GROUP * HEAD_SIZE
 
 
-def attend_kernel(heads, blocks, diagonal, has_state, final, partner, visible_ref, q_ref, known_ref, *refs):
-    pieces, refs = refs[:-4], refs[-4:]
-    state_ref, out_ref, key_ref, ext_ref = refs
+def pick_pages(where_ref, column_ref, up_ref, down_ref, ring_refs, own_ref, other_ref, at):
+    count = own_ref.shape[0]
+    for n in range(2 * count):
+        dz, dy = where_ref[0, n], where_ref[1, n]
+        rows = pl.ds(pl.multiple_of(where_ref[2, n] * BLK, BLK), BLK)
+        for h in range(2):
+            page = column_ref[dy, h, rows, :]
+            page = jnp.where(dz == 1, up_ref[dy, h, rows, :], page)
+            page = jnp.where(dz == 3, down_ref[dy, h, rows, :], page)
+            for k in range(SIDE):
+                page = jnp.where((dz == 2) & (dy == k), ring_refs[k][1, h, rows, :], page)
+            if n < count:
+                own_ref[n, h] = page
+            else:
+                here = slice((n - count) * BLK, (n - count + 1) * BLK)
+                other_ref[0, here, at + h * WIDTH : at + (h + 1) * WIDTH] = page
+
+
+def attend_kernel(
+    heads, count, blocks, diagonal, has_state, final, partner, has_pages, visible_ref, q_ref, known_ref, *refs
+):
+    pieces, state_ref, refs = refs[:count], refs[count], refs[count + 1 :]
+    out_ref = refs[-4] if has_pages else refs[-3]
+    key_ref, ext_ref = refs[-2:]
+    if has_pages:
+        pick_pages(
+            refs[0],
+            refs[1],
+            pieces[0],
+            pieces[1],
+            refs[2 : 2 + SIDE],
+            refs[-3],
+            out_ref,
+            HEAD_COLUMNS + HEAD_SIZE,
+        )
     wide = lax.broadcasted_iota(jnp.int32, (TILE_ROWS, HEAD_SIZE), 1)
     lane = wide[:TOKENS]
     one = jnp.ones((TOKENS, HEAD_SIZE), jnp.bfloat16)
@@ -270,40 +302,80 @@
                 for part, piece in enumerate(parts):
                     stats = jnp.where(lane == part * GROUP + g, piece, stats)
         if final:
-            out_ref[slot, :, HEAD_COLUMNS:] = stats
-
-
-def attend(visible, queries, known, pieces, blocks, after, heads, diagonal=None, state=None, final=False, partner=False):
+            out_ref[slot, :, HEAD_COLUMNS : HEAD_COLUMNS + HEAD_SIZE] = stats
+
+
+def attend(
+    visible,
+    queries,
+    known,
+    pieces,
+    blocks,
+    after,
+    heads,
+    diagonal=None,
+    state=None,
+    final=False,
+    partner=False,
+    page_source=None,
+    before=(),
+):
     shards = sum(len(block) for block in blocks)
     count = len(heads)
     if final:
-        out_shape = (count, TOKENS, HEAD_COLUMNS + HEAD_SIZE)
+        out_shape = (count, TOKENS, HEAD_COLUMNS + HEAD_SIZE + (0 if page_source is None else 2 * WIDTH))
     else:
         out_shape = (count, HEAD_ROWS, WIDTH)
     local = pl.BlockSpec(memory_space=pltpu.VMEM)
+    scalar = pl.BlockSpec(memory_space=pltpu.SMEM)
+    out_shape = jax.ShapeDtypeStruct(out_shape, jnp.bfloat16 if partner and final else jnp.float32)
+    out_specs = local
+    more, more_specs = [], []
+    if page_source is not None:
+        own_pages = jax.ShapeDtypeStruct((TOKENS // BLK, 2, BLK, WIDTH), jnp.bfloat16)
+        out_shape, out_specs = [out_shape, own_pages], [local, local]
+        more, more_specs = list(page_source), [scalar] + [local] * (len(page_source) - 1)
+    more += before
+    more_specs += [pl.BlockSpec(memory_space=pl.ANY)] * len(before)
     return pl.pallas_call(
-        functools.partial(attend_kernel, heads, blocks, diagonal, state is not None, final, partner),
-        in_specs=[pl.BlockSpec(memory_space=pltpu.SMEM)]
+        functools.partial(
+            attend_kernel,
+            heads,
+            len(pieces),
+            blocks,
+            diagonal,
+            state is not None,
+            final,
+            partner,
+            page_source is not None,
+        ),
+        in_specs=[scalar]
         + [local] * (2 + len(pieces))
-        + [pl.BlockSpec(memory_space=pl.ANY) if state is None else local],
-        out_specs=local,
+        + [pl.BlockSpec(memory_space=pl.ANY) if state is None else local]
+        + more_specs,
+        out_specs=out_specs,
         scratch_shapes=[
             pltpu.VMEM((count, shards * TOKENS, HEAD_SIZE), jnp.bfloat16),
             pltpu.VMEM((count, shards * TOKENS, WIDTH), jnp.bfloat16),
         ],
-        out_shape=jax.ShapeDtypeStruct(out_shape, jnp.bfloat16 if partner and final else jnp.float32),
+        out_shape=out_shape,
         compiler_params=pltpu.CompilerParams(vmem_limit_bytes=ATTEND_VMEM * MIB),
         cost_estimate=estimate(ATTEND_US * count * shards / 16),
         name="attend_last" if final else "attend_first",
-    )(visible, queries, known, *pieces, after if state is None else state)
-
-
-def combine_kernel(*refs):
-    own_ref, out_ref = refs[0], refs[3]
+    )(visible, queries, known, *pieces, after if state is None else state, *more)
+
+
+def combine_kernel(where_ref, own_ref, first_ref, second_ref, pages_ref, out_ref, handoff_ref):
+    for n in range(handoff_ref.shape[0]):
+        mine = where_ref[3, n] != 0
+        for h in range(2):
+            at = HEAD_COLUMNS + HEAD_SIZE + h * WIDTH
+            theirs = first_ref[0, n * BLK : (n + 1) * BLK, at : at + WIDTH]
+            handoff_ref[n, h] = jnp.where(mine, pages_ref[n, h], theirs)
     for h in range(2):
-        other_ref = refs[1 + h]
+        other_ref = (first_ref, second_ref)[h]
         own_level = own_ref[h, :, HEAD_COLUMNS:]
-        other_parts = other_ref[0, :, HEAD_COLUMNS:].astype(jnp.float32)
+        other_parts = other_ref[0, :, HEAD_COLUMNS : HEAD_COLUMNS + HEAD_SIZE].astype(jnp.float32)
         for g in range(GROUP):
             mine = own_level[:, g : g + 1]
             theirs = (
@@ -324,21 +396,26 @@
             )
 
 
-def combine(own, other):
+def combine(where, own, other, own_pages):
+    local = pl.BlockSpec(memory_space=pltpu.VMEM)
     return pl.pallas_call(
         combine_kernel,
-        out_shape=jax.ShapeDtypeStruct((TOKENS, 2 * HEAD_COLUMNS), jnp.bfloat16),
+        in_specs=[pl.BlockSpec(memory_space=pltpu.SMEM)] + [local] * 4,
+        out_specs=[local] * 2,
+        out_shape=[
+            jax.ShapeDtypeStruct((TOKENS, 2 * HEAD_COLUMNS), jnp.bfloat16),
+            jax.ShapeDtypeStruct(own_pages.shape, jnp.bfloat16),
+        ],
         compiler_params=pltpu.CompilerParams(vmem_limit_bytes=16 * MIB),
         cost_estimate=estimate(1),
         name="combine",
-    )(own, *other)
+    )(where, own, *other, own_pages)
 
 
 ROW_BLOCK = 8
 
 
-def decode_kernel(length_ref, live_ref, q_ref, cache_ref, fresh_ref, *refs):
-    out_ref = refs[-1]
+def decode_kernel(length_ref, live_ref, q_ref, cache_ref, fresh_ref, out_ref):
     first = pl.program_id(0) * ROW_BLOCK
     query_rows = STEPS * GROUP
     rows = ROW_BLOCK * query_rows
@@ -347,22 +424,32 @@
     fresh_row = lax.broadcasted_iota(jnp.int32, (rows, DECODE), 1) // STEPS
     fresh_step = lax.broadcasted_iota(jnp.int32, (rows, DECODE), 1) % STEPS
     row = lax.broadcasted_iota(jnp.int32, (rows, DECODE), 0) // query_rows
-    step = lax.broadcasted_iota(jnp.int32, (rows, DECODE), 0) % query_rows // GROUP
+    step = lax.broadcasted_iota(jnp.int32, (rows, DECODE), 0) % STEPS
     fresh_seen = (fresh_row == row + first) & (fresh_step <= step)
+    queries = q_ref[...].reshape(ROW_BLOCK * STEPS, q_ref.shape[2]).astype(jnp.float32)
     cached, fresh = [], []
     for h in range(2):
+        of_head = []
+        for n in range(ROW_BLOCK):
+            of_row = jnp.concatenate(
+                [
+                    queries[n * STEPS : (n + 1) * STEPS, g * HEAD_SIZE : (g + 1) * HEAD_SIZE]
+                    for g in range(h * GROUP, (h + 1) * GROUP)
+                ],
+                axis=0,
+            ).astype(jnp.bfloat16)
+            of_head.append(of_row)
+            scores = lax.dot_general(
+                of_row, cache_ref[n, h, :, :HEAD_SIZE], contract, preferred_element_type=jnp.float32
+            )
+            cached.append(jnp.where(slot < length_ref[first + n], scores, neg_large))
         scores = lax.dot_general(
-            q_ref[:, h].reshape(rows, HEAD_SIZE),
+            jnp.concatenate(of_head, axis=0),
             fresh_ref[h, :, :HEAD_SIZE],
             contract,
             preferred_element_type=jnp.float32,
         )
         fresh.append(jnp.where(fresh_seen, scores, neg_large))
-        for n in range(ROW_BLOCK):
-            scores = lax.dot_general(
-                q_ref[n, h], cache_ref[n, h, :, :HEAD_SIZE], contract, preferred_element_type=jnp.float32
-            )
-            cached.append(jnp.where(slot < length_ref[first + n], scores, neg_large))
     cached = jnp.concatenate(cached, axis=0)
     fresh = jnp.concatenate(fresh, axis=0)
     top = jnp.maximum(jnp.max(cached, axis=1, keepdims=True), jnp.max(fresh, axis=1, keepdims=True))
@@ -379,58 +466,51 @@
             here = slice(h * rows + n * query_rows, h * rows + (n + 1) * query_rows)
             out = jnp.dot(cached[here], cache_ref[n, h, :, HEAD_SIZE:], preferred_element_type=jnp.float32)
             out = (out + of_fresh[n * query_rows : (n + 1) * query_rows]) / total[here]
-            out_ref[n, h] = jnp.where(first + n < live_ref[0], out, 0.0).astype(jnp.bfloat16)
-
-
-def decode_attend(lengths, live, queries, cache, fresh, after):
-    rows, heads, query_rows, _ = queries.shape
-    cache_size = cache.shape[2]
+            out = jnp.where(first + n < live_ref[0], out, 0.0)
+            for g in range(GROUP):
+                columns = slice((h * GROUP + g) * HEAD_SIZE, (h * GROUP + g + 1) * HEAD_SIZE)
+                out_ref[n, :, columns] = out[g * STEPS : (g + 1) * STEPS].astype(jnp.bfloat16)
+
+
+def decode_attend(lengths, live, queries, cache, fresh):
+    rows, heads, cache_size, _ = cache.shape
+    block = pl.BlockSpec((ROW_BLOCK,) + queries.shape[1:], lambda i, *_: (i, 0, 0))
     return pl.pallas_call(
         decode_kernel,
         grid_spec=pltpu.PrefetchScalarGridSpec(
             num_scalar_prefetch=2,
             grid=(rows // ROW_BLOCK,),
             in_specs=[
-                pl.BlockSpec((ROW_BLOCK, heads, query_rows, HEAD_SIZE), lambda i, *_: (i, 0, 0, 0)),
-                pl.BlockSpec((ROW_BLOCK, heads, cache_size, 2 * HEAD_SIZE), lambda i, *_: (i, 0, 0, 0)),
-                pl.BlockSpec((heads, DECODE, 2 * HEAD_SIZE), lambda i, *_: (0, 0, 0)),
-            ]
-            + [pl.BlockSpec(memory_space=pl.ANY)] * len(after),
-            out_specs=pl.BlockSpec((ROW_BLOCK, heads, query_rows, HEAD_SIZE), lambda i, *_: (i, 0, 0, 0)),
+                block,
+                pl.BlockSpec((ROW_BLOCK, heads, cache_size, WIDTH), lambda i, *_: (i, 0, 0, 0)),
+                pl.BlockSpec((heads, DECODE, WIDTH), lambda i, *_: (0, 0, 0)),
+            ],
+            out_specs=block,
         ),
         out_shape=jax.ShapeDtypeStruct(queries.shape, jnp.bfloat16),
         compiler_params=pltpu.CompilerParams(vmem_limit_bytes=DECODE_VMEM * MIB),
         cost_estimate=estimate(DECODE_US),
         name="decode",
-    )(lengths, live, queries, cache, fresh, *after)
-
-
-def pages_kernel(where_ref, column_ref, up_ref, down_ref, *refs):
-    ring_refs, out_ref = refs[:SIDE], refs[SIDE]
-    for n in range(out_ref.shape[0]):
-        dz, dy = where_ref[0, n], where_ref[1, n]
-        rows = pl.ds(pl.multiple_of(where_ref[2, n] * BLK, BLK), BLK)
-        for h in range(2):
-            page = column_ref[dy, h, rows, :]
-            page = jnp.where(dz == 1, up_ref[dy, h, rows, :], page)
-            page = jnp.where(dz == 3, down_ref[dy, h, rows, :], page)
-            for k in range(SIDE):
-                page = jnp.where((dz == 2) & (dy == k), ring_refs[k][1, h, rows, :], page)
-            out_ref[n, h] = page
-
-
-def pick_pages(where, column, up, down, rings):
-    count = where.shape[1]
+    )(lengths, live, queries, cache, fresh)
+
+
+def stack_kernel(*refs):
+    out_ref = refs[-1]
+    for y in range(SIDE):
+        out_ref[y] = refs[y][0]
+
+
+def stack_column(rings, after):
     local = pl.BlockSpec(memory_space=pltpu.VMEM)
     return pl.pallas_call(
-        pages_kernel,
-        in_specs=[pl.BlockSpec(memory_space=pltpu.SMEM)] + [local] * (3 + SIDE),
+        stack_kernel,
+        in_specs=[local] * SIDE + [pl.BlockSpec(memory_space=pl.ANY)] * len(after),
         out_specs=local,
-        out_shape=jax.ShapeDtypeStruct((count, 2, BLK, WIDTH), jnp.bfloat16),
-        compiler_params=pltpu.CompilerParams(vmem_limit_bytes=16 * MIB),
-        cost_estimate=estimate(1),
-        name="pages",
-    )(where, column, up, down, *rings)
+        out_shape=jax.ShapeDtypeStruct((SIDE,) + rings[0].shape[1:], jnp.bfloat16),
+        compiler_params=pltpu.CompilerParams(vmem_limit_bytes=8 * MIB),
+        cost_estimate=estimate(0.5),
+        name="stack",
+    )(*rings, *after)
 
 
 def shift(x, dz, dy):
@@ -448,12 +528,14 @@
     return lax.ppermute(x, "tp", [(i, i ^ bit) for i in range(4)])
 
 
-def gather(x):
+def ring(x):
     pair = jnp.stack([x, shift(x, 2, 0)])
     far = {1: shift(pair, 0, 1), 3: shift(pair, 0, 3), 2: shift(pair, 0, 2)}
-    rings = [pair, far[1], far[2], far[3]]
-    column = jnp.stack([r[0] for r in rings])
-    return column, shift(column, 1, 0), shift(column, 3, 0), rings
+    return [pair, far[1], far[2], far[3]]
+
+
+def sides(column):
+    return shift(column, 1, 0), shift(column, 3, 0)
 
 
 def per_device(
@@ -477,7 +559,7 @@
     pool = lax.axis_index("pool")
     my_z, my_y = ctx // SIDE, ctx % SIDE
 
-    prior_column, prior_up, prior_down, prior_rings = gather(earlier_key_values)
+    prior_rings = ring(earlier_key_values)
 
     for_core, kept = project(
         tp.astype(jnp.int32).reshape(1),
@@ -495,39 +577,48 @@
         kept[:2] + from_core[:2], from_chip, span_token_queries, (prior_rings[0],)
     )
 
-    column, up, down, rings = gather(span_kv)
-
-    queries = decode_token_queries.reshape(ROWS, STEPS, 2, GROUP, HEAD_SIZE)
-    queries = jnp.transpose(queries, (0, 2, 1, 3, 4)).reshape(ROWS, 2, STEPS * GROUP, HEAD_SIZE)
-    decoded = decode_attend(cached_row_lengths, group_live_rows, queries, decode_row_cache, decode_kv, ())
-    decoded = jnp.transpose(decoded.reshape(ROWS, 2, STEPS, GROUP, HEAD_SIZE), (0, 2, 1, 3, 4))
-    decode_attention = decoded.reshape(ROWS, STEPS, 2 * GROUP * HEAD_SIZE)
+    rings = ring(span_kv)
+
+    decode_attention = decode_attend(
+        cached_row_lengths, group_live_rows, decode_token_queries, decode_row_cache, decode_kv
+    )
 
     far = jnp.arange(SIDE, dtype=jnp.int32)
     shard_z, shard_y = jnp.mod(my_z - far, SIDE), jnp.mod(my_y - far, SIDE)
     place = shard_z[:, None] * SIDE + shard_y[None, :]
     partner_sees = ((place < ctx) | ((place == ctx) & (pool == 0))).astype(jnp.int32).reshape(-1)
     own_sees = (place <= ctx).astype(jnp.int32).reshape(-1)
-    prior_pieces = [prior_up, prior_down] + prior_rings
-    earlier = [(p, k, None) for p in range(2) for k in range(SIDE)]
-    earlier += [(2 + k, j, None) for j in range(2) for k in range(SIDE)]
+    earlier_sides = [(p, k, None) for p in range(2) for k in range(SIDE)]
+
+    def earlier_pairs(first):
+        return [(first + k, j, None) for j in range(2) for k in range(SIDE)]
 
     def pairs(first):
         return [(first + k, j, 2 * j * SIDE + k) for j in range(2) for k in range(SIDE)]
 
-    sides = [(p, k, (1 + 2 * p) * SIDE + k) for p in range(2) for k in range(SIDE)]
+    beside = [(p, k, (1 + 2 * p) * SIDE + k) for p in range(2) for k in range(SIDE)]
     both = (0, 1)
     partner_queries = swap_pool(late_queries)
     own_state = attend(
-        own_sees, span_token_queries, prior_up, prior_pieces, (tuple(earlier[:8]), tuple(earlier[8:])), column, both
-    )
+        own_sees,
+        span_token_queries,
+        prior_rings[0],
+        prior_rings,
+        (tuple(earlier_pairs(0)),),
+        row_adapter_index,
+        both,
+    )
+
+    prior_up, prior_down = sides(stack_column(prior_rings, (decode_attention, rings[0])))
+    column = stack_column(rings, (own_state, partner_queries))
+    up, down = sides(column)
     partner_state = attend(
         partner_sees,
         partner_queries,
         prior_up,
-        prior_pieces + rings,
-        (tuple(earlier[:12]), tuple(earlier[12:] + pairs(6))),
-        own_state,
+        [prior_up, prior_down] + prior_rings + rings,
+        (tuple(earlier_sides + earlier_pairs(2)[:4]), tuple(earlier_pairs(2)[4:] + pairs(6))),
+        column,
         both,
     )
 
@@ -546,43 +637,46 @@
             jnp.mod(my_z - source_ctx // SIDE, SIDE),
             jnp.mod(my_y - source_ctx % SIDE, SIDE),
             source % pages,
+            (source_shard % 2 == pool).astype(jnp.int32),
         ]
     ).astype(jnp.int32)
-    found = pick_pages(where, column, up, down, rings)
-    from_partner = swap_pool(found[pages:])
-    mine = (source_shard % 2 == pool)[:pages]
-    handoff_pages = jnp.where(mine[:, None, None, None], found[:pages], from_partner)
-
-    other = [
-        swap_pool(
-            attend(
-                partner_sees,
-                partner_queries,
-                prior_up,
-                [up, down],
-                (tuple(sides),),
-                None,
-                (h,),
-                state=partner_state,
-                final=True,
-                partner=True,
-            )
+
+    def attend_partner(h, page_source, before):
+        return attend(
+            partner_sees,
+            partner_queries,
+            prior_up,
+            [up, down],
+            (tuple(beside),),
+            None,
+            (h,),
+            state=partner_state,
+            final=True,
+            partner=True,
+            page_source=page_source,
+            before=before,
         )
-        for h in range(2)
-    ]
+
+    sent, own_pages = attend_partner(0, [where, column] + rings, [])
+    second = attend_partner(1, None, [sent])
+    other = [swap_pool(sent), swap_pool(second)]
     own = attend(
         own_sees,
         span_token_queries,
         prior_up,
-        [up, down] + rings,
-        (tuple(pairs(2)), tuple(sides)),
+        [up, down] + rings + [prior_up, prior_down],
+        (
+            tuple((6 + p, k, None) for p, k, _ in earlier_sides) + tuple(pairs(2)[:4]),
+            tuple(pairs(2)[4:] + beside),
+        ),
         None,
         both,
         diagonal=(2, 0, 0),
         state=own_state,
         final=True,
-    )
-    span_attention = combine(own, other)
+        before=[second],
+    )
+    span_attention, handoff_pages = combine(where, own, other, own_pages)
     return (span_attention, handoff_pages, decode_attention)
 
 

time: 100 us -> 93.6 us (0.936)
  local copies, waits for them, and re-layouts: 7.71 us -> 1.14 us
  Pallas kernels: 42.1 us -> 45.4 us
  starting transfers between devices: 35.7 us -> 33.2 us
  other arithmetic: 3.35 us -> 1.83 us
  waiting for transfers between devices: 8.72 us -> 10.2 us
    reshape x3 -> x0, local copies, waits for them, and re-layouts: 4.52 us -> none  [the longest x2 2.81 us: per_device(): queries = decode_token_queries.reshape(ROWS, STEPS, 2, GROUP, HEAD_SIZE)]
    ppermute x4 -> x3, starting transfers between devices: 10 us -> 7.01 us  [swap_pool(): return lax.ppermute(x, 'pool', [(0, 1), (1, 0)])]
    pallas_call x7 -> x8, Pallas kernels: 30.5 us -> 32.2 us  [the longest x5 29.7 us: attend(): pl.pallas_call(functools.partial(attend_kernel, heads, len(pieces), block...]
    ppermute x12, waiting for transfers between devices: 6.14 us -> 7.47 us  [shift(): return lax.ppermute(x, 'ctx', perm)]
    unnamed x12 -> x16, local copies, waits for them, and re-layouts: 2.21 us -> 0.98 us
  transfers between devices with their start and end apart: 18 -> 17, of which waited for: 3 -> 3; matrix products, arithmetic and copies ran while one was open for 9% -> 2% of each run, Pallas kernels for 30% -> 32%
where the time goes in v8:
time: 93.6 us; the launch traced here: 93.3 us
  Pallas kernels  45.4 us (49%)
  starting transfers between devices  33.2 us (35%)
  waiting for transfers between devices  10.2 us (11%)
  other arithmetic  1.83 us (2%)
  between operations  1.5 us (2%)
  local copies, waits for them, and re-layouts  1.14 us (1%)
    pallas_call x5, Pallas kernels, attend(): pl.pallas_call(functools.partial(attend_kernel, heads, len(pieces), block...  29.7 us
    ppermute x12, starting transfers between devices, shift(): return lax.ppermute(x, 'ctx', perm)  24.5 us
    pallas_call x1, Pallas kernels, project(): pl.pallas_call(project_kernel, in_specs=[scalar, scalar, local] + [far] *...  9.53 us
    ppermute x12, waiting for transfers between devices, shift(): return lax.ppermute(x, 'ctx', perm)  7.47 us
    ppermute x3, starting transfers between devices, swap_pool(): return lax.ppermute(x, 'pool', [(0, 1), (1, 0)])  7.01 us
    pallas_call x1, Pallas kernels, decode_attend(): pl.pallas_call(decode_kernel, grid_spec=pltpu.PrefetchScalarGridSpec(num_...  2.85 us
    ppermute x2, waiting for transfers between devices, swap_tp(): return lax.ppermute(x, 'tp', [(i, i ^ bit) for i in range(4)])  2.75 us
    pallas_call x1, Pallas kernels, combine(): pl.pallas_call(combine_kernel, in_specs=[pl.BlockSpec(memory_space=pltpu....  2.42 us
  transfers between devices with their start and end apart: 17, of which 3 were waited for; matrix products, arithmetic and copies ran while one was open for 2% of the time, Pallas kernels for 32%

profile of v8, /device:TPU:0, one launch (start us, length us, event | category | flops | bytes accessed | tf_op | source)
XLA Modules:
  0.0 93.3 jit_solution(11879185066251215305)
XLA Ops:
  0.6 9.5 %project.1 = (f32[4,192,256]{2,1,0:T(8,128)}, f32[4,192,256]{2,1,0:T(8,128)}) custom-call(s32[1]{0:T(128)} %bitcast.3.tp_ref, s32[16]{0:T(128)} %refs_4_.1, s32[1,128]{1,0:T(1,128)} %bitcast.41, bf16[128,2048]{1,0:T(8,128)(2,1)} %span_ref.1, bf16[16,4,2048]{2,1,0:T(4,128)(2,1)} %decode_ref.1, bf16[2048,2048]{1,0:T(8,128)(2,1)} %weight_ref.1, ...), custom_call_target="tpu_custom_call" | custom-call | flops 1100000000 | bytes 1048576 | tf_op jit(solution)/shard_map/project/pallas_call | solution.py:124
  10.3 4.0 %collective-permute-start = (bf16[2,128,256]{2,1,0:T(8,128)(2,1)S(1)}, bf16[2,128,256]{2,1,0:T(8,128)(2,1)S(1)}, u32[]{:S(2)}, u32[]{:S(2)}) collective-permute-start(bf16[2,128,256]{2,1,0:T(8,128)(2,1)S(1)} %copy-done.6), channel_id=1, source_target_pairs={{0,64},{8,72},{16,80},{24,88},{32,96},{40,104},{48,112},{56,120},{... | collective-permute-start | bytes 393224 | tf_op jit(solution)/shard_map/ppermute | solution.py:520
  14.5 1.4 %slice_add_fusion = (f32[2,192,256]{2,1,0:T(8,128)S(1)}, f32[2,192,256]{2,1,0:T(8,128)S(1)}) fusion(f32[4,192,256]{2,1,0:T(8,128)S(1)} %collective-permute-done.4, f32[4,192,256]{2,1,0:T(8,128)} %get-tuple-element.12), kind=kLoop, calls=%fused_computation | loop fusion | flops 196608 | bytes 2359296 | tf_op jit(solution)/shard_map/add | solution.py:575
  15.8 1.6 %collective-permute-start.5 = (f32[2,192,256]{2,1,0:T(8,128)S(1)}, f32[2,192,256]{2,1,0:T(8,128)S(1)}, u32[]{:S(2)}, u32[]{:S(2)}) collective-permute-start(f32[2,192,256]{2,1,0:T(8,128)S(1)} %get-tuple-element.21), channel_id=1, source_target_pairs={{0,2},{1,3},{2,0},{3,1},{4,6},{5,7},{6,4},{7,5},{8,10},{9,11},{10,... | collective-permute-start | bytes 1179656 | tf_op jit(solution)/shard_map/ppermute | solution.py:528
  18.5 1.6 %collective-permute-start.1 = (bf16[2,2,128,256]{3,2,1,0:T(8,128)(2,1)S(1)}, bf16[2,2,128,256]{3,2,1,0:T(8,128)(2,1)S(1)}, u32[]{:S(2)}, u32[]{:S(2)}) collective-permute-start(bf16[2,2,128,256]{3,2,1,0:T(8,128)(2,1)S(1)} %pad_maximum_fusion.refs_0_.known_ref.refs_2_), channel_id=1, source_target_pairs={{0,8},{8,16},{16,24},{24,0},{32,40},{40,48},{48,56},{56,32},{64,72... | collective-permute-start | bytes 786440 | tf_op jit(solution)/shard_map/ppermute | solution.py:520
  20.1 2.9 %collective-permute-start.2 = (bf16[2,2,128,256]{3,2,1,0:T(8,128)(2,1)S(1)}, bf16[2,2,128,256]{3,2,1,0:T(8,128)(2,1)S(1)}, u32[]{:S(2)}, u32[]{:S(2)}) collective-permute-start(bf16[2,2,128,256]{3,2,1,0:T(8,128)(2,1)S(1)} %pad_maximum_fusion.refs_0_.known_ref.refs_2_), channel_id=1, source_target_pairs={{0,16},{8,24},{16,0},{24,8},{32,48},{40,56},{48,32},{56,40},{64,80... | collective-permute-start | bytes 786440 | tf_op jit(solution)/shard_map/ppermute | solution.py:520
  23.0 1.3 %collective-permute-start.3 = (bf16[2,2,128,256]{3,2,1,0:T(8,128)(2,1)S(1)}, bf16[2,2,128,256]{3,2,1,0:T(8,128)(2,1)S(1)}, u32[]{:S(2)}, u32[]{:S(2)}) collective-permute-start(bf16[2,2,128,256]{3,2,1,0:T(8,128)(2,1)S(1)} %pad_maximum_fusion.refs_0_.known_ref.refs_2_), channel_id=1, source_target_pairs={{0,24},{8,0},{16,8},{24,16},{32,56},{40,32},{48,40},{56,48},{64,88... | collective-permute-start | bytes 786440 | tf_op jit(solution)/shard_map/ppermute | solution.py:520
  24.3 2.7 %collective-permute-done.5.chip_ref = f32[2,192,256]{2,1,0:T(8,128)S(1)} collective-permute-done((f32[2,192,256]{2,1,0:T(8,128)S(1)}, f32[2,192,256]{2,1,0:T(8,128)S(1)}, u32[]{:S(2)}, u32[]{:S(2)}) %collective-permute-start.5) | collective-permute-done | bytes 393248 | tf_op jit(solution)/shard_map/ppermute | solution.py:528
  28.0 2.3 %collective-permute-start.6 = (bf16[2,128,256]{2,1,0:T(8,128)(2,1)S(1)}, bf16[2,128,256]{2,1,0:T(8,128)(2,1)S(1)}, u32[]{:S(2)}, u32[]{:S(2)}) collective-permute-start(bf16[2,128,256]{2,1,0:T(8,128)(2,1)S(1)} %get-tuple-element.15), channel_id=1, source_target_pairs={{0,64},{8,72},{16,80},{24,88},{32,96},{40,104},{48,112},{56,120},{... | collective-permute-start | bytes 393224 | tf_op jit(solution)/shard_map/ppermute | solution.py:520
  30.9 3.1 %collective-permute-start.11 = (bf16[128,2048]{1,0:T(8,128)(2,1)}, bf16[128,2048]{1,0:T(8,128)(2,1)S(1)}, u32[]{:S(2)}, u32[]{:S(2)}) collective-permute-start(bf16[128,2048]{1,0:T(8,128)(2,1)} %get-tuple-element.16), channel_id=1, source_target_pairs={{0,4},{4,0},{1,5},{5,1},{2,6},{6,2},{3,7},{7,3},{8,12},{12,8},{9,1... | collective-permute-start | bytes 1572872 | tf_op jit(solution)/shard_map/ppermute | solution.py:524
  34.0 2.8 %decode.1.refs_4_ = bf16[16,4,2048]{2,1,0:T(4,128)(2,1)} custom-call(s32[16]{0:T(128)S(1)} %copy-done.4, s32[1]{0:T(128)S(6)} %copy.17.live_ref, bf16[16,4,2048]{2,1,0:T(4,128)(2,1)S(1)} %copy-done.2, bf16[16,2,256,256]{3,2,1,0:T(8,128)(2,1)S(1)} %copy-done, bf16[2,64,256]{2,1,0:T(8,128)(2,1)S(1)} %get-tuple-element.14.fresh_ref), custom_call_target="tpu_custom_call" | custom-call | flops 1100000000 | bytes 1048576 | tf_op jit(solution)/shard_map/decode/pallas_call | solution.py:478
  36.9 3.1 %collective-permute-start.10 = (bf16[2,2,128,256]{3,2,1,0:T(8,128)(2,1)S(1)}, bf16[2,2,128,256]{3,2,1,0:T(8,128)(2,1)S(1)}, u32[]{:S(2)}, u32[]{:S(2)}) collective-permute-start(bf16[2,2,128,256]{3,2,1,0:T(8,128)(2,1)S(1)} %pad_maximum_fusion.1.refs_5_.refs_0_.refs_6_.refs_2_), channel_id=1, source_target_pairs={{0,24},{8,0},{16,8},{24,16},{32,56},{40,32},{48,40},{56,48},{64,88... | collective-permute-start | bytes 786440 | tf_op jit(solution)/shard_map/ppermute | solution.py:520
  41.0 1.1 %collective-permute-start.7 = (bf16[4,2,128,256]{3,2,1,0:T(8,128)(2,1)S(1)}, bf16[4,2,128,256]{3,2,1,0:T(8,128)(2,1)}, u32[]{:S(2)}, u32[]{:S(2)}) collective-permute-start(bf16[4,2,128,256]{3,2,1,0:T(8,128)(2,1)S(1)} %stack.34), channel_id=1, source_target_pairs={{0,32},{8,40},{16,48},{24,56},{32,64},{40,72},{48,80},{56,88},{64,... | collective-permute-start | bytes 1572872 | tf_op jit(solution)/shard_map/ppermute | solution.py:520
  42.1 2.2 %collective-permute-start.14 = (bf16[4,2,128,256]{3,2,1,0:T(8,128)(2,1)S(1)}, bf16[4,2,128,256]{3,2,1,0:T(8,128)(2,1)}, u32[]{:S(2)}, u32[]{:S(2)}) collective-permute-start(bf16[4,2,128,256]{3,2,1,0:T(8,128)(2,1)S(1)} %stack.34), channel_id=1, source_target_pairs={{0,96},{8,104},{16,112},{24,120},{32,0},{40,8},{48,16},{56,24},{64... | collective-permute-start | bytes 1572872 | tf_op jit(solution)/shard_map/ppermute | solution.py:520
  44.6 2.5 %collective-permute-start.9 = (bf16[2,2,128,256]{3,2,1,0:T(8,128)(2,1)S(1)}, bf16[2,2,128,256]{3,2,1,0:T(8,128)(2,1)S(1)}, u32[]{:S(2)}, u32[]{:S(2)}) collective-permute-start(bf16[2,2,128,256]{3,2,1,0:T(8,128)(2,1)S(1)} %pad_maximum_fusion.1.refs_5_.refs_0_.refs_6_.refs_2_), channel_id=1, source_target_pairs={{0,16},{8,24},{16,0},{24,8},{32,48},{40,56},{48,32},{56,40},{64,80... | collective-permute-start | bytes 786440 | tf_op jit(solution)/shard_map/ppermute | solution.py:520
  47.1 3.7 %attend_first.2.refs_4_.refs_8_ = f32[2,1024,256]{2,1,0:T(8,128)S(1)} custom-call(s32[16]{0:T(128)S(1)} %reshape.352.visible_ref, bf16[128,2048]{1,0:T(8,128)(2,1)S(1)} %copy-done.5, bf16[2,2,128,256]{3,2,1,0:T(8,128)(2,1)S(1)} %pad_maximum_fusion.refs_0_.known_ref.refs_2_, bf16[2,2,128,256]{3,2,1,0:T(8,128)(2,1)S(1)} %pad_maximum_fusion.refs_0_.known_ref.refs_2_, ...), custom_call_target="tpu_custom_call" | custom-call | flops 3740000000 | bytes 1048576 | tf_op jit(solution)/shard_map/attend_first/pallas_call | solution.py:340
  50.8 6.7 %collective-permute-done.8.refs_1_.refs_7_.refs_6_.refs_3_ = bf16[2,2,128,256]{3,2,1,0:T(8,128)(2,1)S(1)} collective-permute-done((bf16[2,2,128,256]{3,2,1,0:T(8,128)(2,1)S(1)}, bf16[2,2,128,256]{3,2,1,0:T(8,128)(2,1)S(1)}, u32[]{:S(2)}, u32[]{:S(2)}) %collective-permute-start.8) | collective-permute-done | bytes 262176 | tf_op jit(solution)/shard_map/ppermute | solution.py:520
  57.6 3.2 %collective-permute-start.13 = (bf16[4,2,128,256]{3,2,1,0:T(8,128)(2,1)S(1)}, bf16[4,2,128,256]{3,2,1,0:T(8,128)(2,1)S(1)}, u32[]{:S(2)}, u32[]{:S(2)}) collective-permute-start(bf16[4,2,128,256]{3,2,1,0:T(8,128)(2,1)S(1)} %stack.35.refs_10_.refs_4_), channel_id=1, source_target_pairs={{0,96},{8,104},{16,112},{24,120},{32,0},{40,8},{48,16},{56,24},{64... | collective-permute-start | bytes 1572872 | tf_op jit(solution)/shard_map/ppermute | solution.py:520
  60.9 9.4 %attend_first.3.refs_2_ = f32[2,1024,256]{2,1,0:T(8,128)S(1)} custom-call(s32[16]{0:T(128)S(1)} %reshape.353.visible_ref, bf16[128,2048]{1,0:T(8,128)(2,1)S(1)} %collective-permute-done.11.refs_5_.q_ref, bf16[4,2,128,256]{3,2,1,0:T(8,128)(2,1)} %collective-permute-done.7.known_ref.refs_0_.refs_6_, ...), custom_call_target="tpu_custom_call" | custom-call | flops 11219999744 | bytes 1048576 | tf_op jit(solution)/shard_map/attend_first/pallas_call | solution.py:340
  70.3 3.2 %attend_last.3 = (bf16[1,128,1664]{2,1,0:T(8,128)(2,1)S(1)}, bf16[8,2,16,256]{3,2,1,0:T(8,128)(2,1)S(1)}) custom-call(s32[16]{0:T(128)S(1)} %reshape.353.visible_ref, bf16[128,2048]{1,0:T(8,128)(2,1)S(1)} %collective-permute-done.11.refs_5_.q_ref, bf16[4,2,128,256]{3,2,1,0:T(8,128)(2,1)} %collective-permute-done.7.known_ref.refs_0_.refs_6_, ...), custom_call_target="tpu_custom_call" | custom-call | flops 1870000000 | bytes 1048576 | tf_op jit(solution)/shard_map/attend_last/pallas_call | solution.py:340
  74.4 3.0 %attend_last.4.refs_9_ = bf16[1,128,1152]{2,1,0:T(8,128)(2,1)S(1)} custom-call(s32[16]{0:T(128)S(1)} %reshape.353.visible_ref, bf16[128,2048]{1,0:T(8,128)(2,1)S(1)} %collective-permute-done.11.refs_5_.q_ref, bf16[4,2,128,256]{3,2,1,0:T(8,128)(2,1)} %collective-permute-done.7.known_ref.refs_0_.refs_6_, ...), custom_call_target="tpu_custom_call" | custom-call | flops 1870000000 | bytes 1048576 | tf_op jit(solution)/shard_map/attend_last/pallas_call | solution.py:340
  77.4 3.1 %collective-permute-start.16 = (bf16[1,128,1152]{2,1,0:T(8,128)(2,1)S(1)}, bf16[1,128,1152]{2,1,0:T(8,128)(2,1)S(1)}, u32[]{:S(2)}, u32[]{:S(2)}) collective-permute-start(bf16[1,128,1152]{2,1,0:T(8,128)(2,1)S(1)} %attend_last.4.refs_9_), channel_id=1, source_target_pairs={{0,4},{4,0},{1,5},{5,1},{2,6},{6,2},{3,7},{7,3},{8,12},{12,8},{9,1... | collective-permute-start | bytes 884744 | tf_op jit(solution)/shard_map/ppermute | solution.py:524
  80.5 10.3 %attend_last.5.own_ref = f32[2,128,1152]{2,1,0:T(8,128)S(1)} custom-call(s32[16]{0:T(128)S(1)} %reshape.352.visible_ref, bf16[128,2048]{1,0:T(8,128)(2,1)S(1)} %copy-done.5, bf16[4,2,128,256]{3,2,1,0:T(8,128)(2,1)} %collective-permute-done.7.known_ref.refs_0_.refs_6_, bf16[4,2,128,256]{3,2,1,0:T(8,128)(2,1)S(1)} %collective-permute-done.12.refs_0_, ...), custom_call_target="tpu_custom_call" | custom-call | flops 11219999744 | bytes 1048576 | tf_op jit(solution)/shard_map/attend_last/pallas_call | solution.py:340
  90.8 2.4 %combine.1 = (bf16[128,2048]{1,0:T(8,128)(2,1)}, bf16[8,2,16,256]{3,2,1,0:T(8,128)(2,1)}) custom-call(s32[4,16]{1,0:T(4,128)S(1)} %pad_add_fusion.refs_3_.where_ref, f32[2,128,1152]{2,1,0:T(8,128)S(1)} %attend_last.5.own_ref, bf16[1,128,1664]{2,1,0:T(8,128)(2,1)S(1)} %collective-permute-done.15.first_ref, ...), custom_call_target="tpu_custom_call" | custom-call | flops 1100000000 | bytes 1048576 | tf_op jit(solution)/shard_map/combine/pallas_call | solution.py:401
  (50 shorter events, 4.4 us)
Async XLA Ops:
  0.6 9.7 %copy-start.6 = (bf16[2,128,256]{2,1,0:T(8,128)(2,1)S(1)}, bf16[2,128,256]{2,1,0:T(8,128)(2,1)}, u32[]{:S(2)}) copy-start(bf16[2,128,256]{2,1,0:T(8,128)(2,1)} %param.16) | copy-start | bytes 393220
  10.2 7.3 %copy-start.7 = (s32[256]{0:T(256)S(1)}, s32[256]{0:T(256)}, u32[]{:S(2)}) copy-start(s32[256]{0:T(256)} %param.27) | copy-start | bytes 3076
  10.2 16.9 %copy-start.5 = (bf16[128,2048]{1,0:T(8,128)(2,1)S(1)}, bf16[128,2048]{1,0:T(8,128)(2,1)}, u32[]{:S(2)}) copy-start(bf16[128,2048]{1,0:T(8,128)(2,1)} %q_ref.5) | copy-start | bytes 1572868
  10.2 4.2 %collective-permute-start.4 = (f32[4,192,256]{2,1,0:T(8,128)}, f32[4,192,256]{2,1,0:T(8,128)S(1)}, u32[]{:S(2)}, u32[]{:S(2)}) collective-permute-start(f32[4,192,256]{2,1,0:T(8,128)} %get-tuple-element.13), channel_id=1, source_target_pairs={{0,1},{1,0},{2,3},{3,2},{4,5},{5,4},{6,7},{7,6},{8,9},{9,8},{10,11... | collective-permute-start | bytes 2359304 | tf_op jit(solution)/shard_map/ppermute | solution.py:528
  10.3 8.1 %collective-permute-start = (bf16[2,128,256]{2,1,0:T(8,128)(2,1)S(1)}, bf16[2,128,256]{2,1,0:T(8,128)(2,1)S(1)}, u32[]{:S(2)}, u32[]{:S(2)}) collective-permute-start(bf16[2,128,256]{2,1,0:T(8,128)(2,1)S(1)} %copy-done.6), channel_id=1, source_target_pairs={{0,64},{8,72},{16,80},{24,88},{32,96},{40,104},{48,112},{56,120},{... | collective-permute-start | bytes 393224 | tf_op jit(solution)/shard_map/ppermute | solution.py:520
  14.4 19.6 %copy-start = (bf16[16,2,256,256]{3,2,1,0:T(8,128)(2,1)S(1)}, bf16[16,2,256,256]{3,2,1,0:T(8,128)(2,1)}, u32[]{:S(2)}) copy-start(bf16[16,2,256,256]{3,2,1,0:T(8,128)(2,1)} %cache_ref.1) | copy-start | bytes 12582916
  14.4 19.6 %copy-start.2 = (bf16[16,4,2048]{2,1,0:T(4,128)(2,1)S(1)}, bf16[16,4,2048]{2,1,0:T(4,128)(2,1)}, u32[]{:S(2)}) copy-start(bf16[16,4,2048]{2,1,0:T(4,128)(2,1)} %q_ref.3) | copy-start | bytes 786436
  14.5 19.6 %copy-start.4 = (s32[16]{0:T(128)S(1)}, s32[16]{0:T(128)}, u32[]{:S(2)}) copy-start(s32[16]{0:T(128)} %length_ref.1) | copy-start | bytes 196
  15.8 11.2 %collective-permute-start.5 = (f32[2,192,256]{2,1,0:T(8,128)S(1)}, f32[2,192,256]{2,1,0:T(8,128)S(1)}, u32[]{:S(2)}, u32[]{:S(2)}) collective-permute-start(f32[2,192,256]{2,1,0:T(8,128)S(1)} %get-tuple-element.21), channel_id=1, source_target_pairs={{0,2},{1,3},{2,0},{3,1},{4,6},{5,7},{6,4},{7,5},{8,10},{9,11},{10,... | collective-permute-start | bytes 1179656 | tf_op jit(solution)/shard_map/ppermute | solution.py:528
  18.5 21.5 %collective-permute-start.1 = (bf16[2,2,128,256]{3,2,1,0:T(8,128)(2,1)S(1)}, bf16[2,2,128,256]{3,2,1,0:T(8,128)(2,1)S(1)}, u32[]{:S(2)}, u32[]{:S(2)}) collective-permute-start(bf16[2,2,128,256]{3,2,1,0:T(8,128)(2,1)S(1)} %pad_maximum_fusion.refs_0_.known_ref.refs_2_), channel_id=1, source_target_pairs={{0,8},{8,16},{16,24},{24,0},{32,40},{40,48},{48,56},{56,32},{64,72... | collective-permute-start | bytes 786440 | tf_op jit(solution)/shard_map/ppermute | solution.py:520
  20.1 19.9 %collective-permute-start.2 = (bf16[2,2,128,256]{3,2,1,0:T(8,128)(2,1)S(1)}, bf16[2,2,128,256]{3,2,1,0:T(8,128)(2,1)S(1)}, u32[]{:S(2)}, u32[]{:S(2)}) collective-permute-start(bf16[2,2,128,256]{3,2,1,0:T(8,128)(2,1)S(1)} %pad_maximum_fusion.refs_0_.known_ref.refs_2_), channel_id=1, source_target_pairs={{0,16},{8,24},{16,0},{24,8},{32,48},{40,56},{48,32},{56,40},{64,80... | collective-permute-start | bytes 786440 | tf_op jit(solution)/shard_map/ppermute | solution.py:520
  23.0 17.0 %collective-permute-start.3 = (bf16[2,2,128,256]{3,2,1,0:T(8,128)(2,1)S(1)}, bf16[2,2,128,256]{3,2,1,0:T(8,128)(2,1)S(1)}, u32[]{:S(2)}, u32[]{:S(2)}) collective-permute-start(bf16[2,2,128,256]{3,2,1,0:T(8,128)(2,1)S(1)} %pad_maximum_fusion.refs_0_.known_ref.refs_2_), channel_id=1, source_target_pairs={{0,24},{8,0},{16,8},{24,16},{32,56},{40,32},{48,40},{56,48},{64,88... | collective-permute-start | bytes 786440 | tf_op jit(solution)/shard_map/ppermute | solution.py:520
  28.0 8.9 %collective-permute-start.6 = (bf16[2,128,256]{2,1,0:T(8,128)(2,1)S(1)}, bf16[2,128,256]{2,1,0:T(8,128)(2,1)S(1)}, u32[]{:S(2)}, u32[]{:S(2)}) collective-permute-start(bf16[2,128,256]{2,1,0:T(8,128)(2,1)S(1)} %get-tuple-element.15), channel_id=1, source_target_pairs={{0,64},{8,72},{16,80},{24,88},{32,96},{40,104},{48,112},{56,120},{... | collective-permute-start | bytes 393224 | tf_op jit(solution)/shard_map/ppermute | solution.py:520
  30.9 26.6 %collective-permute-start.11 = (bf16[128,2048]{1,0:T(8,128)(2,1)}, bf16[128,2048]{1,0:T(8,128)(2,1)S(1)}, u32[]{:S(2)}, u32[]{:S(2)}) collective-permute-start(bf16[128,2048]{1,0:T(8,128)(2,1)} %get-tuple-element.16), channel_id=1, source_target_pairs={{0,4},{4,0},{1,5},{5,1},{2,6},{6,2},{3,7},{7,3},{8,12},{12,8},{9,1... | collective-permute-start | bytes 1572872 | tf_op jit(solution)/shard_map/ppermute | solution.py:524
  36.9 10.3 %copy-start.3 = (s32[16]{0:T(128)S(1)}, s32[16]{0:T(128)}, u32[]{:S(2)}) copy-start(s32[16]{0:T(128)} %refs_4_.1) | copy-start | bytes 196
  36.9 7.7 %collective-permute-start.10 = (bf16[2,2,128,256]{3,2,1,0:T(8,128)(2,1)S(1)}, bf16[2,2,128,256]{3,2,1,0:T(8,128)(2,1)S(1)}, u32[]{:S(2)}, u32[]{:S(2)}) collective-permute-start(bf16[2,2,128,256]{3,2,1,0:T(8,128)(2,1)S(1)} %pad_maximum_fusion.1.refs_5_.refs_0_.refs_6_.refs_2_), channel_id=1, source_target_pairs={{0,24},{8,0},{16,8},{24,16},{32,56},{40,32},{48,40},{56,48},{64,88... | collective-permute-start | bytes 786440 | tf_op jit(solution)/shard_map/ppermute | solution.py:520
  41.0 19.9 %collective-permute-start.7 = (bf16[4,2,128,256]{3,2,1,0:T(8,128)(2,1)S(1)}, bf16[4,2,128,256]{3,2,1,0:T(8,128)(2,1)}, u32[]{:S(2)}, u32[]{:S(2)}) collective-permute-start(bf16[4,2,128,256]{3,2,1,0:T(8,128)(2,1)S(1)} %stack.34), channel_id=1, source_target_pairs={{0,32},{8,40},{16,48},{24,56},{32,64},{40,72},{48,80},{56,88},{64,... | collective-permute-start | bytes 1572872 | tf_op jit(solution)/shard_map/ppermute | solution.py:520
  42.1 18.8 %collective-permute-start.14 = (bf16[4,2,128,256]{3,2,1,0:T(8,128)(2,1)S(1)}, bf16[4,2,128,256]{3,2,1,0:T(8,128)(2,1)}, u32[]{:S(2)}, u32[]{:S(2)}) collective-permute-start(bf16[4,2,128,256]{3,2,1,0:T(8,128)(2,1)S(1)} %stack.34), channel_id=1, source_target_pairs={{0,96},{8,104},{16,112},{24,120},{32,0},{40,8},{48,16},{56,24},{64... | collective-permute-start | bytes 1572872 | tf_op jit(solution)/shard_map/ppermute | solution.py:520
  44.5 13.0 %collective-permute-start.8 = (bf16[2,2,128,256]{3,2,1,0:T(8,128)(2,1)S(1)}, bf16[2,2,128,256]{3,2,1,0:T(8,128)(2,1)S(1)}, u32[]{:S(2)}, u32[]{:S(2)}) collective-permute-start(bf16[2,2,128,256]{3,2,1,0:T(8,128)(2,1)S(1)} %pad_maximum_fusion.1.refs_5_.refs_0_.refs_6_.refs_2_), channel_id=1, source_target_pairs={{0,8},{8,16},{16,24},{24,0},{32,40},{40,48},{48,56},{56,32},{64,72... | collective-permute-start | bytes 786440 | tf_op jit(solution)/shard_map/ppermute | solution.py:520
  44.6 12.9 %collective-permute-start.9 = (bf16[2,2,128,256]{3,2,1,0:T(8,128)(2,1)S(1)}, bf16[2,2,128,256]{3,2,1,0:T(8,128)(2,1)S(1)}, u32[]{:S(2)}, u32[]{:S(2)}) collective-permute-start(bf16[2,2,128,256]{3,2,1,0:T(8,128)(2,1)S(1)} %pad_maximum_fusion.1.refs_5_.refs_0_.refs_6_.refs_2_), channel_id=1, source_target_pairs={{0,16},{8,24},{16,0},{24,8},{32,48},{40,56},{48,32},{56,40},{64,80... | collective-permute-start | bytes 786440 | tf_op jit(solution)/shard_map/ppermute | solution.py:520
  57.6 12.7 %collective-permute-start.12 = (bf16[4,2,128,256]{3,2,1,0:T(8,128)(2,1)S(1)}, bf16[4,2,128,256]{3,2,1,0:T(8,128)(2,1)S(1)}, u32[]{:S(2)}, u32[]{:S(2)}) collective-permute-start(bf16[4,2,128,256]{3,2,1,0:T(8,128)(2,1)S(1)} %stack.35.refs_10_.refs_4_), channel_id=1, source_target_pairs={{0,32},{8,40},{16,48},{24,56},{32,64},{40,72},{48,80},{56,88},{64,... | collective-permute-start | bytes 1572872 | tf_op jit(solution)/shard_map/ppermute | solution.py:520
  57.6 12.7 %collective-permute-start.13 = (bf16[4,2,128,256]{3,2,1,0:T(8,128)(2,1)S(1)}, bf16[4,2,128,256]{3,2,1,0:T(8,128)(2,1)S(1)}, u32[]{:S(2)}, u32[]{:S(2)}) collective-permute-start(bf16[4,2,128,256]{3,2,1,0:T(8,128)(2,1)S(1)} %stack.35.refs_10_.refs_4_), channel_id=1, source_target_pairs={{0,96},{8,104},{16,112},{24,120},{32,0},{40,8},{48,16},{56,24},{64... | collective-permute-start | bytes 1572872 | tf_op jit(solution)/shard_map/ppermute | solution.py:520
  73.6 17.3 %collective-permute-start.15 = (bf16[1,128,1664]{2,1,0:T(8,128)(2,1)S(1)}, bf16[1,128,1664]{2,1,0:T(8,128)(2,1)S(1)}, u32[]{:S(2)}, u32[]{:S(2)}) collective-permute-start(bf16[1,128,1664]{2,1,0:T(8,128)(2,1)S(1)} %get-tuple-element.17.refs_3_), channel_id=1, source_target_pairs={{0,4},{4,0},{1,5},{5,1},{2,6},{6,2},{3,7},{7,3},{8,12},{12,8},{9,1... | collective-permute-start | bytes 1277960 | tf_op jit(solution)/shard_map/ppermute | solution.py:524
  77.4 13.4 %collective-permute-start.16 = (bf16[1,128,1152]{2,1,0:T(8,128)(2,1)S(1)}, bf16[1,128,1152]{2,1,0:T(8,128)(2,1)S(1)}, u32[]{:S(2)}, u32[]{:S(2)}) collective-permute-start(bf16[1,128,1152]{2,1,0:T(8,128)(2,1)S(1)} %attend_last.4.refs_9_), channel_id=1, source_target_pairs={{0,4},{4,0},{1,5},{5,1},{2,6},{6,2},{3,7},{7,3},{8,12},{12,8},{9,1... | collective-permute-start | bytes 884744 | tf_op jit(solution)/shard_map/ppermute | solution.py:524
  (1 other events, 1.0 us)

commit v9 on v8

--- a/solution.py
+++ b/solution.py
@@ -47,14 +47,17 @@
 
 
 def project_kernel(
-    tp_ref,
-    row_adapter_ref,
-    adapter_ref,
+    row_adapter_hbm,
+    adapter_hbm,
     span_ref,
     decode_ref,
     weight_ref,
     down_ref,
     up_ref,
+    core_hbm,
+    kept_hbm,
+    row_adapter_ref,
+    adapter_ref,
     core_ref,
     kept_ref,
     hidden_ref,
@@ -65,10 +68,13 @@
     up_buffer,
     sems,
     small_sems,
+    out_sems,
 ):
-    tp = tp_ref[0]
+    tp = lax.axis_index("tp")
     depth = weight_ref.shape[0] // CHUNKS
     small = [
+        pltpu.make_async_copy(row_adapter_hbm, row_adapter_ref, small_sems.at[4]),
+        pltpu.make_async_copy(adapter_hbm, adapter_ref, small_sems.at[5]),
         pltpu.make_async_copy(span_ref, hidden_ref.at[pl.ds(0, TOKENS)], small_sems.at[0]),
         pltpu.make_async_copy(decode_ref, decode_buffer, small_sems.at[1]),
         pltpu.make_async_copy(down_ref, down_buffer, small_sems.at[2]),
@@ -91,6 +97,8 @@
     for group in copies:
         for copy in group:
             copy.start()
+    for copy in small[:2]:
+        copy.wait()
     span_owner = jnp.transpose(jnp.broadcast_to(adapter_ref[...], (TOKENS, TOKENS)))
     row = lax.broadcasted_iota(jnp.int32, (DECODE, TOKENS), 0) // STEPS
     decode_owner = jnp.zeros((DECODE, TOKENS), jnp.int32)
@@ -98,12 +106,13 @@
         decode_owner = jnp.where(row == r, row_adapter_ref[r], decode_owner)
     owner = jnp.concatenate([span_owner, decode_owner], axis=0)
     column = lax.broadcasted_iota(jnp.int32, (ALL_ROWS, TOKENS), 1) // ADAPTER_RANK
-    for copy in small:
+    for copy in small[2:]:
         copy.wait()
     hidden_ref[TOKENS:, :] = decode_buffer[...].reshape(DECODE, decode_buffer.shape[2])
     narrow = jnp.dot(hidden_ref[...], down_buffer[...], preferred_element_type=jnp.float32)
     for part, piece in enumerate(split3(jnp.where(column == owner, narrow, 0.0))):
         rank_ref[:, part * TOKENS : (part + 1) * TOKENS] = piece
+    flushes = []
     for i, first in enumerate(columns):
         up = up_buffer[:, pl.ds(first, 2 * WIDTH)]
         out = jnp.dot(rank_ref[...], jnp.concatenate([up, up, up], axis=0), preferred_element_type=jnp.float32)
@@ -111,22 +120,30 @@
             copies[i][k].wait()
             here = slice(k * depth, (k + 1) * depth)
             out = out + jnp.dot(hidden_ref[:, here], buffer_ref[i, here, :], preferred_element_type=jnp.float32)
-        out_ref = core_ref if i < 2 else kept_ref
+        out_ref, out_hbm = (core_ref, core_hbm) if i < 2 else (kept_ref, kept_hbm)
         out_ref[2 * (i % 2)] = out[:, :WIDTH]
         out_ref[2 * (i % 2) + 1] = out[:, WIDTH:]
-
-
-def project(tp, row_adapter, adapter, span, decode, weight, down, up):
+        part = pl.ds(2 * (i % 2), 2)
+        flush = pltpu.make_async_copy(out_ref.at[part], out_hbm.at[part], out_sems.at[i])
+        flush.start()
+        flushes.append(flush)
+    for flush in flushes:
+        flush.wait()
+
+
+def project(row_adapter, adapter, span, decode, weight, down, up):
     depth = span.shape[1]
-    scalar = pl.BlockSpec(memory_space=pltpu.SMEM)
-    local = pl.BlockSpec(memory_space=pltpu.VMEM)
     far = pl.BlockSpec(memory_space=pl.ANY)
     return pl.pallas_call(
         project_kernel,
-        in_specs=[scalar, scalar, local] + [far] * 5,
-        out_specs=[local] * 2,
+        in_specs=[far] * 7,
+        out_specs=[far] * 2,
         out_shape=[jax.ShapeDtypeStruct((4, ALL_ROWS, WIDTH), jnp.float32)] * 2,
         scratch_shapes=[
+            pltpu.SMEM(row_adapter.shape, jnp.int32),
+            pltpu.VMEM(adapter.shape, jnp.int32),
+            pltpu.VMEM((4, ALL_ROWS, WIDTH), jnp.float32),
+            pltpu.VMEM((4, ALL_ROWS, WIDTH), jnp.float32),
             pltpu.VMEM((ALL_ROWS, depth), jnp.bfloat16),
             pltpu.VMEM((ALL_ROWS, 3 * TOKENS), jnp.bfloat16),
             pltpu.VMEM((4, depth, 2 * WIDTH), jnp.bfloat16),
@@ -134,12 +151,13 @@
             pltpu.VMEM(down.shape, jnp.bfloat16),
             pltpu.VMEM(up.shape, jnp.bfloat16),
             pltpu.SemaphoreType.DMA((4, CHUNKS)),
+            pltpu.SemaphoreType.DMA((6,)),
             pltpu.SemaphoreType.DMA((4,)),
         ],
         compiler_params=pltpu.CompilerParams(vmem_limit_bytes=PROJECT_VMEM * MIB),
         cost_estimate=estimate(PROJECT_US),
         name="project",
-    )(tp, row_adapter, adapter, span, decode, weight, down, up)
+    )(row_adapter, adapter, span, decode, weight, down, up)
 
 
 def finish_kernel(own_ref, chip_ref, queries_ref, *refs):
@@ -374,26 +392,22 @@
             handoff_ref[n, h] = jnp.where(mine, pages_ref[n, h], theirs)
     for h in range(2):
         other_ref = (first_ref, second_ref)[h]
-        own_level = own_ref[h, :, HEAD_COLUMNS:]
-        other_parts = other_ref[0, :, HEAD_COLUMNS : HEAD_COLUMNS + HEAD_SIZE].astype(jnp.float32)
+        at = HEAD_COLUMNS
+        mine = own_ref[h, :, at : at + GROUP]
+        parts = other_ref[0, :, at : at + HEAD_SIZE].astype(jnp.float32)
+        theirs = parts[:, :GROUP] + parts[:, GROUP : 2 * GROUP] + parts[:, 2 * GROUP : 3 * GROUP]
+        peak = jnp.maximum(mine, theirs)
+        mine = jnp.exp2(mine - peak)
+        theirs = jnp.exp2(theirs - peak)
+        whole = mine + theirs
+        mine, theirs = mine / whole, theirs / whole
         for g in range(GROUP):
-            mine = own_level[:, g : g + 1]
-            theirs = (
-                other_parts[:, g : g + 1]
-                + other_parts[:, GROUP + g : GROUP + g + 1]
-                + other_parts[:, 2 * GROUP + g : 2 * GROUP + g + 1]
-            )
-            peak = jnp.maximum(mine, theirs)
-            mine = jnp.exp2(mine - peak)
-            theirs = jnp.exp2(theirs - peak)
-            whole = mine + theirs
             columns = slice(g * HEAD_SIZE, (g + 1) * HEAD_SIZE)
-            mixed = (mine / whole) * own_ref[h, :, columns] + (theirs / whole) * other_ref[0, :, columns].astype(
-                jnp.float32
-            )
-            out_ref[:, h * HEAD_COLUMNS + g * HEAD_SIZE : h * HEAD_COLUMNS + (g + 1) * HEAD_SIZE] = mixed.astype(
-                jnp.bfloat16
-            )
+            mixed = mine[:, g : g + 1] * own_ref[h, :, columns] + theirs[:, g : g + 1] * other_ref[
+                0, :, columns
+            ].astype(jnp.float32)
+            at = h * HEAD_COLUMNS + g * HEAD_SIZE
+            out_ref[:, at : at + HEAD_SIZE] = mixed.astype(jnp.bfloat16)
 
 
 def combine(where, own, other, own_pages):
@@ -554,7 +568,6 @@
     cached_row_lengths,
     block_target_page,
 ):
-    tp = lax.axis_index("tp")
     ctx = lax.axis_index("ctx")
     pool = lax.axis_index("pool")
     my_z, my_y = ctx // SIDE, ctx % SIDE
@@ -562,7 +575,6 @@
     prior_rings = ring(earlier_key_values)
 
     for_core, kept = project(
-        tp.astype(jnp.int32).reshape(1),
         row_adapter_index,
         prompt_adapter.reshape(1, TOKENS),
         span_hidden_states,

time: 93.6 us -> 92.7 us (level)
  transfers between devices with their start and end apart: 17 -> 17, of which waited for: 3 -> 3; matrix products, arithmetic and copies ran while one was open for 2% -> 2% of each run, Pallas kernels for 32% -> 33%
where the time goes in v9:
time: 92.7 us; the launch traced here: 92.4 us
  Pallas kernels  44.5 us (48%)
  starting transfers between devices  33.2 us (36%)
  waiting for transfers between devices  10.2 us (11%)
  other arithmetic  1.83 us (2%)
  between operations  1.49 us (2%)
  local copies, waits for them, and re-layouts  1.14 us (1%)
    pallas_call x5, Pallas kernels, attend(): pl.pallas_call(functools.partial(attend_kernel, heads, len(pieces), block...  29.7 us
    ppermute x12, starting transfers between devices, shift(): return lax.ppermute(x, 'ctx', perm)  24.5 us
    pallas_call x1, Pallas kernels, project(): pl.pallas_call(project_kernel, in_specs=[far] * 7, out_specs=[far] * 2, o...  8.63 us
    ppermute x12, waiting for transfers between devices, shift(): return lax.ppermute(x, 'ctx', perm)  7.46 us
    ppermute x3, starting transfers between devices, swap_pool(): return lax.ppermute(x, 'pool', [(0, 1), (1, 0)])  7.02 us
    pallas_call x1, Pallas kernels, decode_attend(): pl.pallas_call(decode_kernel, grid_spec=pltpu.PrefetchScalarGridSpec(num_...  2.85 us
    ppermute x2, waiting for transfers between devices, swap_tp(): return lax.ppermute(x, 'tp', [(i, i ^ bit) for i in range(4)])  2.73 us
    pallas_call x1, Pallas kernels, combine(): pl.pallas_call(combine_kernel, in_specs=[pl.BlockSpec(memory_space=pltpu....  2.42 us
  transfers between devices with their start and end apart: 17, of which 3 were waited for; matrix products, arithmetic and copies ran while one was open for 2% of the time, Pallas kernels for 33%

profile of v9, /device:TPU:0, one launch (start us, length us, event | category | flops | bytes accessed | tf_op | source)
XLA Modules:
  0.0 92.4 jit_solution(15544971512074131758)
XLA Ops:
  0.6 8.6 %project.1 = (f32[4,192,256]{2,1,0:T(8,128)}, f32[4,192,256]{2,1,0:T(8,128)}) custom-call(s32[16]{0:T(128)} %refs_4_.1, s32[1,128]{1,0:T(1,128)} %bitcast.40, bf16[128,2048]{1,0:T(8,128)(2,1)} %span_ref.1, bf16[16,4,2048]{2,1,0:T(4,128)(2,1)} %decode_ref.1, bf16[2048,2048]{1,0:T(8,128)(2,1)} %weight_ref.1, bf16[2048,128]{1,0:T(8,128)(2,1)} %down_ref.1, ...), custom_call_target="tpu_custom_call" | custom-call | flops 1100000000 | bytes 1048576 | tf_op jit(solution)/shard_map/project/pallas_call | solution.py:137
  9.4 4.0 %collective-permute-start = (bf16[2,128,256]{2,1,0:T(8,128)(2,1)S(1)}, bf16[2,128,256]{2,1,0:T(8,128)(2,1)S(1)}, u32[]{:S(2)}, u32[]{:S(2)}) collective-permute-start(bf16[2,128,256]{2,1,0:T(8,128)(2,1)S(1)} %copy-done.6), channel_id=1, source_target_pairs={{0,64},{8,72},{16,80},{24,88},{32,96},{40,104},{48,112},{56,120},{... | collective-permute-start | bytes 393224 | tf_op jit(solution)/shard_map/ppermute | solution.py:534
  13.6 1.4 %slice_add_fusion = (f32[2,192,256]{2,1,0:T(8,128)S(1)}, f32[2,192,256]{2,1,0:T(8,128)S(1)}) fusion(f32[4,192,256]{2,1,0:T(8,128)S(1)} %collective-permute-done.4, f32[4,192,256]{2,1,0:T(8,128)} %get-tuple-element.12), kind=kLoop, calls=%fused_computation | loop fusion | flops 196608 | bytes 2359296 | tf_op jit(solution)/shard_map/add | solution.py:587
  14.9 1.6 %collective-permute-start.5 = (f32[2,192,256]{2,1,0:T(8,128)S(1)}, f32[2,192,256]{2,1,0:T(8,128)S(1)}, u32[]{:S(2)}, u32[]{:S(2)}) collective-permute-start(f32[2,192,256]{2,1,0:T(8,128)S(1)} %get-tuple-element.21), channel_id=1, source_target_pairs={{0,2},{1,3},{2,0},{3,1},{4,6},{5,7},{6,4},{7,5},{8,10},{9,11},{10,... | collective-permute-start | bytes 1179656 | tf_op jit(solution)/shard_map/ppermute | solution.py:542
  17.5 1.7 %collective-permute-start.1 = (bf16[2,2,128,256]{3,2,1,0:T(8,128)(2,1)S(1)}, bf16[2,2,128,256]{3,2,1,0:T(8,128)(2,1)S(1)}, u32[]{:S(2)}, u32[]{:S(2)}) collective-permute-start(bf16[2,2,128,256]{3,2,1,0:T(8,128)(2,1)S(1)} %pad_maximum_fusion.refs_0_.known_ref.refs_2_), channel_id=1, source_target_pairs={{0,8},{8,16},{16,24},{24,0},{32,40},{40,48},{48,56},{56,32},{64,72... | collective-permute-start | bytes 786440 | tf_op jit(solution)/shard_map/ppermute | solution.py:534
  19.2 2.9 %collective-permute-start.2 = (bf16[2,2,128,256]{3,2,1,0:T(8,128)(2,1)S(1)}, bf16[2,2,128,256]{3,2,1,0:T(8,128)(2,1)S(1)}, u32[]{:S(2)}, u32[]{:S(2)}) collective-permute-start(bf16[2,2,128,256]{3,2,1,0:T(8,128)(2,1)S(1)} %pad_maximum_fusion.refs_0_.known_ref.refs_2_), channel_id=1, source_target_pairs={{0,16},{8,24},{16,0},{24,8},{32,48},{40,56},{48,32},{56,40},{64,80... | collective-permute-start | bytes 786440 | tf_op jit(solution)/shard_map/ppermute | solution.py:534
  22.1 1.3 %collective-permute-start.3 = (bf16[2,2,128,256]{3,2,1,0:T(8,128)(2,1)S(1)}, bf16[2,2,128,256]{3,2,1,0:T(8,128)(2,1)S(1)}, u32[]{:S(2)}, u32[]{:S(2)}) collective-permute-start(bf16[2,2,128,256]{3,2,1,0:T(8,128)(2,1)S(1)} %pad_maximum_fusion.refs_0_.known_ref.refs_2_), channel_id=1, source_target_pairs={{0,24},{8,0},{16,8},{24,16},{32,56},{40,32},{48,40},{56,48},{64,88... | collective-permute-start | bytes 786440 | tf_op jit(solution)/shard_map/ppermute | solution.py:534
  23.5 2.7 %collective-permute-done.5.chip_ref = f32[2,192,256]{2,1,0:T(8,128)S(1)} collective-permute-done((f32[2,192,256]{2,1,0:T(8,128)S(1)}, f32[2,192,256]{2,1,0:T(8,128)S(1)}, u32[]{:S(2)}, u32[]{:S(2)}) %collective-permute-start.5) | collective-permute-done | bytes 393248 | tf_op jit(solution)/shard_map/ppermute | solution.py:542
  27.0 2.3 %collective-permute-start.6 = (bf16[2,128,256]{2,1,0:T(8,128)(2,1)S(1)}, bf16[2,128,256]{2,1,0:T(8,128)(2,1)S(1)}, u32[]{:S(2)}, u32[]{:S(2)}) collective-permute-start(bf16[2,128,256]{2,1,0:T(8,128)(2,1)S(1)} %get-tuple-element.15), channel_id=1, source_target_pairs={{0,64},{8,72},{16,80},{24,88},{32,96},{40,104},{48,112},{56,120},{... | collective-permute-start | bytes 393224 | tf_op jit(solution)/shard_map/ppermute | solution.py:534
  30.0 3.1 %collective-permute-start.11 = (bf16[128,2048]{1,0:T(8,128)(2,1)}, bf16[128,2048]{1,0:T(8,128)(2,1)S(1)}, u32[]{:S(2)}, u32[]{:S(2)}) collective-permute-start(bf16[128,2048]{1,0:T(8,128)(2,1)} %get-tuple-element.16), channel_id=1, source_target_pairs={{0,4},{4,0},{1,5},{5,1},{2,6},{6,2},{3,7},{7,3},{8,12},{12,8},{9,1... | collective-permute-start | bytes 1572872 | tf_op jit(solution)/shard_map/ppermute | solution.py:538
  33.1 2.8 %decode.1.refs_4_ = bf16[16,4,2048]{2,1,0:T(4,128)(2,1)} custom-call(s32[16]{0:T(128)S(1)} %copy-done.3, s32[1]{0:T(128)S(6)} %copy.17.live_ref, bf16[16,4,2048]{2,1,0:T(4,128)(2,1)S(1)} %copy-done.2, bf16[16,2,256,256]{3,2,1,0:T(8,128)(2,1)S(1)} %copy-done, bf16[2,64,256]{2,1,0:T(8,128)(2,1)S(1)} %get-tuple-element.14.fresh_ref), custom_call_target="tpu_custom_call" | custom-call | flops 1100000000 | bytes 1048576 | tf_op jit(solution)/shard_map/decode/pallas_call | solution.py:492
  36.0 3.1 %collective-permute-start.10 = (bf16[2,2,128,256]{3,2,1,0:T(8,128)(2,1)S(1)}, bf16[2,2,128,256]{3,2,1,0:T(8,128)(2,1)S(1)}, u32[]{:S(2)}, u32[]{:S(2)}) collective-permute-start(bf16[2,2,128,256]{3,2,1,0:T(8,128)(2,1)S(1)} %pad_maximum_fusion.1.refs_5_.refs_0_.refs_6_.refs_2_), channel_id=1, source_target_pairs={{0,24},{8,0},{16,8},{24,16},{32,56},{40,32},{48,40},{56,48},{64,88... | collective-permute-start | bytes 786440 | tf_op jit(solution)/shard_map/ppermute | solution.py:534
  40.1 1.1 %collective-permute-start.7 = (bf16[4,2,128,256]{3,2,1,0:T(8,128)(2,1)S(1)}, bf16[4,2,128,256]{3,2,1,0:T(8,128)(2,1)}, u32[]{:S(2)}, u32[]{:S(2)}) collective-permute-start(bf16[4,2,128,256]{3,2,1,0:T(8,128)(2,1)S(1)} %stack.34), channel_id=1, source_target_pairs={{0,32},{8,40},{16,48},{24,56},{32,64},{40,72},{48,80},{56,88},{64,... | collective-permute-start | bytes 1572872 | tf_op jit(solution)/shard_map/ppermute | solution.py:534
  41.2 2.2 %collective-permute-start.14 = (bf16[4,2,128,256]{3,2,1,0:T(8,128)(2,1)S(1)}, bf16[4,2,128,256]{3,2,1,0:T(8,128)(2,1)}, u32[]{:S(2)}, u32[]{:S(2)}) collective-permute-start(bf16[4,2,128,256]{3,2,1,0:T(8,128)(2,1)S(1)} %stack.34), channel_id=1, source_target_pairs={{0,96},{8,104},{16,112},{24,120},{32,0},{40,8},{48,16},{56,24},{64... | collective-permute-start | bytes 1572872 | tf_op jit(solution)/shard_map/ppermute | solution.py:534
  43.7 2.5 %collective-permute-start.9 = (bf16[2,2,128,256]{3,2,1,0:T(8,128)(2,1)S(1)}, bf16[2,2,128,256]{3,2,1,0:T(8,128)(2,1)S(1)}, u32[]{:S(2)}, u32[]{:S(2)}) collective-permute-start(bf16[2,2,128,256]{3,2,1,0:T(8,128)(2,1)S(1)} %pad_maximum_fusion.1.refs_5_.refs_0_.refs_6_.refs_2_), channel_id=1, source_target_pairs={{0,16},{8,24},{16,0},{24,8},{32,48},{40,56},{48,32},{56,40},{64,80... | collective-permute-start | bytes 786440 | tf_op jit(solution)/shard_map/ppermute | solution.py:534
  46.2 3.7 %attend_first.2.refs_4_.refs_8_ = f32[2,1024,256]{2,1,0:T(8,128)S(1)} custom-call(s32[16]{0:T(128)S(1)} %reshape.348.visible_ref, bf16[128,2048]{1,0:T(8,128)(2,1)S(1)} %copy-done.5, bf16[2,2,128,256]{3,2,1,0:T(8,128)(2,1)S(1)} %pad_maximum_fusion.refs_0_.known_ref.refs_2_, bf16[2,2,128,256]{3,2,1,0:T(8,128)(2,1)S(1)} %pad_maximum_fusion.refs_0_.known_ref.refs_2_, ...), custom_call_target="tpu_custom_call" | custom-call | flops 3740000000 | bytes 1048576 | tf_op jit(solution)/shard_map/attend_first/pallas_call | solution.py:358
  49.9 6.7 %collective-permute-done.8.refs_1_.refs_7_.refs_6_.refs_3_ = bf16[2,2,128,256]{3,2,1,0:T(8,128)(2,1)S(1)} collective-permute-done((bf16[2,2,128,256]{3,2,1,0:T(8,128)(2,1)S(1)}, bf16[2,2,128,256]{3,2,1,0:T(8,128)(2,1)S(1)}, u32[]{:S(2)}, u32[]{:S(2)}) %collective-permute-start.8) | collective-permute-done | bytes 262176 | tf_op jit(solution)/shard_map/ppermute | solution.py:534
  56.7 3.2 %collective-permute-start.13 = (bf16[4,2,128,256]{3,2,1,0:T(8,128)(2,1)S(1)}, bf16[4,2,128,256]{3,2,1,0:T(8,128)(2,1)S(1)}, u32[]{:S(2)}, u32[]{:S(2)}) collective-permute-start(bf16[4,2,128,256]{3,2,1,0:T(8,128)(2,1)S(1)} %stack.35.refs_10_.refs_4_), channel_id=1, source_target_pairs={{0,96},{8,104},{16,112},{24,120},{32,0},{40,8},{48,16},{56,24},{64... | collective-permute-start | bytes 1572872 | tf_op jit(solution)/shard_map/ppermute | solution.py:534
  60.0 9.4 %attend_first.3.refs_2_ = f32[2,1024,256]{2,1,0:T(8,128)S(1)} custom-call(s32[16]{0:T(128)S(1)} %reshape.349.visible_ref, bf16[128,2048]{1,0:T(8,128)(2,1)S(1)} %collective-permute-done.11.refs_5_.q_ref, bf16[4,2,128,256]{3,2,1,0:T(8,128)(2,1)} %collective-permute-done.7.known_ref.refs_0_.refs_6_, ...), custom_call_target="tpu_custom_call" | custom-call | flops 11219999744 | bytes 1048576 | tf_op jit(solution)/shard_map/attend_first/pallas_call | solution.py:358
  69.4 3.2 %attend_last.3 = (bf16[1,128,1664]{2,1,0:T(8,128)(2,1)S(1)}, bf16[8,2,16,256]{3,2,1,0:T(8,128)(2,1)S(1)}) custom-call(s32[16]{0:T(128)S(1)} %reshape.349.visible_ref, bf16[128,2048]{1,0:T(8,128)(2,1)S(1)} %collective-permute-done.11.refs_5_.q_ref, bf16[4,2,128,256]{3,2,1,0:T(8,128)(2,1)} %collective-permute-done.7.known_ref.refs_0_.refs_6_, ...), custom_call_target="tpu_custom_call" | custom-call | flops 1870000000 | bytes 1048576 | tf_op jit(solution)/shard_map/attend_last/pallas_call | solution.py:358
  73.5 3.0 %attend_last.4.refs_9_ = bf16[1,128,1152]{2,1,0:T(8,128)(2,1)S(1)} custom-call(s32[16]{0:T(128)S(1)} %reshape.349.visible_ref, bf16[128,2048]{1,0:T(8,128)(2,1)S(1)} %collective-permute-done.11.refs_5_.q_ref, bf16[4,2,128,256]{3,2,1,0:T(8,128)(2,1)} %collective-permute-done.7.known_ref.refs_0_.refs_6_, ...), custom_call_target="tpu_custom_call" | custom-call | flops 1870000000 | bytes 1048576 | tf_op jit(solution)/shard_map/attend_last/pallas_call | solution.py:358
  76.5 3.1 %collective-permute-start.16 = (bf16[1,128,1152]{2,1,0:T(8,128)(2,1)S(1)}, bf16[1,128,1152]{2,1,0:T(8,128)(2,1)S(1)}, u32[]{:S(2)}, u32[]{:S(2)}) collective-permute-start(bf16[1,128,1152]{2,1,0:T(8,128)(2,1)S(1)} %attend_last.4.refs_9_), channel_id=1, source_target_pairs={{0,4},{4,0},{1,5},{5,1},{2,6},{6,2},{3,7},{7,3},{8,12},{12,8},{9,1... | collective-permute-start | bytes 884744 | tf_op jit(solution)/shard_map/ppermute | solution.py:538
  79.6 10.3 %attend_last.5.own_ref = f32[2,128,1152]{2,1,0:T(8,128)S(1)} custom-call(s32[16]{0:T(128)S(1)} %reshape.348.visible_ref, bf16[128,2048]{1,0:T(8,128)(2,1)S(1)} %copy-done.5, bf16[4,2,128,256]{3,2,1,0:T(8,128)(2,1)} %collective-permute-done.7.known_ref.refs_0_.refs_6_, bf16[4,2,128,256]{3,2,1,0:T(8,128)(2,1)S(1)} %collective-permute-done.12.refs_0_, ...), custom_call_target="tpu_custom_call" | custom-call | flops 11219999744 | bytes 1048576 | tf_op jit(solution)/shard_map/attend_last/pallas_call | solution.py:358
  90.0 2.4 %combine.1 = (bf16[128,2048]{1,0:T(8,128)(2,1)}, bf16[8,2,16,256]{3,2,1,0:T(8,128)(2,1)}) custom-call(s32[4,16]{1,0:T(4,128)S(1)} %pad_add_fusion.refs_3_.where_ref, f32[2,128,1152]{2,1,0:T(8,128)S(1)} %attend_last.5.own_ref, bf16[1,128,1664]{2,1,0:T(8,128)(2,1)S(1)} %collective-permute-done.15.first_ref, ...), custom_call_target="tpu_custom_call" | custom-call | flops 1100000000 | bytes 1048576 | tf_op jit(solution)/shard_map/combine/pallas_call | solution.py:415
  (50 shorter events, 4.4 us)
Async XLA Ops:
  0.6 8.8 %copy-start.6 = (bf16[2,128,256]{2,1,0:T(8,128)(2,1)S(1)}, bf16[2,128,256]{2,1,0:T(8,128)(2,1)}, u32[]{:S(2)}) copy-start(bf16[2,128,256]{2,1,0:T(8,128)(2,1)} %param.16) | copy-start | bytes 393220
  9.3 7.3 %copy-start.7 = (s32[256]{0:T(256)S(1)}, s32[256]{0:T(256)}, u32[]{:S(2)}) copy-start(s32[256]{0:T(256)} %param.27) | copy-start | bytes 3076
  9.3 16.9 %copy-start.5 = (bf16[128,2048]{1,0:T(8,128)(2,1)S(1)}, bf16[128,2048]{1,0:T(8,128)(2,1)}, u32[]{:S(2)}) copy-start(bf16[128,2048]{1,0:T(8,128)(2,1)} %q_ref.5) | copy-start | bytes 1572868
  9.3 4.2 %collective-permute-start.4 = (f32[4,192,256]{2,1,0:T(8,128)}, f32[4,192,256]{2,1,0:T(8,128)S(1)}, u32[]{:S(2)}, u32[]{:S(2)}) collective-permute-start(f32[4,192,256]{2,1,0:T(8,128)} %get-tuple-element.13), channel_id=1, source_target_pairs={{0,1},{1,0},{2,3},{3,2},{4,5},{5,4},{6,7},{7,6},{8,9},{9,8},{10,11... | collective-permute-start | bytes 2359304 | tf_op jit(solution)/shard_map/ppermute | solution.py:542
  9.4 8.1 %collective-permute-start = (bf16[2,128,256]{2,1,0:T(8,128)(2,1)S(1)}, bf16[2,128,256]{2,1,0:T(8,128)(2,1)S(1)}, u32[]{:S(2)}, u32[]{:S(2)}) collective-permute-start(bf16[2,128,256]{2,1,0:T(8,128)(2,1)S(1)} %copy-done.6), channel_id=1, source_target_pairs={{0,64},{8,72},{16,80},{24,88},{32,96},{40,104},{48,112},{56,120},{... | collective-permute-start | bytes 393224 | tf_op jit(solution)/shard_map/ppermute | solution.py:534
  13.5 19.6 %copy-start = (bf16[16,2,256,256]{3,2,1,0:T(8,128)(2,1)S(1)}, bf16[16,2,256,256]{3,2,1,0:T(8,128)(2,1)}, u32[]{:S(2)}) copy-start(bf16[16,2,256,256]{3,2,1,0:T(8,128)(2,1)} %cache_ref.1) | copy-start | bytes 12582916
  13.5 19.6 %copy-start.2 = (bf16[16,4,2048]{2,1,0:T(4,128)(2,1)S(1)}, bf16[16,4,2048]{2,1,0:T(4,128)(2,1)}, u32[]{:S(2)}) copy-start(bf16[16,4,2048]{2,1,0:T(4,128)(2,1)} %q_ref.3) | copy-start | bytes 786436
  13.5 19.6 %copy-start.3 = (s32[16]{0:T(128)S(1)}, s32[16]{0:T(128)}, u32[]{:S(2)}) copy-start(s32[16]{0:T(128)} %length_ref.1) | copy-start | bytes 196
  14.9 11.2 %collective-permute-start.5 = (f32[2,192,256]{2,1,0:T(8,128)S(1)}, f32[2,192,256]{2,1,0:T(8,128)S(1)}, u32[]{:S(2)}, u32[]{:S(2)}) collective-permute-start(f32[2,192,256]{2,1,0:T(8,128)S(1)} %get-tuple-element.21), channel_id=1, source_target_pairs={{0,2},{1,3},{2,0},{3,1},{4,6},{5,7},{6,4},{7,5},{8,10},{9,11},{10,... | collective-permute-start | bytes 1179656 | tf_op jit(solution)/shard_map/ppermute | solution.py:542
  17.5 21.5 %collective-permute-start.1 = (bf16[2,2,128,256]{3,2,1,0:T(8,128)(2,1)S(1)}, bf16[2,2,128,256]{3,2,1,0:T(8,128)(2,1)S(1)}, u32[]{:S(2)}, u32[]{:S(2)}) collective-permute-start(bf16[2,2,128,256]{3,2,1,0:T(8,128)(2,1)S(1)} %pad_maximum_fusion.refs_0_.known_ref.refs_2_), channel_id=1, source_target_pairs={{0,8},{8,16},{16,24},{24,0},{32,40},{40,48},{48,56},{56,32},{64,72... | collective-permute-start | bytes 786440 | tf_op jit(solution)/shard_map/ppermute | solution.py:534
  19.2 19.9 %collective-permute-start.2 = (bf16[2,2,128,256]{3,2,1,0:T(8,128)(2,1)S(1)}, bf16[2,2,128,256]{3,2,1,0:T(8,128)(2,1)S(1)}, u32[]{:S(2)}, u32[]{:S(2)}) collective-permute-start(bf16[2,2,128,256]{3,2,1,0:T(8,128)(2,1)S(1)} %pad_maximum_fusion.refs_0_.known_ref.refs_2_), channel_id=1, source_target_pairs={{0,16},{8,24},{16,0},{24,8},{32,48},{40,56},{48,32},{56,40},{64,80... | collective-permute-start | bytes 786440 | tf_op jit(solution)/shard_map/ppermute | solution.py:534
  22.1 17.0 %collective-permute-start.3 = (bf16[2,2,128,256]{3,2,1,0:T(8,128)(2,1)S(1)}, bf16[2,2,128,256]{3,2,1,0:T(8,128)(2,1)S(1)}, u32[]{:S(2)}, u32[]{:S(2)}) collective-permute-start(bf16[2,2,128,256]{3,2,1,0:T(8,128)(2,1)S(1)} %pad_maximum_fusion.refs_0_.known_ref.refs_2_), channel_id=1, source_target_pairs={{0,24},{8,0},{16,8},{24,16},{32,56},{40,32},{48,40},{56,48},{64,88... | collective-permute-start | bytes 786440 | tf_op jit(solution)/shard_map/ppermute | solution.py:534
  27.0 8.9 %collective-permute-start.6 = (bf16[2,128,256]{2,1,0:T(8,128)(2,1)S(1)}, bf16[2,128,256]{2,1,0:T(8,128)(2,1)S(1)}, u32[]{:S(2)}, u32[]{:S(2)}) collective-permute-start(bf16[2,128,256]{2,1,0:T(8,128)(2,1)S(1)} %get-tuple-element.15), channel_id=1, source_target_pairs={{0,64},{8,72},{16,80},{24,88},{32,96},{40,104},{48,112},{56,120},{... | collective-permute-start | bytes 393224 | tf_op jit(solution)/shard_map/ppermute | solution.py:534
  30.0 26.6 %collective-permute-start.11 = (bf16[128,2048]{1,0:T(8,128)(2,1)}, bf16[128,2048]{1,0:T(8,128)(2,1)S(1)}, u32[]{:S(2)}, u32[]{:S(2)}) collective-permute-start(bf16[128,2048]{1,0:T(8,128)(2,1)} %get-tuple-element.16), channel_id=1, source_target_pairs={{0,4},{4,0},{1,5},{5,1},{2,6},{6,2},{3,7},{7,3},{8,12},{12,8},{9,1... | collective-permute-start | bytes 1572872 | tf_op jit(solution)/shard_map/ppermute | solution.py:538
  36.0 10.3 %copy-start.4 = (s32[16]{0:T(128)S(1)}, s32[16]{0:T(128)}, u32[]{:S(2)}) copy-start(s32[16]{0:T(128)} %refs_4_.1) | copy-start | bytes 196
  36.0 7.7 %collective-permute-start.10 = (bf16[2,2,128,256]{3,2,1,0:T(8,128)(2,1)S(1)}, bf16[2,2,128,256]{3,2,1,0:T(8,128)(2,1)S(1)}, u32[]{:S(2)}, u32[]{:S(2)}) collective-permute-start(bf16[2,2,128,256]{3,2,1,0:T(8,128)(2,1)S(1)} %pad_maximum_fusion.1.refs_5_.refs_0_.refs_6_.refs_2_), channel_id=1, source_target_pairs={{0,24},{8,0},{16,8},{24,16},{32,56},{40,32},{48,40},{56,48},{64,88... | collective-permute-start | bytes 786440 | tf_op jit(solution)/shard_map/ppermute | solution.py:534
  40.1 19.9 %collective-permute-start.7 = (bf16[4,2,128,256]{3,2,1,0:T(8,128)(2,1)S(1)}, bf16[4,2,128,256]{3,2,1,0:T(8,128)(2,1)}, u32[]{:S(2)}, u32[]{:S(2)}) collective-permute-start(bf16[4,2,128,256]{3,2,1,0:T(8,128)(2,1)S(1)} %stack.34), channel_id=1, source_target_pairs={{0,32},{8,40},{16,48},{24,56},{32,64},{40,72},{48,80},{56,88},{64,... | collective-permute-start | bytes 1572872 | tf_op jit(solution)/shard_map/ppermute | solution.py:534
  41.2 18.8 %collective-permute-start.14 = (bf16[4,2,128,256]{3,2,1,0:T(8,128)(2,1)S(1)}, bf16[4,2,128,256]{3,2,1,0:T(8,128)(2,1)}, u32[]{:S(2)}, u32[]{:S(2)}) collective-permute-start(bf16[4,2,128,256]{3,2,1,0:T(8,128)(2,1)S(1)} %stack.34), channel_id=1, source_target_pairs={{0,96},{8,104},{16,112},{24,120},{32,0},{40,8},{48,16},{56,24},{64... | collective-permute-start | bytes 1572872 | tf_op jit(solution)/shard_map/ppermute | solution.py:534
  43.6 13.0 %collective-permute-start.8 = (bf16[2,2,128,256]{3,2,1,0:T(8,128)(2,1)S(1)}, bf16[2,2,128,256]{3,2,1,0:T(8,128)(2,1)S(1)}, u32[]{:S(2)}, u32[]{:S(2)}) collective-permute-start(bf16[2,2,128,256]{3,2,1,0:T(8,128)(2,1)S(1)} %pad_maximum_fusion.1.refs_5_.refs_0_.refs_6_.refs_2_), channel_id=1, source_target_pairs={{0,8},{8,16},{16,24},{24,0},{32,40},{40,48},{48,56},{56,32},{64,72... | collective-permute-start | bytes 786440 | tf_op jit(solution)/shard_map/ppermute | solution.py:534
  43.7 12.9 %collective-permute-start.9 = (bf16[2,2,128,256]{3,2,1,0:T(8,128)(2,1)S(1)}, bf16[2,2,128,256]{3,2,1,0:T(8,128)(2,1)S(1)}, u32[]{:S(2)}, u32[]{:S(2)}) collective-permute-start(bf16[2,2,128,256]{3,2,1,0:T(8,128)(2,1)S(1)} %pad_maximum_fusion.1.refs_5_.refs_0_.refs_6_.refs_2_), channel_id=1, source_target_pairs={{0,16},{8,24},{16,0},{24,8},{32,48},{40,56},{48,32},{56,40},{64,80... | collective-permute-start | bytes 786440 | tf_op jit(solution)/shard_map/ppermute | solution.py:534
  56.7 12.7 %collective-permute-start.12 = (bf16[4,2,128,256]{3,2,1,0:T(8,128)(2,1)S(1)}, bf16[4,2,128,256]{3,2,1,0:T(8,128)(2,1)S(1)}, u32[]{:S(2)}, u32[]{:S(2)}) collective-permute-start(bf16[4,2,128,256]{3,2,1,0:T(8,128)(2,1)S(1)} %stack.35.refs_10_.refs_4_), channel_id=1, source_target_pairs={{0,32},{8,40},{16,48},{24,56},{32,64},{40,72},{48,80},{56,88},{64,... | collective-permute-start | bytes 1572872 | tf_op jit(solution)/shard_map/ppermute | solution.py:534
  56.7 12.7 %collective-permute-start.13 = (bf16[4,2,128,256]{3,2,1,0:T(8,128)(2,1)S(1)}, bf16[4,2,128,256]{3,2,1,0:T(8,128)(2,1)S(1)}, u32[]{:S(2)}, u32[]{:S(2)}) collective-permute-start(bf16[4,2,128,256]{3,2,1,0:T(8,128)(2,1)S(1)} %stack.35.refs_10_.refs_4_), channel_id=1, source_target_pairs={{0,96},{8,104},{16,112},{24,120},{32,0},{40,8},{48,16},{56,24},{64... | collective-permute-start | bytes 1572872 | tf_op jit(solution)/shard_map/ppermute | solution.py:534
  72.7 17.3 %collective-permute-start.15 = (bf16[1,128,1664]{2,1,0:T(8,128)(2,1)S(1)}, bf16[1,128,1664]{2,1,0:T(8,128)(2,1)S(1)}, u32[]{:S(2)}, u32[]{:S(2)}) collective-permute-start(bf16[1,128,1664]{2,1,0:T(8,128)(2,1)S(1)} %get-tuple-element.17.refs_3_), channel_id=1, source_target_pairs={{0,4},{4,0},{1,5},{5,1},{2,6},{6,2},{3,7},{7,3},{8,12},{12,8},{9,1... | collective-permute-start | bytes 1277960 | tf_op jit(solution)/shard_map/ppermute | solution.py:538
  76.5 13.4 %collective-permute-start.16 = (bf16[1,128,1152]{2,1,0:T(8,128)(2,1)S(1)}, bf16[1,128,1152]{2,1,0:T(8,128)(2,1)S(1)}, u32[]{:S(2)}, u32[]{:S(2)}) collective-permute-start(bf16[1,128,1152]{2,1,0:T(8,128)(2,1)S(1)} %attend_last.4.refs_9_), channel_id=1, source_target_pairs={{0,4},{4,0},{1,5},{5,1},{2,6},{6,2},{3,7},{7,3},{8,12},{12,8},{9,1... | collective-permute-start | bytes 884744 | tf_op jit(solution)/shard_map/ppermute | solution.py:538
  (1 other events, 1.0 us)

commit v10 on v9

--- a/solution.py
+++ b/solution.py
@@ -38,7 +38,7 @@
     low = (rest - mid.astype(jnp.float32)).astype(jnp.bfloat16)
     return hi, mid, low
 
-PROJECT_US, ATTEND_US, DECODE_US = 1, 3.4, 1
+PROJECT_US, ATTEND_US, DECODE_US = 1, 0.3, 0.1
 ATTEND_VMEM, PROJECT_VMEM, DECODE_VMEM = 24, 56, 24
 
 
@@ -181,7 +181,7 @@
             jax.ShapeDtypeStruct(queries.shape, jnp.bfloat16),
         ],
         compiler_params=pltpu.CompilerParams(vmem_limit_bytes=8 * MIB),
-        cost_estimate=estimate(0.5),
+        cost_estimate=estimate(0.02),
         name="finish",
     )(own_sum, from_chip, queries, *after)
 
@@ -429,7 +429,8 @@
 ROW_BLOCK = 8
 
 
-def decode_kernel(length_ref, live_ref, q_ref, cache_ref, fresh_ref, out_ref):
+def decode_kernel(length_ref, live_ref, q_ref, cache_ref, fresh_ref, *refs):
+    out_ref = refs[-1]
     first = pl.program_id(0) * ROW_BLOCK
     query_rows = STEPS * GROUP
     rows = ROW_BLOCK * query_rows
@@ -486,7 +487,7 @@
                 out_ref[n, :, columns] = out[g * STEPS : (g + 1) * STEPS].astype(jnp.bfloat16)
 
 
-def decode_attend(lengths, live, queries, cache, fresh):
+def decode_attend(lengths, live, queries, cache, fresh, after):
     rows, heads, cache_size, _ = cache.shape
     block = pl.BlockSpec((ROW_BLOCK,) + queries.shape[1:], lambda i, *_: (i, 0, 0))
     return pl.pallas_call(
@@ -498,14 +499,15 @@
                 block,
                 pl.BlockSpec((ROW_BLOCK, heads, cache_size, WIDTH), lambda i, *_: (i, 0, 0, 0)),
                 pl.BlockSpec((heads, DECODE, WIDTH), lambda i, *_: (0, 0, 0)),
-            ],
+            ]
+            + [pl.BlockSpec(memory_space=pl.ANY)] * len(after),
             out_specs=block,
         ),
         out_shape=jax.ShapeDtypeStruct(queries.shape, jnp.bfloat16),
         compiler_params=pltpu.CompilerParams(vmem_limit_bytes=DECODE_VMEM * MIB),
         cost_estimate=estimate(DECODE_US),
         name="decode",
-    )(lengths, live, queries, cache, fresh)
+    )(lengths, live, queries, cache, fresh, *after)
 
 
 def stack_kernel(*refs):
@@ -522,7 +524,7 @@
         out_specs=local,
         out_shape=jax.ShapeDtypeStruct((SIDE,) + rings[0].shape[1:], jnp.bfloat16),
         compiler_params=pltpu.CompilerParams(vmem_limit_bytes=8 * MIB),
-        cost_estimate=estimate(0.5),
+        cost_estimate=estimate(0.02),
         name="stack",
     )(*rings, *after)
 
@@ -591,8 +593,18 @@
 
     rings = ring(span_kv)
 
+    prior_column = stack_column(prior_rings, (rings[0],))
+    prior_up, prior_down = sides(prior_column)
+
+    partner_queries = swap_pool(late_queries)
+
     decode_attention = decode_attend(
-        cached_row_lengths, group_live_rows, decode_token_queries, decode_row_cache, decode_kv
+        cached_row_lengths,
+        group_live_rows,
+        decode_token_queries,
+        decode_row_cache,
+        decode_kv,
+        (prior_column, partner_queries),
     )
 
     far = jnp.arange(SIDE, dtype=jnp.int32)
@@ -610,19 +622,17 @@
 
     beside = [(p, k, (1 + 2 * p) * SIDE + k) for p in range(2) for k in range(SIDE)]
     both = (0, 1)
-    partner_queries = swap_pool(late_queries)
     own_state = attend(
         own_sees,
         span_token_queries,
         prior_rings[0],
         prior_rings,
         (tuple(earlier_pairs(0)),),
-        row_adapter_index,
+        decode_attention,
         both,
     )
 
-    prior_up, prior_down = sides(stack_column(prior_rings, (decode_attention, rings[0])))
-    column = stack_column(rings, (own_state, partner_queries))
+    column = stack_column(rings, (own_state, partner_queries, decode_attention))
     up, down = sides(column)
     partner_state = attend(
         partner_sees,

time: 92.7 us -> 106 us (1.14)
  local copies, waits for them, and re-layouts: 1.14 us -> 13.9 us
  starting transfers between devices: 33.2 us -> 30.9 us
  Pallas kernels: 44.5 us -> 46.1 us
    unnamed x16 -> x56, local copies, waits for them, and re-layouts: 0.98 us -> 13.7 us
    ppermute x12, starting transfers between devices: 24.5 us -> 22.5 us  [shift(): return lax.ppermute(x, 'ctx', perm)]
    pallas_call x2, Pallas kernels: 0.07 us -> 1.81 us  [stack_column(): pl.pallas_call(stack_kernel, in_specs=[local] * SIDE + [pl.BlockSpec(memo...]
  transfers between devices with their start and end apart: 17 -> 17, of which waited for: 3 -> 3; matrix products, arithmetic and copies ran while one was open for 2% -> 1% of each run, Pallas kernels for 33% -> 30%
where the time goes in v10:
time: 106 us; the launch traced here: 105 us
  Pallas kernels  46.1 us (43%)
  starting transfers between devices  30.9 us (29%)
  local copies, waits for them, and re-layouts  13.9 us (13%)
  waiting for transfers between devices  10.6 us (10%)
  other arithmetic  1.69 us (2%)
  between operations  1.58 us (1%)
    pallas_call x5, Pallas kernels, attend(): pl.pallas_call(functools.partial(attend_kernel, heads, len(pieces), block...  29.6 us
    ppermute x12, starting transfers between devices, shift(): return lax.ppermute(x, 'ctx', perm)  22.5 us
    unnamed x56, local copies, waits for them, and re-layouts  13.7 us
    pallas_call x1, Pallas kernels, project(): pl.pallas_call(project_kernel, in_specs=[far] * 7, out_specs=[far] * 2, o...  8.64 us
    ppermute x12, waiting for transfers between devices, shift(): return lax.ppermute(x, 'ctx', perm)  8.13 us
    ppermute x3, starting transfers between devices, swap_pool(): return lax.ppermute(x, 'pool', [(0, 1), (1, 0)])  6.64 us
    pallas_call x1, Pallas kernels, decode_attend(): pl.pallas_call(decode_kernel, grid_spec=pltpu.PrefetchScalarGridSpec(num_...  2.85 us
    ppermute x2, waiting for transfers between devices, swap_tp(): return lax.ppermute(x, 'tp', [(i, i ^ bit) for i in range(4)])  2.49 us
  transfers between devices with their start and end apart: 17, of which 3 were waited for; matrix products, arithmetic and copies ran while one was open for 1% of the time, Pallas kernels for 30%

profile of v10, /device:TPU:0, one launch (start us, length us, event | category | flops | bytes accessed | tf_op | source)
XLA Modules:
  0.0 104.9 jit_solution(7642429134005503528)
XLA Ops:
  0.6 8.6 %project.1 = (f32[4,192,256]{2,1,0:T(8,128)}, f32[4,192,256]{2,1,0:T(8,128)}) custom-call(s32[16]{0:T(128)} %row_adapter_hbm.1, s32[1,128]{1,0:T(1,128)} %bitcast.40, bf16[128,2048]{1,0:T(8,128)(2,1)} %span_ref.1, bf16[16,4,2048]{2,1,0:T(4,128)(2,1)} %decode_ref.1, bf16[2048,2048]{1,0:T(8,128)(2,1)} %weight_ref.1, bf16[2048,128]{1,0:T(8,128)(2,1)} %down_ref.1, ...), custom_call_target="tpu_custom_call" | custom-call | flops 1100000000 | bytes 1048576 | tf_op jit(solution)/shard_map/project/pallas_call | solution.py:137
  9.4 2.5 %collective-permute-done.4 = f32[4,192,256]{2,1,0:T(8,128)S(1)} collective-permute-done((f32[4,192,256]{2,1,0:T(8,128)}, f32[4,192,256]{2,1,0:T(8,128)S(1)}, u32[]{:S(2)}, u32[]{:S(2)}) %collective-permute-start.4) | collective-permute-done | bytes 786464 | tf_op jit(solution)/shard_map/ppermute | solution.py:544
  11.9 1.2 %slice_add_fusion = (f32[2,192,256]{2,1,0:T(8,128)S(1)}, f32[2,192,256]{2,1,0:T(8,128)S(1)}) fusion(f32[4,192,256]{2,1,0:T(8,128)S(1)} %collective-permute-done.4, f32[4,192,256]{2,1,0:T(8,128)} %get-tuple-element.12), kind=kLoop, calls=%fused_computation | loop fusion | flops 196608 | bytes 2359296 | tf_op jit(solution)/shard_map/add | solution.py:589
  13.1 1.7 %collective-permute-start.5 = (f32[2,192,256]{2,1,0:T(8,128)S(1)}, f32[2,192,256]{2,1,0:T(8,128)S(1)}, u32[]{:S(2)}, u32[]{:S(2)}) collective-permute-start(f32[2,192,256]{2,1,0:T(8,128)S(1)} %get-tuple-element.21), channel_id=1, source_target_pairs={{0,2},{1,3},{2,0},{3,1},{4,6},{5,7},{6,4},{7,5},{8,10},{9,11},{10,... | collective-permute-start | bytes 1179656 | tf_op jit(solution)/shard_map/ppermute | solution.py:544
  14.8 3.9 %collective-permute-start = (bf16[2,128,256]{2,1,0:T(8,128)(2,1)S(1)}, bf16[2,128,256]{2,1,0:T(8,128)(2,1)S(1)}, u32[]{:S(2)}, u32[]{:S(2)}) collective-permute-start(bf16[2,128,256]{2,1,0:T(8,128)(2,1)S(1)} %copy-done.26), channel_id=1, source_target_pairs={{0,64},{8,72},{16,80},{24,88},{32,96},{40,104},{48,112},{56,120},{... | collective-permute-start | bytes 393224 | tf_op jit(solution)/shard_map/ppermute | solution.py:536
  18.7 3.5 %collective-permute-done = bf16[2,128,256]{2,1,0:T(8,128)(2,1)S(1)} collective-permute-done((bf16[2,128,256]{2,1,0:T(8,128)(2,1)S(1)}, bf16[2,128,256]{2,1,0:T(8,128)(2,1)S(1)}, u32[]{:S(2)}, u32[]{:S(2)}) %collective-permute-start) | collective-permute-done | bytes 131104 | tf_op jit(solution)/shard_map/ppermute | solution.py:536
  22.2 1.7 %collective-permute-start.1 = (bf16[2,2,128,256]{3,2,1,0:T(8,128)(2,1)S(1)}, bf16[2,2,128,256]{3,2,1,0:T(8,128)(2,1)S(1)}, u32[]{:S(2)}, u32[]{:S(2)}) collective-permute-start(bf16[2,2,128,256]{3,2,1,0:T(8,128)(2,1)S(1)} %pad_maximum_fusion.refs_0_.known_ref.refs_2_), channel_id=1, source_target_pairs={{0,8},{8,16},{16,24},{24,0},{32,40},{40,48},{48,56},{56,32},{64,72... | collective-permute-start | bytes 786440 | tf_op jit(solution)/shard_map/ppermute | solution.py:536
  23.9 2.9 %collective-permute-start.2 = (bf16[2,2,128,256]{3,2,1,0:T(8,128)(2,1)S(1)}, bf16[2,2,128,256]{3,2,1,0:T(8,128)(2,1)S(1)}, u32[]{:S(2)}, u32[]{:S(2)}) collective-permute-start(bf16[2,2,128,256]{3,2,1,0:T(8,128)(2,1)S(1)} %pad_maximum_fusion.refs_0_.known_ref.refs_2_), channel_id=1, source_target_pairs={{0,16},{8,24},{16,0},{24,8},{32,48},{40,56},{48,32},{56,40},{64,80... | collective-permute-start | bytes 786440 | tf_op jit(solution)/shard_map/ppermute | solution.py:536
  27.6 3.2 %collective-permute-start.6 = (bf16[2,128,256]{2,1,0:T(8,128)(2,1)S(1)}, bf16[2,128,256]{2,1,0:T(8,128)(2,1)S(1)}, u32[]{:S(2)}, u32[]{:S(2)}) collective-permute-start(bf16[2,128,256]{2,1,0:T(8,128)(2,1)S(1)} %get-tuple-element.14), channel_id=1, source_target_pairs={{0,64},{8,72},{16,80},{24,88},{32,96},{40,104},{48,112},{56,120},{... | collective-permute-start | bytes 393224 | tf_op jit(solution)/shard_map/ppermute | solution.py:536
  30.9 2.7 %collective-permute-start.11 = (bf16[128,2048]{1,0:T(8,128)(2,1)}, bf16[128,2048]{1,0:T(8,128)(2,1)S(1)}, u32[]{:S(2)}, u32[]{:S(2)}) collective-permute-start(bf16[128,2048]{1,0:T(8,128)(2,1)} %get-tuple-element.16), channel_id=1, source_target_pairs={{0,4},{4,0},{1,5},{5,1},{2,6},{6,2},{3,7},{7,3},{8,12},{12,8},{9,1... | collective-permute-start | bytes 1572872 | tf_op jit(solution)/shard_map/ppermute | solution.py:540
  34.4 1.7 %collective-permute-start.3 = (bf16[2,2,128,256]{3,2,1,0:T(8,128)(2,1)S(1)}, bf16[2,2,128,256]{3,2,1,0:T(8,128)(2,1)S(1)}, u32[]{:S(2)}, u32[]{:S(2)}) collective-permute-start(bf16[2,2,128,256]{3,2,1,0:T(8,128)(2,1)S(1)} %pad_maximum_fusion.refs_0_.known_ref.refs_2_), channel_id=1, source_target_pairs={{0,24},{8,0},{16,8},{24,16},{32,56},{40,32},{48,40},{56,48},{64,88... | collective-permute-start | bytes 786440 | tf_op jit(solution)/shard_map/ppermute | solution.py:536
  37.0 1.3 %collective-permute-start.8 = (bf16[2,2,128,256]{3,2,1,0:T(8,128)(2,1)S(1)}, bf16[2,2,128,256]{3,2,1,0:T(8,128)(2,1)S(1)}, u32[]{:S(2)}, u32[]{:S(2)}) collective-permute-start(bf16[2,2,128,256]{3,2,1,0:T(8,128)(2,1)S(1)} %pad_maximum_fusion.1.refs_4_.refs_0_.refs_6_.refs_5_.refs_2_), channel_id=1, source_target_pairs={{0,8},{8,16},{16,24},{24,0},{32,40},{40,48},{48,56},{56,32},{64,72... | collective-permute-start | bytes 786440 | tf_op jit(solution)/shard_map/ppermute | solution.py:536
  39.1 4.6 %collective-permute-done.3.refs_3_.refs_5_ = bf16[2,2,128,256]{3,2,1,0:T(8,128)(2,1)S(1)} collective-permute-done((bf16[2,2,128,256]{3,2,1,0:T(8,128)(2,1)S(1)}, bf16[2,2,128,256]{3,2,1,0:T(8,128)(2,1)S(1)}, u32[]{:S(2)}, u32[]{:S(2)}) %collective-permute-start.3) | collective-permute-done | bytes 262176 | tf_op jit(solution)/shard_map/ppermute | solution.py:536
  45.7 2.2 %collective-permute-start.14 = (bf16[4,2,128,256]{3,2,1,0:T(8,128)(2,1)}, bf16[4,2,128,256]{3,2,1,0:T(8,128)(2,1)}, u32[]{:S(2)}, u32[]{:S(2)}) collective-permute-start(bf16[4,2,128,256]{3,2,1,0:T(8,128)(2,1)} %stack.34.refs_0_), channel_id=1, source_target_pairs={{0,96},{8,104},{16,112},{24,120},{32,0},{40,8},{48,16},{56,24},{64... | collective-permute-start | bytes 1572872 | tf_op jit(solution)/shard_map/ppermute | solution.py:536
  47.9 2.2 %copy-done.14 = bf16[16,2,256,256]{3,2,1,0:T(8,128)(2,1)S(1)} copy-done((bf16[16,2,256,256]{3,2,1,0:T(8,128)(2,1)S(1)}, bf16[16,2,256,256]{3,2,1,0:T(8,128)(2,1)}, u32[]{:S(2)}) %copy-start.14) | copy-done | bytes 4194328
  51.0 2.8 %decode.1.refs_4_.refs_6_ = bf16[16,4,2048]{2,1,0:T(4,128)(2,1)} custom-call(s32[16]{0:T(128)S(1)} %copy-done.25, s32[1]{0:T(128)S(6)} %copy.17.live_ref, bf16[16,4,2048]{2,1,0:T(4,128)(2,1)S(1)} %copy-done.24, bf16[16,2,256,256]{3,2,1,0:T(8,128)(2,1)S(1)} %copy-done.14, bf16[2,64,256]{2,1,0:T(8,128)(2,1)S(1)} %get-tuple-element.15.fresh_ref, ...), custom_call_target="tpu_custom_call" | custom-call | flops 110000000 | bytes 1048576 | tf_op jit(solution)/shard_map/decode/pallas_call | solution.py:493
  57.7 3.7 %attend_first.2.refs_4_.refs_8_ = f32[2,1024,256]{2,1,0:T(8,128)S(1)} custom-call(s32[16]{0:T(128)S(1)} %reshape.348.visible_ref, bf16[128,2048]{1,0:T(8,128)(2,1)S(1)} %copy-done.4, bf16[2,2,128,256]{3,2,1,0:T(8,128)(2,1)S(1)} %copy-done.1, bf16[2,2,128,256]{3,2,1,0:T(8,128)(2,1)S(1)} %copy-done.1, bf16[2,2,128,256]{3,2,1,0:T(8,128)(2,1)S(1)} %copy-done.16, ...), custom_call_target="tpu_custom_call" | custom-call | flops 330000000 | bytes 1048576 | tf_op jit(solution)/shard_map/attend_first/pallas_call | solution.py:358
  62.5 3.2 %collective-permute-start.13 = (bf16[4,2,128,256]{3,2,1,0:T(8,128)(2,1)}, bf16[4,2,128,256]{3,2,1,0:T(8,128)(2,1)}, u32[]{:S(2)}, u32[]{:S(2)}) collective-permute-start(bf16[4,2,128,256]{3,2,1,0:T(8,128)(2,1)} %stack.35.refs_10_.refs_4_), channel_id=1, source_target_pairs={{0,96},{8,104},{16,112},{24,120},{32,0},{40,8},{48,16},{56,24},{64... | collective-permute-start | bytes 1572872 | tf_op jit(solution)/shard_map/ppermute | solution.py:536
  72.5 9.1 %attend_first.3.refs_2_ = f32[2,1024,256]{2,1,0:T(8,128)S(1)} custom-call(s32[16]{0:T(128)S(1)} %reshape.349.visible_ref, bf16[128,2048]{1,0:T(8,128)(2,1)S(1)} %collective-permute-done.11.refs_1_.refs_5_.q_ref, bf16[4,2,128,256]{3,2,1,0:T(8,128)(2,1)S(1)} %collective-permute-done.7.known_ref.refs_0_.refs_6_, ...), custom_call_target="tpu_custom_call" | custom-call | flops 990000000 | bytes 1048576 | tf_op jit(solution)/shard_map/attend_first/pallas_call | solution.py:358
  81.7 3.5 %attend_last.3 = (bf16[1,128,1664]{2,1,0:T(8,128)(2,1)S(1)}, bf16[8,2,16,256]{3,2,1,0:T(8,128)(2,1)S(1)}) custom-call(s32[16]{0:T(128)S(1)} %reshape.349.visible_ref, bf16[128,2048]{1,0:T(8,128)(2,1)S(1)} %collective-permute-done.11.refs_1_.refs_5_.q_ref, bf16[4,2,128,256]{3,2,1,0:T(8,128)(2,1)S(1)} %collective-permute-done.7.known_ref.refs_0_.refs_6_, ...), custom_call_target="tpu_custom_call" | custom-call | flops 165000000 | bytes 1048576 | tf_op jit(solution)/shard_map/attend_last/pallas_call | solution.py:358
  86.3 3.2 %attend_last.4.refs_9_ = bf16[1,128,1152]{2,1,0:T(8,128)(2,1)S(1)} custom-call(s32[16]{0:T(128)S(1)} %reshape.349.visible_ref, bf16[128,2048]{1,0:T(8,128)(2,1)S(1)} %collective-permute-done.11.refs_1_.refs_5_.q_ref, bf16[4,2,128,256]{3,2,1,0:T(8,128)(2,1)S(1)} %collective-permute-done.7.known_ref.refs_0_.refs_6_, ...), custom_call_target="tpu_custom_call" | custom-call | flops 165000000 | bytes 1048576 | tf_op jit(solution)/shard_map/attend_last/pallas_call | solution.py:358
  89.5 2.8 %collective-permute-start.16 = (bf16[1,128,1152]{2,1,0:T(8,128)(2,1)S(1)}, bf16[1,128,1152]{2,1,0:T(8,128)(2,1)S(1)}, u32[]{:S(2)}, u32[]{:S(2)}) collective-permute-start(bf16[1,128,1152]{2,1,0:T(8,128)(2,1)S(1)} %attend_last.4.refs_9_), channel_id=1, source_target_pairs={{0,4},{4,0},{1,5},{5,1},{2,6},{6,2},{3,7},{7,3},{8,12},{12,8},{9,1... | collective-permute-start | bytes 884744 | tf_op jit(solution)/shard_map/ppermute | solution.py:540
  92.3 10.1 %attend_last.5.own_ref = f32[2,128,1152]{2,1,0:T(8,128)S(1)} custom-call(s32[16]{0:T(128)S(1)} %reshape.348.visible_ref, bf16[128,2048]{1,0:T(8,128)(2,1)S(1)} %copy-done.5, bf16[4,2,128,256]{3,2,1,0:T(8,128)(2,1)S(1)} %collective-permute-done.7.known_ref.refs_0_.refs_6_, bf16[4,2,128,256]{3,2,1,0:T(8,128)(2,1)} %collective-permute-done.12.refs_0_, ...), custom_call_target="tpu_custom_call" | custom-call | flops 990000000 | bytes 1048576 | tf_op jit(solution)/shard_map/attend_last/pallas_call | solution.py:358
  102.4 2.4 %combine.1 = (bf16[128,2048]{1,0:T(8,128)(2,1)}, bf16[8,2,16,256]{3,2,1,0:T(8,128)(2,1)}) custom-call(s32[4,16]{1,0:T(4,128)S(1)} %pad_add_fusion.refs_3_.where_ref, f32[2,128,1152]{2,1,0:T(8,128)S(1)} %attend_last.5.own_ref, bf16[1,128,1664]{2,1,0:T(8,128)(2,1)S(1)} %collective-permute-done.15.first_ref, ...), custom_call_target="tpu_custom_call" | custom-call | flops 1100000000 | bytes 1048576 | tf_op jit(solution)/shard_map/combine/pallas_call | solution.py:415
  (90 shorter events, 18.5 us)
Async XLA Ops:
  9.3 17.5 %copy-start.3 = (bf16[128,2048]{1,0:T(8,128)(2,1)S(1)}, bf16[128,2048]{1,0:T(8,128)(2,1)}, u32[]{:S(2)}) copy-start(bf16[128,2048]{1,0:T(8,128)(2,1)} %q_ref.5) | copy-start | bytes 1572868
  9.3 2.6 %collective-permute-start.4 = (f32[4,192,256]{2,1,0:T(8,128)}, f32[4,192,256]{2,1,0:T(8,128)S(1)}, u32[]{:S(2)}, u32[]{:S(2)}) collective-permute-start(f32[4,192,256]{2,1,0:T(8,128)} %get-tuple-element.13), channel_id=1, source_target_pairs={{0,1},{1,0},{2,3},{3,2},{4,5},{5,4},{6,7},{7,6},{8,9},{9,8},{10,11... | collective-permute-start | bytes 2359304 | tf_op jit(solution)/shard_map/ppermute | solution.py:544
  11.9 27.1 %copy-start.27 = (s32[256]{0:T(256)S(1)}, s32[256]{0:T(256)}, u32[]{:S(2)}) copy-start(s32[256]{0:T(256)} %param.27) | copy-start | bytes 3076
  13.1 13.7 %collective-permute-start.5 = (f32[2,192,256]{2,1,0:T(8,128)S(1)}, f32[2,192,256]{2,1,0:T(8,128)S(1)}, u32[]{:S(2)}, u32[]{:S(2)}) collective-permute-start(f32[2,192,256]{2,1,0:T(8,128)S(1)} %get-tuple-element.21), channel_id=1, source_target_pairs={{0,2},{1,3},{2,0},{3,1},{4,6},{5,7},{6,4},{7,5},{8,10},{9,11},{10,... | collective-permute-start | bytes 1179656 | tf_op jit(solution)/shard_map/ppermute | solution.py:544
  14.8 7.4 %collective-permute-start = (bf16[2,128,256]{2,1,0:T(8,128)(2,1)S(1)}, bf16[2,128,256]{2,1,0:T(8,128)(2,1)S(1)}, u32[]{:S(2)}, u32[]{:S(2)}) collective-permute-start(bf16[2,128,256]{2,1,0:T(8,128)(2,1)S(1)} %copy-done.26), channel_id=1, source_target_pairs={{0,64},{8,72},{16,80},{24,88},{32,96},{40,104},{48,112},{56,120},{... | collective-permute-start | bytes 393224 | tf_op jit(solution)/shard_map/ppermute | solution.py:536
  22.2 25.7 %copy-start = (bf16[2,2,128,256]{3,2,1,0:T(8,128)(2,1)}, bf16[2,2,128,256]{3,2,1,0:T(8,128)(2,1)S(1)}, u32[]{:S(2)}) copy-start(bf16[2,2,128,256]{3,2,1,0:T(8,128)(2,1)S(1)} %pad_maximum_fusion.refs_0_.known_ref.refs_2_) | copy-start | bytes 786436
  22.2 25.7 %copy-start.25 = (s32[16]{0:T(128)S(1)}, s32[16]{0:T(128)}, u32[]{:S(2)}) copy-start(s32[16]{0:T(128)} %length_ref.1) | copy-start | bytes 196
  22.2 14.7 %collective-permute-start.1 = (bf16[2,2,128,256]{3,2,1,0:T(8,128)(2,1)S(1)}, bf16[2,2,128,256]{3,2,1,0:T(8,128)(2,1)S(1)}, u32[]{:S(2)}, u32[]{:S(2)}) collective-permute-start(bf16[2,2,128,256]{3,2,1,0:T(8,128)(2,1)S(1)} %pad_maximum_fusion.refs_0_.known_ref.refs_2_), channel_id=1, source_target_pairs={{0,8},{8,16},{16,24},{24,0},{32,40},{40,48},{48,56},{56,32},{64,72... | collective-permute-start | bytes 786440 | tf_op jit(solution)/shard_map/ppermute | solution.py:536
  23.9 14.4 %collective-permute-start.2 = (bf16[2,2,128,256]{3,2,1,0:T(8,128)(2,1)S(1)}, bf16[2,2,128,256]{3,2,1,0:T(8,128)(2,1)S(1)}, u32[]{:S(2)}, u32[]{:S(2)}) collective-permute-start(bf16[2,2,128,256]{3,2,1,0:T(8,128)(2,1)S(1)} %pad_maximum_fusion.refs_0_.known_ref.refs_2_), channel_id=1, source_target_pairs={{0,16},{8,24},{16,0},{24,8},{32,48},{40,56},{48,32},{56,40},{64,80... | collective-permute-start | bytes 786440 | tf_op jit(solution)/shard_map/ppermute | solution.py:536
  27.6 8.5 %collective-permute-start.6 = (bf16[2,128,256]{2,1,0:T(8,128)(2,1)S(1)}, bf16[2,128,256]{2,1,0:T(8,128)(2,1)S(1)}, u32[]{:S(2)}, u32[]{:S(2)}) collective-permute-start(bf16[2,128,256]{2,1,0:T(8,128)(2,1)S(1)} %get-tuple-element.14), channel_id=1, source_target_pairs={{0,64},{8,72},{16,80},{24,88},{32,96},{40,104},{48,112},{56,120},{... | collective-permute-start | bytes 393224 | tf_op jit(solution)/shard_map/ppermute | solution.py:536
  30.9 14.8 %collective-permute-start.11 = (bf16[128,2048]{1,0:T(8,128)(2,1)}, bf16[128,2048]{1,0:T(8,128)(2,1)S(1)}, u32[]{:S(2)}, u32[]{:S(2)}) collective-permute-start(bf16[128,2048]{1,0:T(8,128)(2,1)} %get-tuple-element.16), channel_id=1, source_target_pairs={{0,4},{4,0},{1,5},{5,1},{2,6},{6,2},{3,7},{7,3},{8,12},{12,8},{9,1... | collective-permute-start | bytes 1572872 | tf_op jit(solution)/shard_map/ppermute | solution.py:540
  34.4 9.3 %collective-permute-start.3 = (bf16[2,2,128,256]{3,2,1,0:T(8,128)(2,1)S(1)}, bf16[2,2,128,256]{3,2,1,0:T(8,128)(2,1)S(1)}, u32[]{:S(2)}, u32[]{:S(2)}) collective-permute-start(bf16[2,2,128,256]{3,2,1,0:T(8,128)(2,1)S(1)} %pad_maximum_fusion.refs_0_.known_ref.refs_2_), channel_id=1, source_target_pairs={{0,24},{8,0},{16,8},{24,16},{32,56},{40,32},{48,40},{56,48},{64,88... | collective-permute-start | bytes 786440 | tf_op jit(solution)/shard_map/ppermute | solution.py:536
  36.1 25.2 %collective-permute-start.10 = (bf16[2,2,128,256]{3,2,1,0:T(8,128)(2,1)S(1)}, bf16[2,2,128,256]{3,2,1,0:T(8,128)(2,1)S(1)}, u32[]{:S(2)}, u32[]{:S(2)}) collective-permute-start(bf16[2,2,128,256]{3,2,1,0:T(8,128)(2,1)S(1)} %pad_maximum_fusion.1.refs_4_.refs_0_.refs_6_.refs_5_.refs_2_), channel_id=1, source_target_pairs={{0,24},{8,0},{16,8},{24,16},{32,56},{40,32},{48,40},{56,48},{64,88... | collective-permute-start | bytes 786440 | tf_op jit(solution)/shard_map/ppermute | solution.py:536
  37.0 10.9 %copy-start.15 = (bf16[2,2,128,256]{3,2,1,0:T(8,128)(2,1)}, bf16[2,2,128,256]{3,2,1,0:T(8,128)(2,1)S(1)}, u32[]{:S(2)}) copy-start(bf16[2,2,128,256]{3,2,1,0:T(8,128)(2,1)S(1)} %collective-permute-done.1.refs_1_.refs_3_) | copy-start | bytes 786436
  37.0 24.4 %collective-permute-start.8 = (bf16[2,2,128,256]{3,2,1,0:T(8,128)(2,1)S(1)}, bf16[2,2,128,256]{3,2,1,0:T(8,128)(2,1)S(1)}, u32[]{:S(2)}, u32[]{:S(2)}) collective-permute-start(bf16[2,2,128,256]{3,2,1,0:T(8,128)(2,1)S(1)} %pad_maximum_fusion.1.refs_4_.refs_0_.refs_6_.refs_5_.refs_2_), channel_id=1, source_target_pairs={{0,8},{8,16},{16,24},{24,0},{32,40},{40,48},{48,56},{56,32},{64,72... | collective-permute-start | bytes 786440 | tf_op jit(solution)/shard_map/ppermute | solution.py:536
  38.2 9.6 %copy-start.18 = (bf16[2,2,128,256]{3,2,1,0:T(8,128)(2,1)}, bf16[2,2,128,256]{3,2,1,0:T(8,128)(2,1)S(1)}, u32[]{:S(2)}) copy-start(bf16[2,2,128,256]{3,2,1,0:T(8,128)(2,1)S(1)} %collective-permute-done.2.refs_2_.refs_4_) | copy-start | bytes 786436
  38.2 23.2 %collective-permute-start.9 = (bf16[2,2,128,256]{3,2,1,0:T(8,128)(2,1)S(1)}, bf16[2,2,128,256]{3,2,1,0:T(8,128)(2,1)S(1)}, u32[]{:S(2)}, u32[]{:S(2)}) collective-permute-start(bf16[2,2,128,256]{3,2,1,0:T(8,128)(2,1)S(1)} %pad_maximum_fusion.1.refs_4_.refs_0_.refs_6_.refs_5_.refs_2_), channel_id=1, source_target_pairs={{0,16},{8,24},{16,0},{24,8},{32,48},{40,56},{48,32},{56,40},{64,80... | collective-permute-start | bytes 786440 | tf_op jit(solution)/shard_map/ppermute | solution.py:536
  43.8 10.1 %copy-start.22 = (bf16[2,2,128,256]{3,2,1,0:T(8,128)(2,1)}, bf16[2,2,128,256]{3,2,1,0:T(8,128)(2,1)S(1)}, u32[]{:S(2)}) copy-start(bf16[2,2,128,256]{3,2,1,0:T(8,128)(2,1)S(1)} %collective-permute-done.3.refs_3_.refs_5_) | copy-start | bytes 786436
  44.6 21.2 %collective-permute-start.7 = (bf16[4,2,128,256]{3,2,1,0:T(8,128)(2,1)}, bf16[4,2,128,256]{3,2,1,0:T(8,128)(2,1)S(1)}, u32[]{:S(2)}, u32[]{:S(2)}) collective-permute-start(bf16[4,2,128,256]{3,2,1,0:T(8,128)(2,1)} %stack.34.refs_0_), channel_id=1, source_target_pairs={{0,32},{8,40},{16,48},{24,56},{32,64},{40,72},{48,80},{56,88},{64,... | collective-permute-start | bytes 1572872 | tf_op jit(solution)/shard_map/ppermute | solution.py:536
  45.7 20.2 %collective-permute-start.14 = (bf16[4,2,128,256]{3,2,1,0:T(8,128)(2,1)}, bf16[4,2,128,256]{3,2,1,0:T(8,128)(2,1)}, u32[]{:S(2)}, u32[]{:S(2)}) collective-permute-start(bf16[4,2,128,256]{3,2,1,0:T(8,128)(2,1)} %stack.34.refs_0_), channel_id=1, source_target_pairs={{0,96},{8,104},{16,112},{24,120},{32,0},{40,8},{48,16},{56,24},{64... | collective-permute-start | bytes 1572872 | tf_op jit(solution)/shard_map/ppermute | solution.py:536
  62.4 19.2 %collective-permute-start.12 = (bf16[4,2,128,256]{3,2,1,0:T(8,128)(2,1)}, bf16[4,2,128,256]{3,2,1,0:T(8,128)(2,1)}, u32[]{:S(2)}, u32[]{:S(2)}) collective-permute-start(bf16[4,2,128,256]{3,2,1,0:T(8,128)(2,1)} %stack.35.refs_10_.refs_4_), channel_id=1, source_target_pairs={{0,32},{8,40},{16,48},{24,56},{32,64},{40,72},{48,80},{56,88},{64,... | collective-permute-start | bytes 1572872 | tf_op jit(solution)/shard_map/ppermute | solution.py:536
  62.5 19.2 %collective-permute-start.13 = (bf16[4,2,128,256]{3,2,1,0:T(8,128)(2,1)}, bf16[4,2,128,256]{3,2,1,0:T(8,128)(2,1)}, u32[]{:S(2)}, u32[]{:S(2)}) collective-permute-start(bf16[4,2,128,256]{3,2,1,0:T(8,128)(2,1)} %stack.35.refs_10_.refs_4_), channel_id=1, source_target_pairs={{0,96},{8,104},{16,112},{24,120},{32,0},{40,8},{48,16},{56,24},{64... | collective-permute-start | bytes 1572872 | tf_op jit(solution)/shard_map/ppermute | solution.py:536
  85.2 17.2 %collective-permute-start.15 = (bf16[1,128,1664]{2,1,0:T(8,128)(2,1)S(1)}, bf16[1,128,1664]{2,1,0:T(8,128)(2,1)S(1)}, u32[]{:S(2)}, u32[]{:S(2)}) collective-permute-start(bf16[1,128,1664]{2,1,0:T(8,128)(2,1)S(1)} %get-tuple-element.17.refs_3_), channel_id=1, source_target_pairs={{0,4},{4,0},{1,5},{5,1},{2,6},{6,2},{3,7},{7,3},{8,12},{12,8},{9,1... | collective-permute-start | bytes 1277960 | tf_op jit(solution)/shard_map/ppermute | solution.py:540
  89.5 12.9 %collective-permute-start.16 = (bf16[1,128,1152]{2,1,0:T(8,128)(2,1)S(1)}, bf16[1,128,1152]{2,1,0:T(8,128)(2,1)S(1)}, u32[]{:S(2)}, u32[]{:S(2)}) collective-permute-start(bf16[1,128,1152]{2,1,0:T(8,128)(2,1)S(1)} %attend_last.4.refs_9_), channel_id=1, source_target_pairs={{0,4},{4,0},{1,5},{5,1},{2,6},{6,2},{3,7},{7,3},{8,12},{12,8},{9,1... | collective-permute-start | bytes 884744 | tf_op jit(solution)/shard_map/ppermute | solution.py:540
  (21 other events, 46.3 us)

commit v11 on v9

--- a/solution.py
+++ b/solution.py
@@ -38,7 +38,7 @@
     low = (rest - mid.astype(jnp.float32)).astype(jnp.bfloat16)
     return hi, mid, low
 
-PROJECT_US, ATTEND_US, DECODE_US = 1, 3.4, 1
+PROJECT_US, ATTEND_US, DECODE_US = 1, 1.7, 1
 ATTEND_VMEM, PROJECT_VMEM, DECODE_VMEM = 24, 56, 24
 
 
@@ -621,17 +621,29 @@
         both,
     )
 
+    partner_first = attend(
+        partner_sees,
+        partner_queries,
+        prior_rings[0],
+        prior_rings,
+        (tuple(earlier_pairs(0)),),
+        own_state,
+        both,
+    )
+
     prior_up, prior_down = sides(stack_column(prior_rings, (decode_attention, rings[0])))
-    column = stack_column(rings, (own_state, partner_queries))
+    column = stack_column(rings, (own_state, partner_first))
     up, down = sides(column)
     partner_state = attend(
         partner_sees,
         partner_queries,
         prior_up,
-        [prior_up, prior_down] + prior_rings + rings,
-        (tuple(earlier_sides + earlier_pairs(2)[:4]), tuple(earlier_pairs(2)[4:] + pairs(6))),
-        column,
+        [prior_up, prior_down] + rings,
+        (tuple(earlier_sides), tuple(pairs(2))),
+        None,
         both,
+        state=partner_first,
+        before=[column],
     )
 
     pages = TOKENS // BLK

time: 92.7 us -> 98 us (1.057)
  waiting for transfers between devices: 10.2 us -> 21.6 us
  starting transfers between devices: 33.2 us -> 28.5 us
  Pallas kernels: 44.5 us -> 43.5 us
    ppermute x12, waiting for transfers between devices: 7.46 us -> 15.1 us  [shift(): return lax.ppermute(x, 'ctx', perm)]
    ppermute x12, starting transfers between devices: 24.5 us -> 19.8 us  [shift(): return lax.ppermute(x, 'ctx', perm)]
    ppermute x3, waiting for transfers between devices: 0.01 us -> 2.68 us  [swap_pool(): return lax.ppermute(x, 'pool', [(0, 1), (1, 0)])]
    ppermute x2, waiting for transfers between devices: 2.73 us -> 3.78 us  [swap_tp(): return lax.ppermute(x, 'tp', [(i, i ^ bit) for i in range(4)])]
    pallas_call x5 -> x6, Pallas kernels: 29.7 us -> 29.4 us  [attend(): pl.pallas_call(functools.partial(attend_kernel, heads, len(pieces), block...]
  transfers between devices with their start and end apart: 17 -> 17, of which waited for: 3 -> 8; matrix products, arithmetic and copies ran while one was open for 2% -> 2% of each run, Pallas kernels for 33% -> 30%
where the time goes in v11:
time: 98 us; the launch traced here: 97.9 us
  Pallas kernels  43.5 us (44%)
  starting transfers between devices  28.5 us (29%)
  waiting for transfers between devices  21.6 us (22%)
  other arithmetic  1.7 us (2%)
  between operations  1.46 us (1%)
  local copies, waits for them, and re-layouts  1.15 us (1%)
    pallas_call x6, Pallas kernels, attend(): pl.pallas_call(functools.partial(attend_kernel, heads, len(pieces), block...  29.4 us
    ppermute x12, starting transfers between devices, shift(): return lax.ppermute(x, 'ctx', perm)  19.8 us
    ppermute x12, waiting for transfers between devices, shift(): return lax.ppermute(x, 'ctx', perm)  15.1 us
    pallas_call x1, Pallas kernels, project(): pl.pallas_call(project_kernel, in_specs=[far] * 7, out_specs=[far] * 2, o...  8.63 us
    ppermute x3, starting transfers between devices, swap_pool(): return lax.ppermute(x, 'pool', [(0, 1), (1, 0)])  7.01 us
    ppermute x2, waiting for transfers between devices, swap_tp(): return lax.ppermute(x, 'tp', [(i, i ^ bit) for i in range(4)])  3.78 us
    pallas_call x1, Pallas kernels, decode_attend(): pl.pallas_call(decode_kernel, grid_spec=pltpu.PrefetchScalarGridSpec(num_...  2.88 us
    ppermute x3, waiting for transfers between devices, swap_pool(): return lax.ppermute(x, 'pool', [(0, 1), (1, 0)])  2.68 us
  transfers between devices with their start and end apart: 17, of which 8 were waited for; matrix products, arithmetic and copies ran while one was open for 2% of the time, Pallas kernels for 30%

profile of v11, /device:TPU:0, one launch (start us, length us, event | category | flops | bytes accessed | tf_op | source)
XLA Modules:
  0.0 97.9 jit_solution(9494114081438009339)
XLA Ops:
  0.6 8.6 %project.1 = (f32[4,192,256]{2,1,0:T(8,128)}, f32[4,192,256]{2,1,0:T(8,128)}) custom-call(s32[16]{0:T(128)} %refs_4_.1, s32[1,128]{1,0:T(1,128)} %bitcast.40, bf16[128,2048]{1,0:T(8,128)(2,1)} %span_ref.1, bf16[16,4,2048]{2,1,0:T(4,128)(2,1)} %decode_ref.1, bf16[2048,2048]{1,0:T(8,128)(2,1)} %weight_ref.1, bf16[2048,128]{1,0:T(8,128)(2,1)} %down_ref.1, ...), custom_call_target="tpu_custom_call" | custom-call | flops 1100000000 | bytes 1048576 | tf_op jit(solution)/shard_map/project/pallas_call | solution.py:137
  9.4 4.0 %collective-permute-start = (bf16[2,128,256]{2,1,0:T(8,128)(2,1)S(1)}, bf16[2,128,256]{2,1,0:T(8,128)(2,1)S(1)}, u32[]{:S(2)}, u32[]{:S(2)}) collective-permute-start(bf16[2,128,256]{2,1,0:T(8,128)(2,1)S(1)} %copy-done.6), channel_id=1, source_target_pairs={{0,64},{8,72},{16,80},{24,88},{32,96},{40,104},{48,112},{56,120},{... | collective-permute-start | bytes 393224 | tf_op jit(solution)/shard_map/ppermute | solution.py:534
  14.8 1.6 %collective-permute-start.5 = (f32[2,192,256]{2,1,0:T(8,128)S(1)}, f32[2,192,256]{2,1,0:T(8,128)S(1)}, u32[]{:S(2)}, u32[]{:S(2)}) collective-permute-start(f32[2,192,256]{2,1,0:T(8,128)S(1)} %get-tuple-element.21), channel_id=1, source_target_pairs={{0,2},{1,3},{2,0},{3,1},{4,6},{5,7},{6,4},{7,5},{8,10},{9,11},{10,... | collective-permute-start | bytes 1179656 | tf_op jit(solution)/shard_map/ppermute | solution.py:542
  17.5 3.1 %collective-permute-start.3 = (bf16[2,2,128,256]{3,2,1,0:T(8,128)(2,1)S(1)}, bf16[2,2,128,256]{3,2,1,0:T(8,128)(2,1)S(1)}, u32[]{:S(2)}, u32[]{:S(2)}) collective-permute-start(bf16[2,2,128,256]{3,2,1,0:T(8,128)(2,1)S(1)} %pad_maximum_fusion.refs_0_.known_ref), channel_id=1, source_target_pairs={{0,24},{8,0},{16,8},{24,16},{32,56},{40,32},{48,40},{56,48},{64,88... | collective-permute-start | bytes 786440 | tf_op jit(solution)/shard_map/ppermute | solution.py:534
  22.2 3.8 %collective-permute-done.5.chip_ref = f32[2,192,256]{2,1,0:T(8,128)S(1)} collective-permute-done((f32[2,192,256]{2,1,0:T(8,128)S(1)}, f32[2,192,256]{2,1,0:T(8,128)S(1)}, u32[]{:S(2)}, u32[]{:S(2)}) %collective-permute-start.5) | collective-permute-done | bytes 393248 | tf_op jit(solution)/shard_map/ppermute | solution.py:542
  26.1 3.1 %collective-permute-start.11 = (bf16[128,2048]{1,0:T(8,128)(2,1)S(1)}, bf16[128,2048]{1,0:T(8,128)(2,1)S(1)}, u32[]{:S(2)}, u32[]{:S(2)}) collective-permute-start(bf16[128,2048]{1,0:T(8,128)(2,1)S(1)} %get-tuple-element.16), channel_id=1, source_target_pairs={{0,4},{4,0},{1,5},{5,1},{2,6},{6,2},{3,7},{7,3},{8,12},{12,8},{9,1... | collective-permute-start | bytes 1572872 | tf_op jit(solution)/shard_map/ppermute | solution.py:538
  30.1 2.4 %collective-permute-start.6 = (bf16[2,128,256]{2,1,0:T(8,128)(2,1)S(1)}, bf16[2,128,256]{2,1,0:T(8,128)(2,1)S(1)}, u32[]{:S(2)}, u32[]{:S(2)}) collective-permute-start(bf16[2,128,256]{2,1,0:T(8,128)(2,1)S(1)} %get-tuple-element.15), channel_id=1, source_target_pairs={{0,64},{8,72},{16,80},{24,88},{32,96},{40,104},{48,112},{56,120},{... | collective-permute-start | bytes 393224 | tf_op jit(solution)/shard_map/ppermute | solution.py:534
  32.5 3.1 %collective-permute-done.1.refs_1_ = bf16[2,2,128,256]{3,2,1,0:T(8,128)(2,1)S(1)} collective-permute-done((bf16[2,2,128,256]{3,2,1,0:T(8,128)(2,1)S(1)}, bf16[2,2,128,256]{3,2,1,0:T(8,128)(2,1)S(1)}, u32[]{:S(2)}, u32[]{:S(2)}) %collective-permute-start.1) | collective-permute-done | bytes 262176 | tf_op jit(solution)/shard_map/ppermute | solution.py:534
  35.5 3.7 %attend_first.3.refs_4_.refs_8_ = f32[2,1024,256]{2,1,0:T(8,128)S(1)} custom-call(s32[16]{0:T(128)S(1)} %reshape.348.visible_ref, bf16[128,2048]{1,0:T(8,128)(2,1)S(1)} %copy-done.5, bf16[2,2,128,256]{3,2,1,0:T(8,128)(2,1)S(1)} %pad_maximum_fusion.refs_0_.known_ref, bf16[2,2,128,256]{3,2,1,0:T(8,128)(2,1)S(1)} %pad_maximum_fusion.refs_0_.known_ref, ...), custom_call_target="tpu_custom_call" | custom-call | flops 1870000000 | bytes 1048576 | tf_op jit(solution)/shard_map/attend_first/pallas_call | solution.py:358
  41.4 2.9 %decode.1.refs_4_ = bf16[16,4,2048]{2,1,0:T(4,128)(2,1)} custom-call(s32[16]{0:T(128)S(1)} %copy-done.3, s32[1]{0:T(128)S(6)} %copy.17.live_ref, bf16[16,4,2048]{2,1,0:T(4,128)(2,1)S(1)} %copy-done.2, bf16[16,2,256,256]{3,2,1,0:T(8,128)(2,1)S(1)} %copy-done, bf16[2,64,256]{2,1,0:T(8,128)(2,1)S(1)} %get-tuple-element.14.fresh_ref), custom_call_target="tpu_custom_call" | custom-call | flops 1100000000 | bytes 1048576 | tf_op jit(solution)/shard_map/decode/pallas_call | solution.py:492
  45.3 3.3 %collective-permute-start.14 = (bf16[4,2,128,256]{3,2,1,0:T(8,128)(2,1)S(1)}, bf16[4,2,128,256]{3,2,1,0:T(8,128)(2,1)S(1)}, u32[]{:S(2)}, u32[]{:S(2)}) collective-permute-start(bf16[4,2,128,256]{3,2,1,0:T(8,128)(2,1)S(1)} %stack.34), channel_id=1, source_target_pairs={{0,96},{8,104},{16,112},{24,120},{32,0},{40,8},{48,16},{56,24},{64... | collective-permute-start | bytes 1572872 | tf_op jit(solution)/shard_map/ppermute | solution.py:534
  48.6 3.7 %attend_first.4.refs_5_.refs_6_ = f32[2,1024,256]{2,1,0:T(8,128)S(1)} custom-call(s32[16]{0:T(128)S(1)} %reshape.349.visible_ref, bf16[128,2048]{1,0:T(8,128)(2,1)S(1)} %collective-permute-done.11.q_ref, bf16[2,2,128,256]{3,2,1,0:T(8,128)(2,1)S(1)} %pad_maximum_fusion.refs_0_.known_ref, bf16[2,2,128,256]{3,2,1,0:T(8,128)(2,1)S(1)} %pad_maximum_fusion.refs_0_.known_ref, ...), custom_call_target="tpu_custom_call" | custom-call | flops 1870000000 | bytes 1048576 | tf_op jit(solution)/shard_map/attend_first/pallas_call | solution.py:358
  52.3 2.5 %collective-permute-done.8.refs_1_.refs_3_.refs_6_ = bf16[2,2,128,256]{3,2,1,0:T(8,128)(2,1)S(1)} collective-permute-done((bf16[2,2,128,256]{3,2,1,0:T(8,128)(2,1)S(1)}, bf16[2,2,128,256]{3,2,1,0:T(8,128)(2,1)S(1)}, u32[]{:S(2)}, u32[]{:S(2)}) %collective-permute-start.8) | collective-permute-done | bytes 262176 | tf_op jit(solution)/shard_map/ppermute | solution.py:534
  54.8 3.3 %collective-permute-start.13 = (bf16[4,2,128,256]{3,2,1,0:T(8,128)(2,1)S(1)}, bf16[4,2,128,256]{3,2,1,0:T(8,128)(2,1)S(1)}, u32[]{:S(2)}, u32[]{:S(2)}) collective-permute-start(bf16[4,2,128,256]{3,2,1,0:T(8,128)(2,1)S(1)} %stack.35.refs_7_.refs_4_), channel_id=1, source_target_pairs={{0,96},{8,104},{16,112},{24,120},{32,0},{40,8},{48,16},{56,24},{64... | collective-permute-start | bytes 1572872 | tf_op jit(solution)/shard_map/ppermute | solution.py:534
  58.1 2.2 %collective-permute-done.14.refs_1_.refs_7_ = bf16[4,2,128,256]{3,2,1,0:T(8,128)(2,1)S(1)} collective-permute-done((bf16[4,2,128,256]{3,2,1,0:T(8,128)(2,1)S(1)}, bf16[4,2,128,256]{3,2,1,0:T(8,128)(2,1)S(1)}, u32[]{:S(2)}, u32[]{:S(2)}) %collective-permute-start.14) | collective-permute-done | bytes 524320 | tf_op jit(solution)/shard_map/ppermute | solution.py:534
  60.4 3.4 %collective-permute-done.7.known_ref.refs_0_.refs_6_ = bf16[4,2,128,256]{3,2,1,0:T(8,128)(2,1)S(1)} collective-permute-done((bf16[4,2,128,256]{3,2,1,0:T(8,128)(2,1)S(1)}, bf16[4,2,128,256]{3,2,1,0:T(8,128)(2,1)S(1)}, u32[]{:S(2)}, u32[]{:S(2)}) %collective-permute-start.7) | collective-permute-done | bytes 524320 | tf_op jit(solution)/shard_map/ppermute | solution.py:534
  63.8 7.2 %attend_first.5.refs_2_ = f32[2,1024,256]{2,1,0:T(8,128)S(1)} custom-call(s32[16]{0:T(128)S(1)} %reshape.349.visible_ref, bf16[128,2048]{1,0:T(8,128)(2,1)S(1)} %collective-permute-done.11.q_ref, bf16[4,2,128,256]{3,2,1,0:T(8,128)(2,1)S(1)} %collective-permute-done.7.known_ref.refs_0_.refs_6_, ...), custom_call_target="tpu_custom_call" | custom-call | flops 3740000000 | bytes 1048576 | tf_op jit(solution)/shard_map/attend_first/pallas_call | solution.py:358
  71.0 3.0 %collective-permute-done.12.refs_0_ = bf16[4,2,128,256]{3,2,1,0:T(8,128)(2,1)S(1)} collective-permute-done((bf16[4,2,128,256]{3,2,1,0:T(8,128)(2,1)S(1)}, bf16[4,2,128,256]{3,2,1,0:T(8,128)(2,1)S(1)}, u32[]{:S(2)}, u32[]{:S(2)}) %collective-permute-start.12) | collective-permute-done | bytes 524320 | tf_op jit(solution)/shard_map/ppermute | solution.py:534
  74.0 2.7 %attend_last.3 = (bf16[1,128,1664]{2,1,0:T(8,128)(2,1)S(1)}, bf16[8,2,16,256]{3,2,1,0:T(8,128)(2,1)S(1)}) custom-call(s32[16]{0:T(128)S(1)} %reshape.349.visible_ref, bf16[128,2048]{1,0:T(8,128)(2,1)S(1)} %collective-permute-done.11.q_ref, bf16[4,2,128,256]{3,2,1,0:T(8,128)(2,1)S(1)} %collective-permute-done.7.known_ref.refs_0_.refs_6_, ...), custom_call_target="tpu_custom_call" | custom-call | flops 935000000 | bytes 1048576 | tf_op jit(solution)/shard_map/attend_last/pallas_call | solution.py:358
  76.7 3.1 %collective-permute-start.15 = (bf16[1,128,1664]{2,1,0:T(8,128)(2,1)S(1)}, bf16[1,128,1664]{2,1,0:T(8,128)(2,1)S(1)}, u32[]{:S(2)}, u32[]{:S(2)}) collective-permute-start(bf16[1,128,1664]{2,1,0:T(8,128)(2,1)S(1)} %get-tuple-element.17.refs_3_), channel_id=1, source_target_pairs={{0,4},{4,0},{1,5},{5,1},{2,6},{6,2},{3,7},{7,3},{8,12},{12,8},{9,1... | collective-permute-start | bytes 1277960 | tf_op jit(solution)/shard_map/ppermute | solution.py:538
  79.8 2.6 %attend_last.4.refs_9_ = bf16[1,128,1152]{2,1,0:T(8,128)(2,1)S(1)} custom-call(s32[16]{0:T(128)S(1)} %reshape.349.visible_ref, bf16[128,2048]{1,0:T(8,128)(2,1)S(1)} %collective-permute-done.11.q_ref, bf16[4,2,128,256]{3,2,1,0:T(8,128)(2,1)S(1)} %collective-permute-done.7.known_ref.refs_0_.refs_6_, ...), custom_call_target="tpu_custom_call" | custom-call | flops 935000000 | bytes 1048576 | tf_op jit(solution)/shard_map/attend_last/pallas_call | solution.py:358
  83.2 9.5 %attend_last.5.own_ref = f32[2,128,1152]{2,1,0:T(8,128)S(1)} custom-call(s32[16]{0:T(128)S(1)} %reshape.348.visible_ref, bf16[128,2048]{1,0:T(8,128)(2,1)S(1)} %copy-done.5, bf16[4,2,128,256]{3,2,1,0:T(8,128)(2,1)S(1)} %collective-permute-done.7.known_ref.refs_0_.refs_6_, bf16[4,2,128,256]{3,2,1,0:T(8,128)(2,1)S(1)} %collective-permute-done.12.refs_0_, ...), custom_call_target="tpu_custom_call" | custom-call | flops 5609999872 | bytes 1048576 | tf_op jit(solution)/shard_map/attend_last/pallas_call | solution.py:358
  92.8 2.7 %collective-permute-done.16.second_ref = bf16[1,128,1152]{2,1,0:T(8,128)(2,1)S(1)} collective-permute-done((bf16[1,128,1152]{2,1,0:T(8,128)(2,1)S(1)}, bf16[1,128,1152]{2,1,0:T(8,128)(2,1)S(1)}, u32[]{:S(2)}, u32[]{:S(2)}) %collective-permute-start.16) | collective-permute-done | bytes 294944 | tf_op jit(solution)/shard_map/ppermute | solution.py:538
  95.4 2.4 %combine.1 = (bf16[128,2048]{1,0:T(8,128)(2,1)}, bf16[8,2,16,256]{3,2,1,0:T(8,128)(2,1)}) custom-call(s32[4,16]{1,0:T(4,128)S(1)} %pad_add_fusion.refs_3_.where_ref, f32[2,128,1152]{2,1,0:T(8,128)S(1)} %attend_last.5.own_ref, bf16[1,128,1664]{2,1,0:T(8,128)(2,1)S(1)} %collective-permute-done.15.first_ref, ...), custom_call_target="tpu_custom_call" | custom-call | flops 1100000000 | bytes 1048576 | tf_op jit(solution)/shard_map/combine/pallas_call | solution.py:415
  (51 shorter events, 8.5 us)
Async XLA Ops:
  0.6 8.8 %copy-start.6 = (bf16[2,128,256]{2,1,0:T(8,128)(2,1)S(1)}, bf16[2,128,256]{2,1,0:T(8,128)(2,1)}, u32[]{:S(2)}) copy-start(bf16[2,128,256]{2,1,0:T(8,128)(2,1)} %param.16) | copy-start | bytes 393220
  9.3 7.2 %copy-start.7 = (s32[256]{0:T(256)S(1)}, s32[256]{0:T(256)}, u32[]{:S(2)}) copy-start(s32[256]{0:T(256)} %param.27) | copy-start | bytes 3076
  9.3 16.7 %copy-start.5 = (bf16[128,2048]{1,0:T(8,128)(2,1)S(1)}, bf16[128,2048]{1,0:T(8,128)(2,1)}, u32[]{:S(2)}) copy-start(bf16[128,2048]{1,0:T(8,128)(2,1)} %q_ref.5) | copy-start | bytes 1572868
  9.3 4.2 %collective-permute-start.4 = (f32[4,192,256]{2,1,0:T(8,128)}, f32[4,192,256]{2,1,0:T(8,128)S(1)}, u32[]{:S(2)}, u32[]{:S(2)}) collective-permute-start(f32[4,192,256]{2,1,0:T(8,128)} %get-tuple-element.13), channel_id=1, source_target_pairs={{0,1},{1,0},{2,3},{3,2},{4,5},{5,4},{6,7},{7,6},{8,9},{9,8},{10,11... | collective-permute-start | bytes 2359304 | tf_op jit(solution)/shard_map/ppermute | solution.py:542
  9.4 8.1 %collective-permute-start = (bf16[2,128,256]{2,1,0:T(8,128)(2,1)S(1)}, bf16[2,128,256]{2,1,0:T(8,128)(2,1)S(1)}, u32[]{:S(2)}, u32[]{:S(2)}) collective-permute-start(bf16[2,128,256]{2,1,0:T(8,128)(2,1)S(1)} %copy-done.6), channel_id=1, source_target_pairs={{0,64},{8,72},{16,80},{24,88},{32,96},{40,104},{48,112},{56,120},{... | collective-permute-start | bytes 393224 | tf_op jit(solution)/shard_map/ppermute | solution.py:534
  13.5 22.0 %copy-start.4 = (s32[16]{0:T(128)S(1)}, s32[16]{0:T(128)}, u32[]{:S(2)}) copy-start(s32[16]{0:T(128)} %refs_4_.1) | copy-start | bytes 196
  14.8 11.2 %collective-permute-start.5 = (f32[2,192,256]{2,1,0:T(8,128)S(1)}, f32[2,192,256]{2,1,0:T(8,128)S(1)}, u32[]{:S(2)}, u32[]{:S(2)}) collective-permute-start(f32[2,192,256]{2,1,0:T(8,128)S(1)} %get-tuple-element.21), channel_id=1, source_target_pairs={{0,2},{1,3},{2,0},{3,1},{4,6},{5,7},{6,4},{7,5},{8,10},{9,11},{10,... | collective-permute-start | bytes 1179656 | tf_op jit(solution)/shard_map/ppermute | solution.py:542
  17.5 14.9 %collective-permute-start.3 = (bf16[2,2,128,256]{3,2,1,0:T(8,128)(2,1)S(1)}, bf16[2,2,128,256]{3,2,1,0:T(8,128)(2,1)S(1)}, u32[]{:S(2)}, u32[]{:S(2)}) collective-permute-start(bf16[2,2,128,256]{3,2,1,0:T(8,128)(2,1)S(1)} %pad_maximum_fusion.refs_0_.known_ref), channel_id=1, source_target_pairs={{0,24},{8,0},{16,8},{24,16},{32,56},{40,32},{48,40},{56,48},{64,88... | collective-permute-start | bytes 786440 | tf_op jit(solution)/shard_map/ppermute | solution.py:534
  20.6 11.8 %collective-permute-start.2 = (bf16[2,2,128,256]{3,2,1,0:T(8,128)(2,1)S(1)}, bf16[2,2,128,256]{3,2,1,0:T(8,128)(2,1)S(1)}, u32[]{:S(2)}, u32[]{:S(2)}) collective-permute-start(bf16[2,2,128,256]{3,2,1,0:T(8,128)(2,1)S(1)} %pad_maximum_fusion.refs_0_.known_ref), channel_id=1, source_target_pairs={{0,16},{8,24},{16,0},{24,8},{32,48},{40,56},{48,32},{56,40},{64,80... | collective-permute-start | bytes 786440 | tf_op jit(solution)/shard_map/ppermute | solution.py:534
  21.3 14.3 %collective-permute-start.1 = (bf16[2,2,128,256]{3,2,1,0:T(8,128)(2,1)S(1)}, bf16[2,2,128,256]{3,2,1,0:T(8,128)(2,1)S(1)}, u32[]{:S(2)}, u32[]{:S(2)}) collective-permute-start(bf16[2,2,128,256]{3,2,1,0:T(8,128)(2,1)S(1)} %pad_maximum_fusion.refs_0_.known_ref), channel_id=1, source_target_pairs={{0,8},{8,16},{16,24},{24,0},{32,40},{40,48},{48,56},{56,32},{64,72... | collective-permute-start | bytes 786440 | tf_op jit(solution)/shard_map/ppermute | solution.py:534
  26.1 22.4 %collective-permute-start.11 = (bf16[128,2048]{1,0:T(8,128)(2,1)S(1)}, bf16[128,2048]{1,0:T(8,128)(2,1)S(1)}, u32[]{:S(2)}, u32[]{:S(2)}) collective-permute-start(bf16[128,2048]{1,0:T(8,128)(2,1)S(1)} %get-tuple-element.16), channel_id=1, source_target_pairs={{0,4},{4,0},{1,5},{5,1},{2,6},{6,2},{3,7},{7,3},{8,12},{12,8},{9,1... | collective-permute-start | bytes 1572872 | tf_op jit(solution)/shard_map/ppermute | solution.py:538
  30.1 11.3 %copy-start = (bf16[16,2,256,256]{3,2,1,0:T(8,128)(2,1)S(1)}, bf16[16,2,256,256]{3,2,1,0:T(8,128)(2,1)}, u32[]{:S(2)}) copy-start(bf16[16,2,256,256]{3,2,1,0:T(8,128)(2,1)} %cache_ref.1) | copy-start | bytes 12582916
  30.1 11.3 %copy-start.2 = (bf16[16,4,2048]{2,1,0:T(4,128)(2,1)S(1)}, bf16[16,4,2048]{2,1,0:T(4,128)(2,1)}, u32[]{:S(2)}) copy-start(bf16[16,4,2048]{2,1,0:T(4,128)(2,1)} %q_ref.3) | copy-start | bytes 786436
  30.1 11.3 %copy-start.3 = (s32[16]{0:T(128)S(1)}, s32[16]{0:T(128)}, u32[]{:S(2)}) copy-start(s32[16]{0:T(128)} %length_ref.1) | copy-start | bytes 196
  30.1 9.1 %collective-permute-start.6 = (bf16[2,128,256]{2,1,0:T(8,128)(2,1)S(1)}, bf16[2,128,256]{2,1,0:T(8,128)(2,1)S(1)}, u32[]{:S(2)}, u32[]{:S(2)}) collective-permute-start(bf16[2,128,256]{2,1,0:T(8,128)(2,1)S(1)} %get-tuple-element.15), channel_id=1, source_target_pairs={{0,64},{8,72},{16,80},{24,88},{32,96},{40,104},{48,112},{56,120},{... | collective-permute-start | bytes 393224 | tf_op jit(solution)/shard_map/ppermute | solution.py:534
  39.3 13.0 %collective-permute-start.10 = (bf16[2,2,128,256]{3,2,1,0:T(8,128)(2,1)S(1)}, bf16[2,2,128,256]{3,2,1,0:T(8,128)(2,1)S(1)}, u32[]{:S(2)}, u32[]{:S(2)}) collective-permute-start(bf16[2,2,128,256]{3,2,1,0:T(8,128)(2,1)S(1)} %pad_maximum_fusion.1.refs_5_.refs_0_.refs_2_), channel_id=1, source_target_pairs={{0,24},{8,0},{16,8},{24,16},{32,56},{40,32},{48,40},{56,48},{64,88... | collective-permute-start | bytes 786440 | tf_op jit(solution)/shard_map/ppermute | solution.py:534
  39.9 12.3 %collective-permute-start.9 = (bf16[2,2,128,256]{3,2,1,0:T(8,128)(2,1)S(1)}, bf16[2,2,128,256]{3,2,1,0:T(8,128)(2,1)S(1)}, u32[]{:S(2)}, u32[]{:S(2)}) collective-permute-start(bf16[2,2,128,256]{3,2,1,0:T(8,128)(2,1)S(1)} %pad_maximum_fusion.1.refs_5_.refs_0_.refs_2_), channel_id=1, source_target_pairs={{0,16},{8,24},{16,0},{24,8},{32,48},{40,56},{48,32},{56,40},{64,80... | collective-permute-start | bytes 786440 | tf_op jit(solution)/shard_map/ppermute | solution.py:534
  40.6 14.2 %collective-permute-start.8 = (bf16[2,2,128,256]{3,2,1,0:T(8,128)(2,1)S(1)}, bf16[2,2,128,256]{3,2,1,0:T(8,128)(2,1)S(1)}, u32[]{:S(2)}, u32[]{:S(2)}) collective-permute-start(bf16[2,2,128,256]{3,2,1,0:T(8,128)(2,1)S(1)} %pad_maximum_fusion.1.refs_5_.refs_0_.refs_2_), channel_id=1, source_target_pairs={{0,8},{8,16},{16,24},{24,0},{32,40},{40,48},{48,56},{56,32},{64,72... | collective-permute-start | bytes 786440 | tf_op jit(solution)/shard_map/ppermute | solution.py:534
  45.3 15.1 %collective-permute-start.14 = (bf16[4,2,128,256]{3,2,1,0:T(8,128)(2,1)S(1)}, bf16[4,2,128,256]{3,2,1,0:T(8,128)(2,1)S(1)}, u32[]{:S(2)}, u32[]{:S(2)}) collective-permute-start(bf16[4,2,128,256]{3,2,1,0:T(8,128)(2,1)S(1)} %stack.34), channel_id=1, source_target_pairs={{0,96},{8,104},{16,112},{24,120},{32,0},{40,8},{48,16},{56,24},{64... | collective-permute-start | bytes 1572872 | tf_op jit(solution)/shard_map/ppermute | solution.py:534
  48.6 15.2 %collective-permute-start.7 = (bf16[4,2,128,256]{3,2,1,0:T(8,128)(2,1)S(1)}, bf16[4,2,128,256]{3,2,1,0:T(8,128)(2,1)S(1)}, u32[]{:S(2)}, u32[]{:S(2)}) collective-permute-start(bf16[4,2,128,256]{3,2,1,0:T(8,128)(2,1)S(1)} %stack.34), channel_id=1, source_target_pairs={{0,32},{8,40},{16,48},{24,56},{32,64},{40,72},{48,80},{56,88},{64,... | collective-permute-start | bytes 1572872 | tf_op jit(solution)/shard_map/ppermute | solution.py:534
  54.8 16.2 %collective-permute-start.13 = (bf16[4,2,128,256]{3,2,1,0:T(8,128)(2,1)S(1)}, bf16[4,2,128,256]{3,2,1,0:T(8,128)(2,1)S(1)}, u32[]{:S(2)}, u32[]{:S(2)}) collective-permute-start(bf16[4,2,128,256]{3,2,1,0:T(8,128)(2,1)S(1)} %stack.35.refs_7_.refs_4_), channel_id=1, source_target_pairs={{0,96},{8,104},{16,112},{24,120},{32,0},{40,8},{48,16},{56,24},{64... | collective-permute-start | bytes 1572872 | tf_op jit(solution)/shard_map/ppermute | solution.py:534
  58.1 15.9 %collective-permute-start.12 = (bf16[4,2,128,256]{3,2,1,0:T(8,128)(2,1)S(1)}, bf16[4,2,128,256]{3,2,1,0:T(8,128)(2,1)S(1)}, u32[]{:S(2)}, u32[]{:S(2)}) collective-permute-start(bf16[4,2,128,256]{3,2,1,0:T(8,128)(2,1)S(1)} %stack.35.refs_7_.refs_4_), channel_id=1, source_target_pairs={{0,32},{8,40},{16,48},{24,56},{32,64},{40,72},{48,80},{56,88},{64,... | collective-permute-start | bytes 1572872 | tf_op jit(solution)/shard_map/ppermute | solution.py:534
  76.7 18.7 %collective-permute-start.15 = (bf16[1,128,1664]{2,1,0:T(8,128)(2,1)S(1)}, bf16[1,128,1664]{2,1,0:T(8,128)(2,1)S(1)}, u32[]{:S(2)}, u32[]{:S(2)}) collective-permute-start(bf16[1,128,1664]{2,1,0:T(8,128)(2,1)S(1)} %get-tuple-element.17.refs_3_), channel_id=1, source_target_pairs={{0,4},{4,0},{1,5},{5,1},{2,6},{6,2},{3,7},{7,3},{8,12},{12,8},{9,1... | collective-permute-start | bytes 1277960 | tf_op jit(solution)/shard_map/ppermute | solution.py:538
  82.4 13.0 %collective-permute-start.16 = (bf16[1,128,1152]{2,1,0:T(8,128)(2,1)S(1)}, bf16[1,128,1152]{2,1,0:T(8,128)(2,1)S(1)}, u32[]{:S(2)}, u32[]{:S(2)}) collective-permute-start(bf16[1,128,1152]{2,1,0:T(8,128)(2,1)S(1)} %attend_last.4.refs_9_), channel_id=1, source_target_pairs={{0,4},{4,0},{1,5},{5,1},{2,6},{6,2},{3,7},{7,3},{8,12},{12,8},{9,1... | collective-permute-start | bytes 884744 | tf_op jit(solution)/shard_map/ppermute | solution.py:538
  (1 other events, 0.9 us)
